TPU v7x, 32 devices: a whole 2x2x4 slice. The times are simulated.
32 devices in a mesh: fsdp: 2 (over core), ctx: 4 (over z), tp: 4 (over y, x).
Axes of the slice: x: 2, y: 2, z: 4, core: 2. Of those that a mesh axis runs over, the one named last changes fastest.
Arguments:
- inputs: bfloat16 [8, 1024, 1152], P('fsdp', 'ctx'), may hold values from -6 to 6
- target: bfloat16 [8, 1024, 1152], P('fsdp', 'ctx'), may hold values from -6 to 6
- segment_ids: int32 [8, 1024], P('fsdp', 'ctx'), may hold values from 0 to 16, as said below
- w_query: bfloat16 [1152, 1024], P(('fsdp', 'ctx'), 'tp'), may hold values from -0.1875 to 0.1875
- w_key: bfloat16 [1152, 256], P(('fsdp', 'ctx')), may hold values from -0.1875 to 0.1875
- w_value: bfloat16 [1152, 256], P(('fsdp', 'ctx')), may hold values from -0.1875 to 0.1875
- w_out: bfloat16 [1024, 1152], P('tp', ('fsdp', 'ctx')), may hold values from -0.1875 to 0.1875
- w_gate: bfloat16 [1152, 6912], P(('fsdp', 'ctx'), 'tp'), may hold values from -0.1875 to 0.1875
- w_up: bfloat16 [1152, 6912], P(('fsdp', 'ctx'), 'tp'), may hold values from -0.1875 to 0.1875
- w_down: bfloat16 [6912, 1152], P('tp', ('fsdp', 'ctx')), may hold values from -0.078125 to 0.078125
- gain_input: bfloat16 [1152], P(('fsdp', 'ctx')), may hold values from 0.5 to 1.5
- gain_query: bfloat16 [256], P(('fsdp', 'ctx')), may hold values from 0.5 to 1.5
- gain_key: bfloat16 [256], P(('fsdp', 'ctx')), may hold values from 0.5 to 1.5
- gain_post_attn: bfloat16 [1152], P(('fsdp', 'ctx')), may hold values from 0.5 to 1.5
- gain_pre_ffn: bfloat16 [1152], P(('fsdp', 'ctx')), may hold values from 0.5 to 1.5
- gain_post_ffn: bfloat16 [1152], P(('fsdp', 'ctx')), may hold values from 0.5 to 1.5
Outputs:
- output: bfloat16 [8, 1024, 1152], P('fsdp', ('ctx', 'tp'))
- loss: float32 [], replicated
- grad_input: float32 [8, 1024, 1152], P('fsdp', ('ctx', 'tp'))
- grad_query: float32 [1152, 1024], P(('fsdp', 'ctx'), 'tp')
- grad_key: float32 [1152, 256], P(('fsdp', 'ctx'))
- grad_value: float32 [1152, 256], P(('fsdp', 'ctx'))
- grad_out: float32 [1024, 1152], P('tp', ('fsdp', 'ctx'))
- grad_gate: float32 [1152, 6912], P(('fsdp', 'ctx'), 'tp')
- grad_up: float32 [1152, 6912], P(('fsdp', 'ctx'), 'tp')
- grad_down: float32 [6912, 1152], P('tp', ('fsdp', 'ctx'))
- grad_gain_input: float32 [1152], P(('fsdp', 'ctx'))
- grad_gain_query: float32 [256], P(('fsdp', 'ctx'))
- grad_gain_key: float32 [256], P(('fsdp', 'ctx'))
- grad_gain_post_attn: float32 [1152], P(('fsdp', 'ctx'))
- grad_gain_pre_ffn: float32 [1152], P(('fsdp', 'ctx'))
- grad_gain_post_ffn: float32 [1152], P(('fsdp', 'ctx'))
Inputs may be any that keep to these rules, and one draw needn't show every extreme that they name: `segment_ids`: in each sequence the nonzero ids number its 16 documents from 1 in order of position, each document a contiguous run of positions; padding (0) stands only after the last document.
All inputs are finite; a program needn't handle non-finite values.
Results may differ from a plain program's by a relative error of at most 0.018.
Values may be sent and summed in bfloat16 or wider, within the bound.
No kernel may reach another device: no remote copies, remote signals or barrier semaphores. Data moves between devices by JAX's collectives and lax.ppermute only.
A program may use at most 192 MiB of HBM per device.

v0:
```python
import jax
import jax.numpy as jnp
from jax import lax
from jax.sharding import PartitionSpec as P

WIN = 512
DOCS = 16


epsilon = 1e-06
masked_score = -1e30
far_position = 1 << 30


def carried_in(part, axis, combine, identity):
    place = lax.axis_index(axis)
    gathered = lax.all_gather(part, axis)
    state = jnp.zeros_like(part) + jnp.asarray(identity, part.dtype)

    def one(step, state):
        return combine(state, lax.dynamic_index_in_dim(gathered, step, 0, False))

    return lax.fori_loop(0, place, one, state)


def shifted(shard, axis, by):
    size = lax.axis_size(axis)
    pairs = [(i, i + by) for i in range(size) if 0 <= i + by < size]
    return lax.ppermute(shard, axis, pairs)


def rms_norm(values, gain_row):
    return (
        values * lax.rsqrt(jnp.mean(values * values, axis=-1, keepdims=True) + epsilon) * gain_row
    )


def turn_half(values):
    half_width = values.shape[-1] // 2
    return jnp.concatenate([-values[..., half_width:], values[..., :half_width]], axis=-1)


def rotary_tables(positions, head_width):
    frequency = 10000.0 ** (-2.0 * jnp.arange(head_width // 2, dtype=jnp.float32) / head_width)
    angles = positions.astype(jnp.float32)[:, None] * frequency[None, :]
    angles = jnp.concatenate([angles, angles], axis=-1)
    return (jnp.cos(angles), jnp.sin(angles))


def head_finish(values, gain_row, cos_table, sin_table, factor):
    normed = rms_norm(values, gain_row)
    return (normed * cos_table + turn_half(normed) * sin_table) * factor


def gated_units(gate, up_proj):
    return jax.nn.gelu(gate, approximate=True) * up_proj


def reduce_full(partial_sum):
    return lax.psum(partial_sum, "tp")


def shards(
    inputs,
    target,
    segment_ids,
    w_query,
    w_key,
    w_value,
    w_out,
    w_gate,
    w_up,
    w_down,
    gain_input,
    gain_query,
    gain_key,
    gain_post_attn,
    gain_pre_ffn,
    gain_post_ffn,
):
    gathered = (
        lax.all_gather(w_query, ("fsdp", "ctx"), axis=0, tiled=True),
        lax.all_gather(w_key, ("fsdp", "ctx"), axis=0, tiled=True),
        lax.all_gather(w_value, ("fsdp", "ctx"), axis=0, tiled=True),
        lax.all_gather(w_out, ("fsdp", "ctx"), axis=1, tiled=True),
        lax.all_gather(w_gate, ("fsdp", "ctx"), axis=0, tiled=True),
        lax.all_gather(w_up, ("fsdp", "ctx"), axis=0, tiled=True),
        lax.all_gather(w_down, ("fsdp", "ctx"), axis=1, tiled=True),
        lax.all_gather(gain_input, ("fsdp", "ctx"), axis=0, tiled=True),
        lax.all_gather(gain_query, ("fsdp", "ctx"), axis=0, tiled=True),
        lax.all_gather(gain_key, ("fsdp", "ctx"), axis=0, tiled=True),
        lax.all_gather(gain_post_attn, ("fsdp", "ctx"), axis=0, tiled=True),
        lax.all_gather(gain_pre_ffn, ("fsdp", "ctx"), axis=0, tiled=True),
        lax.all_gather(gain_post_ffn, ("fsdp", "ctx"), axis=0, tiled=True),
    )
    full_query, full_key, full_value, full_out, full_gate, full_up, full_down = gathered[:7]
    g_input, g_query, g_key, g_post_attn, g_pre_ffn, g_post_ffn = [
        gain_shard.astype(jnp.float32) for gain_shard in gathered[7:]
    ]
    seq_count, block_rows, width_model = inputs.shape
    head_width = full_query.shape[1]
    rows_total = seq_count * block_rows
    tp_count = lax.axis_size("tp")
    quarter = block_rows // tp_count
    tp_pos = lax.axis_index("tp")

    def own_rows(values):
        return lax.dynamic_slice_in_dim(values, tp_pos * quarter, quarter, 1)

    halo_blocks = -(-(WIN - 1) // block_rows)
    span_rows = (halo_blocks + 1) * block_rows
    block_index = lax.axis_index("ctx")
    positions = block_index * block_rows + jnp.arange(block_rows, dtype=jnp.int32)
    key_positions = (
        block_index * block_rows - halo_blocks * block_rows + jnp.arange(span_rows, dtype=jnp.int32)
    )
    cos_table, sin_table = rotary_tables(positions, head_width)
    cos_table = jnp.tile(cos_table, (seq_count, 1))
    sin_table = jnp.tile(sin_table, (seq_count, 1))
    doc_numbers = jnp.arange(DOCS + 1, dtype=jnp.int32)
    matches = segment_ids[:, :, None] == doc_numbers[None, None, :]
    first_own = jnp.min(jnp.where(matches, positions[None, :, None], far_position), axis=1)
    earlier = carried_in(first_own, "ctx", jnp.minimum, jnp.full_like(first_own, far_position))
    first_seen = jnp.minimum(earlier, first_own)
    doc_start = jnp.sum(jnp.where(matches, first_seen[:, None, :], 0), axis=2)
    x_whole = inputs.astype(jnp.float32)
    normed_f, back_input = jax.vjp(rms_norm, x_whole, g_input)
    normed = normed_f.astype(jnp.bfloat16).reshape(rows_total, width_model)
    query_f = jnp.dot(normed, full_query, preferred_element_type=jnp.float32)
    key_f = jnp.dot(normed, full_key, preferred_element_type=jnp.float32)
    value_low = jnp.dot(normed, full_value, preferred_element_type=jnp.float32).astype(jnp.bfloat16)
    query_scale = head_width ** (-0.5)
    query_rot_f, back_query = jax.vjp(
        lambda values, gain_row: head_finish(values, gain_row, cos_table, sin_table, query_scale),
        query_f,
        g_query,
    )
    key_rot_f, back_key = jax.vjp(
        lambda values, gain_row: head_finish(values, gain_row, cos_table, sin_table, 1.0),
        key_f,
        g_key,
    )
    query_rot = query_rot_f.astype(jnp.bfloat16).reshape(seq_count, block_rows, head_width)
    key_rot = key_rot_f.astype(jnp.bfloat16)
    own_pair = jnp.stack([key_rot, value_low]).reshape(2, seq_count, block_rows, head_width)
    pieces = []
    for distance in range(halo_blocks, 0, -1):
        pieces.append(shifted(own_pair, "ctx", distance))
    pair_rows = jnp.concatenate(pieces + [own_pair], axis=2)
    key_rows = pair_rows[0]
    value_rows = pair_rows[1]
    allowed = (
        (key_positions[None, None, :] >= doc_start[:, :, None])
        & (key_positions[None, None, :] <= positions[None, :, None])
        & (key_positions[None, None, :] > positions[None, :, None] - WIN)
    )

    def score_block():
        raw_scores = jnp.einsum(
            "sqd,skd->sqk", query_rot, key_rows, preferred_element_type=jnp.float32
        )
        return jnp.where(allowed, raw_scores, masked_score)

    scores = score_block()
    row_top = jnp.max(scores, axis=-1, keepdims=True)
    expos = jnp.exp(scores - row_top)
    row_total = jnp.sum(expos, axis=-1, keepdims=True)
    log_total = row_top + jnp.log(row_total)
    prob_low = (expos / row_total).astype(jnp.bfloat16)
    attended = (
        jnp.einsum("sqk,skd->sqd", prob_low, value_rows, preferred_element_type=jnp.float32)
        .astype(jnp.bfloat16)
        .reshape(rows_total, head_width)
    )
    branch_part = jnp.dot(attended, full_out, preferred_element_type=jnp.float32).reshape(
        seq_count, block_rows, width_model
    )
    valid_all = (segment_ids != 0).astype(jnp.float32)
    target_rows = target.astype(jnp.float32)
    branch = reduce_full(branch_part)
    post_attn, back_post_attn = jax.vjp(rms_norm, branch, g_post_attn)
    hidden = x_whole + post_attn
    ffn_f, back_pre_ffn = jax.vjp(rms_norm, hidden, g_pre_ffn)
    ffn_low = ffn_f.astype(jnp.bfloat16)
    ffn_in = ffn_low.reshape(rows_total, width_model)
    gate = jnp.dot(ffn_in, full_gate, preferred_element_type=jnp.float32)
    up_proj = jnp.dot(ffn_in, full_up, preferred_element_type=jnp.float32)
    act_f, back_act = jax.vjp(gated_units, gate, up_proj)
    act_low = act_f.astype(jnp.bfloat16)
    ffn_part = jnp.dot(act_low, full_down, preferred_element_type=jnp.float32).reshape(
        seq_count, block_rows, width_model
    )
    ffn_out = reduce_full(ffn_part)
    post_ffn, back_post_ffn = jax.vjp(rms_norm, ffn_out, g_post_ffn)
    result = hidden + post_ffn
    mismatch = result - target_rows
    err_local = jnp.sum(valid_all[:, :, None] * mismatch * mismatch) * (quarter / result.shape[1])
    count_local = jnp.sum(valid_all) / tp_count
    err_total, count_total = lax.psum((err_local, count_local), ("fsdp", "ctx", "tp"))
    loss = err_total / (2.0 * width_model * count_total)
    all_tokens = seq_count * block_rows * lax.axis_size("fsdp") * lax.axis_size("ctx")
    d_result = all_tokens / count_total * valid_all[:, :, None] * mismatch
    d_ffn_out, grad_post_ffn = back_post_ffn(d_result)
    d_ffn_share = d_ffn_out.astype(jnp.bfloat16)
    d_ffn_low = d_ffn_share.reshape(rows_total, width_model)
    grad_down = jnp.einsum("nf,nd->fd", act_low, d_ffn_low, preferred_element_type=jnp.float32)
    d_act = jnp.einsum("nd,fd->nf", d_ffn_low, full_down, preferred_element_type=jnp.float32)
    d_gate, d_up = back_act(d_act)
    d_gate_low = d_gate.astype(jnp.bfloat16)
    d_up_low = d_up.astype(jnp.bfloat16)
    grad_gate = jnp.einsum("nd,nf->df", ffn_in, d_gate_low, preferred_element_type=jnp.float32)
    grad_up = jnp.einsum("nd,nf->df", ffn_in, d_up_low, preferred_element_type=jnp.float32)
    d_ffn_part = (
        jnp.einsum("nf,df->nd", d_gate_low, full_gate, preferred_element_type=jnp.float32)
        + jnp.einsum("nf,df->nd", d_up_low, full_up, preferred_element_type=jnp.float32)
    ).reshape(seq_count, block_rows, width_model)
    d_ffn_in = reduce_full(d_ffn_part)
    d_hidden_add, grad_pre_ffn = back_pre_ffn(d_ffn_in)
    d_hidden = d_result + d_hidden_add
    d_branch, grad_post_attn = back_post_attn(d_hidden)
    d_branch_share = d_branch.astype(jnp.bfloat16)
    d_branch_low = d_branch_share.reshape(rows_total, width_model)
    grad_out = jnp.einsum("nh,nd->hd", attended, d_branch_low, preferred_element_type=jnp.float32)
    d_attended = (
        jnp.einsum("nd,hd->nh", d_branch_low, full_out, preferred_element_type=jnp.float32)
        .astype(jnp.bfloat16)
        .reshape(seq_count, block_rows, head_width)
    )
    scores = score_block()
    prob_f = jnp.where(allowed, jnp.exp(scores - log_total), 0.0)
    prob_low = prob_f.astype(jnp.bfloat16)
    d_prob = jnp.einsum("sqd,skd->sqk", d_attended, value_rows, preferred_element_type=jnp.float32)
    d_value_rows = jnp.einsum(
        "sqk,sqd->skd", prob_low, d_attended, preferred_element_type=jnp.float32
    )
    row_delta = jnp.sum(prob_f * d_prob, axis=-1, keepdims=True)
    d_scores = (prob_f * (d_prob - row_delta)).astype(jnp.bfloat16)
    d_query_rot = jnp.einsum("sqk,skd->sqd", d_scores, key_rows, preferred_element_type=jnp.float32)
    d_key_rows = jnp.einsum("sqk,sqd->skd", d_scores, query_rot, preferred_element_type=jnp.float32)
    d_pair = jnp.stack([d_key_rows, d_value_rows])
    own_grad = d_pair[:, :, halo_blocks * block_rows :]
    for distance in range(1, halo_blocks + 1):
        grad_piece = d_pair[
            :, :, (halo_blocks - distance) * block_rows : (halo_blocks - distance + 1) * block_rows
        ]
        own_grad = own_grad + shifted(grad_piece, "ctx", -distance)
    d_query, grad_query_gain = back_query(d_query_rot.reshape(rows_total, head_width))
    key_sum, value_sum, query_gain_sum = lax.psum(
        (
            own_grad[0].reshape(rows_total, head_width),
            own_grad[1].reshape(rows_total, head_width),
            grad_query_gain,
        ),
        "tp",
    )
    d_key, grad_key_gain = back_key(key_sum)
    d_query_low = d_query.astype(jnp.bfloat16)
    d_key_low = d_key.astype(jnp.bfloat16)
    d_value_low = value_sum.astype(jnp.bfloat16)
    grad_query = jnp.einsum("nd,nh->dh", normed, d_query_low, preferred_element_type=jnp.float32)
    grad_key = jnp.einsum("nd,nh->dh", normed, d_key_low, preferred_element_type=jnp.float32)
    grad_value = jnp.einsum("nd,nh->dh", normed, d_value_low, preferred_element_type=jnp.float32)
    d_normed_part = jnp.einsum(
        "nh,dh->nd", d_query_low, full_query, preferred_element_type=jnp.float32
    ).reshape(seq_count, block_rows, width_model)
    key_grad3 = d_key_low.reshape(seq_count, block_rows, head_width)
    value_grad3 = d_value_low.reshape(seq_count, block_rows, head_width)
    d_normed_heads = reduce_full(d_normed_part)
    d_normed = (
        d_normed_heads
        + jnp.einsum("sqh,dh->sqd", key_grad3, full_key, preferred_element_type=jnp.float32)
        + jnp.einsum("sqh,dh->sqd", value_grad3, full_value, preferred_element_type=jnp.float32)
    )
    d_input_add, grad_input_gain = back_input(d_normed)
    grad_input = d_hidden + d_input_add
    all_shards = (
        lax.psum_scatter(grad_query, ("fsdp", "ctx"), scatter_dimension=0, tiled=True),
        lax.psum_scatter(grad_key, ("fsdp", "ctx"), scatter_dimension=0, tiled=True),
        lax.psum_scatter(grad_value, ("fsdp", "ctx"), scatter_dimension=0, tiled=True),
        lax.psum_scatter(grad_out, ("fsdp", "ctx"), scatter_dimension=1, tiled=True),
        lax.psum_scatter(grad_gate, ("fsdp", "ctx"), scatter_dimension=0, tiled=True),
        lax.psum_scatter(grad_up, ("fsdp", "ctx"), scatter_dimension=0, tiled=True),
        lax.psum_scatter(grad_down, ("fsdp", "ctx"), scatter_dimension=1, tiled=True),
        lax.psum_scatter(grad_input_gain, ("fsdp", "ctx"), scatter_dimension=0, tiled=True),
        lax.psum_scatter(query_gain_sum, ("fsdp", "ctx"), scatter_dimension=0, tiled=True),
        lax.psum_scatter(grad_key_gain, ("fsdp", "ctx"), scatter_dimension=0, tiled=True),
        lax.psum_scatter(grad_post_attn, ("fsdp", "ctx"), scatter_dimension=0, tiled=True),
        lax.psum_scatter(grad_pre_ffn, ("fsdp", "ctx"), scatter_dimension=0, tiled=True),
        lax.psum_scatter(grad_post_ffn, ("fsdp", "ctx"), scatter_dimension=0, tiled=True),
    )
    shard_query, shard_key, shard_value, shard_out, shard_gate, shard_up, shard_down = all_shards[
        :7
    ]
    shard_input, shard_qgain, shard_kgain, shard_post_attn, shard_pre_ffn, shard_post_ffn = (
        all_shards[7:]
    )
    output = own_rows(result).astype(jnp.bfloat16)
    grad_input_out = own_rows(grad_input)
    return (
        output,
        loss,
        grad_input_out,
        shard_query,
        shard_key,
        shard_value,
        shard_out,
        shard_gate,
        shard_up,
        shard_down,
        shard_input,
        shard_qgain,
        shard_kgain,
        shard_post_attn,
        shard_pre_ffn,
        shard_post_ffn,
    )


def solution(mesh):
    return jax.shard_map(
        shards,
        mesh=mesh,
        in_specs=(
            P("fsdp", "ctx", None),
            P("fsdp", "ctx", None),
            P("fsdp", "ctx"),
            P(("fsdp", "ctx"), "tp"),
            P(("fsdp", "ctx"), None),
            P(("fsdp", "ctx"), None),
            P("tp", ("fsdp", "ctx")),
            P(("fsdp", "ctx"), "tp"),
            P(("fsdp", "ctx"), "tp"),
            P("tp", ("fsdp", "ctx")),
            P(("fsdp", "ctx")),
            P(("fsdp", "ctx")),
            P(("fsdp", "ctx")),
            P(("fsdp", "ctx")),
            P(("fsdp", "ctx")),
            P(("fsdp", "ctx")),
        ),
        out_specs=(
            P("fsdp", ("ctx", "tp"), None),
            P(),
            P("fsdp", ("ctx", "tp"), None),
            P(("fsdp", "ctx"), "tp"),
            P(("fsdp", "ctx"), None),
            P(("fsdp", "ctx"), None),
            P("tp", ("fsdp", "ctx")),
            P(("fsdp", "ctx"), "tp"),
            P(("fsdp", "ctx"), "tp"),
            P("tp", ("fsdp", "ctx")),
            P(("fsdp", "ctx")),
            P(("fsdp", "ctx")),
            P(("fsdp", "ctx")),
            P(("fsdp", "ctx")),
            P(("fsdp", "ctx")),
            P(("fsdp", "ctx")),
        ),
        check_vma=False,
    )
```

profile of v0, /device:TPU:0, one launch (start us, length us, event | category | flops | bytes accessed | tf_op | source)
XLA Modules:
  0.0 1551.2 jit_solution(6100341030211792133)
XLA Ops:
  8.1 1.4 fusion.55
  15.9 30.8 %all-reduce.18 = (bf16[1152]{0:T(1024)(128)(2,1)S(1)}, bf16[256]{0:T(256)(128)(2,1)S(1)}, bf16[256]{0:T(256)(128)(2,1)S(1)}, bf16[1152]{0:T(1024)(128)(2,1)}, bf...) all-reduce(bf16[1152]{0:T(1024)(128)(2,1)S(1)} %dynamic-update-slic, ...), channel_id=1, replica_groups=mesh['fsdp'=2,'ctx'=4,'tp'=4] {'fsdp','ctx'}, use_global_device_ids=true, to_apply=%add.4 | all-reduce | flops 5120 | bytes 20480
  46.7 2.2 multiply_reduce_fusion.11
  49.5 26.9 %all_gather.48 = bf16[1152,256]{1,0:T(8,128)(2,1)S(1)} all-gather(bf16[144,256]{1,0:T(8,128)(2,1)} %param.21), channel_id=1, replica_groups=mesh['fsdp'=2,'ctx'=4,'tp'=4] {'fsdp','ctx'}, dimensions={0}, use_global_device_ids=true | all-gather | bytes 663552 | tf_op jit(solution)/shard_map/all_gather | solution.py:82
  78.0 26.5 %all_gather.50 = bf16[1152,256]{1,0:T(8,128)(2,1)S(1)} all-gather(bf16[144,256]{1,0:T(8,128)(2,1)S(1)} %copy-done.59), channel_id=1, replica_groups=mesh['fsdp'=2,'ctx'=4,'tp'=4] {'fsdp','ctx'}, dimensions={0}, use_global_device_ids=true | all-gather | bytes 663552 | tf_op jit(solution)/shard_map/all_gather | solution.py:83
  110.2 26.9 %all_gather.52 = bf16[1152,256]{1,0:T(8,128)(2,1)S(1)} all-gather(bf16[144,256]{1,0:T(8,128)(2,1)S(1)} %copy-done.60), channel_id=1, replica_groups=mesh['fsdp'=2,'ctx'=4,'tp'=4] {'fsdp','ctx'}, dimensions={0}, use_global_device_ids=true | all-gather | bytes 663552 | tf_op jit(solution)/shard_map/all_gather | solution.py:84
  137.1 2.7 convolution_convert_fusion.1
  139.9 1.2 fusion.28
  143.0 3.8 collective-permute-start
  146.8 3.9 collective-permute-start.1
  151.2 70.3 %all-gather.1 = s32[4,4,17]{2,1,0:T(4,128)S(1)} all-gather(s32[1,4,17]{2,1,0:T(4,128)S(1)} %bitcast.163), channel_id=2, replica_groups=mesh['fsdp'=2,'ctx'=4,'tp'=4] {'ctx'}, dimensions={0}, use_global_device_ids=true | all-gather | bytes 1360 | tf_op jit(solution)/shard_map/all_gather | solution.py:17
  222.1 26.0 %all_gather.53 = bf16[256,1152]{0,1:T(8,128)(2,1)S(1)} all-gather(bf16[256,144]{0,1:T(8,128)(2,1)S(1)} %copy-done.61), channel_id=1, replica_groups=mesh['fsdp'=2,'ctx'=4,'tp'=4] {'fsdp','ctx'}, dimensions={1}, use_global_device_ids=true | all-gather | bytes 663552 | tf_op jit(solution)/shard_map/all_gather | solution.py:85
  248.1 2.2 maximum_maximum_fusion
  254.4 3.0 fusion.35
  259.3 109.5 %all-reduce.25.cloned.1.call-done = f32[4,256,1152]{2,1,0:T(8,128)} async-done(((f32[4,256,1152]{2,1,0:T(8,128)}), f32[4,256,1152]{2,1,0:T(8,128)}) %all-reduce.25.cloned.1.call-update) | async-done | bytes 4718608 | tf_op jit(solution)/shard_map/psum | solution.py:60
  368.7 2.9 multiply_reduce_fusion.10
  373.8 2.2 copy-done
  376.5 9.9 fusion.57
  386.4 12.3 multiply_convert_fusion.1
  398.7 10.4 fusion.58
  410.4 40.1 %psum.66 = f32[]{:T(128)} all-reduce(f32[]{:T(128)S(6)} %div.105), channel_id=1, replica_groups=mesh['fsdp'=2,'ctx'=4,'tp'=4] {'fsdp','ctx','tp'}, use_global_device_ids=true, to_apply=%region_17.18 | all-reduce | flops 1 | bytes 8 | tf_op jit(solution)/shard_map/psum | solution.py:199
  451.3 71.1 %all-reduce.27.cloned.1.call-done = f32[4,256,1152]{2,1,0:T(8,128)} async-done(((f32[4,256,1152]{2,1,0:T(8,128)}), f32[4,256,1152]{2,1,0:T(8,128)}) %all-reduce.27.cloned.1.call-update) | async-done | bytes 4718608 | tf_op jit(solution)/shard_map/psum | solution.py:60
  522.3 2.9 multiply_reduce_fusion.8
  526.1 5.5 multiply_reduce_fusion
  531.6 1.5 fusion.8
  534.0 2.3 copy-done.72
  536.3 15.3 multiply_convert_fusion
  551.7 7.2 fusion.59
  558.9 6.9 convolution_add_fusion.2
  565.8 112.6 %all-reduce.29.cloned.1.call-done = f32[4,256,1152]{2,1,0:T(8,128)} async-done(((f32[4,256,1152]{2,1,0:T(8,128)}), f32[4,256,1152]{2,1,0:T(8,128)}) %all-reduce.29.cloned.1.call-update) | async-done | bytes 4718608 | tf_op jit(solution)/shard_map/psum | solution.py:60
  678.4 5.1 multiply_reduce_fusion.1
  683.6 7.0 multiply_reduce_fusion.2
  694.7 1.5 convolution_bitcast_fusion.1
  696.2 1.5 multiply_reduce_fusion.12
  697.6 1.4 multiply_convert_fusion.4
  700.2 1.4 collective-permute-start.2
  701.7 1.4 collective-permute-start.3
  704.8 3.0 fusion.60
  707.9 42.0 %collective-permute-done.2 = f32[2,4,256,256]{3,2,1,0:T(8,128)S(1)} collective-permute-done((f32[2,4,256,256]{3,2,1,0:T(8,128)S(1)}, f32[2,4,256,256]{3,2,1,0:T(8,128)S(1)}, u32[]{:S(2)}, u32[]{:S(2)}) %collective-permute-start.2) | collective-permute-done | bytes 2097184 | tf_op jit(solution)/shard_map/ppermute | solution.py:29
  749.8 90.6 %collective-permute-done.3 = f32[2,4,256,256]{3,2,1,0:T(8,128)S(1)} collective-permute-done((f32[2,4,256,256]{3,2,1,0:T(8,128)S(1)}, f32[2,4,256,256]{3,2,1,0:T(8,128)S(1)}, u32[]{:S(2)}, u32[]{:S(2)}) %collective-permute-start.3) | collective-permute-done | bytes 2097184 | tf_op jit(solution)/shard_map/ppermute | solution.py:29
  840.8 1.5 fusion.52
  842.4 3.1 convolution_bitcast_fusion
  845.9 3.7 fusion.61
  849.6 63.1 %all-reduce.32 = bf16[1024,256]{1,0:T(8,128)(2,1)S(1)} all-reduce(f32[1024,256]{1,0:T(8,128)S(1)} %bitcast.143), channel_id=1, replica_groups=mesh['fsdp'=2,'ctx'=4,'tp'=4] {'tp'}, use_global_device_ids=true, to_apply=%region_27.28 | all-reduce | flops 262144 | bytes 1572864 | tf_op jit(solution)/shard_map/psum | solution.py:248
  912.7 3.7 fusion.63
  916.5 78.2 %all-reduce.31.cloned.1.call-done = (f32[4,256,1152]{2,1,0:T(8,128)}, f32[1024,256]{1,0:T(8,128)}) async-done(((f32[4,256,1152]{2,1,0:T(8,128)}, f32[1024,256]{1,0:T(8,128)}), (f32[4,256,1152]{2,1,0:T(8,128)}, f32[1024,256]{1,0:T(8,128)})) %all-reduce.31.cloned.1.call-update) | async-done | bytes 5767184 | tf_op jit(solution)/shard_map/psum | solution.py:60
  994.8 1.4 bitcast_multiply_fusion
  998.1 1.9 fusion.62
  1000.0 8.6 fusion.66
  1008.7 1.6 copy-done.42
  1010.3 8.6 fusion.64
  1018.9 8.6 fusion.65
  1027.6 1.6 copy-done.3
  1029.2 2.4 convert_element_type.91
  1034.4 43.6 %psum.65 = f32[]{:T(128)} all-reduce(f32[]{:T(128)S(6)} %mul.516), channel_id=1, replica_groups=mesh['fsdp'=2,'ctx'=4,'tp'=4] {'fsdp','ctx','tp'}, use_global_device_ids=true, to_apply=%region_15.16 | all-reduce | flops 1 | bytes 8 | tf_op jit(solution)/shard_map/psum | solution.py:199
  1078.6 2.2 dynamic-slice_convert_fusion
  1080.8 3.3 convolution_add_fusion.1
  1084.2 3.5 multiply_reduce_fusion.3
  1087.6 36.7 %all-reduce.16 = (f32[1152]{0:T(1024)S(1)}, f32[256]{0:T(256)S(1)}, f32[256]{0:T(256)S(1)}, f32[1152]{0:T(1024)S(1)}, f32[1152]{0:T(1024)S(1)}, /*index=5*/f32[1152]{0:T(1024)S(1)}) all-reduce(f32[1152]{0:T(1024)S(1)} %get-tuple-element.47, ...), channel_id=10, replica_groups=mesh['fsdp'=2,'ctx'=4,'tp'=4] {'fsdp','ctx'}, use_global_device_ids=true, to_apply=%region_37.38.clone | all-reduce | flops 5120 | bytes 40960
  1127.6 10.9 psum.72
  1138.5 3.3 fusion.23
  1141.8 64.1 %reduce-scatter.20.cloned.1.call-done = f32[1728,144]{0,1:T(8,128)} async-done(((f32[1728,1152]{0,1:T(8,128)}), f32[1728,144]{0,1:T(8,128)}) %reduce-scatter.20.cloned.1.call-update) | async-done | bytes 995344 | tf_op jit(solution)/shard_map/reduce_scatter | solution.py:283
  1205.9 168.3 %reduce-scatter.16.cloned.1.call-done = f32[144,1728]{1,0:T(8,128)} async-done(((f32[1152,1728]{1,0:T(8,128)}), f32[144,1728]{1,0:T(8,128)}) %reduce-scatter.16.cloned.1.call-update) | async-done | bytes 995344 | tf_op jit(solution)/shard_map/reduce_scatter | solution.py:281
  1374.2 168.2 %reduce-scatter.18.cloned.1.call-done = f32[144,1728]{1,0:T(8,128)} async-done(((f32[1152,1728]{1,0:T(8,128)}), f32[144,1728]{1,0:T(8,128)}) %reduce-scatter.18.cloned.1.call-update) | async-done | bytes 995344 | tf_op jit(solution)/shard_map/reduce_scatter | solution.py:282
  (267 shorter events, 39.8 us)
Async XLA Ops:
  8.0 68.4 %copy-start.2 = (bf16[4,256,1152]{2,1,0:T(8,128)(2,1)S(1)}, bf16[4,256,1152]{2,1,0:T(8,128)(2,1)}, u32[]{:S(2)}) copy-start(bf16[4,256,1152]{2,1,0:T(8,128)(2,1)} %param.18) | copy-start | bytes 7077892
  8.0 360.7 %all-reduce.25.cloned.1.call-start = ((), (), s32[]{:S(2)}) async-start(), calls=%async_computation.7 | async-start | bytes 9437184 | tf_op jit(solution)/shard_map/psum | solution.py:60
  46.7 31.3 %copy-start.62 = (f32[1152]{0:T(1024)}, f32[1152]{0:T(1024)S(1)}, u32[]{:S(2)}) copy-start(f32[1152]{0:T(1024)S(1)} %convert_element_type.92) | copy-start | bytes 13828
  49.5 28.5 %copy-start.64 = (f32[4,256]{1,0:T(4,128)}, f32[4,256]{1,0:T(4,128)S(1)}, u32[]{:S(2)}) copy-start(f32[4,256]{1,0:T(4,128)S(1)} %fusion.41) | copy-start | bytes 12292
  77.0 28.5 %copy-start.37 = (bf16[4,256,1152]{2,1,0:T(8,128)(2,1)}, bf16[4,256,1152]{2,1,0:T(8,128)(2,1)S(1)}, u32[]{:S(2)}) copy-start(bf16[4,256,1152]{2,1,0:T(8,128)(2,1)S(1)} %multiply_convert_fusion.3) | copy-start | bytes 7077892
  78.0 27.9 %copy-start.11 = (f32[1024,256]{1,0:T(8,128)}, f32[1024,256]{1,0:T(8,128)S(1)}, u32[]{:S(2)}) copy-start(f32[1024,256]{1,0:T(8,128)S(1)} %get-tuple-element.107) | copy-start | bytes 3145732
  105.6 4.6 copy-start.60
  109.1 30.7 %copy-start.14 = (f32[1024,256]{1,0:T(8,128)S(1)}, f32[1024,256]{1,0:T(8,128)}, u32[]{:S(2)}) copy-start(f32[1024,256]{1,0:T(8,128)} %copy-done.13) | copy-start | bytes 3145732
  109.1 30.7 %copy-start.16 = (f32[1024,256]{1,0:T(8,128)S(1)}, f32[1024,256]{1,0:T(8,128)}, u32[]{:S(2)}) copy-start(f32[1024,256]{1,0:T(8,128)} %copy-done.15) | copy-start | bytes 3145732
  109.1 30.7 %copy-start.51 = (f32[1024,128]{1,0:T(8,128)S(1)}, f32[1024,128]{1,0:T(8,128)}, u32[]{:S(2)}) copy-start(f32[1024,128]{1,0:T(8,128)} %get-tuple-element.94) | copy-start | bytes 1572868
  109.2 30.7 %copy-start.52 = (f32[1024,128]{1,0:T(8,128)S(1)}, f32[1024,128]{1,0:T(8,128)}, u32[]{:S(2)}) copy-start(f32[1024,128]{1,0:T(8,128)} %get-tuple-element.95) | copy-start | bytes 1572868
  109.2 30.7 %copy-start.53 = (f32[1024,128]{1,0:T(8,128)S(1)}, f32[1024,128]{1,0:T(8,128)}, u32[]{:S(2)}) copy-start(f32[1024,128]{1,0:T(8,128)} %get-tuple-element.96) | copy-start | bytes 1572868
  109.2 30.7 %copy-start.54 = (f32[1024,128]{1,0:T(8,128)S(1)}, f32[1024,128]{1,0:T(8,128)}, u32[]{:S(2)}) copy-start(f32[1024,128]{1,0:T(8,128)} %get-tuple-element.97) | copy-start | bytes 1572868
  110.2 31.0 %copy-start.18 = (f32[256,256]{1,0:T(8,128)}, f32[256,256]{1,0:T(8,128)S(1)}, u32[]{:S(2)}) copy-start(f32[256,256]{1,0:T(8,128)S(1)} %get-tuple-element.100) | copy-start | bytes 786436
  110.2 31.0 %copy-start.21 = (f32[256,256]{1,0:T(8,128)}, f32[256,256]{1,0:T(8,128)S(1)}, u32[]{:S(2)}) copy-start(f32[256,256]{1,0:T(8,128)S(1)} %get-tuple-element.101) | copy-start | bytes 786436
  139.8 3.2 copy-start.47
  139.8 10.9 copy-start.68
  139.9 82.1 %copy-start.61 = (bf16[256,144]{0,1:T(8,128)(2,1)S(1)}, bf16[256,144]{0,1:T(8,128)(2,1)}, u32[]{:S(2)}) copy-start(bf16[256,144]{0,1:T(8,128)(2,1)} %param.24) | copy-start | bytes 221188
  143.0 105.1 %collective-permute-start = (bf16[2,4,256,256]{3,2,1,0:T(8,128)(2,1)}, bf16[2,4,256,256]{3,2,1,0:T(8,128)(2,1)}, u32[]{:S(2)}, u32[]{:S(2)}) collective-permute-start(bf16[2,4,256,256]{3,2,1,0:T(8,128)(2,1)} %pad_maximum_fusion.1), channel_id=1, source_target_pairs={{0,8},{4,12},{1,9},{5,13},{2,10},{6,14},{3,11},{7,15},{16,24},{20,... | collective-permute-start | bytes 3145736 | tf_op jit(solution)/shard_map/ppermute | solution.py:29
  146.8 101.2 %collective-permute-start.1 = (bf16[2,4,256,256]{3,2,1,0:T(8,128)(2,1)}, bf16[2,4,256,256]{3,2,1,0:T(8,128)(2,1)}, u32[]{:S(2)}, u32[]{:S(2)}) collective-permute-start(bf16[2,4,256,256]{3,2,1,0:T(8,128)(2,1)} %pad_maximum_fusion.1), channel_id=1, source_target_pairs={{0,4},{4,8},{8,12},{1,5},{5,9},{9,13},{2,6},{6,10},{10,14},{3,7},{... | collective-permute-start | bytes 3145736 | tf_op jit(solution)/shard_map/ppermute | solution.py:29
  221.6 28.6 %copy-start.48 = (bf16[1024,256]{1,0:T(8,128)(2,1)S(1)}, bf16[1024,256]{1,0:T(8,128)(2,1)}, u32[]{:S(2)}) copy-start(bf16[1024,256]{1,0:T(8,128)(2,1)} %get-tuple-element.98) | copy-start | bytes 1572868
  222.0 29.4 %copy-start.55 = (pred[256,768]{1,0:T(8,128)(4,1)}, pred[256,768]{1,0:T(8,128)(4,1)S(1)}, u32[]{:S(2)}) copy-start(pred[256,768]{1,0:T(8,128)(4,1)S(1)} %get-tuple-element.102) | copy-start | bytes 589828
  222.1 29.4 %copy-start.57 = (pred[256,768]{1,0:T(8,128)(4,1)}, pred[256,768]{1,0:T(8,128)(4,1)S(1)}, u32[]{:S(2)}) copy-start(pred[256,768]{1,0:T(8,128)(4,1)S(1)} %get-tuple-element.103) | copy-start | bytes 589828
  248.1 5.5 copy-start.39
  257.4 119.0 %all-gather.6.cloned.1.call-start = ((), (), s32[]{:S(2)}) async-start(), calls=%async_computation.8 | async-start | bytes 4644864 | tf_op jit(solution)/shard_map/all_gather | solution.py:86
  258.0 128.3 %all-gather.8.cloned.1.call-start = ((), (), s32[]{:S(2)}) async-start(), calls=%async_computation.9 | async-start | bytes 4644864 | tf_op jit(solution)/shard_map/all_gather | solution.py:87
  258.6 140.1 %all-gather.10.cloned.1.call-start = ((), (), s32[]{:S(2)}) async-start(), calls=%async_computation.10 | async-start | bytes 4644864 | tf_op jit(solution)/shard_map/all_gather | solution.py:88
  259.2 263.2 %all-reduce.27.cloned.1.call-start = ((), (), s32[]{:S(2)}) async-start(), calls=%async_computation.11 | async-start | bytes 9437184 | tf_op jit(solution)/shard_map/psum | solution.py:60
  368.7 3.8 copy-start.1
  376.4 9.9 copy-start.41
  409.1 116.1 %copy-start.7 = (bf16[4,256,1152]{2,1,0:T(8,128)(2,1)S(1)}, bf16[4,256,1152]{2,1,0:T(8,128)(2,1)}, u32[]{:S(2)}) copy-start(bf16[4,256,1152]{2,1,0:T(8,128)(2,1)} %param.19) | copy-start | bytes 7077892
  409.1 269.3 %all-reduce.29.cloned.1.call-start = ((), (), s32[]{:S(2)}) async-start(), calls=%async_computation.12 | async-start | bytes 9437184 | tf_op jit(solution)/shard_map/psum | solution.py:60
  522.3 3.8 copy-start.5
  531.6 4.7 copy-start.72
  534.0 17.6 %copy-start.35 = (bf16[4,256,1152]{2,1,0:T(8,128)(2,1)}, bf16[4,256,1152]{2,1,0:T(8,128)(2,1)S(1)}, u32[]{:S(2)}) copy-start(bf16[4,256,1152]{2,1,0:T(8,128)(2,1)S(1)} %fusion.8) | copy-start | bytes 7077892
  536.3 15.3 copy-start.70
  551.7 7.2 copy-start.71
  551.7 7.2 copy-start.73
  565.8 429.0 %all-reduce.31.cloned.1.call-start = ((), (), s32[]{:S(2)}) async-start(), calls=%async_computation.20 | async-start | bytes 11534336 | tf_op jit(solution)/shard_map/psum | solution.py:60
  678.4 5.1 copy-start.8
  678.4 12.2 slice-start
  683.6 7.1 slice-start.1
  700.2 3.5 copy-start.22
  700.2 49.6 %collective-permute-start.2 = (f32[2,4,256,256]{3,2,1,0:T(8,128)S(1)}, f32[2,4,256,256]{3,2,1,0:T(8,128)S(1)}, u32[]{:S(2)}, u32[]{:S(2)}) collective-permute-start(f32[2,4,256,256]{3,2,1,0:T(8,128)S(1)} %get-tuple-element.86), channel_id=1, source_target_pairs={{4,0},{8,4},{12,8},{5,1},{9,5},{13,9},{6,2},{10,6},{14,10},{7,3},{... | collective-permute-start | bytes 6291464 | tf_op jit(solution)/shard_map/ppermute | solution.py:29
  701.7 138.7 %collective-permute-start.3 = (f32[2,4,256,256]{3,2,1,0:T(8,128)S(1)}, f32[2,4,256,256]{3,2,1,0:T(8,128)S(1)}, u32[]{:S(2)}, u32[]{:S(2)}) collective-permute-start(f32[2,4,256,256]{3,2,1,0:T(8,128)S(1)} %get-tuple-element.87), channel_id=1, source_target_pairs={{8,0},{12,4},{9,1},{13,5},{10,2},{14,6},{11,3},{15,7},{24,16},{28,... | collective-permute-start | bytes 6291464 | tf_op jit(solution)/shard_map/ppermute | solution.py:29
  704.8 3.0 copy-start.26
  842.4 299.4 %reduce-scatter.14.cloned.1.call-start = ((), (), s32[]{:S(2)}) async-start(), calls=%async_computation.16 | async-start | bytes 1327104 | tf_op jit(solution)/shard_map/reduce_scatter | solution.py:280
  845.6 4.1 copy-start.25
  845.6 296.2 %reduce-scatter.8.cloned.1.call-start = ((), (), s32[]{:S(2)}) async-start(), calls=%async_computation.13 | async-start | bytes 1327104 | tf_op jit(solution)/shard_map/reduce_scatter | solution.py:277
  849.6 292.2 %reduce-scatter.12.cloned.1.call-start = ((), (), s32[]{:S(2)}) async-start(), calls=%async_computation.15 | async-start | bytes 1327104 | tf_op jit(solution)/shard_map/reduce_scatter | solution.py:279
  912.7 82.0 %copy-start.43 = (bf16[1024,256]{1,0:T(8,128)(2,1)}, bf16[1024,256]{1,0:T(8,128)(2,1)S(1)}, u32[]{:S(2)}) copy-start(bf16[1024,256]{1,0:T(8,128)(2,1)S(1)} %all-reduce.32) | copy-start | bytes 1572868
  912.7 82.0 %copy-start.23 = (f32[256,256]{1,0:T(8,128)S(1)}, f32[256,256]{1,0:T(8,128)}, u32[]{:S(2)}) copy-start(f32[256,256]{1,0:T(8,128)} %copy-done.21) | copy-start | bytes 786436
  916.5 79.8 %copy-start.20 = (f32[256,256]{1,0:T(8,128)S(1)}, f32[256,256]{1,0:T(8,128)}, u32[]{:S(2)}) copy-start(f32[256,256]{1,0:T(8,128)} %copy-done.18) | copy-start | bytes 786436
  916.5 225.3 %reduce-scatter.10.cloned.1.call-start = ((), (), s32[]{:S(2)}) async-start(), calls=%async_computation.14 | async-start | bytes 1327104 | tf_op jit(solution)/shard_map/reduce_scatter | solution.py:278
  1000.0 206.0 %reduce-scatter.20.cloned.1.call-start = ((), (), s32[]{:S(2)}) async-start(), calls=%async_computation.19 | async-start | bytes 9289728 | tf_op jit(solution)/shard_map/reduce_scatter | solution.py:283
  1008.6 365.6 %reduce-scatter.16.cloned.1.call-start = ((), (), s32[]{:S(2)}) async-start(), calls=%async_computation.17 | async-start | bytes 9289728 | tf_op jit(solution)/shard_map/reduce_scatter | solution.py:281
  1018.9 523.6 %reduce-scatter.18.cloned.1.call-start = ((), (), s32[]{:S(2)}) async-start(), calls=%async_computation.18 | async-start | bytes 9289728 | tf_op jit(solution)/shard_map/reduce_scatter | solution.py:282
  1027.6 5.4 copy-start.65
  1029.2 51.6 %copy-start.30 = (bf16[1152,256]{1,0:T(8,128)(2,1)S(1)}, bf16[1152,256]{1,0:T(8,128)(2,1)}, u32[]{:S(2)}) copy-start(bf16[1152,256]{1,0:T(8,128)(2,1)} %copy-done.29) | copy-start | bytes 1769476
  1029.2 51.6 %copy-start.46 = (bf16[1024,256]{1,0:T(8,128)(2,1)S(1)}, bf16[1024,256]{1,0:T(8,128)(2,1)}, u32[]{:S(2)}) copy-start(bf16[1024,256]{1,0:T(8,128)(2,1)} %copy-done.45) | copy-start | bytes 1572868
  1080.8 3.3 copy-start.32
  1080.8 3.3 copy-start.44
  1080.8 3.4 copy-start.63
  1084.2 54.3 %copy-start.67 = (f32[4,256]{1,0:T(4,128)S(1)}, f32[4,256]{1,0:T(4,128)}, u32[]{:S(2)}) copy-start(f32[4,256]{1,0:T(4,128)} %copy-done.66) | copy-start | bytes 12292
  (30 other events, 51.2 us)
Sparse Core Ops, SparseCore 0:
  257.6 111.1 all-reduce.24
  409.2 113.0 all-reduce.26
  565.9 112.4 all-reduce.28
  842.5 152.2 all-reduce.30
Sparse Core Ops, SparseCore 1:
  259.5 44.8 all-gather.5
  305.9 45.0 all-gather.7
  352.4 45.0 all-gather.9
  846.0 33.5 reduce-scatter.13
  882.5 35.7 reduce-scatter.7
  921.1 35.8 reduce-scatter.11
  1000.1 36.2 reduce-scatter.9
  1039.1 166.8 reduce-scatter.19
  1208.8 165.3 reduce-scatter.15
  1377.1 165.3 reduce-scatter.17
where the time goes:
time: 1560 us; the launch traced here: 1550 us
  waiting for transfers between devices  906 us (58%)
  blocking collectives  402 us (26%)
  matrix products  125 us (8%)
  other arithmetic  52.2 us (3%)
  local copies, waits for them, and re-layouts  30.5 us (2%)
  between operations  24.1 us (2%)
    psum x4, waiting for transfers between devices, reduce_full(): return lax.psum(partial_sum, 'tp')  371 us
    reduce_scatter x1, waiting for transfers between devices, shards(): lax.psum_scatter(grad_gate, ('fsdp', 'ctx'), scatter_dimension=0, tiled=T...  168 us
    reduce_scatter x1, waiting for transfers between devices, shards(): lax.psum_scatter(grad_up, ('fsdp', 'ctx'), scatter_dimension=0, tiled=True)  168 us
    ppermute x4, waiting for transfers between devices, shifted(): return lax.ppermute(shard, axis, pairs)  133 us
    psum x2, blocking collectives, shards(): lax.psum((err_local, count_local), ('fsdp', 'ctx', 'tp'))  83.7 us
    psum x2, blocking collectives, shards(): lax.psum((own_grad[0].reshape(rows_total, head_width), own_grad[1].reshap...  74 us
    all_gather x1, blocking collectives, carried_in(): gathered = lax.all_gather(part, axis)  70.3 us
    unnamed x2, blocking collectives  67.5 us
  transfers between devices with their start and end apart: 18, of which 9 were waited for; matrix products, arithmetic and copies ran while one was open for 6% of the time, Pallas kernels for 0%

commit v1 on v0

v1 whole, which is shorter than its diff:
```python
import functools

import jax
import jax.numpy as jnp
from jax import lax
from jax.experimental import pallas as pl
from jax.experimental.pallas import tpu as pltpu
from jax.sharding import PartitionSpec as P

WIN = 512
EPS = 1e-06
MASKED = -1e30
LOW = jnp.bfloat16
F32 = jnp.float32


def swap(values, axis, bits):
    return lax.ppermute(values, axis, [(i, i ^ bits) for i in range(lax.axis_size(axis))])


def shifted(values, axis, by):
    size = lax.axis_size(axis)
    return lax.ppermute(values, axis, [(i, i + by) for i in range(size) if 0 <= i + by < size])


def exchange(values, axes):
    return lax.all_to_all(values, axes, 0, 0, tiled=True)


def dot(left, right, contract):
    return lax.dot_general(left, right, (contract, ((), ())), preferred_element_type=F32)


def mm(left, right):
    return dot(left, right, ((1,), (0,)))


def mm_t(left, right):
    return dot(left, right, ((1,), (1,)))


def t_mm(left, right):
    return dot(left, right, ((0,), (0,)))


def inverse_rms(values):
    return lax.rsqrt(jnp.mean(values * values, axis=-1, keepdims=True) + EPS)


def rms_back(grad, values, inverse, gain_row):
    n = values * inverse
    eg = grad * gain_row
    return inverse * (eg - n * jnp.mean(eg * n, axis=-1, keepdims=True)), grad * n


def turn(values):
    half = values.shape[-1] // 2
    return jnp.concatenate([-values[..., half:], values[..., :half]], axis=-1)


def turn_back(values):
    half = values.shape[-1] // 2
    return jnp.concatenate([values[..., half:], -values[..., :half]], axis=-1)


def rotary_tables(positions, head_width):
    frequency = 10000.0 ** (-2.0 * jnp.arange(head_width // 2, dtype=F32) / head_width)
    angles = positions.astype(F32)[:, None] * frequency[None, :]
    angles = jnp.concatenate([angles, angles], axis=-1)
    return jnp.cos(angles), jnp.sin(angles)


def heads_of(values, heads):
    width = values.shape[1] // heads
    return [values[:, h * width : (h + 1) * width] for h in range(heads)]


def mask_of(qinfo_ref, kinfo_ref):
    qpos, qseg = qinfo_ref[0, :, 0:1], qinfo_ref[0, :, 1:2]
    kpos, kseg = kinfo_ref[0, 0:1, :], kinfo_ref[0, 1:2, :]
    return (kseg == qseg) & (kpos <= qpos) & (kpos > qpos - WIN)


def attend_kernel(heads, qinfo_ref, kinfo_ref, q_ref, gain_ref, cos_ref, sin_ref, kv_ref, rot_ref, out_ref, lse_ref):
    width = q_ref.shape[1] // heads
    scale = width ** (-0.5)
    spans = kv_ref.shape[0] * kv_ref.shape[2]
    rotated = []
    for h, q in enumerate(heads_of(q_ref[...], heads)):
        n = q * inverse_rms(q) * gain_ref[...]
        rot = ((n * cos_ref[...] + turn(n) * sin_ref[...]) * scale).astype(LOW)
        rot_ref[:, h * width : (h + 1) * width] = rot
        rotated.append(rot)
    rows = jnp.concatenate(rotated, axis=0)
    keys = kv_ref[:, 0, :, :width].reshape(spans, width)
    vals = kv_ref[:, 0, :, width:].reshape(spans, width)
    bias = jnp.where(mask_of(qinfo_ref, kinfo_ref), 0.0, MASKED)
    allowed = jnp.concatenate([bias] * heads, axis=0) == 0.0
    scores = jnp.where(allowed, mm_t(rows, keys), MASKED)
    top = jnp.max(scores, axis=1, keepdims=True)
    expos = jnp.exp(scores - top)
    total = jnp.sum(expos, axis=1, keepdims=True)
    lse_ref[0] = top + jnp.log(total)
    probs = (expos / total).astype(LOW)
    attended = mm(probs, vals).astype(LOW)
    count = q_ref.shape[0]
    for h in range(heads):
        out_ref[:, h * width : (h + 1) * width] = attended[h * count : (h + 1) * count]


def attend_back_kernel(heads, chunks, qinfo_ref, kinfo_ref, q_ref, gain_ref, cos_ref, sin_ref, kv_ref, rot_ref, lse_ref, dout_ref,
                       dq_ref, dgain_ref, *dkv_refs):
    width = q_ref.shape[1] // heads
    scale = width ** (-0.5)
    spans = kv_ref.shape[0] * kv_ref.shape[2]
    count = q_ref.shape[0]
    rows = jnp.concatenate(heads_of(rot_ref[...], heads), axis=0)
    douts = jnp.concatenate(heads_of(dout_ref[...], heads), axis=0)
    keys = kv_ref[:, 0, :, :width].reshape(spans, width)
    vals = kv_ref[:, 0, :, width:].reshape(spans, width)
    bias = jnp.where(mask_of(qinfo_ref, kinfo_ref), 0.0, MASKED)
    allowed = jnp.concatenate([bias] * heads, axis=0) == 0.0
    probs = jnp.where(allowed, jnp.exp(mm_t(rows, keys) - lse_ref[0]), 0.0)
    d_probs = mm_t(douts, vals)
    delta = jnp.sum(probs * d_probs, axis=1, keepdims=True)
    d_scores = (probs * (d_probs - delta)).astype(LOW)
    d_rows = mm(d_scores, keys)
    d_keys = t_mm(d_scores, rows)
    d_vals = t_mm(probs.astype(LOW), douts)
    per = kv_ref.shape[2]
    blocks = kv_ref.shape[0] // chunks
    for b in range(blocks):
        for p in range(chunks):
            at = (b * chunks + p) * per
            dkv_refs[p][b, 0, :, :width] = d_keys[at : at + per].astype(dkv_refs[p].dtype)
            dkv_refs[p][b, 0, :, width:] = d_vals[at : at + per].astype(dkv_refs[p].dtype)
    gain_sum = jnp.zeros((1, width), F32)
    for h, q in enumerate(heads_of(q_ref[...], heads)):
        e = d_rows[h * count : (h + 1) * count] * scale
        e = e * cos_ref[...] + turn_back(e * sin_ref[...])
        d_q, d_g = rms_back(e, q, inverse_rms(q), gain_ref[...])
        gain_sum = gain_sum + jnp.sum(d_g, axis=0, keepdims=True)
        dq_ref[:, h * width : (h + 1) * width] = d_q.astype(LOW)
    dgain_ref[0] = gain_sum


def attention_specs(seqs, rows, spans, chunk_count, wide, width):
    whole = lambda *shape: pl.BlockSpec(shape, lambda s: (0,) * len(shape))
    return dict(
        qinfo=pl.BlockSpec((1, rows, 2), lambda s: (s, 0, 0)),
        kinfo=pl.BlockSpec((1, 2, spans), lambda s: (s, 0, 0)),
        q=pl.BlockSpec((rows, wide), lambda s: (s, 0)),
        gain=whole(1, width),
        table=whole(rows, width),
        kv=pl.BlockSpec((chunk_count, 1, rows, 2 * width), lambda s: (0, s, 0, 0)),
        lse=pl.BlockSpec((1, rows * (wide // width), 1), lambda s: (s, 0, 0)),
        dgain=pl.BlockSpec((1, 1, width), lambda s: (s, 0, 0)),
    )


def shards(inputs, target, segment_ids, w_query, w_key, w_value, w_out, w_gate, w_up, w_down,
           gain_input, gain_query, gain_key, gain_post_attn, gain_pre_ffn, gain_post_ffn):
    F, C, T = (lax.axis_size(a) for a in ("fsdp", "ctx", "tp"))
    f, z, t = (lax.axis_index(a) for a in ("fsdp", "ctx", "tp"))
    me = f * C + z
    seqs, block_rows, width_model = inputs.shape
    piece = w_query.shape[0]
    head_width = w_key.shape[1]
    gain_piece = gain_query.shape[0]
    sub = block_rows // T
    own = seqs * sub
    half = C * piece
    halo = -(-(WIN - 1) // block_rows)
    spans = (halo + 1) * block_rows

    packed = jnp.concatenate(
        [gain_input, gain_post_attn, gain_pre_ffn, gain_post_ffn, gain_query, gain_key, segment_ids.astype(LOW).reshape(-1)]
    )
    packed = exchange(jnp.broadcast_to(packed[None], (F * C, packed.shape[0])), ("fsdp", "ctx")).astype(F32)
    at = 4 * piece
    g_input, g_post_attn, g_pre_ffn, g_post_ffn = [
        packed[:, i * piece : (i + 1) * piece].reshape(1, width_model) for i in range(4)
    ]
    g_query, g_key = [
        packed[:, at + i * gain_piece : at + (i + 1) * gain_piece].reshape(1, head_width) for i in range(2)
    ]
    seg_blocks = packed[:, at + 2 * gain_piece :].astype(jnp.int32)
    count = jnp.sum((seg_blocks != 0).astype(F32))

    def both_cores(mine):
        other = swap(mine, "fsdp", 1)
        return jnp.where(f == 0, jnp.concatenate([mine, other], axis=0), jnp.concatenate([other, mine], axis=0))

    near = lax.all_gather(jnp.concatenate([w_query, w_out.T, w_key, w_value], axis=1), "ctx", axis=0, tiled=True)
    kv_full = both_cores(near[:, 2 * head_width :])
    gate_full = lax.all_gather(w_gate, ("fsdp", "ctx"), axis=0, tiled=True)
    up_full = lax.all_gather(w_up, ("fsdp", "ctx"), axis=0, tiled=True)
    down_full = lax.all_gather(w_down.T, ("fsdp", "ctx"), axis=0, tiled=True)
    near = near[:, : 2 * head_width]
    near = [near] + [swap(near, "tp", p) for p in range(1, T)]
    q_full, out_full = [
        both_cores(jnp.concatenate([v[:, i * head_width : (i + 1) * head_width] for v in near], axis=1)) for i in range(2)
    ]

    def sub_rows(values):
        return [lax.dynamic_slice_in_dim(values, (t ^ p) * sub, sub, 1) for p in range(T)]

    x_low = jnp.stack(sub_rows(inputs)).reshape(T * own, width_model)
    target_own = lax.dynamic_slice_in_dim(target, t * sub, sub, 1).reshape(own, width_model).astype(F32)
    positions = jnp.concatenate([z * block_rows + (t ^ p) * sub + jnp.arange(sub, dtype=jnp.int32) for p in range(T)])
    segs = [segment_ids + 1]
    for d in range(1, halo + 1):
        far = lax.dynamic_index_in_dim(seg_blocks, jnp.maximum(me - d, 0), 0, False).reshape(seqs, block_rows)
        segs.append(jnp.where(z >= d, far + 1, 0))
    key_seg = jnp.concatenate([v for seg in segs for v in sub_rows(seg)], axis=1)
    key_pos = jnp.concatenate([positions - d * block_rows for d in range(halo + 1)])
    kinfo = jnp.stack([jnp.broadcast_to(key_pos, (seqs, spans)), key_seg], axis=1)
    qinfo = jnp.stack([jnp.broadcast_to(positions[:sub], (seqs, sub)), key_seg[:, :sub]], axis=2)
    valid_own = (key_seg[:, :sub] != 1).astype(F32).reshape(own, 1)

    cos_all, sin_all = rotary_tables(positions, head_width)
    tile_rows = lambda table: jnp.broadcast_to(table.reshape(T, 1, sub, head_width), (T, seqs, sub, head_width)).reshape(T * own, head_width)
    x_all = x_low.astype(F32)
    normed = (x_all * inverse_rms(x_all) * g_input).astype(LOW)
    kv_raw = mm(normed, kv_full)
    key_raw = kv_raw[:, :head_width]
    key_n = key_raw * inverse_rms(key_raw) * g_key
    key_rot = (key_n * tile_rows(cos_all) + turn(key_n) * tile_rows(sin_all)).astype(LOW)
    pair = jnp.concatenate([key_rot, kv_raw[:, head_width:].astype(LOW)], axis=1).reshape(T, seqs, sub, 2 * head_width)
    pieces = [pair]
    for d in range(1, halo + 1):
        far = shifted(pair[0], "ctx", d)
        pieces.append(jnp.stack([far] + [swap(far, "tp", p) for p in range(1, T)]))
    kv_rows = jnp.concatenate(pieces, axis=0)
    normed_own = normed[:own]
    x_own = x_all[:own]
    q_raw = mm(normed_own, q_full)
    heads = q_raw.shape[1] // head_width
    wide = q_raw.shape[1]
    chunk_count = (halo + 1) * T
    specs = attention_specs(seqs, sub, spans, chunk_count, wide, head_width)
    cos_own, sin_own = cos_all[:sub], sin_all[:sub]
    q_rot, attended, lse = pl.pallas_call(
        functools.partial(attend_kernel, heads),
        grid=(seqs,),
        in_specs=[specs[k] for k in ("qinfo", "kinfo", "q", "gain", "table", "table", "kv")],
        out_specs=[specs["q"], specs["q"], specs["lse"]],
        out_shape=[
            jax.ShapeDtypeStruct((own, wide), LOW),
            jax.ShapeDtypeStruct((own, wide), LOW),
            jax.ShapeDtypeStruct((seqs, sub * heads, 1), F32),
        ],
        compiler_params=pltpu.CompilerParams(vmem_limit_bytes=32 * 1024 * 1024),
        name="attend",
    )(qinfo, kinfo, q_raw, g_query, cos_own, sin_own, kv_rows)
    branch = mm_t(attended, out_full)
    inv_branch = inverse_rms(branch)
    hidden = x_own + branch * inv_branch * g_post_attn
    inv_hidden = inverse_rms(hidden)
    ffn_in = (hidden * inv_hidden * g_pre_ffn).astype(LOW)

    ffn_ins = [ffn_in] + [swap(ffn_in, "tp", p) for p in range(1, T)]
    gates, ups, acts, ffn_out = [], [], [], None
    for p, rows in enumerate(ffn_ins):
        gate, up = mm(rows, gate_full), mm(rows, up_full)
        act = (jax.nn.gelu(gate, approximate=True) * up).astype(LOW)
        part = mm_t(act, down_full)
        ffn_out = part if p == 0 else ffn_out + swap(part.astype(LOW), "tp", p).astype(F32)
        gates.append(gate)
        ups.append(up)
        acts.append(act)
    inv_ffn = inverse_rms(ffn_out)
    result = hidden + ffn_out * inv_ffn * g_post_ffn
    mismatch = result - target_own
    error = jnp.sum(valid_own * mismatch * mismatch)
    all_tokens = seqs * block_rows * F * C
    d_result = (all_tokens / count) * valid_own * mismatch
    d_ffn, dg_post_ffn = rms_back(d_result, ffn_out, inv_ffn, g_post_ffn)
    d_ffn_low = d_ffn.astype(LOW)
    d_outs = [d_ffn_low] + [swap(d_ffn_low, "tp", p) for p in range(1, T)]
    d_gates, d_ups, d_ffn_in = [], [], None
    for p, rows in enumerate(d_outs):
        d_act = mm(rows, down_full)
        _, back = jax.vjp(lambda g, u: jax.nn.gelu(g, approximate=True) * u, gates[p], ups[p])
        d_gate, d_up = (v.astype(LOW) for v in back(d_act))
        part = mm_t(d_gate, gate_full) + mm_t(d_up, up_full)
        d_ffn_in = part if p == 0 else d_ffn_in + swap(part.astype(LOW), "tp", p).astype(F32)
        d_gates.append(d_gate)
        d_ups.append(d_up)

    def collect_core(partial):
        low = partial.astype(LOW).reshape(F, half, partial.shape[1])
        other = swap(lax.dynamic_index_in_dim(low, f ^ 1, 0, False), "fsdp", 1)
        return lax.dynamic_index_in_dim(low, f, 0, False).astype(F32) + other.astype(F32)

    def collect_ctx(sums):
        return jnp.sum(exchange(sums.astype(LOW).reshape(C, piece, sums.shape[1]), "ctx").astype(F32), axis=0)

    def collect(partial):
        return lax.psum_scatter(collect_core(partial).astype(LOW), "ctx", scatter_dimension=0, tiled=True).astype(F32)

    all_rows = lambda parts: jnp.concatenate(parts, axis=0)
    ffn_in_all = all_rows(ffn_ins)
    grad_down = collect(t_mm(all_rows(d_outs), all_rows(acts)))
    grad_gate = collect(t_mm(ffn_in_all, all_rows(d_gates)))
    grad_up = collect(t_mm(ffn_in_all, all_rows(d_ups)))

    d_hidden_add, dg_pre_ffn = rms_back(d_ffn_in, hidden, inv_hidden, g_pre_ffn)
    d_hidden = d_result + d_hidden_add
    d_branch, dg_post_attn = rms_back(d_hidden, branch, inv_branch, g_post_attn)
    d_branch_low = d_branch.astype(LOW)
    d_attended = mm(d_branch_low, out_full).astype(LOW)
    d_query, dg_query, *d_pairs = pl.pallas_call(
        functools.partial(attend_back_kernel, heads, T),
        grid=(seqs,),
        in_specs=[specs[k] for k in ("qinfo", "kinfo", "q", "gain", "table", "table", "kv", "q", "lse", "q")],
        out_specs=[specs["q"], specs["dgain"]]
        + [pl.BlockSpec((halo + 1, 1, sub, 2 * head_width), lambda s: (0, s, 0, 0))] * T,
        out_shape=[
            jax.ShapeDtypeStruct((own, wide), LOW),
            jax.ShapeDtypeStruct((seqs, 1, head_width), F32),
        ]
        + [jax.ShapeDtypeStruct((halo + 1, seqs, sub, 2 * head_width), F32 if p == 0 else LOW) for p in range(T)],
        compiler_params=pltpu.CompilerParams(vmem_limit_bytes=32 * 1024 * 1024),
        name="attend_back",
    )(qinfo, kinfo, q_raw, g_query, cos_own, sin_own, kv_rows, q_rot, lse, d_attended)
    d_pair = d_pairs[0]
    for p in range(1, T):
        d_pair = d_pair + swap(d_pairs[p], "tp", p).astype(F32)
    d_pair_low = d_pair.astype(LOW)
    d_kv = d_pair[0]
    for d in range(1, halo + 1):
        d_kv = d_kv + shifted(d_pair_low[d], "ctx", -d).astype(F32)
    d_kv = d_kv.reshape(own, 2 * head_width)
    own_rows = lambda table: jnp.tile(table[:sub], (seqs, 1))
    e = d_kv[:, :head_width]
    e = e * own_rows(cos_all) + turn_back(e * own_rows(sin_all))
    key_own = key_raw[:own]
    d_key, dg_key = rms_back(e, key_own, inverse_rms(key_own), g_key)
    d_kv_low = jnp.concatenate([d_key.astype(LOW), d_kv[:, head_width:].astype(LOW)], axis=1)
    d_normed = mm_t(d_query, q_full) + mm_t(d_kv_low, kv_full)
    inv_x = inverse_rms(x_own)
    d_x, dg_input = rms_back(d_normed, x_own, inv_x, g_input)
    grad_input = d_hidden + d_x
    output = result.astype(LOW)

    out_sum = collect_core(t_mm(d_branch_low, attended))
    out_low = out_sum.astype(LOW)
    out_head = out_sum[:, :head_width]
    for p in range(1, T):
        out_head = out_head + swap(out_low[:, p * head_width : (p + 1) * head_width], "tp", p).astype(F32)
    grad_out = collect_ctx(out_head)
    d_query_head = all_rows(
        [d_query[:, :head_width]] + [swap(d_query[:, p * head_width : (p + 1) * head_width], "tp", p) for p in range(1, T)]
    )
    grad_qkv = collect_ctx(
        collect_core(jnp.concatenate([t_mm(normed, d_query_head), t_mm(normed_own, d_kv_low)], axis=1))
    )
    grad_query = grad_qkv[:, :head_width]
    kv_low = lax.optimization_barrier(grad_qkv[:, head_width:].astype(LOW))

    kv_sums = {p: (swap(kv_low, "tp", p) if p else kv_low).astype(F32) for p in range(T)}
    bit = 1
    while bit < T:
        kv_sums = {p: kv_sums[p] + kv_sums[p ^ bit] for p in kv_sums if not p & bit}
        bit *= 2
    grad_kv = kv_sums[0]

    sums = [jnp.sum(v, axis=0) for v in (dg_input, dg_post_attn, dg_pre_ffn, dg_post_ffn)]
    small = [jnp.sum(dg_query, axis=(0, 1)), jnp.sum(dg_key, axis=0)]
    rows = [v.reshape(F * C, piece) for v in sums] + [v.reshape(F * C, gain_piece) for v in small]
    rows = jnp.concatenate(rows + [jnp.full((F * C, 1), error)], axis=1)
    total = jnp.sum(exchange(rows, ("fsdp", "ctx")), axis=0)
    total = jnp.sum(exchange(jnp.broadcast_to(total[None], (T, total.shape[0])), "tp"), axis=0)
    loss = total[-1] / (2.0 * width_model * count)
    return (
        output.reshape(seqs, sub, width_model),
        loss,
        grad_input.reshape(seqs, sub, width_model),
        grad_query,
        grad_kv[:, :head_width],
        grad_kv[:, head_width:],
        grad_out.T,
        grad_gate,
        grad_up,
        grad_down.T,
        total[:piece],
        total[at : at + gain_piece],
        total[at + gain_piece : at + 2 * gain_piece],
        total[piece : 2 * piece],
        total[2 * piece : 3 * piece],
        total[3 * piece : 4 * piece],
    )


def solution(mesh):
    rows = P(("fsdp", "ctx"), "tp")
    cols = P("tp", ("fsdp", "ctx"))
    split = P(("fsdp", "ctx"), None)
    gain = P(("fsdp", "ctx"))
    token = P("fsdp", "ctx", None)
    own = P("fsdp", ("ctx", "tp"), None)
    weights = (rows, split, split, cols, rows, rows, cols)
    return jax.shard_map(
        shards,
        mesh=mesh,
        in_specs=(token, token, P("fsdp", "ctx")) + weights + (gain,) * 6,
        out_specs=(own, P(), own) + weights + (gain,) * 6,
        check_vma=False,
    )
```

time: 1560 us -> 554 us (0.36)
  waiting for transfers between devices: 906 us -> 143 us
  blocking collectives: 402 us -> 0 us
  starting transfers between devices: 11.4 us -> 77.6 us
  local copies, waits for them, and re-layouts: 30.5 us -> 86.9 us
  other arithmetic: 52.2 us -> 83.7 us
    reduce_scatter x7 -> x3, waiting for transfers between devices: 401 us -> 0.01 us  [collect(): lax.psum_scatter(collect_core(partial).astype(LOW), 'ctx', scatter_dimens...]
    psum x4 -> x0, waiting for transfers between devices: 371 us -> none  [reduce_full(): return lax.psum(partial_sum, 'tp')]
    all_gather x5 -> x0, blocking collectives: 177 us -> none  [the longest x1 70.3 us: carried_in(): gathered = lax.all_gather(part, axis)]
    psum x4 -> x0, blocking collectives: 158 us -> none  [the longest x2 83.7 us: shards(): lax.psum((err_local, count_local), ('fsdp', 'ctx', 'tp'))]
    unnamed x2 -> x0, blocking collectives: 67.5 us -> none
    ppermute x4 -> x45, starting transfers between devices: 10.6 us -> 57.4 us  [the longest x41 45 us: swap(): lax.ppermute(values, axis, [(i, i ^ bits) for i in range(lax.axis_size(ax...]
    select_n x0 -> x3, other arithmetic: none -> 29.9 us  [the longest x2 29.9 us: both_cores(): jnp.where(f == 0, jnp.concatenate([mine, other], axis=0), jnp.concatenate...]
    ppermute x4 -> x45, waiting for transfers between devices: 133 us -> 108 us  [the longest x41 90.3 us: swap(): lax.ppermute(values, axis, [(i, i ^ bits) for i in range(lax.axis_size(ax...]
  transfers between devices with their start and end apart: 18 -> 57, of which waited for: 9 -> 21; matrix products, arithmetic and copies ran while one was open for 6% -> 50% of each run, Pallas kernels for 0% -> 2%
where the time goes in v1:
time: 554 us; the launch traced here: 545 us
  waiting for transfers between devices  143 us (26%)
  matrix products  126 us (23%)
  local copies, waits for them, and re-layouts  86.9 us (16%)
  other arithmetic  83.7 us (15%)
  starting transfers between devices  77.6 us (14%)
  between operations  19.4 us (4%)
  Pallas kernels  9.29 us (2%)
    dot_general x36, matrix products, dot(): lax.dot_general(left, right, (contract, ((), ())), preferred_element_type...  126 us
    ppermute x41, waiting for transfers between devices, swap(): lax.ppermute(values, axis, [(i, i ^ bits) for i in range(lax.axis_size(ax...  90.3 us
    ppermute x41, starting transfers between devices, swap(): lax.ppermute(values, axis, [(i, i ^ bits) for i in range(lax.axis_size(ax...  45 us
    select_n x2, other arithmetic, both_cores(): jnp.where(f == 0, jnp.concatenate([mine, other], axis=0), jnp.concatenate...  29.9 us
    unnamed x238, local copies, waits for them, and re-layouts  22.8 us
    all_to_all x5, waiting for transfers between devices, exchange(): return lax.all_to_all(values, axes, 0, 0, tiled=True)  22.5 us
    convert_element_type x3, local copies, waits for them, and re-layouts, collect_core(): low = partial.astype(LOW).reshape(F, half, partial.shape[1])  19.9 us
    all_to_all x5, starting transfers between devices, exchange(): return lax.all_to_all(values, axes, 0, 0, tiled=True)  19.9 us
  transfers between devices with their start and end apart: 57, of which 21 were waited for; matrix products, arithmetic and copies ran while one was open for 50% of the time, Pallas kernels for 2%

profile of v1, /device:TPU:0, one launch (start us, length us, event | category | flops | bytes accessed | tf_op | source)
XLA Modules:
  0.0 545.2 jit_solution(9950526553568014397)
XLA Ops:
  13.0 6.3 %all-to-all-start = ((bf16[8,2,832]{2,1,0:T(2,128)(2,1)}), bf16[8,2,832]{2,1,0:T(2,128)(2,1)S(1)}, u32[]{:S(2)}, u32[]{:S(2)}) async-start(bf16[8,2,832]{2,1,0:T(2,128)(2,1)} %reshape.383), calls=%async_computation | async-start | bytes 57344 | tf_op jit(solution)/shard_map/all_to_all | solution.py:27
  22.6 2.5 maximum_convert_fusion
  34.8 6.0 %copy.86 = f32[1024,1152]{0,1:T(8,128)} copy(f32[1024,1152]{1,0:T(8,128)} %bitcast.178) | data formatting | bytes 9437184 | tf_op jit(solution)/shard_map/convert_element_type | solution.py:223
  41.5 2.8 multiply_convert_fusion
  44.3 3.0 fusion.111
  49.6 2.5 collective-permute-start.2
  55.1 2.8 fusion.89
  61.4 5.4 collective-permute-start.9
  66.8 4.3 collective-permute-start.5
  72.2 6.6 %collective-permute-done.1 = bf16[576,512]{1,0:T(8,128)(2,1)} collective-permute-done((bf16[576,512]{1,0:T(8,128)(2,1)}, bf16[576,512]{1,0:T(8,128)(2,1)}, u32[]{:S(2)}, u32[]{:S(2)}) %collective-permute-start.1) | collective-permute-done | bytes 589856 | tf_op jit(solution)/shard_map/ppermute | solution.py:18
  85.7 3.7 collective-permute-done.5
  97.2 3.3 collective-permute-start.12
  100.5 9.8 %collective-permute-done.7 = bf16[4,64,512]{2,1,0:T(8,128)(2,1)S(1)} collective-permute-done((bf16[4,64,512]{2,1,0:T(8,128)(2,1)}, bf16[4,64,512]{2,1,0:T(8,128)(2,1)S(1)}, u32[]{:S(2)}, u32[]{:S(2)}) %collective-permute-start.7) | collective-permute-done | bytes 262176 | tf_op jit(solution)/shard_map/ppermute | solution.py:18
  115.0 3.6 collective-permute-done.10
  118.8 14.6 %maximum_select_fusion = bf16[1152,1024]{1,0:T(8,128)(2,1)S(1)} fusion(bf16[576,1024]{1,0:T(8,128)(2,1)} %collective-permute-done.3, bf16[576,256]{1,0:T(8,128)(2,1)S(1)} %copy-done.57, bf16[576,256]{1,0:T(8,128)(2,1)S(1)} %copy-done.59, bf16[576,256]{1,0:T(8,128)(2,1)S(1)} %copy-done.61, bf16[576,256]{1,0:T(8,128)(2,1)S(1)} %copy-done.49, pred[]{:T(512)S(6)} %eq.2), kind=kLoop, calls=%fused_computation.54 | loop fusion | flops 24772608 | bytes 4718593 | tf_op jit(solution)/shard_map/jit(_where)/select_n | solution.py:192
  136.7 4.0 attend.1
  140.9 15.3 %maximum_select_fusion.1 = bf16[1152,1024]{1,0:T(8,128)(2,1)S(1)} fusion(bf16[576,1024]{1,0:T(8,128)(2,1)} %collective-permute-done.13, bf16[576,256]{1,0:T(8,128)(2,1)S(1)} %copy-done.51, bf16[576,256]{1,0:T(8,128)(2,1)S(1)} %copy-done.53, bf16[576,256]{1,0:T(8,128)(2,1)S(1)} %copy-done.55, bf16[576,256]{1,0:T(8,128)(2,1)S(1)} %copy-done.47, pred[]{:T(512)S(6)} %eq.2), kind=kLoop, calls=%fused_computation.55 | loop fusion | flops 24772608 | bytes 4718593 | tf_op jit(solution)/shard_map/jit(_where)/select_n | solution.py:192
  167.2 11.0 %collective-permute-done.18 = bf16[256,1152]{1,0:T(8,128)(2,1)} collective-permute-done((bf16[256,1152]{1,0:T(8,128)(2,1)}, bf16[256,1152]{1,0:T(8,128)(2,1)}, u32[]{:S(2)}, u32[]{:S(2)}) %collective-permute-start.18) | collective-permute-done | bytes 589856 | tf_op jit(solution)/shard_map/ppermute | solution.py:18
  178.2 5.3 fusion.125
  183.6 6.4 %multiply_convert_fusion.5 = (bf16[256,1728]{0,1:T(8,128)(2,1)}, f32[256,1728]{0,1:T(8,128)}) fusion(f32[256,1728]{0,1:T(8,128)} %fusion.125, bf16[256,1152]{1,0:T(8,128)(2,1)} %collective-permute-done.18, bf16[1152,1728]{1,0:T(8,128)(2,1)} %all-gather.9.cloned.1.call-done), kind=kOutput, calls=%fused_computation.107 | convolution fusion | flops 1023639552 | bytes 8994816 | tf_op jit(solution)/shard_map/dot_general | solution.py:31
  190.0 10.0 %all-gather.11.cloned.1.call-done = bf16[1152,1728]{1,0:T(8,128)(2,1)} async-done(((bf16[144,1728]{1,0:T(8,128)(2,1)}), bf16[1152,1728]{1,0:T(8,128)(2,1)}) %all-gather.11.cloned.1.call-update) | async-done | bytes 3981328 | tf_op jit(solution)/shard_map/all_gather | solution.py:198
  200.0 4.0 convolution_convert_fusion.5
  206.5 2.8 fusion.124
  209.3 4.8 multiply_convert_fusion.6
  216.4 2.8 fusion.123
  219.3 4.7 multiply_convert_fusion.7
  226.3 2.8 fusion.122
  229.1 3.0 multiply_convert_fusion.8
  233.1 7.3 %collective-permute-done.15 = bf16[256,1152]{1,0:T(8,128)(2,1)S(1)} collective-permute-done((bf16[256,1152]{1,0:T(8,128)(2,1)S(1)}, bf16[256,1152]{1,0:T(8,128)(2,1)S(1)}, u32[]{:S(2)}, u32[]{:S(2)}) %collective-permute-start.15) | collective-permute-done | bytes 589856 | tf_op jit(solution)/shard_map/ppermute | solution.py:18
  248.7 5.1 multiply_convert_fusion.4
  253.9 5.0 fusion.126
  258.9 14.2 %collective-permute-done.20 = bf16[256,1152]{1,0:T(8,128)(2,1)} collective-permute-done((bf16[256,1152]{1,0:T(8,128)(2,1)}, bf16[256,1152]{1,0:T(8,128)(2,1)}, u32[]{:S(2)}, u32[]{:S(2)}) %collective-permute-start.20) | collective-permute-done | bytes 589856 | tf_op jit(solution)/shard_map/ppermute | solution.py:18
  273.1 4.6 multiply_convert_fusion.3
  283.1 4.1 multiply_convert_fusion.2
  291.5 4.9 multiply_convert_fusion.1
  297.3 8.5 %convolution_convert_fusion.1 = bf16[1152,1728]{0,1:T(8,128)(2,1)} fusion(bf16[256,1728]{0,1:T(8,128)(2,1)S(1)} %get-tuple-element.69, bf16[256,1728]{0,1:T(8,128)(2,1)S(1)} %get-tuple-element.67, bf16[256,1728]{0,1:T(8,128)(2,1)S(1)} %get-tuple-element.63, bf16[256,1728]{0,1:T(8,128)(2,1)S(1)} %copy-done.67, bf16[256,1152]{1,0:T(8,128)(2,1)} %collective-permute-done.18, ...), kind=kOutput, calls=%fused_computation.1 | convolution fusion | flops 4102447104 | bytes 9879552 | tf_op jit(solution)/shard_map/dot_general | solution.py:31
  305.8 6.6 %copy.99 = bf16[1152,1728]{1,0:T(8,128)(2,1)} copy(bf16[1152,1728]{0,1:T(8,128)(2,1)} %convolution_convert_fusion.1) | data formatting | bytes 7962624 | tf_op jit(solution)/shard_map/convert_element_type | solution.py:292
  315.2 2.8 fusion.129
  322.6 8.5 %convolution_convert_fusion = bf16[1152,1728]{0,1:T(8,128)(2,1)} fusion(bf16[256,1728]{0,1:T(8,128)(2,1)S(1)} %copy-done.101, bf16[256,1728]{0,1:T(8,128)(2,1)S(1)} %copy-done.103, bf16[256,1728]{0,1:T(8,128)(2,1)S(1)} %copy-done.105, bf16[256,1728]{0,1:T(8,128)(2,1)S(1)} %copy-done.107, bf16[256,1152]{1,0:T(8,128)(2,1)} %collective-permute-done.24, ...), kind=kOutput, calls=%fused_computation | convolution fusion | flops 4102447104 | bytes 9879552 | tf_op jit(solution)/shard_map/dot_general | solution.py:31
  333.0 9.3 %convolution_convert_fusion.2 = bf16[1152,1728]{0,1:T(8,128)(2,1)} fusion(bf16[256,1728]{0,1:T(8,128)(2,1)} %get-tuple-element.70, bf16[256,1728]{0,1:T(8,128)(2,1)} %copy-done.111, bf16[256,1728]{0,1:T(8,128)(2,1)} %copy-done.110, bf16[256,1728]{0,1:T(8,128)(2,1)} %get-tuple-element.66, bf16[256,1152]{1,0:T(8,128)(2,1)} %collective-permute-done.18, ...), kind=kOutput, calls=%fused_computation.2 | convolution fusion | flops 4102447104 | bytes 9879552 | tf_op jit(solution)/shard_map/dot_general | solution.py:31
  342.3 6.8 %copy.100 = bf16[1152,1728]{1,0:T(8,128)(2,1)} copy(bf16[1152,1728]{0,1:T(8,128)(2,1)} %convolution_convert_fusion) | data formatting | bytes 7962624 | tf_op jit(solution)/shard_map/convert_element_type | solution.py:292
  349.1 6.5 %copy.98 = bf16[1152,1728]{1,0:T(8,128)(2,1)} copy(bf16[1152,1728]{0,1:T(8,128)(2,1)} %convolution_convert_fusion.2) | data formatting | bytes 7962624 | tf_op jit(solution)/shard_map/convert_element_type | solution.py:292
  358.2 4.8 multiply_reduce_fusion.3
  368.8 5.2 attend_back.1
  381.6 3.1 dynamic-slice_bitcast_fusion.2
  390.4 6.3 %collective-permute-done.26 = bf16[3,4,64,512]{3,2,1,0:T(8,128)(2,1)S(1)} collective-permute-done((bf16[3,4,64,512]{3,2,1,0:T(8,128)(2,1)}, bf16[3,4,64,512]{3,2,1,0:T(8,128)(2,1)S(1)}, u32[]{:S(2)}, u32[]{:S(2)}) %collective-permute-start.26) | collective-permute-done | bytes 786464 | tf_op jit(solution)/shard_map/ppermute | solution.py:18
  397.3 17.3 %collective-permute-done.27 = bf16[3,4,64,512]{3,2,1,0:T(8,128)(2,1)S(1)} collective-permute-done((bf16[3,4,64,512]{3,2,1,0:T(8,128)(2,1)}, bf16[3,4,64,512]{3,2,1,0:T(8,128)(2,1)S(1)}, u32[]{:S(2)}, u32[]{:S(2)}) %collective-permute-start.27) | collective-permute-done | bytes 786464 | tf_op jit(solution)/shard_map/ppermute | solution.py:18
  414.6 3.2 collective-permute-start.31
  424.6 8.3 %collective-permute-done.29 = bf16[4,64,512]{2,1,0:T(8,128)(2,1)S(1)} collective-permute-done((bf16[4,64,512]{2,1,0:T(8,128)(2,1)S(1)}, bf16[4,64,512]{2,1,0:T(8,128)(2,1)S(1)}, u32[]{:S(2)}, u32[]{:S(2)}) %collective-permute-start.29) | collective-permute-done | bytes 262176 | tf_op jit(solution)/shard_map/ppermute | solution.py:23
  432.9 5.7 %collective-permute-done.30 = bf16[4,64,512]{2,1,0:T(8,128)(2,1)S(1)} collective-permute-done((bf16[4,64,512]{2,1,0:T(8,128)(2,1)S(1)}, bf16[4,64,512]{2,1,0:T(8,128)(2,1)S(1)}, u32[]{:S(2)}, u32[]{:S(2)}) %collective-permute-start.30) | collective-permute-done | bytes 262176 | tf_op jit(solution)/shard_map/ppermute | solution.py:23
  448.9 3.0 fusion.88
  451.8 3.6 fusion.2
  456.1 3.7 multiply_reduce_fusion.1
  461.3 3.3 all-to-all-start.1
  464.7 6.2 %all-to-all-done.1 = f32[8,1,641]{2,1,0:T(1,128)S(1)} async-done(((f32[8,1,641]{2,1,0:T(1,128)}), f32[8,1,641]{2,1,0:T(1,128)S(1)}, u32[]{:S(2)}, u32[]{:S(2)}) %all-to-all-start.1) | async-done | bytes 20544 | tf_op jit(solution)/shard_map/all_to_all | solution.py:27
  471.4 3.3 all-to-all-start.2
  474.7 2.6 fusion.62
  479.4 3.5 all-to-all-start.3
  482.9 3.3 fusion.105
  491.2 5.1 collective-permute-done.39
  496.3 5.0 collective-permute-done.41
  504.5 10.4 %all-to-all-done.3 = bf16[4,144,768]{2,1,0:T(8,128)(2,1)S(1)} async-done(((bf16[4,144,768]{2,1,0:T(8,128)(2,1)}), bf16[4,144,768]{2,1,0:T(8,128)(2,1)S(1)}, u32[]{:S(2)}, u32[]{:S(2)}) %all-to-all-start.3) | async-done | bytes 884768 | tf_op jit(solution)/shard_map/all_to_all | solution.py:27
  514.9 3.5 all-to-all-start.4
  524.5 4.0 all-to-all-done.4
  (480 shorter events, 163.0 us)
Async XLA Ops:
  7.3 37.1 %all-gather.5.cloned.1.call-start = ((), (), s32[]{:S(2)}) async-start(), calls=%async_computation.8 | async-start | bytes 1474560 | tf_op jit(solution)/shard_map/all_gather | solution.py:194
  9.2 169.0 %all-gather.7.cloned.1.call-start = ((), (), s32[]{:S(2)}) async-start(), calls=%async_computation.9 | async-start | bytes 4644864 | tf_op jit(solution)/shard_map/all_gather | solution.py:196
  10.0 173.6 %all-gather.9.cloned.1.call-start = ((), (), s32[]{:S(2)}) async-start(), calls=%async_computation.10 | async-start | bytes 4644864 | tf_op jit(solution)/shard_map/all_gather | solution.py:197
  13.0 28.0 %all-to-all-start = ((bf16[8,2,832]{2,1,0:T(2,128)(2,1)}), bf16[8,2,832]{2,1,0:T(2,128)(2,1)S(1)}, u32[]{:S(2)}, u32[]{:S(2)}) async-start(bf16[8,2,832]{2,1,0:T(2,128)(2,1)} %reshape.383), calls=%async_computation | async-start | bytes 57344 | tf_op jit(solution)/shard_map/all_to_all | solution.py:27
  19.3 180.7 %all-gather.11.cloned.1.call-start = ((), (), s32[]{:S(2)}) async-start(), calls=%async_computation.11 | async-start | bytes 4644864 | tf_op jit(solution)/shard_map/all_gather | solution.py:198
  19.9 510.8 %reduce-scatter.6.cloned.1.call-start = ((), (), s32[]{:S(2)}) async-start(), calls=%async_computation.13 | async-start | bytes 2580480 | tf_op jit(solution)/shard_map/reduce_scatter | solution.py:300
  47.3 7.8 %collective-permute-start.4 = (bf16[576,512]{1,0:T(8,128)(2,1)S(1)}, bf16[576,512]{1,0:T(8,128)(2,1)}, u32[]{:S(2)}, u32[]{:S(2)}) collective-permute-start(bf16[576,512]{1,0:T(8,128)(2,1)S(1)} %get-tuple-element.82), channel_id=1, source_target_pairs={{0,16},{16,0},{1,17},{17,1},{2,18},{18,2},{3,19},{19,3},{4,20},{20... | collective-permute-start | bytes 1769480 | tf_op jit(solution)/shard_map/ppermute | solution.py:18
  49.6 21.5 %collective-permute-start.2 = (bf16[576,512]{1,0:T(8,128)(2,1)}, bf16[576,512]{1,0:T(8,128)(2,1)}, u32[]{:S(2)}, u32[]{:S(2)}) collective-permute-start(bf16[576,512]{1,0:T(8,128)(2,1)} %get-tuple-element.83), channel_id=1, source_target_pairs={{0,3},{1,2},{2,1},{3,0},{4,7},{5,6},{6,5},{7,4},{8,11},{9,10},{10,... | collective-permute-start | bytes 1769480 | tf_op jit(solution)/shard_map/ppermute | solution.py:18
  52.1 26.7 %collective-permute-start.1 = (bf16[576,512]{1,0:T(8,128)(2,1)}, bf16[576,512]{1,0:T(8,128)(2,1)}, u32[]{:S(2)}, u32[]{:S(2)}) collective-permute-start(bf16[576,512]{1,0:T(8,128)(2,1)} %get-tuple-element.83), channel_id=1, source_target_pairs={{0,2},{1,3},{2,0},{3,1},{4,6},{5,7},{6,4},{7,5},{8,10},{9,11},{10,... | collective-permute-start | bytes 1769480 | tf_op jit(solution)/shard_map/ppermute | solution.py:18
  52.6 27.4 %collective-permute-start = (bf16[576,512]{1,0:T(8,128)(2,1)}, bf16[576,512]{1,0:T(8,128)(2,1)}, u32[]{:S(2)}, u32[]{:S(2)}) collective-permute-start(bf16[576,512]{1,0:T(8,128)(2,1)} %get-tuple-element.83), channel_id=1, source_target_pairs={{0,1},{1,0},{2,3},{3,2},{4,5},{5,4},{6,7},{7,6},{8,9},{9,8},{10,11... | collective-permute-start | bytes 1769480 | tf_op jit(solution)/shard_map/ppermute | solution.py:18
  61.4 20.0 %copy-start.48 = (bf16[576,256]{1,0:T(8,128)(2,1)S(1)}, bf16[576,256]{1,0:T(8,128)(2,1)}, u32[]{:S(2)}) copy-start(bf16[576,256]{1,0:T(8,128)(2,1)} %get-tuple-element.81) | copy-start | bytes 884740
  61.4 33.4 %collective-permute-start.9 = (bf16[4,64,512]{2,1,0:T(8,128)(2,1)}, bf16[4,64,512]{2,1,0:T(8,128)(2,1)}, u32[]{:S(2)}, u32[]{:S(2)}) collective-permute-start(bf16[4,64,512]{2,1,0:T(8,128)(2,1)} %bitcast.11), channel_id=1, source_target_pairs={{0,8},{4,12},{1,9},{5,13},{2,10},{6,14},{3,11},{7,15},{16,24},{20,... | collective-permute-start | bytes 786440 | tf_op jit(solution)/shard_map/ppermute | solution.py:23
  66.8 22.6 %collective-permute-start.5 = (bf16[4,64,512]{2,1,0:T(8,128)(2,1)}, bf16[4,64,512]{2,1,0:T(8,128)(2,1)}, u32[]{:S(2)}, u32[]{:S(2)}) collective-permute-start(bf16[4,64,512]{2,1,0:T(8,128)(2,1)} %bitcast.11), channel_id=1, source_target_pairs={{0,4},{4,8},{8,12},{1,5},{5,9},{9,13},{2,6},{6,10},{10,14},{3,7},{... | collective-permute-start | bytes 786440 | tf_op jit(solution)/shard_map/ppermute | solution.py:23
  82.5 36.2 %collective-permute-start.3 = (bf16[576,1024]{1,0:T(8,128)(2,1)}, bf16[576,1024]{1,0:T(8,128)(2,1)}, u32[]{:S(2)}, u32[]{:S(2)}) collective-permute-start(bf16[576,1024]{1,0:T(8,128)(2,1)} %pad_maximum_fusion.2), channel_id=1, source_target_pairs={{0,16},{16,0},{1,17},{17,1},{2,18},{18,2},{3,19},{19,3},{4,20},{20... | collective-permute-start | bytes 3538952 | tf_op jit(solution)/shard_map/ppermute | solution.py:18
  83.8 57.0 %collective-permute-start.13 = (bf16[576,1024]{1,0:T(8,128)(2,1)}, bf16[576,1024]{1,0:T(8,128)(2,1)}, u32[]{:S(2)}, u32[]{:S(2)}) collective-permute-start(bf16[576,1024]{1,0:T(8,128)(2,1)} %pad_maximum_fusion.3), channel_id=1, source_target_pairs={{0,16},{16,0},{1,17},{17,1},{2,18},{18,2},{3,19},{19,3},{4,20},{20... | collective-permute-start | bytes 3538952 | tf_op jit(solution)/shard_map/ppermute | solution.py:18
  89.4 7.8 %collective-permute-start.6 = (bf16[4,64,512]{2,1,0:T(8,128)(2,1)}, bf16[4,64,512]{2,1,0:T(8,128)(2,1)S(1)}, u32[]{:S(2)}, u32[]{:S(2)}) collective-permute-start(bf16[4,64,512]{2,1,0:T(8,128)(2,1)} %collective-permute-done.5), channel_id=1, source_target_pairs={{0,1},{1,0},{2,3},{3,2},{4,5},{5,4},{6,7},{7,6},{8,9},{9,8},{10,11... | collective-permute-start | bytes 786440 | tf_op jit(solution)/shard_map/ppermute | solution.py:18
  92.2 18.2 %collective-permute-start.7 = (bf16[4,64,512]{2,1,0:T(8,128)(2,1)}, bf16[4,64,512]{2,1,0:T(8,128)(2,1)S(1)}, u32[]{:S(2)}, u32[]{:S(2)}) collective-permute-start(bf16[4,64,512]{2,1,0:T(8,128)(2,1)} %collective-permute-done.5), channel_id=1, source_target_pairs={{0,2},{1,3},{2,0},{3,1},{4,6},{5,7},{6,4},{7,5},{8,10},{9,11},{10,... | collective-permute-start | bytes 786440 | tf_op jit(solution)/shard_map/ppermute | solution.py:18
  94.7 24.0 %copy-start.49 = (bf16[576,256]{1,0:T(8,128)(2,1)S(1)}, bf16[576,256]{1,0:T(8,128)(2,1)}, u32[]{:S(2)}) copy-start(bf16[576,256]{1,0:T(8,128)(2,1)} %get-tuple-element.81) | copy-start | bytes 884740
  94.8 24.0 %copy-start.57 = (bf16[576,256]{1,0:T(8,128)(2,1)S(1)}, bf16[576,256]{1,0:T(8,128)(2,1)}, u32[]{:S(2)}) copy-start(bf16[576,256]{1,0:T(8,128)(2,1)} %copy-done.56) | copy-start | bytes 884740
  94.8 24.0 %copy-start.59 = (bf16[576,256]{1,0:T(8,128)(2,1)S(1)}, bf16[576,256]{1,0:T(8,128)(2,1)}, u32[]{:S(2)}) copy-start(bf16[576,256]{1,0:T(8,128)(2,1)} %copy-done.58) | copy-start | bytes 884740
  94.8 24.0 %copy-start.61 = (bf16[576,256]{1,0:T(8,128)(2,1)S(1)}, bf16[576,256]{1,0:T(8,128)(2,1)}, u32[]{:S(2)}) copy-start(bf16[576,256]{1,0:T(8,128)(2,1)} %copy-done.60) | copy-start | bytes 884740
  94.8 17.1 %collective-permute-start.8 = (bf16[4,64,512]{2,1,0:T(8,128)(2,1)}, bf16[4,64,512]{2,1,0:T(8,128)(2,1)S(1)}, u32[]{:S(2)}, u32[]{:S(2)}) collective-permute-start(bf16[4,64,512]{2,1,0:T(8,128)(2,1)} %collective-permute-done.5), channel_id=1, source_target_pairs={{0,3},{1,2},{2,1},{3,0},{4,7},{5,6},{6,5},{7,4},{8,11},{9,10},{10,... | collective-permute-start | bytes 786440 | tf_op jit(solution)/shard_map/ppermute | solution.py:18
  97.2 21.4 %collective-permute-start.12 = (bf16[4,64,512]{2,1,0:T(8,128)(2,1)}, bf16[4,64,512]{2,1,0:T(8,128)(2,1)S(1)}, u32[]{:S(2)}, u32[]{:S(2)}) collective-permute-start(bf16[4,64,512]{2,1,0:T(8,128)(2,1)} %collective-permute-done.9), channel_id=1, source_target_pairs={{0,3},{1,2},{2,1},{3,0},{4,7},{5,6},{6,5},{7,4},{8,11},{9,10},{10,... | collective-permute-start | bytes 786440 | tf_op jit(solution)/shard_map/ppermute | solution.py:18
  110.3 8.3 %collective-permute-start.11 = (bf16[4,64,512]{2,1,0:T(8,128)(2,1)}, bf16[4,64,512]{2,1,0:T(8,128)(2,1)S(1)}, u32[]{:S(2)}, u32[]{:S(2)}) collective-permute-start(bf16[4,64,512]{2,1,0:T(8,128)(2,1)} %collective-permute-done.9), channel_id=1, source_target_pairs={{0,2},{1,3},{2,0},{3,1},{4,6},{5,7},{6,4},{7,5},{8,10},{9,11},{10,... | collective-permute-start | bytes 786440 | tf_op jit(solution)/shard_map/ppermute | solution.py:18
  111.9 6.7 %collective-permute-start.10 = (bf16[4,64,512]{2,1,0:T(8,128)(2,1)}, bf16[4,64,512]{2,1,0:T(8,128)(2,1)S(1)}, u32[]{:S(2)}, u32[]{:S(2)}) collective-permute-start(bf16[4,64,512]{2,1,0:T(8,128)(2,1)} %collective-permute-done.9), channel_id=1, source_target_pairs={{0,1},{1,0},{2,3},{3,2},{4,5},{5,4},{6,7},{7,6},{8,9},{9,8},{10,11... | collective-permute-start | bytes 786440 | tf_op jit(solution)/shard_map/ppermute | solution.py:18
  160.7 17.5 %collective-permute-start.18 = (bf16[256,1152]{1,0:T(8,128)(2,1)}, bf16[256,1152]{1,0:T(8,128)(2,1)}, u32[]{:S(2)}, u32[]{:S(2)}) collective-permute-start(bf16[256,1152]{1,0:T(8,128)(2,1)} %multiply_convert_fusion.11), channel_id=1, source_target_pairs={{0,3},{1,2},{2,1},{3,0},{4,7},{5,6},{6,5},{7,4},{8,11},{9,10},{10,... | collective-permute-start | bytes 1769480 | tf_op jit(solution)/shard_map/ppermute | solution.py:18
  164.6 41.8 %collective-permute-start.16 = (bf16[256,1152]{1,0:T(8,128)(2,1)}, bf16[256,1152]{1,0:T(8,128)(2,1)}, u32[]{:S(2)}, u32[]{:S(2)}) collective-permute-start(bf16[256,1152]{1,0:T(8,128)(2,1)} %multiply_convert_fusion.11), channel_id=1, source_target_pairs={{0,2},{1,3},{2,0},{3,1},{4,6},{5,7},{6,4},{7,5},{8,10},{9,11},{10,... | collective-permute-start | bytes 1769480 | tf_op jit(solution)/shard_map/ppermute | solution.py:18
  166.6 49.8 %collective-permute-start.14 = (bf16[256,1152]{1,0:T(8,128)(2,1)}, bf16[256,1152]{1,0:T(8,128)(2,1)}, u32[]{:S(2)}, u32[]{:S(2)}) collective-permute-start(bf16[256,1152]{1,0:T(8,128)(2,1)} %multiply_convert_fusion.11), channel_id=1, source_target_pairs={{0,1},{1,0},{2,3},{3,2},{4,5},{5,4},{6,7},{7,6},{8,9},{9,8},{10,11... | collective-permute-start | bytes 1769480 | tf_op jit(solution)/shard_map/ppermute | solution.py:18
  204.0 28.2 %collective-permute-start.19 = (bf16[256,1152]{1,0:T(8,128)(2,1)S(1)}, bf16[256,1152]{1,0:T(8,128)(2,1)S(1)}, u32[]{:S(2)}, u32[]{:S(2)}) collective-permute-start(bf16[256,1152]{1,0:T(8,128)(2,1)S(1)} %convolution_convert_fusion.5), channel_id=1, source_target_pairs={{0,3},{1,2},{2,1},{3,0},{4,7},{5,6},{6,5},{7,4},{8,11},{9,10},{10,... | collective-permute-start | bytes 1769480 | tf_op jit(solution)/shard_map/ppermute | solution.py:18
  215.8 17.3 %collective-permute-start.17 = (bf16[256,1152]{1,0:T(8,128)(2,1)S(1)}, bf16[256,1152]{1,0:T(8,128)(2,1)S(1)}, u32[]{:S(2)}, u32[]{:S(2)}) collective-permute-start(bf16[256,1152]{1,0:T(8,128)(2,1)S(1)} %convolution_convert_fusion.6), channel_id=1, source_target_pairs={{0,2},{1,3},{2,0},{3,1},{4,6},{5,7},{6,4},{7,5},{8,10},{9,11},{10,... | collective-permute-start | bytes 1769480 | tf_op jit(solution)/shard_map/ppermute | solution.py:18
  225.4 15.0 %collective-permute-start.15 = (bf16[256,1152]{1,0:T(8,128)(2,1)S(1)}, bf16[256,1152]{1,0:T(8,128)(2,1)S(1)}, u32[]{:S(2)}, u32[]{:S(2)}) collective-permute-start(bf16[256,1152]{1,0:T(8,128)(2,1)S(1)} %convolution_convert_fusion.7), channel_id=1, source_target_pairs={{0,1},{1,0},{2,3},{3,2},{4,5},{5,4},{6,7},{7,6},{8,9},{9,8},{10,11... | collective-permute-start | bytes 1769480 | tf_op jit(solution)/shard_map/ppermute | solution.py:18
  245.2 46.3 %collective-permute-start.24 = (bf16[256,1152]{1,0:T(8,128)(2,1)}, bf16[256,1152]{1,0:T(8,128)(2,1)}, u32[]{:S(2)}, u32[]{:S(2)}) collective-permute-start(bf16[256,1152]{1,0:T(8,128)(2,1)} %multiply_convert_fusion.10), channel_id=1, source_target_pairs={{0,3},{1,2},{2,1},{3,0},{4,7},{5,6},{6,5},{7,4},{8,11},{9,10},{10,... | collective-permute-start | bytes 1769480 | tf_op jit(solution)/shard_map/ppermute | solution.py:18
  246.6 36.5 %collective-permute-start.22 = (bf16[256,1152]{1,0:T(8,128)(2,1)}, bf16[256,1152]{1,0:T(8,128)(2,1)}, u32[]{:S(2)}, u32[]{:S(2)}) collective-permute-start(bf16[256,1152]{1,0:T(8,128)(2,1)} %multiply_convert_fusion.10), channel_id=1, source_target_pairs={{0,2},{1,3},{2,0},{3,1},{4,6},{5,7},{6,4},{7,5},{8,10},{9,11},{10,... | collective-permute-start | bytes 1769480 | tf_op jit(solution)/shard_map/ppermute | solution.py:18
  247.4 25.7 %collective-permute-start.20 = (bf16[256,1152]{1,0:T(8,128)(2,1)}, bf16[256,1152]{1,0:T(8,128)(2,1)}, u32[]{:S(2)}, u32[]{:S(2)}) collective-permute-start(bf16[256,1152]{1,0:T(8,128)(2,1)} %multiply_convert_fusion.10), channel_id=1, source_target_pairs={{0,1},{1,0},{2,3},{3,2},{4,5},{5,4},{6,7},{7,6},{8,9},{9,8},{10,11... | collective-permute-start | bytes 1769480 | tf_op jit(solution)/shard_map/ppermute | solution.py:18
  282.5 75.1 %collective-permute-start.21 = (bf16[256,1152]{1,0:T(8,128)(2,1)}, bf16[256,1152]{1,0:T(8,128)(2,1)}, u32[]{:S(2)}, u32[]{:S(2)}) collective-permute-start(bf16[256,1152]{1,0:T(8,128)(2,1)} %fusion.24), channel_id=1, source_target_pairs={{0,1},{1,0},{2,3},{3,2},{4,5},{5,4},{6,7},{7,6},{8,9},{9,8},{10,11... | collective-permute-start | bytes 1769480 | tf_op jit(solution)/shard_map/ppermute | solution.py:18
  290.9 66.7 %collective-permute-start.23 = (bf16[256,1152]{1,0:T(8,128)(2,1)}, bf16[256,1152]{1,0:T(8,128)(2,1)}, u32[]{:S(2)}, u32[]{:S(2)}) collective-permute-start(bf16[256,1152]{1,0:T(8,128)(2,1)} %fusion.25), channel_id=1, source_target_pairs={{0,2},{1,3},{2,0},{3,1},{4,6},{5,7},{6,4},{7,5},{8,10},{9,11},{10,... | collective-permute-start | bytes 1769480 | tf_op jit(solution)/shard_map/ppermute | solution.py:18
  314.3 16.8 %collective-permute-start.43 = (bf16[576,1728]{1,0:T(8,128)(2,1)S(1)}, bf16[576,1728]{1,0:T(8,128)(2,1)S(1)}, u32[]{:S(2)}, u32[]{:S(2)}) collective-permute-start(bf16[576,1728]{1,0:T(8,128)(2,1)S(1)} %dynamic-slice_bitcast_fusion.1), channel_id=1, source_target_pairs={{0,16},{16,0},{1,17},{17,1},{2,18},{18,2},{3,19},{19,3},{4,20},{20... | collective-permute-start | bytes 5971976 | tf_op jit(solution)/shard_map/ppermute | solution.py:18
  320.2 37.4 %collective-permute-start.25 = (bf16[256,1152]{1,0:T(8,128)(2,1)}, bf16[256,1152]{1,0:T(8,128)(2,1)}, u32[]{:S(2)}, u32[]{:S(2)}) collective-permute-start(bf16[256,1152]{1,0:T(8,128)(2,1)} %fusion.26), channel_id=1, source_target_pairs={{0,3},{1,2},{2,1},{3,0},{4,7},{5,6},{6,5},{7,4},{8,11},{9,10},{10,... | collective-permute-start | bytes 1769480 | tf_op jit(solution)/shard_map/ppermute | solution.py:18
  333.0 199.9 %reduce-scatter.8.cloned.1.call-start = ((), (), s32[]{:S(2)}) async-start(), calls=%async_computation.14 | async-start | bytes 2580480 | tf_op jit(solution)/shard_map/reduce_scatter | solution.py:300
  357.5 22.0 %collective-permute-start.44 = (bf16[576,1728]{1,0:T(8,128)(2,1)S(1)}, bf16[576,1728]{1,0:T(8,128)(2,1)S(1)}, u32[]{:S(2)}, u32[]{:S(2)}) collective-permute-start(bf16[576,1728]{1,0:T(8,128)(2,1)S(1)} %dynamic-slice_bitcast_fusion), channel_id=1, source_target_pairs={{0,16},{16,0},{1,17},{17,1},{2,18},{18,2},{3,19},{19,3},{4,20},{20... | collective-permute-start | bytes 5971976 | tf_op jit(solution)/shard_map/ppermute | solution.py:18
  376.1 20.6 %collective-permute-start.26 = (bf16[3,4,64,512]{3,2,1,0:T(8,128)(2,1)}, bf16[3,4,64,512]{3,2,1,0:T(8,128)(2,1)S(1)}, u32[]{:S(2)}, u32[]{:S(2)}) collective-permute-start(bf16[3,4,64,512]{3,2,1,0:T(8,128)(2,1)} %get-tuple-element.30), channel_id=1, source_target_pairs={{0,1},{1,0},{2,3},{3,2},{4,5},{5,4},{6,7},{7,6},{8,9},{9,8},{10,11... | collective-permute-start | bytes 2359304 | tf_op jit(solution)/shard_map/ppermute | solution.py:18
  376.6 38.0 %collective-permute-start.27 = (bf16[3,4,64,512]{3,2,1,0:T(8,128)(2,1)}, bf16[3,4,64,512]{3,2,1,0:T(8,128)(2,1)S(1)}, u32[]{:S(2)}, u32[]{:S(2)}) collective-permute-start(bf16[3,4,64,512]{3,2,1,0:T(8,128)(2,1)} %get-tuple-element.31), channel_id=1, source_target_pairs={{0,2},{1,3},{2,0},{3,1},{4,6},{5,7},{6,4},{7,5},{8,10},{9,11},{10,... | collective-permute-start | bytes 2359304 | tf_op jit(solution)/shard_map/ppermute | solution.py:18
  377.5 40.3 %collective-permute-start.28 = (bf16[3,4,64,512]{3,2,1,0:T(8,128)(2,1)}, bf16[3,4,64,512]{3,2,1,0:T(8,128)(2,1)}, u32[]{:S(2)}, u32[]{:S(2)}) collective-permute-start(bf16[3,4,64,512]{3,2,1,0:T(8,128)(2,1)} %get-tuple-element.32), channel_id=1, source_target_pairs={{0,3},{1,2},{2,1},{3,0},{4,7},{5,6},{6,5},{7,4},{8,11},{9,10},{10,... | collective-permute-start | bytes 2359304 | tf_op jit(solution)/shard_map/ppermute | solution.py:18
  381.5 153.5 %reduce-scatter.4.cloned.1.call-start = ((), (), s32[]{:S(2)}) async-start(), calls=%async_computation.12 | async-start | bytes 2580480 | tf_op jit(solution)/shard_map/reduce_scatter | solution.py:300
  384.7 67.1 %collective-permute-start.42 = (bf16[576,1728]{1,0:T(8,128)(2,1)}, bf16[576,1728]{1,0:T(8,128)(2,1)}, u32[]{:S(2)}, u32[]{:S(2)}) collective-permute-start(bf16[576,1728]{1,0:T(8,128)(2,1)} %dynamic-slice_bitcast_fusion.2), channel_id=1, source_target_pairs={{0,16},{16,0},{1,17},{17,1},{2,18},{18,2},{3,19},{19,3},{4,20},{20... | collective-permute-start | bytes 5971976 | tf_op jit(solution)/shard_map/ppermute | solution.py:18
  386.2 33.9 %collective-permute-start.33 = (bf16[256,256]{1,0:T(8,128)(2,1)S(1)}, bf16[256,256]{1,0:T(8,128)(2,1)S(1)}, u32[]{:S(2)}, u32[]{:S(2)}) collective-permute-start(bf16[256,256]{1,0:T(8,128)(2,1)S(1)} %get-tuple-element.95), channel_id=1, source_target_pairs={{0,3},{1,2},{2,1},{3,0},{4,7},{5,6},{6,5},{7,4},{8,11},{9,10},{10,... | collective-permute-start | bytes 393224 | tf_op jit(solution)/shard_map/ppermute | solution.py:18
  387.9 29.9 %copy-start.9 = (f32[3,4,64,512]{3,2,1,0:T(8,128)S(1)}, f32[3,4,64,512]{3,2,1,0:T(8,128)}, u32[]{:S(2)}) copy-start(f32[3,4,64,512]{3,2,1,0:T(8,128)} %copy-done.8) | copy-start | bytes 4718596
  396.7 21.1 %copy-start.69 = (bf16[3,4,64,512]{3,2,1,0:T(8,128)(2,1)}, bf16[3,4,64,512]{3,2,1,0:T(8,128)(2,1)S(1)}, u32[]{:S(2)}) copy-start(bf16[3,4,64,512]{3,2,1,0:T(8,128)(2,1)S(1)} %collective-permute-done.26) | copy-start | bytes 2359300
  396.7 24.7 %collective-permute-start.32 = (bf16[256,256]{1,0:T(8,128)(2,1)S(1)}, bf16[256,256]{1,0:T(8,128)(2,1)S(1)}, u32[]{:S(2)}, u32[]{:S(2)}) collective-permute-start(bf16[256,256]{1,0:T(8,128)(2,1)S(1)} %get-tuple-element.96), channel_id=1, source_target_pairs={{0,2},{1,3},{2,0},{3,1},{4,6},{5,7},{6,4},{7,5},{8,10},{9,11},{10,... | collective-permute-start | bytes 393224 | tf_op jit(solution)/shard_map/ppermute | solution.py:18
  414.6 8.3 %collective-permute-start.31 = (bf16[256,256]{1,0:T(8,128)(2,1)S(1)}, bf16[256,256]{1,0:T(8,128)(2,1)S(1)}, u32[]{:S(2)}, u32[]{:S(2)}) collective-permute-start(bf16[256,256]{1,0:T(8,128)(2,1)S(1)} %get-tuple-element.97), channel_id=1, source_target_pairs={{0,1},{1,0},{2,3},{3,2},{4,5},{5,4},{6,7},{7,6},{8,9},{9,8},{10,11... | collective-permute-start | bytes 393224 | tf_op jit(solution)/shard_map/ppermute | solution.py:18
  417.8 65.1 %collective-permute-start.38 = (bf16[576,1024]{1,0:T(8,128)(2,1)}, bf16[576,1024]{1,0:T(8,128)(2,1)}, u32[]{:S(2)}, u32[]{:S(2)}) collective-permute-start(bf16[576,1024]{1,0:T(8,128)(2,1)} %dynamic-slice_bitcast_fusion.3), channel_id=1, source_target_pairs={{0,16},{16,0},{1,17},{17,1},{2,18},{18,2},{3,19},{19,3},{4,20},{20... | collective-permute-start | bytes 3538952 | tf_op jit(solution)/shard_map/ppermute | solution.py:18
  420.1 12.7 %collective-permute-start.29 = (bf16[4,64,512]{2,1,0:T(8,128)(2,1)S(1)}, bf16[4,64,512]{2,1,0:T(8,128)(2,1)S(1)}, u32[]{:S(2)}, u32[]{:S(2)}) collective-permute-start(bf16[4,64,512]{2,1,0:T(8,128)(2,1)S(1)} %get-tuple-element.86), channel_id=1, source_target_pairs={{4,0},{8,4},{12,8},{5,1},{9,5},{13,9},{6,2},{10,6},{14,10},{7,3},{... | collective-permute-start | bytes 786440 | tf_op jit(solution)/shard_map/ppermute | solution.py:23
  421.5 17.2 %collective-permute-start.30 = (bf16[4,64,512]{2,1,0:T(8,128)(2,1)S(1)}, bf16[4,64,512]{2,1,0:T(8,128)(2,1)S(1)}, u32[]{:S(2)}, u32[]{:S(2)}) collective-permute-start(bf16[4,64,512]{2,1,0:T(8,128)(2,1)S(1)} %get-tuple-element.87), channel_id=1, source_target_pairs={{8,0},{12,4},{9,1},{13,5},{10,2},{14,6},{11,3},{15,7},{24,16},{28,... | collective-permute-start | bytes 786440 | tf_op jit(solution)/shard_map/ppermute | solution.py:23
  448.9 25.9 %collective-permute-start.34 = (bf16[576,768]{1,0:T(8,128)(2,1)}, bf16[576,768]{1,0:T(8,128)(2,1)}, u32[]{:S(2)}, u32[]{:S(2)}) collective-permute-start(bf16[576,768]{1,0:T(8,128)(2,1)} %fusion.68), channel_id=1, source_target_pairs={{0,16},{16,0},{1,17},{17,1},{2,18},{18,2},{3,19},{19,3},{4,20},{20... | collective-permute-start | bytes 2654216 | tf_op jit(solution)/shard_map/ppermute | solution.py:18
  461.3 9.5 %all-to-all-start.1 = ((f32[8,1,641]{2,1,0:T(1,128)}), f32[8,1,641]{2,1,0:T(1,128)S(1)}, u32[]{:S(2)}, u32[]{:S(2)}) async-start(f32[8,1,641]{2,1,0:T(1,128)} %all_to_all.21), calls=%async_computation.1 | async-start | bytes 49152 | tf_op jit(solution)/shard_map/all_to_all | solution.py:27
  471.4 7.9 %all-to-all-start.2 = ((f32[4,1,641]{2,1,0:T(1,128)}), f32[4,1,641]{2,1,0:T(1,128)S(1)}, u32[]{:S(2)}, u32[]{:S(2)}) async-start(f32[4,1,641]{2,1,0:T(1,128)} %broadcast_in_dim.20), calls=%async_computation.2 | async-start | bytes 24576 | tf_op jit(solution)/shard_map/all_to_all | solution.py:27
  479.4 35.5 %all-to-all-start.3 = ((bf16[4,144,768]{2,1,0:T(8,128)(2,1)}), bf16[4,144,768]{2,1,0:T(8,128)(2,1)S(1)}, u32[]{:S(2)}, u32[]{:S(2)}) async-start(bf16[4,144,768]{2,1,0:T(8,128)(2,1)} %bitcast.193), calls=%async_computation.3 | async-start | bytes 1769472 | tf_op jit(solution)/shard_map/all_to_all | solution.py:27
  486.3 10.0 %collective-permute-start.39 = (bf16[576,256]{1,0:T(8,128)(2,1)S(1)}, bf16[576,256]{1,0:T(8,128)(2,1)S(1)}, u32[]{:S(2)}, u32[]{:S(2)}) collective-permute-start(bf16[576,256]{1,0:T(8,128)(2,1)S(1)} %get-tuple-element.76), channel_id=1, source_target_pairs={{0,1},{1,0},{2,3},{3,2},{4,5},{5,4},{6,7},{7,6},{8,9},{9,8},{10,11... | collective-permute-start | bytes 884744 | tf_op jit(solution)/shard_map/ppermute | solution.py:18
  487.0 14.3 %collective-permute-start.41 = (bf16[576,256]{1,0:T(8,128)(2,1)S(1)}, bf16[576,256]{1,0:T(8,128)(2,1)S(1)}, u32[]{:S(2)}, u32[]{:S(2)}) collective-permute-start(bf16[576,256]{1,0:T(8,128)(2,1)S(1)} %get-tuple-element.77), channel_id=1, source_target_pairs={{0,3},{1,2},{2,1},{3,0},{4,7},{5,6},{6,5},{7,4},{8,11},{9,10},{10,... | collective-permute-start | bytes 884744 | tf_op jit(solution)/shard_map/ppermute | solution.py:18
  488.5 14.2 %collective-permute-start.40 = (bf16[576,256]{1,0:T(8,128)(2,1)S(1)}, bf16[576,256]{1,0:T(8,128)(2,1)S(1)}, u32[]{:S(2)}, u32[]{:S(2)}) collective-permute-start(bf16[576,256]{1,0:T(8,128)(2,1)S(1)} %get-tuple-element.78), channel_id=1, source_target_pairs={{0,2},{1,3},{2,0},{3,1},{4,6},{5,7},{6,4},{7,5},{8,10},{9,11},{10,... | collective-permute-start | bytes 884744 | tf_op jit(solution)/shard_map/ppermute | solution.py:18
  514.9 13.5 %all-to-all-start.4 = ((bf16[4,144,256]{2,1,0:T(8,128)(2,1)}), bf16[4,144,256]{2,1,0:T(8,128)(2,1)S(1)}, u32[]{:S(2)}, u32[]{:S(2)}) async-start(bf16[4,144,256]{2,1,0:T(8,128)(2,1)} %bitcast.41), calls=%async_computation.4 | async-start | bytes 589824 | tf_op jit(solution)/shard_map/all_to_all | solution.py:27
  519.2 10.7 %collective-permute-start.37 = (bf16[144,512]{1,0:T(8,128)(2,1)S(1)}, bf16[144,512]{1,0:T(8,128)(2,1)S(1)}, u32[]{:S(2)}, u32[]{:S(2)}) collective-permute-start(bf16[144,512]{1,0:T(8,128)(2,1)S(1)} %slice.319), channel_id=1, source_target_pairs={{0,3},{1,2},{2,1},{3,0},{4,7},{5,6},{6,5},{7,4},{8,11},{9,10},{10,... | collective-permute-start | bytes 442376 | tf_op jit(solution)/shard_map/ppermute | solution.py:18
  521.6 8.2 %collective-permute-start.36 = (bf16[144,512]{1,0:T(8,128)(2,1)S(1)}, bf16[144,512]{1,0:T(8,128)(2,1)S(1)}, u32[]{:S(2)}, u32[]{:S(2)}) collective-permute-start(bf16[144,512]{1,0:T(8,128)(2,1)S(1)} %slice.319), channel_id=1, source_target_pairs={{0,2},{1,3},{2,0},{3,1},{4,6},{5,7},{6,4},{7,5},{8,10},{9,11},{10,... | collective-permute-start | bytes 442376 | tf_op jit(solution)/shard_map/ppermute | solution.py:18
  522.1 7.7 %collective-permute-start.35 = (bf16[144,512]{1,0:T(8,128)(2,1)S(1)}, bf16[144,512]{1,0:T(8,128)(2,1)S(1)}, u32[]{:S(2)}, u32[]{:S(2)}) collective-permute-start(bf16[144,512]{1,0:T(8,128)(2,1)S(1)} %slice.319), channel_id=1, source_target_pairs={{0,1},{1,0},{2,3},{3,2},{4,5},{5,4},{6,7},{7,6},{8,9},{9,8},{10,11... | collective-permute-start | bytes 442376 | tf_op jit(solution)/shard_map/ppermute | solution.py:18
  (105 other events, 487.4 us)
Sparse Core Ops, SparseCore 0:
  10.2 33.6 all-gather.4
  45.5 51.7 all-gather.6
  98.9 54.2 all-gather.8
  154.7 45.2 all-gather.10
  333.1 40.6 reduce-scatter.5
  381.6 40.5 reduce-scatter.7
  455.6 49.2 reduce-scatter.3

commit v2 on v1

v2 whole, which is shorter than its diff:
```python
import functools
import math

import jax
import jax.numpy as jnp
from jax import lax
from jax.experimental import pallas as pl
from jax.experimental.pallas import tpu as pltpu
from jax.sharding import PartitionSpec as P

WIN = 512
EPS = 1e-06
MASKED = -1e30
LOW = jnp.bfloat16
F32 = jnp.float32


def swap(values, axis, bits):
    return lax.ppermute(values, axis, [(i, i ^ bits) for i in range(lax.axis_size(axis))])


def shifted(values, axis, by):
    size = lax.axis_size(axis)
    return lax.ppermute(values, axis, [(i, i + by) for i in range(size) if 0 <= i + by < size])


def exchange(values, axes):
    return lax.all_to_all(values, axes, 0, 0, tiled=True)


def after(value, *earlier):
    return lax.optimization_barrier((value,) + earlier)[0]


def dot(left, right, contract):
    return lax.dot_general(left, right, (contract, ((), ())), preferred_element_type=F32)


def mm(left, right):
    return dot(left, right, ((1,), (0,)))


def mm_t(left, right):
    return dot(left, right, ((1,), (1,)))


def t_mm(left, right):
    return dot(left, right, ((0,), (0,)))


def inverse_rms(values):
    return lax.rsqrt(jnp.mean(values * values, axis=-1, keepdims=True) + EPS)


def rms_back(grad, values, inverse, gain_row):
    n = values * inverse
    eg = grad * gain_row
    return inverse * (eg - n * jnp.mean(eg * n, axis=-1, keepdims=True)), grad * n


def turn(values):
    half = values.shape[-1] // 2
    return jnp.concatenate([-values[..., half:], values[..., :half]], axis=-1)


def turn_back(values):
    half = values.shape[-1] // 2
    return jnp.concatenate([values[..., half:], -values[..., :half]], axis=-1)


def rotary_tables(positions, head_width):
    frequency = 10000.0 ** (-2.0 * jnp.arange(head_width // 2, dtype=F32) / head_width)
    angles = positions.astype(F32)[:, None] * frequency[None, :]
    angles = jnp.concatenate([angles, angles], axis=-1)
    return jnp.cos(angles), jnp.sin(angles)


def heads_of(values, heads):
    width = values.shape[1] // heads
    return [values[:, h * width : (h + 1) * width] for h in range(heads)]


VMEM = pl.BlockSpec(memory_space=pltpu.VMEM)
SMEM = pl.BlockSpec(memory_space=pltpu.SMEM)
ROOM = pltpu.CompilerParams(vmem_limit_bytes=60 * 1024 * 1024)


def cost(multiply_adds, *arrays):
    moved = sum(math.prod(v.shape) * jnp.dtype(v.dtype).itemsize for v in arrays)
    return pl.CostEstimate(flops=2 * multiply_adds, bytes_accessed=moved, transcendentals=0)


def struct(shape, dtype):
    return jax.ShapeDtypeStruct(shape, dtype)


def column_sum(values):
    return jnp.sum(values, axis=0, keepdims=True)


def assemble_kernel(pieces, core_ref, *refs):
    width = refs[0].shape[1] // 2
    results = refs[2 * pieces :]
    for step in range(2):

        @pl.when(pl.program_id(0) == step)
        def _():
            for i, result in enumerate(results):
                for p in range(pieces):
                    result[0, :, p * width : (p + 1) * width] = refs[step * pieces + p][:, i * width : (i + 1) * width]


def assemble(core, mine, others):
    half, width = mine[0].shape
    pieces = len(mine)
    wide = pieces * width // 2
    out = pl.BlockSpec((1, half, wide), lambda i, core: (i ^ core[0], 0, 0))
    results = pl.pallas_call(
        functools.partial(assemble_kernel, pieces),
        grid_spec=pltpu.PrefetchScalarGridSpec(
            num_scalar_prefetch=1,
            grid=(2,),
            in_specs=[pl.BlockSpec((half, width), lambda i, core: (0, 0))] * (2 * pieces),
            out_specs=[out, out],
        ),
        out_shape=[struct((2, half, wide), LOW)] * 2,
        compiler_params=ROOM,
        cost_estimate=cost(0, *mine, *others, *mine, *others),
        name="assemble",
    )(core.reshape(1), *mine, *others)
    return [v.reshape(2 * half, wide) for v in results]


def norm_rows_kernel(chunks, place_ref, x_ref, gain_ref, out_ref):
    sub = x_ref.shape[1] // chunks
    for p in range(chunks):
        x = x_ref[0, pl.ds(pl.multiple_of((place_ref[0] ^ p) * sub, sub), sub), :].astype(F32)
        out_ref[p, 0] = (x * inverse_rms(x) * gain_ref[...]).astype(LOW)


def norm_rows(place, x, gain_row, chunks):
    seqs, rows, width = x.shape
    sub = rows // chunks
    return pl.pallas_call(
        functools.partial(norm_rows_kernel, chunks),
        grid=(seqs,),
        in_specs=[
            pl.BlockSpec(memory_space=pltpu.SMEM),
            pl.BlockSpec((1, rows, width), lambda s: (s, 0, 0)),
            pl.BlockSpec((1, width), lambda s: (0, 0)),
        ],
        out_specs=pl.BlockSpec((chunks, 1, sub, width), lambda s: (0, s, 0, 0)),
        out_shape=jax.ShapeDtypeStruct((chunks, seqs, sub, width), LOW),
        compiler_params=ROOM,
        cost_estimate=cost(0, x, x, x, x),
        name="norm_rows",
    )(place.reshape(1), x, gain_row).reshape(chunks * seqs * sub, width)


def keys_kernel(core_ref, x_ref, near_ref, far_ref, gain_ref, cos_ref, sin_ref, pair_ref, first_ref, raw_ref, full_ref):
    chunks, _, sub, width = x_ref.shape
    half = near_ref.shape[0]
    head = gain_ref.shape[1]

    @pl.when(pl.program_id(0) == 0)
    def _():
        for place, source in ((core_ref[0], near_ref), (1 - core_ref[0], far_ref)):
            full_ref[pl.ds(pl.multiple_of(place * half, half), half), :] = source[...]

    kv = mm(x_ref[...].reshape(chunks * sub, width), full_ref[...])
    key = kv[:, :head]
    n = key * inverse_rms(key) * gain_ref[...]
    rot = (n * cos_ref[...] + turn(n) * sin_ref[...]).astype(LOW)
    value = kv[:, head:].astype(LOW)
    raw_ref[...] = key[:sub]
    pair_ref[:, 0, :, :head] = rot.reshape(chunks, sub, head)
    pair_ref[:, 0, :, head:] = value.reshape(chunks, sub, head)
    first_ref[0, :, :head] = rot[:sub]
    first_ref[0, :, head:] = value[:sub]


def project_keys(core, normed, near, far, gain_row, cos, sin):
    chunks, seqs, sub, width = normed.shape
    half, both = near.shape
    head = both // 2
    whole = lambda *shape: pl.BlockSpec(shape, lambda s: (0,) * len(shape))
    return pl.pallas_call(
        keys_kernel,
        grid=(seqs,),
        in_specs=[
            SMEM,
            pl.BlockSpec((chunks, 1, sub, width), lambda s: (0, s, 0, 0)),
            whole(half, both),
            whole(half, both),
            whole(1, head),
            whole(chunks * sub, head),
            whole(chunks * sub, head),
        ],
        out_specs=[
            pl.BlockSpec((chunks, 1, sub, both), lambda s: (0, s, 0, 0)),
            pl.BlockSpec((1, sub, both), lambda s: (s, 0, 0)),
            pl.BlockSpec((sub, head), lambda s: (s, 0)),
            whole(2 * half, both),
        ],
        out_shape=[
            struct((chunks, seqs, sub, both), LOW),
            struct((seqs, sub, both), LOW),
            struct((seqs * sub, head), F32),
            struct((2 * half, both), LOW),
        ],
        compiler_params=ROOM,
        cost_estimate=cost(seqs * chunks * sub * width * both, normed, normed),
        name="project_keys",
    )(core.reshape(1), normed, near, far, gain_row, cos, sin)


def mask_of(qinfo_ref, kinfo_ref):
    qpos, qseg = qinfo_ref[0, :, 0:1], qinfo_ref[0, :, 1:2]
    kpos, kseg = kinfo_ref[0, 0:1, :], kinfo_ref[0, 1:2, :]
    return (kseg == qseg) & (kpos <= qpos) & (kpos > qpos - WIN)


def key_rows(kv_refs, width):
    own_ref, *far_refs = kv_refs
    sides = []
    for at in (0, width):
        own = own_ref[:, 0, :, at : at + width].reshape(own_ref.shape[0] * own_ref.shape[2], width)
        sides.append(jnp.concatenate([own] + [r[0, :, at : at + width] for r in far_refs], axis=0))
    return sides


def attend_kernel(heads, qinfo_ref, kinfo_ref, q_ref, gain_ref, cos_ref, sin_ref, *refs):
    kv_refs, (rot_ref, out_ref, lse_ref) = refs[:-3], refs[-3:]
    width = q_ref.shape[1] // heads
    scale = width ** (-0.5)
    rotated = []
    for h, q in enumerate(heads_of(q_ref[...], heads)):
        n = q * inverse_rms(q) * gain_ref[...]
        rot = ((n * cos_ref[...] + turn(n) * sin_ref[...]) * scale).astype(LOW)
        rot_ref[:, h * width : (h + 1) * width] = rot
        rotated.append(rot)
    rows = jnp.concatenate(rotated, axis=0)
    keys, vals = key_rows(kv_refs, width)
    bias = jnp.where(mask_of(qinfo_ref, kinfo_ref), 0.0, MASKED)
    allowed = jnp.concatenate([bias] * heads, axis=0) == 0.0
    scores = jnp.where(allowed, mm_t(rows, keys), MASKED)
    top = jnp.max(scores, axis=1, keepdims=True)
    expos = jnp.exp(scores - top)
    total = jnp.sum(expos, axis=1, keepdims=True)
    lse_ref[0] = top + jnp.log(total)
    probs = (expos / total).astype(LOW)
    attended = mm(probs, vals).astype(LOW)
    count = q_ref.shape[0]
    for h in range(heads):
        out_ref[:, h * width : (h + 1) * width] = attended[h * count : (h + 1) * count]


def attend_back_kernel(heads, chunks, blocks, place_ref, qinfo_ref, kinfo_ref, q_ref, gain_ref, cos_ref, sin_ref, rot_ref, lse_ref,
                       dout_ref, *refs):
    far_count = (blocks - 1) * chunks
    kv_refs, (dq_ref, dgain_ref), dkv_refs = refs[: far_count + 1], refs[far_count + 1 : far_count + 3], refs[far_count + 3 :]
    width = q_ref.shape[1] // heads
    scale = width ** (-0.5)
    count = q_ref.shape[0]
    rows = jnp.concatenate(heads_of(rot_ref[...], heads), axis=0)
    douts = jnp.concatenate(heads_of(dout_ref[...], heads), axis=0)
    keys, vals = key_rows(kv_refs, width)
    bias = jnp.where(mask_of(qinfo_ref, kinfo_ref), 0.0, MASKED)
    allowed = jnp.concatenate([bias] * heads, axis=0) == 0.0
    probs = jnp.where(allowed, jnp.exp(mm_t(rows, keys) - lse_ref[0]), 0.0)
    d_probs = mm_t(douts, vals)
    delta = jnp.sum(probs * d_probs, axis=1, keepdims=True)
    d_scores = (probs * (d_probs - delta)).astype(LOW)
    d_rows = mm(d_scores, keys)
    d_keys = t_mm(d_scores, rows)
    d_vals = t_mm(probs.astype(LOW), douts)
    per = kv_refs[0].shape[2]
    for part, at in ((d_keys, 0), (d_vals, width)):
        piece = lambda b, p: part[(b * chunks + p) * per : (b * chunks + p + 1) * per]
        for b in range(blocks):
            dkv_refs[0][b, 0, :, at : at + width] = piece(b, 0)
        for p in range(1, chunks):
            earlier = (place_ref[0] ^ p) < place_ref[0]
            for b in range(1, blocks - 1):
                dkv_refs[p][b - 1, 0, :, at : at + width] = piece(b, p).astype(LOW)
            dkv_refs[p][blocks - 2, 0, :, at : at + width] = jnp.where(earlier, piece(0, p), piece(blocks - 1, p)).astype(LOW)
    gain_sum = jnp.zeros((1, width), F32)
    for h, q in enumerate(heads_of(q_ref[...], heads)):
        e = d_rows[h * count : (h + 1) * count] * scale
        e = e * cos_ref[...] + turn_back(e * sin_ref[...])
        d_q, d_g = rms_back(e, q, inverse_rms(q), gain_ref[...])
        gain_sum = gain_sum + column_sum(d_g)
        dq_ref[:, h * width : (h + 1) * width] = d_q.astype(LOW)
    dgain_ref[0] = gain_sum


def pair_sum_kernel(*refs):
    out = refs[-1]
    for i in range(out.shape[0]):
        out[i] = (refs[2 * i][...].astype(F32) + refs[2 * i + 1][...].astype(F32)).astype(LOW)


def pair_sum(*pairs):
    rows, width = pairs[0][0].shape
    step = rows // 4 if rows % 64 == 0 else rows
    arrays = [v for pair in pairs for v in pair]
    return pl.pallas_call(
        pair_sum_kernel,
        grid=(rows // step,),
        in_specs=[pl.BlockSpec((step, width), lambda j: (j, 0))] * len(arrays),
        out_specs=pl.BlockSpec((len(pairs), step, width), lambda j: (0, j, 0)),
        out_shape=struct((len(pairs), rows, width), LOW),
        compiler_params=ROOM,
        name="pair_sum",
    )(*arrays)


def attention_specs(seqs, rows, spans, chunks, wide, width):
    whole = lambda *shape: pl.BlockSpec(shape, lambda s: (0,) * len(shape))
    return dict(
        qinfo=pl.BlockSpec((1, rows, 2), lambda s: (s, 0, 0)),
        kinfo=pl.BlockSpec((1, 2, spans), lambda s: (s, 0, 0)),
        q=pl.BlockSpec((rows, wide), lambda s: (s, 0)),
        gain=whole(1, width),
        table=whole(rows, width),
        own=pl.BlockSpec((chunks, 1, rows, 2 * width), lambda s: (0, s, 0, 0)),
        far=pl.BlockSpec((1, rows, 2 * width), lambda s: (s, 0, 0)),
        lse=pl.BlockSpec((1, rows * (wide // width), 1), lambda s: (s, 0, 0)),
        dgain=pl.BlockSpec((1, 1, width), lambda s: (s, 0, 0)),
    )


def mix_kernel(att_ref, out_ref, x_ref, gain_attn_ref, gain_ffn_ref, branch_ref, hidden_ref, ffn_ref):
    branch = mm_t(att_ref[...], out_ref[...])
    branch_ref[...] = branch
    hidden = x_ref[...].astype(F32) + branch * inverse_rms(branch) * gain_attn_ref[...]
    hidden_ref[...] = hidden
    ffn_ref[...] = (hidden * inverse_rms(hidden) * gain_ffn_ref[...]).astype(LOW)


def for_blocks(width, step, block):
    full, rest = divmod(width, step)

    @pl.when(pl.program_id(0) < full)
    def _():
        block(step)

    if rest:

        @pl.when(pl.program_id(0) == full)
        def _():
            block(rest)


def ffn_kernel(units, chunks, *refs):
    rows_refs, (gate_ref, up_ref, down_ref) = refs[:chunks], refs[chunks : chunks + 3]
    part_refs, (act_ref, slope_ref, curve_ref, sums) = refs[chunks + 3 : 2 * chunks + 3], refs[2 * chunks + 3 :]

    @pl.when(pl.program_id(0) == 0)
    def _():
        sums[...] = jnp.zeros_like(sums)

    def block(size):
        rows = jnp.concatenate([r[...] for r in rows_refs], axis=0)
        gate, up = mm(rows, gate_ref[0, :, :size]), mm(rows, up_ref[0, :, :size])
        root = (2.0 / math.pi) ** 0.5
        square = gate * gate
        bend = jnp.tanh(root * (gate + 0.044715 * (square * gate)))
        share = 0.5 * (1.0 + bend)
        curve = gate * share
        slope = share + 0.5 * gate * (1.0 - bend * bend) * (root * (1.0 + 3.0 * 0.044715 * square))
        act = (curve * up).astype(LOW)
        act_ref[:, :size] = act
        slope_ref[:, :size] = (slope * up).astype(LOW)
        curve_ref[:, :size] = curve.astype(LOW)
        sums[...] += mm_t(act, down_ref[0, :, :size])

    for_blocks(units, act_ref.shape[1], block)
    split_rows(sums, part_refs)


def split_rows(sums, part_refs):
    @pl.when(pl.program_id(0) == pl.num_programs(0) - 1)
    def _():
        count = part_refs[0].shape[0]
        for p, part in enumerate(part_refs):
            part[...] = sums[p * count : (p + 1) * count].astype(part.dtype)


def ffn_back_kernel(units, chunks, *refs):
    rows_refs, (gate_ref, up_ref, down_ref, slope_ref, curve_ref) = refs[:chunks], refs[chunks : chunks + 5]
    part_refs, (dgate_ref, dup_ref, sums) = refs[chunks + 5 : 2 * chunks + 5], refs[2 * chunks + 5 :]

    @pl.when(pl.program_id(0) == 0)
    def _():
        sums[...] = jnp.zeros_like(sums)

    def block(size):
        rows = jnp.concatenate([r[...] for r in rows_refs], axis=0)
        d_act = mm(rows, down_ref[0, :, :size])
        d_gate = (d_act * slope_ref[:, :size].astype(F32)).astype(LOW)
        d_up = (d_act * curve_ref[:, :size].astype(F32)).astype(LOW)
        dgate_ref[:, :size] = d_gate
        dup_ref[:, :size] = d_up
        sums[...] += mm_t(d_gate, gate_ref[0, :, :size]) + mm_t(d_up, up_ref[0, :, :size])

    for_blocks(units, dgate_ref.shape[1], block)
    split_rows(sums, part_refs)


def ffn_call(kernel, name, rows, weights, saved, results, dtype, step=640):
    chunks = len(rows)
    count, width = rows[0].shape
    units = weights.shape[2]
    whole = pl.BlockSpec((count, width), lambda j: (0, 0))
    strip = pl.BlockSpec((chunks * count, step), lambda j: (0, j))
    flat = pl.pallas_call(
        functools.partial(kernel, units, chunks),
        grid=(pl.cdiv(units, step),),
        in_specs=[whole] * chunks
        + [pl.BlockSpec((1, width, step), lambda j, i=i: (i, 0, j)) for i in range(3)]
        + [strip] * len(saved),
        out_specs=[whole] * chunks + [strip] * results,
        out_shape=[struct((count, width), dtype)] * chunks + [struct((chunks * count, units), LOW)] * results,
        scratch_shapes=[pltpu.VMEM((chunks * count, width), F32)],
        compiler_params=ROOM,
        cost_estimate=cost(3 * chunks * count * width * units, *rows, weights, *saved),
        name=name,
    )(*rows, weights, weights, weights, *saved)
    return flat[:chunks], flat[chunks:]


def loss_kernel(factor_ref, hidden_ref, target_ref, valid_ref, gain_ref, *refs):
    parts, (out_ref, dres_ref, dffn_ref, dgain_ref, error_ref) = refs[:-5], refs[-5:]
    ffn = sum(r[...].astype(F32) for r in parts)
    inverse = inverse_rms(ffn)
    result = hidden_ref[...] + ffn * inverse * gain_ref[...]
    out_ref[...] = result.astype(LOW)
    mismatch = result - target_ref[...].astype(F32)
    marked = valid_ref[...] * mismatch
    error_ref[...] = jnp.broadcast_to(column_sum(jnp.sum(marked * mismatch, axis=1, keepdims=True)), error_ref.shape)
    d_result = factor_ref[0] * marked
    dres_ref[...] = d_result
    d_ffn, d_gain = rms_back(d_result, ffn, inverse, gain_ref[...])
    dffn_ref[...] = d_ffn.astype(LOW)
    dgain_ref[...] = column_sum(d_gain)


def middle_kernel(dres_ref, hidden_ref, branch_ref, out_ref, gain_ffn_ref, gain_attn_ref, *refs):
    parts, (dhid_ref, dbranch_ref, datt_ref, dgain_ffn_ref, dgain_attn_ref) = refs[:-5], refs[-5:]
    d_ffn_in = sum(r[...].astype(F32) for r in parts)
    hidden = hidden_ref[...]
    d_add, d_gain = rms_back(d_ffn_in, hidden, inverse_rms(hidden), gain_ffn_ref[...])
    dgain_ffn_ref[...] = column_sum(d_gain)
    d_hidden = dres_ref[...] + d_add
    dhid_ref[...] = d_hidden
    branch = branch_ref[...]
    d_branch, d_gain = rms_back(d_hidden, branch, inverse_rms(branch), gain_attn_ref[...])
    dgain_attn_ref[...] = column_sum(d_gain)
    low = d_branch.astype(LOW)
    dbranch_ref[...] = low
    datt_ref[...] = mm(low, out_ref[...]).astype(LOW)


def finish_kernel(core_ref, raw_ref, cos_ref, sin_ref, gain_key_ref, dq_ref, q_ref, kv_ref, dhid_ref, x_ref, gain_ref, normed_ref, *refs):
    parts, (din_ref, dgain_ref, dgain_key_ref, send_ref, own_ref, sums) = refs[:-6], refs[-6:]
    head = raw_ref.shape[1]
    d_kv = sum(r[...].astype(F32) for r in parts)
    key = raw_ref[...]
    e = d_kv[:, :head]
    e = e * cos_ref[...] + turn_back(e * sin_ref[...])
    d_key, d_gain = rms_back(e, key, inverse_rms(key), gain_key_ref[...])
    dgain_key_ref[...] = column_sum(d_gain)
    low = jnp.concatenate([d_key.astype(LOW), d_kv[:, head:].astype(LOW)], axis=1)
    sums[...] = mm(normed_ref[...].T, low)
    half = own_ref.shape[0]
    core = core_ref[0]
    own_ref[...] = sums[pl.ds(pl.multiple_of(core * half, half), half), :].astype(LOW)
    send_ref[...] = sums[pl.ds(pl.multiple_of((1 - core) * half, half), half), :].astype(LOW)
    d_normed = mm_t(dq_ref[...], q_ref[...]) + mm_t(low, kv_ref[...])
    x = x_ref[...].astype(F32)
    d_x, d_gain = rms_back(d_normed, x, inverse_rms(x), gain_ref[...])
    dgain_ref[...] = column_sum(d_gain)
    din_ref[...] = dhid_ref[...] + d_x


def weight_grad_kernel(chunks, sets, core_ref, *refs):
    lefts, refs = refs[:chunks], refs[chunks:]
    rights, refs = refs[: chunks * sets], refs[chunks * sets :]
    outs, (turned, sums) = refs[: 2 * sets], refs[2 * sets :]
    rows = lefts[0].shape[0]
    half = outs[0].shape[0]

    @pl.when(pl.program_id(0) == 0)
    def _():
        for p in range(chunks):
            turned[:, p * rows : (p + 1) * rows] = lefts[p][...].T

    core = core_ref[0]
    for i in range(sets):
        right = jnp.concatenate([r[...] for r in rights[i * chunks : (i + 1) * chunks]], axis=0)
        sums[i] = mm(turned[...], right)
        for place, out in ((1 - core, outs[2 * i]), (core, outs[2 * i + 1])):
            out[...] = sums[i, pl.ds(pl.multiple_of(place * half, half), half), :].astype(LOW)


def weight_grad(core, rows, lefts, *rights, step=256):
    chunks, sets = len(lefts), len(rights)
    height = lefts[0][0].shape[1]
    width = rights[0][0][0].shape[1]
    rights = [pair for group in rights for pair in group]
    out = pl.BlockSpec((height // 2, step), lambda j: (0, j))
    flat = pl.pallas_call(
        functools.partial(weight_grad_kernel, chunks, sets),
        grid=(pl.cdiv(width, step),),
        in_specs=[SMEM]
        + [pl.BlockSpec((rows, height), lambda j, at=at: (at, 0)) for _, at in lefts]
        + [pl.BlockSpec((rows, step), lambda j, at=at: (at, j)) for _, at in rights],
        out_specs=[out] * (2 * sets),
        out_shape=[struct((height // 2, width), LOW)] * (2 * sets),
        scratch_shapes=[pltpu.VMEM((height, chunks * rows), LOW), pltpu.VMEM((sets, height, step), F32)],
        compiler_params=ROOM,
        cost_estimate=cost(sets * chunks * rows * height * width, *[v for v, _ in lefts], struct((height, sets * width), LOW)),
        name="weight_grad",
    )(core.reshape(1), *[v for v, _ in lefts], *[v for v, _ in rights])
    return [flat[2 * i : 2 * i + 2] for i in range(sets)]


def shards(inputs, target, segment_ids, w_query, w_key, w_value, w_out, w_gate, w_up, w_down,
           gain_input, gain_query, gain_key, gain_post_attn, gain_pre_ffn, gain_post_ffn):
    F, C, T = (lax.axis_size(a) for a in ("fsdp", "ctx", "tp"))
    f, z, t = (lax.axis_index(a) for a in ("fsdp", "ctx", "tp"))
    me = f * C + z
    seqs, block_rows, width_model = inputs.shape
    piece = w_query.shape[0]
    head_width = w_key.shape[1]
    gain_piece = gain_query.shape[0]
    sub = block_rows // T
    own = seqs * sub
    half = C * piece
    halo = -(-(WIN - 1) // block_rows)
    spans = (halo + 1) * block_rows

    both = 2 * head_width
    blocks = jnp.stack([jnp.concatenate([w_query, w_out.T], axis=1), jnp.concatenate([w_key, w_value], axis=1)])
    near = lax.all_gather(blocks, "ctx", axis=1, tiled=True)
    weights = lax.all_gather(jnp.stack([w_gate, w_up, w_down.T]), ("fsdp", "ctx"), axis=1, tiled=True)
    packed = jnp.concatenate(
        [gain_input, gain_post_attn, gain_pre_ffn, gain_post_ffn, gain_query, gain_key, segment_ids.astype(LOW).reshape(-1)]
    )
    packed = exchange(jnp.broadcast_to(packed[None], (F * C, packed.shape[0])), ("fsdp", "ctx")).astype(F32)
    at = 4 * piece
    g_input, g_post_attn, g_pre_ffn, g_post_ffn = [
        packed[:, i * piece : (i + 1) * piece].reshape(1, width_model) for i in range(4)
    ]
    g_query, g_key = [
        packed[:, at + i * gain_piece : at + (i + 1) * gain_piece].reshape(1, head_width) for i in range(2)
    ]
    seg_blocks = packed[:, at + 2 * gain_piece :].astype(jnp.int32)
    count = jnp.sum((seg_blocks != 0).astype(F32))
    normed = norm_rows(t, inputs, g_input, T)
    def sub_rows(values):
        return [lax.dynamic_slice_in_dim(values, (t ^ p) * sub, sub, 1) for p in range(T)]

    x_own = lax.dynamic_slice_in_dim(inputs, t * sub, sub, 1).reshape(own, width_model)
    target_own = lax.dynamic_slice_in_dim(target, t * sub, sub, 1).reshape(own, width_model)
    positions = jnp.concatenate([z * block_rows + (t ^ p) * sub + jnp.arange(sub, dtype=jnp.int32) for p in range(T)])
    segs = [segment_ids + 1]
    for d in range(1, halo + 1):
        far = lax.dynamic_index_in_dim(seg_blocks, jnp.maximum(me - d, 0), 0, False).reshape(seqs, block_rows)
        segs.append(jnp.where(z >= d, far + 1, 0))
    key_seg = jnp.concatenate([v for seg in segs for v in sub_rows(seg)], axis=1)
    key_pos = jnp.concatenate([positions - d * block_rows for d in range(halo + 1)])
    kinfo = jnp.stack([jnp.broadcast_to(key_pos, (seqs, spans)), key_seg], axis=1)
    qinfo = jnp.stack([jnp.broadcast_to(positions[:sub], (seqs, sub)), key_seg[:, :sub]], axis=2)
    valid_own = (key_seg[:, :sub] != 1).astype(F32).reshape(own, 1)
    cos_all, sin_all = rotary_tables(positions, head_width)
    cos_own, sin_own = cos_all[:sub], sin_all[:sub]

    ready = (normed, kinfo, qinfo, cos_all, sin_all, cos_own, sin_own, g_query, g_key, g_post_attn, g_pre_ffn, x_own)
    (near, *ready) = lax.optimization_barrier((near,) + ready)
    normed, kinfo, qinfo, cos_all, sin_all, cos_own, sin_own, g_query, g_key, g_post_attn, g_pre_ffn, x_own = ready
    near_qo, near_kv = near
    far_kv = swap(near_kv, "fsdp", 1)
    near_qo = [near_qo] + [swap(near_qo, "tp", p) for p in range(1, T)]
    pair, first, key_own, kv_full = project_keys(f, normed.reshape(T, seqs, sub, width_model), near_kv, far_kv, g_key, cos_all, sin_all)
    q_full, out_full = assemble(f, near_qo, [swap(after(v, first), "fsdp", 1) for v in near_qo])
    kv_rows, far = [pair], first
    for d in range(halo):
        far = shifted(far, "ctx", 1)
        kv_rows += [swap(far, "tp", p) if p else far for p in range(T)]
    normed_own = normed[:own]
    q_raw = mm(normed_own, q_full)
    wide = q_raw.shape[1]
    heads = wide // head_width
    specs = attention_specs(seqs, sub, spans, T, wide, head_width)
    kv_specs = [specs["own"]] + [specs["far"]] * (halo * T)
    q_rot, attended, lse = pl.pallas_call(
        functools.partial(attend_kernel, heads),
        grid=(seqs,),
        in_specs=[specs[k] for k in ("qinfo", "kinfo", "q", "gain", "table", "table")] + kv_specs,
        out_specs=[specs["q"], specs["q"], specs["lse"]],
        out_shape=[struct((own, wide), LOW), struct((own, wide), LOW), struct((seqs, sub * heads, 1), F32)],
        compiler_params=ROOM,
        cost_estimate=cost(4 * own * spans * wide // seqs, *kv_rows, q_raw),
        name="attend",
    )(qinfo, kinfo, q_raw, g_query, cos_own, sin_own, *kv_rows)
    token = struct((own, width_model), F32)
    token_low = struct((own, width_model), LOW)
    gain_row = struct((1, width_model), F32)
    branch, hidden, ffn_in = pl.pallas_call(
        mix_kernel, out_shape=[token, token, token_low], compiler_params=ROOM, cost_estimate=cost(own * wide * width_model, out_full, out_full), name="mix"
    )(attended, out_full, x_own, g_post_attn, g_pre_ffn)

    from_tp = lambda parts: parts[:1] + [swap(v, "tp", p) for p, v in enumerate(parts) if p]
    ffn_ins = from_tp([ffn_in] * T)
    groups = [[0], [1], list(range(2, T))]
    place = {p: (g, i) for g, group in enumerate(groups) for i, p in enumerate(group)}
    done = [ffn_call(ffn_kernel, "ffn", [ffn_ins[p] for p in group], weights, (), 3, LOW if g else F32) for g, group in enumerate(groups)]
    parts = [done[place[p][0]][0][place[p][1]] for p in range(T)]
    acts, slopes, curves = zip(*[results for _, results in done])
    acts = [(acts[place[p][0]], place[p][1]) for p in range(T)]
    all_tokens = seqs * block_rows * F * C
    output, d_result, d_ffn_low, dg_post_ffn, error = pl.pallas_call(
        loss_kernel,
        in_specs=[SMEM] + [VMEM] * (4 + T),
        out_shape=[token_low, token, token_low, gain_row, struct((1, 128), F32)],
        compiler_params=ROOM,
        cost_estimate=cost(own, *parts, *parts),
        name="loss",
    )((all_tokens / count).reshape(1), hidden, target_own, valid_own, g_post_ffn, *from_tp(parts))

    def collect_core(send, mine, *earlier):
        other = swap(send, "fsdp", 1)
        return mine.astype(F32) + (after(other, *earlier) if earlier else other).astype(F32)

    def scatter_ctx(sums):
        return lax.psum_scatter(sums, "ctx", scatter_dimension=1, tiled=True).astype(F32)

    d_outs = from_tp([d_ffn_low] * T)
    done = []
    for g, group in enumerate(groups):
        rows = [d_outs[p] for p in group]
        if g == 1:
            rows[0] = after(rows[0], done[0][0][0])
        if g == 2:
            (down_halves,) = weight_grad(f, own, [(after(v, done[1][0][0]) if p == 2 else v, 0) for p, v in enumerate(d_outs)], acts)
            down_sum = pair_sum((down_halves[1], swap(down_halves[0], "fsdp", 1)))
            rows[0] = after(rows[0], down_sum)
        done.append(ffn_call(ffn_back_kernel, "ffn_back", rows, weights, (slopes[g], curves[g]), 2, LOW if g else F32))
    (grad_down,) = scatter_ctx(down_sum)
    parts = [done[place[p][0]][0][place[p][1]] for p in range(T)]
    d_gates, d_ups = [[(done[place[p][0]][1][i], place[p][1]) for p in range(T)] for i in range(2)]
    first_in = after(ffn_ins[0], parts[-1])
    gate_halves, up_halves = weight_grad(f, own, [(v, 0) for v in [first_in] + ffn_ins[1:]], d_gates, d_ups)

    parts = [after(v, *gate_halves, *up_halves) if p == 0 else v for p, v in enumerate(from_tp(parts))]
    d_hidden, d_branch, d_attended, dg_pre_ffn, dg_post_attn = pl.pallas_call(
        middle_kernel,
        out_shape=[token, token_low, struct((own, wide), LOW), gain_row, gain_row],
        compiler_params=ROOM,
        name="middle",
    )(d_result, hidden, branch, out_full, g_pre_ffn, g_post_attn, *parts)
    assert halo * block_rows == WIN
    others = [after(swap(after(v[0], *parts[1:]), "fsdp", 1), d_branch) for v in (gate_halves, up_halves)]
    both_sums = pair_sum((gate_halves[1], others[0]), (up_halves[1], others[1]))
    grad_gate, grad_up = scatter_ctx(both_sums)
    d_attended = after(d_attended, both_sums)
    (out_halves,) = weight_grad(f, own, [(d_branch, 0)], [(attended, 0)])
    out_sum = collect_core(*out_halves)
    out_low = out_sum.astype(LOW)
    d_query, dg_query, *d_pairs = pl.pallas_call(
        functools.partial(attend_back_kernel, heads, T, halo + 1),
        grid=(seqs,),
        in_specs=[SMEM] + [specs[k] for k in ("qinfo", "kinfo", "q", "gain", "table", "table", "q", "lse", "q")] + kv_specs,
        out_specs=[specs["q"], specs["dgain"]]
        + [pl.BlockSpec((halo + (p == 0), 1, sub, 2 * head_width), lambda s: (0, s, 0, 0)) for p in range(T)],
        out_shape=[struct((own, wide), LOW), struct((seqs, 1, head_width), F32)]
        + [struct((halo + (p == 0), seqs, sub, 2 * head_width), F32 if p == 0 else LOW) for p in range(T)],
        compiler_params=ROOM,
        name="attend_back",
    )(t.reshape(1), qinfo, kinfo, q_raw, g_query, cos_own, sin_own, q_rot, lse, d_attended, *kv_rows)
    d_blocks = [d_pairs[0][b] for b in range(halo + 1)]
    for p in range(1, T):
        got = after(swap(d_pairs[p], "tp", p), out_low).astype(F32)
        for b in range(1, halo):
            d_blocks[b] = d_blocks[b] + got[b - 1]
        later = (t ^ p) > t
        d_blocks[0] = d_blocks[0] + jnp.where(later, got[halo - 1], 0.0)
        d_blocks[halo] = d_blocks[halo] + jnp.where(later, 0.0, got[halo - 1])
    d_kv = d_blocks[halo]
    for d in range(halo, 0, -1):
        come = shifted(d_kv.astype(LOW), "ctx", -1)
        if d == halo:
            d_query_late, out_low = after(d_query, come), after(out_low, come)
        if d > 1:
            d_kv = d_blocks[d - 1] + come.astype(F32)
    d_kv = [d_blocks[0], come]
    out_head = out_sum[:, :head_width]
    for p in range(1, T):
        out_head = out_head + swap(out_low[:, p * head_width : (p + 1) * head_width], "tp", p).astype(F32)
    head_of = lambda p: d_query_late[:, p * head_width : (p + 1) * head_width]
    normed_late = after(normed, d_kv[1])
    (q_halves,) = weight_grad(
        f, own, [(normed_late, p) for p in range(T)], [(swap(head_of(p), "tp", p) if p else head_of(p), 0) for p in range(T)]
    )
    out_low = out_head.astype(LOW)
    d_kv[0] = after(d_kv[0], *q_halves, out_low)
    own_rows = lambda table: jnp.tile(table, (seqs, 1))
    grad_input, dg_input, dg_key, *kv_halves = pl.pallas_call(
        finish_kernel,
        in_specs=[SMEM] + [VMEM] * (11 + len(d_kv)),
        out_shape=[token, gain_row, struct((1, head_width), F32)] + [struct((half, 2 * head_width), LOW)] * 2,
        scratch_shapes=[pltpu.VMEM((2 * half, 2 * head_width), F32)],
        compiler_params=ROOM,
        name="finish",
    )(f.reshape(1), key_own, own_rows(cos_own), own_rows(sin_own), g_key, d_query, q_full, kv_full, d_hidden, x_own, g_input,
      normed_own, *[v.reshape(own, 2 * head_width) for v in d_kv])

    def pack(values, wide):
        top = lax.reduce_precision(values, 8, 7)
        flat = jnp.concatenate([top, values - top], axis=1).astype(LOW)
        rows = -(-flat.shape[1] // wide)
        return jnp.pad(flat, ((0, 0), (0, rows * wide - flat.shape[1]))).reshape(values.shape[0], rows, wide)

    def unpack(rows, n):
        flat = rows.reshape(-1)
        return flat[:n] + flat[n : 2 * n]

    sums = [dg_input, dg_post_attn, dg_pre_ffn, dg_post_ffn]
    small = [jnp.sum(dg_query, axis=(0, 1)), dg_key]
    extra = [v.reshape(F * C, piece) for v in sums] + [v.reshape(F * C, gain_piece) for v in small]
    extra = jnp.concatenate(extra + [jnp.broadcast_to(error[:, :1], (F * C, 1))], axis=1).reshape(F, C, -1)
    n = extra.shape[2]
    extra = lax.dynamic_index_in_dim(extra, f, 0, False) + swap(lax.dynamic_index_in_dim(extra, f ^ 1, 0, False), "fsdp", 1)
    q_low = collect_core(after(q_halves[0], dg_key), q_halves[1]).astype(LOW)
    grads = jnp.concatenate([q_low, out_low, collect_core(*kv_halves).astype(LOW)], axis=1)
    grads = jnp.concatenate([grads.reshape(C, piece, grads.shape[1]), pack(extra, grads.shape[1])], axis=1)
    grads = jnp.sum(exchange(grads, "ctx").astype(F32), axis=0)
    grad_query, grad_out = grads[:piece, :head_width], grads[:piece, head_width : 2 * head_width]
    kv_low = grads[:piece, 2 * head_width :]
    kv_low = jnp.concatenate([kv_low.astype(LOW), pack(unpack(grads[piece:], n)[None], kv_low.shape[1])[0]], axis=0)
    kv_low = lax.optimization_barrier(kv_low)
    totals = {p: (swap(kv_low, "tp", p) if p else kv_low).astype(F32) for p in range(T)}
    bit = 1
    while bit < T:
        totals = {p: totals[p] + totals[p ^ bit] for p in totals if not p & bit}
        bit *= 2
    grad_kv, total = totals[0][:piece], unpack(totals[0][piece:], n)
    loss = total[-1] / (2.0 * width_model * count)
    at = 4 * piece
    return (
        output.reshape(seqs, sub, width_model),
        loss,
        grad_input.reshape(seqs, sub, width_model),
        grad_query,
        grad_kv[:, :head_width],
        grad_kv[:, head_width:],
        grad_out.T,
        grad_gate,
        grad_up,
        grad_down.T,
        total[:piece],
        total[at : at + gain_piece],
        total[at + gain_piece : at + 2 * gain_piece],
        total[piece : 2 * piece],
        total[2 * piece : 3 * piece],
        total[3 * piece : 4 * piece],
    )


def solution(mesh):
    rows = P(("fsdp", "ctx"), "tp")
    cols = P("tp", ("fsdp", "ctx"))
    split = P(("fsdp", "ctx"), None)
    gain = P(("fsdp", "ctx"))
    token = P("fsdp", "ctx", None)
    own = P("fsdp", ("ctx", "tp"), None)
    weights = (rows, split, split, cols, rows, rows, cols)
    return jax.shard_map(
        shards,
        mesh=mesh,
        in_specs=(token, token, P("fsdp", "ctx")) + weights + (gain,) * 6,
        out_specs=(own, P(), own) + weights + (gain,) * 6,
        check_vma=False,
    )
```

time: 554 us -> 506 us (0.913)
  Pallas kernels: 9.29 us -> 160 us
  matrix products: 126 us -> 3.73 us
  other arithmetic: 83.7 us -> 23.7 us
  waiting for transfers between devices: 143 us -> 203 us
  local copies, waits for them, and re-layouts: 86.9 us -> 31.4 us
  starting transfers between devices: 77.6 us -> 61.2 us
    pallas_call x1 -> x20, Pallas kernels: 5.24 us -> 154 us  [the longest x6 64.9 us: ffn_call(): pl.pallas_call(functools.partial(kernel, units, chunks), grid=(pl.cdiv(un...]
    dot_general x36 -> x1, matrix products: 126 us -> 3.73 us  [dot(): lax.dot_general(left, right, (contract, ((), ())), preferred_element_type...]
    ppermute x4, waiting for transfers between devices: 17.8 us -> 50.6 us  [shifted(): lax.ppermute(values, axis, [(i, i + by) for i in range(size) if 0 <= i +...]
    select_n x2 -> x0, other arithmetic: 29.9 us -> none  [both_cores(): jnp.where(f == 0, jnp.concatenate([mine, other], axis=0), jnp.concatenate...]
    convert_element_type x5 -> x0, local copies, waits for them, and re-layouts: 26.1 us -> none  [the longest x3 19.9 us: collect_core(): low = partial.astype(LOW).reshape(F, half, partial.shape[1])]
    convert_element_type x16 -> x9, other arithmetic: 31.5 us -> 7.3 us  [the longest x3 2.43 us: shards(): got = after(swap(d_pairs[p], 'tp', p), out_low).astype(F32)]
    ppermute x41 -> x45, waiting for transfers between devices: 90.3 us -> 105 us  [swap(): lax.ppermute(values, axis, [(i, i ^ bits) for i in range(lax.axis_size(ax...]
    unnamed x238 -> x108, local copies, waits for them, and re-layouts: 22.8 us -> 9.14 us
  transfers between devices with their start and end apart: 57 -> 55, of which waited for: 21 -> 27; matrix products, arithmetic and copies ran while one was open for 50% -> 9% of each run, Pallas kernels for 2% -> 28%
where the time goes in v2:
time: 506 us; the launch traced here: 501 us
  waiting for transfers between devices  203 us (40%)
  Pallas kernels  160 us (32%)
  starting transfers between devices  61.2 us (12%)
  local copies, waits for them, and re-layouts  31.4 us (6%)
  other arithmetic  23.7 us (5%)
  between operations  17.9 us (4%)
    ppermute x45, waiting for transfers between devices, swap(): lax.ppermute(values, axis, [(i, i ^ bits) for i in range(lax.axis_size(ax...  105 us
    pallas_call x6, Pallas kernels, ffn_call(): pl.pallas_call(functools.partial(kernel, units, chunks), grid=(pl.cdiv(un...  64.9 us
    ppermute x4, waiting for transfers between devices, shifted(): lax.ppermute(values, axis, [(i, i + by) for i in range(size) if 0 <= i +...  50.6 us
    ppermute x45, starting transfers between devices, swap(): lax.ppermute(values, axis, [(i, i ^ bits) for i in range(lax.axis_size(ax...  43.3 us
    pallas_call x4, Pallas kernels, weight_grad(): pl.pallas_call(functools.partial(weight_grad_kernel, chunks, sets), grid=...  34.2 us
    all_to_all x2, waiting for transfers between devices, exchange(): return lax.all_to_all(values, axes, 0, 0, tiled=True)  28.9 us
    pallas_call x2, Pallas kernels, pair_sum(): pl.pallas_call(pair_sum_kernel, grid=(rows // step,), in_specs=[pl.BlockS...  10.3 us
  transfers between devices with their start and end apart: 55, of which 27 were waited for; matrix products, arithmetic and copies ran while one was open for 9% of the time, Pallas kernels for 28%

profile of v2, /device:TPU:0, one launch (start us, length us, event | category | flops | bytes accessed | tf_op | source)
XLA Modules:
  0.0 500.8 jit_solution(9633140060205816278)
XLA Ops:
  9.4 2.4 pad_maximum_fusion
  14.0 6.3 %all-to-all-start = ((bf16[8,2,832]{2,1,0:T(2,128)(2,1)}), bf16[8,2,832]{2,1,0:T(2,128)(2,1)S(1)}, u32[]{:S(2)}, u32[]{:S(2)}) async-start(bf16[8,2,832]{2,1,0:T(2,128)(2,1)} %reshape.324), calls=%async_computation | async-start | bytes 57344 | tf_op jit(solution)/shard_map/all_to_all | solution.py:28
  21.8 2.1 constant_dynamic-slice_fusion.1
  30.6 4.3 norm_rows.1
  35.6 8.6 %all-gather.3.cloned.1.call-done = bf16[2,576,512]{2,1,0:T(8,128)(2,1)} async-done(((bf16[2,144,512]{2,1,0:T(8,128)(2,1)}), bf16[2,576,512]{2,1,0:T(8,128)(2,1)}) %all-gather.3.cloned.1.call-update) | async-done | bytes 1179664 | tf_op jit(solution)/shard_map/all_gather | solution.py:546
  45.6 2.4 collective-permute-start.2
  50.0 6.3 %project_keys.1 = (bf16[4,4,64,512]{3,2,1,0:T(8,128)(2,1)}, bf16[4,64,512]{2,1,0:T(8,128)(2,1)}, f32[256,256]{1,0:T(8,128)}, bf16[1152,512]{1,0:T(8,128)(2,1)}) custom-call(s32[1]{0:T(128)} %bitcast.8.core_ref, bf16[4,4,64,1152]{3,2,1,0:T(8,128)(2,1)} %norm_rows.1, bf16[576,512]{1,0:T(8,128)(2,1)} %copy-done.18, bf16[576,512]{1,0:T(8,128)(2,1)} %copy-done.49, ...), custom_call_target="tpu_custom_call" | custom-call | flops 1207959552 | bytes 4718592 | tf_op jit(solution)/shard_map/project_keys/pallas_call | solution.py:187
  56.2 2.4 collective-permute-start.8
  58.6 4.2 collective-permute-done.2.refs_3_
  62.8 12.1 %collective-permute-done.1.refs_2_ = bf16[576,512]{1,0:T(8,128)(2,1)} collective-permute-done((bf16[576,512]{1,0:T(8,128)(2,1)S(1)}, bf16[576,512]{1,0:T(8,128)(2,1)}, u32[]{:S(2)}, u32[]{:S(2)}) %collective-permute-start.1) | collective-permute-done | bytes 589856 | tf_op jit(solution)/shard_map/ppermute | solution.py:19
  75.6 2.7 collective-permute-start.12
  78.3 11.9 %collective-permute-done.12.refs_5_ = bf16[4,64,512]{2,1,0:T(8,128)(2,1)S(1)} collective-permute-done((bf16[4,64,512]{2,1,0:T(8,128)(2,1)S(1)}, bf16[4,64,512]{2,1,0:T(8,128)(2,1)S(1)}, u32[]{:S(2)}, u32[]{:S(2)}) %collective-permute-start.12) | collective-permute-done | bytes 262176 | tf_op jit(solution)/shard_map/ppermute | solution.py:24
  90.2 1.5 collective-permute-start.10
  97.1 4.8 assemble.1
  101.9 3.2 collective-permute-done.10.refs_3_
  105.1 2.1 collective-permute-start.15
  107.3 3.7 fusion.20.q_ref
  111.0 2.0 collective-permute-done.13.refs_6_
  113.0 4.8 collective-permute-done.15.refs_8_
  118.5 6.3 %attend.1 = (bf16[256,1024]{1,0:T(8,128)(2,1)}, bf16[256,1024]{1,0:T(8,128)(2,1)}, f32[4,256,1]{2,1,0:T(8,128)}) custom-call(s32[4,64,2]{2,1,0:T(8,128)} %copy.35.qinfo_ref, s32[4,2,768]{2,1,0:T(2,128)} %pad_add_fusion.kinfo_ref, f32[256,1024]{1,0:T(8,128)} %fusion.20.q_ref, f32[1,256]{1,0:T(1,128)} %reshape.271.gain_ref, f32[64,256]{1,0:T(8,128)} %slice.193.cos_ref, ...), custom_call_target="tpu_custom_call" | custom-call | flops 402653184 | bytes 4194304 | tf_op jit(solution)/shard_map/attend/pallas_call | solution.py:598
  124.8 4.5 mix.1
  129.7 1.6 collective-permute-start.19
  132.8 23.1 %collective-permute-done.18.refs_0_.refs_2_ = bf16[256,1152]{1,0:T(8,128)(2,1)S(1)} collective-permute-done((bf16[256,1152]{1,0:T(8,128)(2,1)}, bf16[256,1152]{1,0:T(8,128)(2,1)S(1)}, u32[]{:S(2)}, u32[]{:S(2)}) %collective-permute-start.18) | collective-permute-done | bytes 589856 | tf_op jit(solution)/shard_map/ppermute | solution.py:19
  155.9 9.5 %all-gather.5.cloned.1.call-done.refs_1_.refs_2_.refs_3_.refs_4_ = bf16[3,1152,1728]{2,1,0:T(8,128)(2,1)} async-done(((bf16[3,144,1728]{2,1,0:T(8,128)(2,1)}), bf16[3,1152,1728]{2,1,0:T(8,128)(2,1)}) %all-gather.5.cloned.1.call-update) | async-done | bytes 11943952 | tf_op jit(solution)/shard_map/all_gather | solution.py:547
  165.4 13.1 %ffn.5 = (bf16[256,1152]{1,0:T(8,128)(2,1)}, bf16[256,1152]{1,0:T(8,128)(2,1)}, bf16[512,1728]{1,0:T(8,128)(2,1)}, bf16[512,1728]{1,0:T(8,128)(2,1)}, bf16[512,1728]{1,0:T(8,128)(2,1)}) custom-call(bf16[256,1152]{1,0:T(8,128)(2,1)} %copy-done.22, bf16[256,1152]{1,0:T(8,128)(2,1)} %copy-done.23, ...), custom_call_target="tpu_custom_call" | custom-call | flops 6115295232 | bytes 13123584 | tf_op jit(solution)/shard_map/ffn/pallas_call | solution.py:417
  178.6 1.7 collective-permute-start.20
  181.7 9.1 %ffn.4 = (bf16[256,1152]{1,0:T(8,128)(2,1)}, bf16[256,1728]{1,0:T(8,128)(2,1)}, bf16[256,1728]{1,0:T(8,128)(2,1)}, bf16[256,1728]{1,0:T(8,128)(2,1)}) custom-call(bf16[256,1152]{1,0:T(8,128)(2,1)} %collective-permute-done.16.refs_0_.refs_1_, bf16[3,1152,1728]{2,1,0:T(8,128)(2,1)} %all-gather.5.cloned.1.call-done.refs_1_.refs_2_.refs_3_.refs_4_, ...), custom_call_target="tpu_custom_call" | custom-call | flops 3057647616 | bytes 12533760 | tf_op jit(solution)/shard_map/ffn/pallas_call | solution.py:417
  194.1 9.4 %ffn.3 = (f32[256,1152]{1,0:T(8,128)}, bf16[256,1728]{1,0:T(8,128)(2,1)}, bf16[256,1728]{1,0:T(8,128)(2,1)}, bf16[256,1728]{1,0:T(8,128)(2,1)}) custom-call(bf16[256,1152]{1,0:T(8,128)(2,1)} %get-tuple-element.168.refs_0_, bf16[3,1152,1728]{2,1,0:T(8,128)(2,1)} %all-gather.5.cloned.1.call-done.refs_1_.refs_2_.refs_3_.refs_4_, ...), custom_call_target="tpu_custom_call" | custom-call | flops 3057647616 | bytes 12533760 | tf_op jit(solution)/shard_map/ffn/pallas_call | solution.py:417
  203.6 3.1 collective-permute-done.20.refs_2_
  208.0 4.6 loss.1
  212.6 1.5 collective-permute-start.23
  216.1 9.3 %ffn_back.3 = (f32[256,1152]{1,0:T(8,128)}, bf16[256,1728]{1,0:T(8,128)(2,1)}, bf16[256,1728]{1,0:T(8,128)(2,1)}) custom-call(bf16[256,1152]{1,0:T(8,128)(2,1)} %get-tuple-element.150.refs_0_, bf16[3,1152,1728]{2,1,0:T(8,128)(2,1)} %all-gather.5.cloned.1.call-done.refs_1_.refs_2_.refs_3_.refs_4_, ...), custom_call_target="tpu_custom_call" | custom-call | flops 3057647616 | bytes 14303232 | tf_op jit(solution)/shard_map/ffn_back/pallas_call | solution.py:417
  225.3 3.7 collective-permute-done.23.refs_0_.refs_1_
  229.9 9.1 %ffn_back.4 = (bf16[256,1152]{1,0:T(8,128)(2,1)}, bf16[256,1728]{1,0:T(8,128)(2,1)}, bf16[256,1728]{1,0:T(8,128)(2,1)}) custom-call(bf16[256,1152]{1,0:T(8,128)(2,1)} %copy-done.26, bf16[3,1152,1728]{2,1,0:T(8,128)(2,1)} %all-gather.5.cloned.1.call-done.refs_1_.refs_2_.refs_3_.refs_4_, ...), custom_call_target="tpu_custom_call" | custom-call | flops 3057647616 | bytes 14303232 | tf_op jit(solution)/shard_map/ffn_back/pallas_call | solution.py:417
  239.0 1.7 collective-permute-done.22.refs_2_.refs_0_
  241.7 10.7 %weight_grad.4 = (bf16[576,1728]{1,0:T(8,128)(2,1)}, bf16[576,1728]{1,0:T(8,128)(2,1)}) custom-call(s32[1]{0:T(128)} %bitcast.8.core_ref, bf16[256,1152]{1,0:T(8,128)(2,1)} %get-tuple-element.150.refs_0_, bf16[256,1152]{1,0:T(8,128)(2,1)} %copy-done.26, bf16[256,1152]{1,0:T(8,128)(2,1)} %copy-done.24, bf16[256,1152]{1,0:T(8,128)(2,1)} %copy-done.25, ...), custom_call_target="tpu_custom_call" | custom-call | flops 4076863488 | bytes 6340608 | tf_op jit(solution)/shard_map/weight_grad/pallas_call | solution.py:513
  252.4 4.3 collective-permute-done.25.refs_1_
  258.1 4.3 pair_sum.2
  264.5 15.0 %ffn_back.5 = (bf16[256,1152]{1,0:T(8,128)(2,1)}, bf16[256,1152]{1,0:T(8,128)(2,1)}, bf16[512,1728]{1,0:T(8,128)(2,1)}, bf16[512,1728]{1,0:T(8,128)(2,1)}) custom-call(bf16[256,1152]{1,0:T(8,128)(2,1)} %copy-done.24, bf16[256,1152]{1,0:T(8,128)(2,1)} %copy-done.25, bf16[3,1152,1728]{2,1,0:T(8,128)(2,1)} %all-gather.5.cloned.1.call-done.refs_1_.refs_2_.refs_3_.refs_4_, ...), custom_call_target="tpu_custom_call" | custom-call | flops 6115295232 | bytes 16662528 | tf_op jit(solution)/shard_map/ffn_back/pallas_call | solution.py:417
  279.4 1.9 collective-permute-start.28
  281.9 15.3 %weight_grad.5 = (bf16[576,1728]{1,0:T(8,128)(2,1)}, bf16[576,1728]{1,0:T(8,128)(2,1)}, bf16[576,1728]{1,0:T(8,128)(2,1)}, bf16[576,1728]{1,0:T(8,128)(2,1)}) custom-call(s32[1]{0:T(128)} %bitcast.8.core_ref, bf16[256,1152]{1,0:T(8,128)(2,1)} %get-tuple-element.168.refs_0_, bf16[256,1152]{1,0:T(8,128)(2,1)} %collective-permute-done.16.refs_0_.refs_1_, ...), custom_call_target="tpu_custom_call" | custom-call | flops 8153726976 | bytes 10321920 | tf_op jit(solution)/shard_map/weight_grad/pallas_call | solution.py:513
  297.3 11.0 %collective-permute-done.27.refs_2_ = bf16[256,1152]{1,0:T(8,128)(2,1)S(1)} collective-permute-done((bf16[256,1152]{1,0:T(8,128)(2,1)}, bf16[256,1152]{1,0:T(8,128)(2,1)S(1)}, u32[]{:S(2)}, u32[]{:S(2)}) %collective-permute-start.27) | collective-permute-done | bytes 589856 | tf_op jit(solution)/shard_map/ppermute | solution.py:19
  309.3 6.4 %middle.1 = (f32[256,1152]{1,0:T(8,128)}, bf16[256,1152]{1,0:T(8,128)(2,1)}, bf16[256,1024]{1,0:T(8,128)(2,1)}, f32[1,1152]{1,0:T(1,128)}, f32[1,1152]{1,0:T(1,128)}) custom-call(f32[256,1152]{1,0:T(8,128)} %get-tuple-element.148.dres_ref, f32[256,1152]{1,0:T(8,128)} %get-tuple-element.139.hidden_ref, f32[256,1152]{1,0:T(8,128)} %get-tuple-element.149.branch_ref, ...), custom_call_target="tpu_custom_call" | custom-call | tf_op jit(solution)/shard_map/middle/pallas_call | solution.py:658
  315.7 4.7 weight_grad.6
  321.7 6.0 %pair_sum.3 = bf16[2,576,1728]{2,1,0:T(8,128)(2,1)} custom-call(bf16[576,1728]{1,0:T(8,128)(2,1)} %get-tuple-element.176.refs_0_, bf16[576,1728]{1,0:T(8,128)(2,1)} %collective-permute-done.29.refs_1_, bf16[576,1728]{1,0:T(8,128)(2,1)} %get-tuple-element.178.refs_2_, bf16[576,1728]{1,0:T(8,128)(2,1)} %copy-done.5), custom_call_target="tpu_custom_call" | custom-call | tf_op jit(solution)/shard_map/pair_sum/pallas_call | solution.py:307
  327.7 7.2 %attend_back.1 = (bf16[256,1024]{1,0:T(8,128)(2,1)}, f32[4,1,256]{2,1,0:T(1,128)}, f32[3,4,64,512]{3,2,1,0:T(8,128)}, bf16[2,4,64,512]{3,2,1,0:T(8,128)(2,1)}, b...) custom-call(s32[1]{0:T(128)} %bitcast.4.place_ref, s32[4,64,2]{2,1,0:T(8,128)} %copy.35.qinfo_ref, ...), custom_call_target="tpu_custom_call" | custom-call | tf_op jit(solution)/shard_map/attend_back/pallas_call | solution.py:672
  338.5 2.0 convert_add_fusion
  340.5 9.5 %collective-permute-done.31 = bf16[2,4,64,512]{3,2,1,0:T(8,128)(2,1)S(1)} collective-permute-done((bf16[2,4,64,512]{3,2,1,0:T(8,128)(2,1)}, bf16[2,4,64,512]{3,2,1,0:T(8,128)(2,1)S(1)}, u32[]{:S(2)}, u32[]{:S(2)}) %collective-permute-start.31) | collective-permute-done | bytes 524320 | tf_op jit(solution)/shard_map/ppermute | solution.py:19
  350.1 11.6 %collective-permute-done.33 = bf16[2,4,64,512]{3,2,1,0:T(8,128)(2,1)} collective-permute-done((bf16[2,4,64,512]{3,2,1,0:T(8,128)(2,1)}, bf16[2,4,64,512]{3,2,1,0:T(8,128)(2,1)}, u32[]{:S(2)}, u32[]{:S(2)}) %collective-permute-start.33) | collective-permute-done | bytes 524320 | tf_op jit(solution)/shard_map/ppermute | solution.py:19
  366.6 23.4 %collective-permute-done.35 = bf16[4,64,512]{2,1,0:T(8,128)(2,1)S(1)} collective-permute-done((bf16[4,64,512]{2,1,0:T(8,128)(2,1)S(1)}, bf16[4,64,512]{2,1,0:T(8,128)(2,1)S(1)}, u32[]{:S(2)}, u32[]{:S(2)}) %collective-permute-start.35) | collective-permute-done | bytes 262176 | tf_op jit(solution)/shard_map/ppermute | solution.py:24
  393.0 1.6 collective-permute-start.40
  396.6 1.7 collective-permute-start.38
  398.3 15.3 %collective-permute-done.36 = bf16[4,64,512]{2,1,0:T(8,128)(2,1)S(1)} collective-permute-done((bf16[4,64,512]{2,1,0:T(8,128)(2,1)S(1)}, bf16[4,64,512]{2,1,0:T(8,128)(2,1)S(1)}, u32[]{:S(2)}, u32[]{:S(2)}) %collective-permute-start.36) | collective-permute-done | bytes 262176 | tf_op jit(solution)/shard_map/ppermute | solution.py:24
  413.7 2.0 collective-permute-start.39
  415.7 1.9 slice.153.normed_ref
  420.2 3.4 weight_grad.7
  426.3 6.3 %finish.1 = (f32[256,1152]{1,0:T(8,128)}, f32[1,1152]{1,0:T(1,128)}, f32[1,256]{1,0:T(1,128)}, bf16[576,512]{1,0:T(8,128)(2,1)}, bf16[576,512]{1,0:T(8,128)(2,1)}) custom-call(s32[1]{0:T(128)} %bitcast.8.core_ref, f32[256,256]{1,0:T(8,128)} %get-tuple-element.202.raw_ref, f32[256,256]{1,0:T(8,128)} %bitcast.90, f32[256,256]{1,0:T(8,128)} %bitcast.91, ...), custom_call_target="tpu_custom_call" | custom-call | tf_op jit(solution)/shard_map/finish/pallas_call | solution.py:710
  441.0 3.5 all-to-all-start.1
  445.2 2.1 convert_bitcast_fusion
  447.3 28.0 %all-to-all-done.1 = bf16[4,146,1024]{2,1,0:T(8,128)(2,1)S(1)} async-done(((bf16[4,146,1024]{2,1,0:T(8,128)(2,1)}), bf16[4,146,1024]{2,1,0:T(8,128)(2,1)S(1)}, u32[]{:S(2)}, u32[]{:S(2)}) %all-to-all-start.1) | async-done | bytes 1196064 | tf_op jit(solution)/shard_map/all_to_all | solution.py:28
  475.8 2.5 collective-permute-start.46
  480.8 1.9 collective-permute-done.46
  482.7 4.0 collective-permute-done.47
  490.0 1.5 convert_element_type.141
  (279 shorter events, 74.6 us)
Async XLA Ops:
  7.2 184.7 %copy-start = (bf16[4,256,1152]{2,1,0:T(8,128)(2,1)S(1)}, bf16[4,256,1152]{2,1,0:T(8,128)(2,1)}, u32[]{:S(2)}) copy-start(bf16[4,256,1152]{2,1,0:T(8,128)(2,1)} %param.17) | copy-start | bytes 7077892
  7.2 36.9 %all-gather.3.cloned.1.call-start = ((), (), s32[]{:S(2)}) async-start(), calls=%async_computation.4 | async-start | bytes 1474560 | tf_op jit(solution)/shard_map/all_gather | solution.py:546
  9.2 156.2 %all-gather.5.cloned.1.call-start = ((), (), s32[]{:S(2)}) async-start(), calls=%async_computation.5 | async-start | bytes 13934592 | tf_op jit(solution)/shard_map/all_gather | solution.py:547
  14.0 12.1 %all-to-all-start = ((bf16[8,2,832]{2,1,0:T(2,128)(2,1)}), bf16[8,2,832]{2,1,0:T(2,128)(2,1)S(1)}, u32[]{:S(2)}, u32[]{:S(2)}) async-start(bf16[8,2,832]{2,1,0:T(2,128)(2,1)} %reshape.324), calls=%async_computation | async-start | bytes 57344 | tf_op jit(solution)/shard_map/all_to_all | solution.py:28
  20.4 424.9 %reduce-scatter.5.cloned.1.call-start = ((), (), s32[]{:S(2)}) async-start(), calls=%async_computation.7 | async-start | bytes 2580480 | tf_op jit(solution)/shard_map/reduce_scatter | solution.py:638
  45.5 30.0 %copy-start.2 = (bf16[576,512]{1,0:T(8,128)(2,1)}, bf16[576,512]{1,0:T(8,128)(2,1)S(1)}, u32[]{:S(2)}) copy-start(bf16[576,512]{1,0:T(8,128)(2,1)S(1)} %get-tuple-element.125.refs_0_) | copy-start | bytes 1769476
  45.5 3.6 collective-permute-start.3
  45.6 17.2 %collective-permute-start.2 = (bf16[576,512]{1,0:T(8,128)(2,1)S(1)}, bf16[576,512]{1,0:T(8,128)(2,1)}, u32[]{:S(2)}, u32[]{:S(2)}) collective-permute-start(bf16[576,512]{1,0:T(8,128)(2,1)S(1)} %get-tuple-element.125.refs_0_), channel_id=1, source_target_pairs={{0,3},{1,2},{2,1},{3,0},{4,7},{5,6},{6,5},{7,4},{8,11},{9,10},{10,... | collective-permute-start | bytes 1769480 | tf_op jit(solution)/shard_map/ppermute | solution.py:19
  48.0 27.0 %collective-permute-start.1 = (bf16[576,512]{1,0:T(8,128)(2,1)S(1)}, bf16[576,512]{1,0:T(8,128)(2,1)}, u32[]{:S(2)}, u32[]{:S(2)}) collective-permute-start(bf16[576,512]{1,0:T(8,128)(2,1)S(1)} %get-tuple-element.125.refs_0_), channel_id=1, source_target_pairs={{0,2},{1,3},{2,0},{3,1},{4,6},{5,7},{6,4},{7,5},{8,10},{9,11},{10,... | collective-permute-start | bytes 1769480 | tf_op jit(solution)/shard_map/ppermute | solution.py:19
  48.6 26.5 %collective-permute-start = (bf16[576,512]{1,0:T(8,128)(2,1)S(1)}, bf16[576,512]{1,0:T(8,128)(2,1)}, u32[]{:S(2)}, u32[]{:S(2)}) collective-permute-start(bf16[576,512]{1,0:T(8,128)(2,1)S(1)} %get-tuple-element.125.refs_0_), channel_id=1, source_target_pairs={{0,1},{1,0},{2,3},{3,2},{4,5},{5,4},{6,7},{7,6},{8,9},{9,8},{10,11... | collective-permute-start | bytes 1769480 | tf_op jit(solution)/shard_map/ppermute | solution.py:19
  56.2 19.3 %collective-permute-start.8 = (bf16[4,64,512]{2,1,0:T(8,128)(2,1)}, bf16[4,64,512]{2,1,0:T(8,128)(2,1)S(1)}, u32[]{:S(2)}, u32[]{:S(2)}) collective-permute-start(bf16[4,64,512]{2,1,0:T(8,128)(2,1)} %get-tuple-element.124), channel_id=1, source_target_pairs={{0,4},{4,8},{8,12},{1,5},{5,9},{9,13},{2,6},{6,10},{10,14},{3,7},{... | collective-permute-start | bytes 786440 | tf_op jit(solution)/shard_map/ppermute | solution.py:24
  62.8 29.6 %collective-permute-start.7 = (bf16[576,512]{1,0:T(8,128)(2,1)}, bf16[576,512]{1,0:T(8,128)(2,1)}, u32[]{:S(2)}, u32[]{:S(2)}) collective-permute-start(bf16[576,512]{1,0:T(8,128)(2,1)} %collective-permute-done.2.refs_3_), channel_id=1, source_target_pairs={{0,16},{16,0},{1,17},{17,1},{2,18},{18,2},{3,19},{19,3},{4,20},{20... | collective-permute-start | bytes 1769480 | tf_op jit(solution)/shard_map/ppermute | solution.py:19
  75.0 18.9 %collective-permute-start.6 = (bf16[576,512]{1,0:T(8,128)(2,1)}, bf16[576,512]{1,0:T(8,128)(2,1)}, u32[]{:S(2)}, u32[]{:S(2)}) collective-permute-start(bf16[576,512]{1,0:T(8,128)(2,1)} %collective-permute-done.1.refs_2_), channel_id=1, source_target_pairs={{0,16},{16,0},{1,17},{17,1},{2,18},{18,2},{3,19},{19,3},{4,20},{20... | collective-permute-start | bytes 1769480 | tf_op jit(solution)/shard_map/ppermute | solution.py:19
  75.0 19.4 %collective-permute-start.5 = (bf16[576,512]{1,0:T(8,128)(2,1)}, bf16[576,512]{1,0:T(8,128)(2,1)}, u32[]{:S(2)}, u32[]{:S(2)}) collective-permute-start(bf16[576,512]{1,0:T(8,128)(2,1)} %collective-permute-done.refs_1_), channel_id=1, source_target_pairs={{0,16},{16,0},{1,17},{17,1},{2,18},{18,2},{3,19},{19,3},{4,20},{20... | collective-permute-start | bytes 1769480 | tf_op jit(solution)/shard_map/ppermute | solution.py:19
  75.5 20.5 %collective-permute-start.4 = (bf16[576,512]{1,0:T(8,128)(2,1)S(1)}, bf16[576,512]{1,0:T(8,128)(2,1)}, u32[]{:S(2)}, u32[]{:S(2)}) collective-permute-start(bf16[576,512]{1,0:T(8,128)(2,1)S(1)} %get-tuple-element.125.refs_0_), channel_id=1, source_target_pairs={{0,16},{16,0},{1,17},{17,1},{2,18},{18,2},{3,19},{19,3},{4,20},{20... | collective-permute-start | bytes 1769480 | tf_op jit(solution)/shard_map/ppermute | solution.py:19
  75.6 26.4 %copy-start.10 = (bf16[4,64,512]{2,1,0:T(8,128)(2,1)}, bf16[4,64,512]{2,1,0:T(8,128)(2,1)S(1)}, u32[]{:S(2)}) copy-start(bf16[4,64,512]{2,1,0:T(8,128)(2,1)S(1)} %collective-permute-done.8.refs_1_) | copy-start | bytes 786436
  75.6 14.6 %collective-permute-start.12 = (bf16[4,64,512]{2,1,0:T(8,128)(2,1)S(1)}, bf16[4,64,512]{2,1,0:T(8,128)(2,1)S(1)}, u32[]{:S(2)}, u32[]{:S(2)}) collective-permute-start(bf16[4,64,512]{2,1,0:T(8,128)(2,1)S(1)} %collective-permute-done.8.refs_1_), channel_id=1, source_target_pairs={{0,4},{4,8},{8,12},{1,5},{5,9},{9,13},{2,6},{6,10},{10,14},{3,7},{... | collective-permute-start | bytes 786440 | tf_op jit(solution)/shard_map/ppermute | solution.py:24
  90.2 14.9 %collective-permute-start.10 = (bf16[4,64,512]{2,1,0:T(8,128)(2,1)S(1)}, bf16[4,64,512]{2,1,0:T(8,128)(2,1)}, u32[]{:S(2)}, u32[]{:S(2)}) collective-permute-start(bf16[4,64,512]{2,1,0:T(8,128)(2,1)S(1)} %collective-permute-done.8.refs_1_), channel_id=1, source_target_pairs={{0,2},{1,3},{2,0},{3,1},{4,6},{5,7},{6,4},{7,5},{8,10},{9,11},{10,... | collective-permute-start | bytes 786440 | tf_op jit(solution)/shard_map/ppermute | solution.py:19
  92.5 18.5 %collective-permute-start.11 = (bf16[4,64,512]{2,1,0:T(8,128)(2,1)S(1)}, bf16[4,64,512]{2,1,0:T(8,128)(2,1)S(1)}, u32[]{:S(2)}, u32[]{:S(2)}) collective-permute-start(bf16[4,64,512]{2,1,0:T(8,128)(2,1)S(1)} %collective-permute-done.8.refs_1_), channel_id=1, source_target_pairs={{0,3},{1,2},{2,1},{3,0},{4,7},{5,6},{6,5},{7,4},{8,11},{9,10},{10,... | collective-permute-start | bytes 786440 | tf_op jit(solution)/shard_map/ppermute | solution.py:19
  93.9 17.1 %collective-permute-start.9 = (bf16[4,64,512]{2,1,0:T(8,128)(2,1)S(1)}, bf16[4,64,512]{2,1,0:T(8,128)(2,1)S(1)}, u32[]{:S(2)}, u32[]{:S(2)}) collective-permute-start(bf16[4,64,512]{2,1,0:T(8,128)(2,1)S(1)} %collective-permute-done.8.refs_1_), channel_id=1, source_target_pairs={{0,1},{1,0},{2,3},{3,2},{4,5},{5,4},{6,7},{7,6},{8,9},{9,8},{10,11... | collective-permute-start | bytes 786440 | tf_op jit(solution)/shard_map/ppermute | solution.py:19
  94.5 18.6 %collective-permute-start.13 = (bf16[4,64,512]{2,1,0:T(8,128)(2,1)S(1)}, bf16[4,64,512]{2,1,0:T(8,128)(2,1)}, u32[]{:S(2)}, u32[]{:S(2)}) collective-permute-start(bf16[4,64,512]{2,1,0:T(8,128)(2,1)S(1)} %collective-permute-done.12.refs_5_), channel_id=1, source_target_pairs={{0,1},{1,0},{2,3},{3,2},{4,5},{5,4},{6,7},{7,6},{8,9},{9,8},{10,11... | collective-permute-start | bytes 786440 | tf_op jit(solution)/shard_map/ppermute | solution.py:19
  96.0 17.1 %collective-permute-start.14 = (bf16[4,64,512]{2,1,0:T(8,128)(2,1)S(1)}, bf16[4,64,512]{2,1,0:T(8,128)(2,1)S(1)}, u32[]{:S(2)}, u32[]{:S(2)}) collective-permute-start(bf16[4,64,512]{2,1,0:T(8,128)(2,1)S(1)} %collective-permute-done.12.refs_5_), channel_id=1, source_target_pairs={{0,2},{1,3},{2,0},{3,1},{4,6},{5,7},{6,4},{7,5},{8,10},{9,11},{10,... | collective-permute-start | bytes 786440 | tf_op jit(solution)/shard_map/ppermute | solution.py:19
  105.1 12.6 %collective-permute-start.15 = (bf16[4,64,512]{2,1,0:T(8,128)(2,1)S(1)}, bf16[4,64,512]{2,1,0:T(8,128)(2,1)S(1)}, u32[]{:S(2)}, u32[]{:S(2)}) collective-permute-start(bf16[4,64,512]{2,1,0:T(8,128)(2,1)S(1)} %collective-permute-done.12.refs_5_), channel_id=1, source_target_pairs={{0,3},{1,2},{2,1},{3,0},{4,7},{5,6},{6,5},{7,4},{8,11},{9,10},{10,... | collective-permute-start | bytes 786440 | tf_op jit(solution)/shard_map/ppermute | solution.py:19
  129.3 26.6 %collective-permute-start.18 = (bf16[256,1152]{1,0:T(8,128)(2,1)}, bf16[256,1152]{1,0:T(8,128)(2,1)S(1)}, u32[]{:S(2)}, u32[]{:S(2)}) collective-permute-start(bf16[256,1152]{1,0:T(8,128)(2,1)} %get-tuple-element.168.refs_0_), channel_id=1, source_target_pairs={{0,2},{1,3},{2,0},{3,1},{4,6},{5,7},{6,4},{7,5},{8,10},{9,11},{10,... | collective-permute-start | bytes 1769480 | tf_op jit(solution)/shard_map/ppermute | solution.py:19
  129.7 26.2 %collective-permute-start.19 = (bf16[256,1152]{1,0:T(8,128)(2,1)}, bf16[256,1152]{1,0:T(8,128)(2,1)S(1)}, u32[]{:S(2)}, u32[]{:S(2)}) collective-permute-start(bf16[256,1152]{1,0:T(8,128)(2,1)} %get-tuple-element.168.refs_0_), channel_id=1, source_target_pairs={{0,3},{1,2},{2,1},{3,0},{4,7},{5,6},{6,5},{7,4},{8,11},{9,10},{10,... | collective-permute-start | bytes 1769480 | tf_op jit(solution)/shard_map/ppermute | solution.py:19
  131.3 50.4 %collective-permute-start.16 = (bf16[256,1152]{1,0:T(8,128)(2,1)}, bf16[256,1152]{1,0:T(8,128)(2,1)}, u32[]{:S(2)}, u32[]{:S(2)}) collective-permute-start(bf16[256,1152]{1,0:T(8,128)(2,1)} %get-tuple-element.168.refs_0_), channel_id=1, source_target_pairs={{0,1},{1,0},{2,3},{3,2},{4,5},{5,4},{6,7},{7,6},{8,9},{9,8},{10,11... | collective-permute-start | bytes 1769480 | tf_op jit(solution)/shard_map/ppermute | solution.py:19
  178.6 28.1 %collective-permute-start.20 = (bf16[256,1152]{1,0:T(8,128)(2,1)}, bf16[256,1152]{1,0:T(8,128)(2,1)S(1)}, u32[]{:S(2)}, u32[]{:S(2)}) collective-permute-start(bf16[256,1152]{1,0:T(8,128)(2,1)} %get-tuple-element.143), channel_id=1, source_target_pairs={{0,2},{1,3},{2,0},{3,1},{4,6},{5,7},{6,4},{7,5},{8,10},{9,11},{10,... | collective-permute-start | bytes 1769480 | tf_op jit(solution)/shard_map/ppermute | solution.py:19
  180.3 26.4 %collective-permute-start.21 = (bf16[256,1152]{1,0:T(8,128)(2,1)}, bf16[256,1152]{1,0:T(8,128)(2,1)S(1)}, u32[]{:S(2)}, u32[]{:S(2)}) collective-permute-start(bf16[256,1152]{1,0:T(8,128)(2,1)} %get-tuple-element.144), channel_id=1, source_target_pairs={{0,3},{1,2},{2,1},{3,0},{4,7},{5,6},{6,5},{7,4},{8,11},{9,10},{10,... | collective-permute-start | bytes 1769480 | tf_op jit(solution)/shard_map/ppermute | solution.py:19
  190.8 17.2 %collective-permute-start.17 = (bf16[256,1152]{1,0:T(8,128)(2,1)}, bf16[256,1152]{1,0:T(8,128)(2,1)}, u32[]{:S(2)}, u32[]{:S(2)}) collective-permute-start(bf16[256,1152]{1,0:T(8,128)(2,1)} %get-tuple-element.142), channel_id=1, source_target_pairs={{0,1},{1,0},{2,3},{3,2},{4,5},{5,4},{6,7},{7,6},{8,9},{9,8},{10,11... | collective-permute-start | bytes 1769480 | tf_op jit(solution)/shard_map/ppermute | solution.py:19
  212.6 16.5 %collective-permute-start.23 = (bf16[256,1152]{1,0:T(8,128)(2,1)}, bf16[256,1152]{1,0:T(8,128)(2,1)S(1)}, u32[]{:S(2)}, u32[]{:S(2)}) collective-permute-start(bf16[256,1152]{1,0:T(8,128)(2,1)} %get-tuple-element.150.refs_0_), channel_id=1, source_target_pairs={{0,1},{1,0},{2,3},{3,2},{4,5},{5,4},{6,7},{7,6},{8,9},{9,8},{10,11... | collective-permute-start | bytes 1769480 | tf_op jit(solution)/shard_map/ppermute | solution.py:19
  214.1 26.6 %collective-permute-start.22 = (bf16[256,1152]{1,0:T(8,128)(2,1)}, bf16[256,1152]{1,0:T(8,128)(2,1)S(1)}, u32[]{:S(2)}, u32[]{:S(2)}) collective-permute-start(bf16[256,1152]{1,0:T(8,128)(2,1)} %get-tuple-element.150.refs_0_), channel_id=1, source_target_pairs={{0,2},{1,3},{2,0},{3,1},{4,6},{5,7},{6,4},{7,5},{8,10},{9,11},{10,... | collective-permute-start | bytes 1769480 | tf_op jit(solution)/shard_map/ppermute | solution.py:19
  215.6 25.1 %collective-permute-start.24 = (bf16[256,1152]{1,0:T(8,128)(2,1)}, bf16[256,1152]{1,0:T(8,128)(2,1)S(1)}, u32[]{:S(2)}, u32[]{:S(2)}) collective-permute-start(bf16[256,1152]{1,0:T(8,128)(2,1)} %get-tuple-element.150.refs_0_), channel_id=1, source_target_pairs={{0,3},{1,2},{2,1},{3,0},{4,7},{5,6},{6,5},{7,4},{8,11},{9,10},{10,... | collective-permute-start | bytes 1769480 | tf_op jit(solution)/shard_map/ppermute | solution.py:19
  252.4 4.3 collective-permute-start.25
  262.4 227.5 %reduce-scatter.3.cloned.1.call-start = ((), (), s32[]{:S(2)}) async-start(), calls=%async_computation.6 | async-start | bytes 5160960 | tf_op jit(solution)/shard_map/reduce_scatter | solution.py:638
  263.5 33.8 %collective-permute-start.26 = (bf16[256,1152]{1,0:T(8,128)(2,1)S(1)}, bf16[256,1152]{1,0:T(8,128)(2,1)S(1)}, u32[]{:S(2)}, u32[]{:S(2)}) collective-permute-start(bf16[256,1152]{1,0:T(8,128)(2,1)S(1)} %copy-done.48), channel_id=1, source_target_pairs={{0,1},{1,0},{2,3},{3,2},{4,5},{5,4},{6,7},{7,6},{8,9},{9,8},{10,11... | collective-permute-start | bytes 1769480 | tf_op jit(solution)/shard_map/ppermute | solution.py:19
  279.4 28.8 %collective-permute-start.28 = (bf16[256,1152]{1,0:T(8,128)(2,1)}, bf16[256,1152]{1,0:T(8,128)(2,1)S(1)}, u32[]{:S(2)}, u32[]{:S(2)}) collective-permute-start(bf16[256,1152]{1,0:T(8,128)(2,1)} %get-tuple-element.167), channel_id=1, source_target_pairs={{0,3},{1,2},{2,1},{3,0},{4,7},{5,6},{6,5},{7,4},{8,11},{9,10},{10,... | collective-permute-start | bytes 1769480 | tf_op jit(solution)/shard_map/ppermute | solution.py:19
  281.4 26.9 %collective-permute-start.27 = (bf16[256,1152]{1,0:T(8,128)(2,1)}, bf16[256,1152]{1,0:T(8,128)(2,1)S(1)}, u32[]{:S(2)}, u32[]{:S(2)}) collective-permute-start(bf16[256,1152]{1,0:T(8,128)(2,1)} %get-tuple-element.180), channel_id=1, source_target_pairs={{0,2},{1,3},{2,0},{3,1},{4,6},{5,7},{6,4},{7,5},{8,10},{9,11},{10,... | collective-permute-start | bytes 1769480 | tf_op jit(solution)/shard_map/ppermute | solution.py:19
  308.3 12.1 %collective-permute-start.30 = (bf16[576,1728]{1,0:T(8,128)(2,1)}, bf16[576,1728]{1,0:T(8,128)(2,1)S(1)}, u32[]{:S(2)}, u32[]{:S(2)}) collective-permute-start(bf16[576,1728]{1,0:T(8,128)(2,1)} %get-tuple-element.185), channel_id=1, source_target_pairs={{0,16},{16,0},{1,17},{17,1},{2,18},{18,2},{3,19},{19,3},{4,20},{20... | collective-permute-start | bytes 5971976 | tf_op jit(solution)/shard_map/ppermute | solution.py:19
  308.4 12.0 %collective-permute-start.29 = (bf16[576,1728]{1,0:T(8,128)(2,1)}, bf16[576,1728]{1,0:T(8,128)(2,1)}, u32[]{:S(2)}, u32[]{:S(2)}) collective-permute-start(bf16[576,1728]{1,0:T(8,128)(2,1)} %get-tuple-element.182), channel_id=1, source_target_pairs={{0,16},{16,0},{1,17},{17,1},{2,18},{18,2},{3,19},{19,3},{4,20},{20... | collective-permute-start | bytes 5971976 | tf_op jit(solution)/shard_map/ppermute | solution.py:19
  320.4 18.1 %collective-permute-start.32 = (bf16[576,1024]{1,0:T(8,128)(2,1)}, bf16[576,1024]{1,0:T(8,128)(2,1)S(1)}, u32[]{:S(2)}, u32[]{:S(2)}) collective-permute-start(bf16[576,1024]{1,0:T(8,128)(2,1)} %get-tuple-element.191), channel_id=1, source_target_pairs={{0,16},{16,0},{1,17},{17,1},{2,18},{18,2},{3,19},{19,3},{4,20},{20... | collective-permute-start | bytes 3538952 | tf_op jit(solution)/shard_map/ppermute | solution.py:19
  335.0 15.0 %collective-permute-start.31 = (bf16[2,4,64,512]{3,2,1,0:T(8,128)(2,1)}, bf16[2,4,64,512]{3,2,1,0:T(8,128)(2,1)S(1)}, u32[]{:S(2)}, u32[]{:S(2)}) collective-permute-start(bf16[2,4,64,512]{3,2,1,0:T(8,128)(2,1)} %get-tuple-element.189), channel_id=1, source_target_pairs={{0,1},{1,0},{2,3},{3,2},{4,5},{5,4},{6,7},{7,6},{8,9},{9,8},{10,11... | collective-permute-start | bytes 1572872 | tf_op jit(solution)/shard_map/ppermute | solution.py:19
  336.1 25.5 %collective-permute-start.33 = (bf16[2,4,64,512]{3,2,1,0:T(8,128)(2,1)}, bf16[2,4,64,512]{3,2,1,0:T(8,128)(2,1)}, u32[]{:S(2)}, u32[]{:S(2)}) collective-permute-start(bf16[2,4,64,512]{3,2,1,0:T(8,128)(2,1)} %get-tuple-element.193), channel_id=1, source_target_pairs={{0,2},{1,3},{2,0},{3,1},{4,6},{5,7},{6,4},{7,5},{8,10},{9,11},{10,... | collective-permute-start | bytes 1572872 | tf_op jit(solution)/shard_map/ppermute | solution.py:19
  337.3 25.5 %collective-permute-start.34 = (bf16[2,4,64,512]{3,2,1,0:T(8,128)(2,1)}, bf16[2,4,64,512]{3,2,1,0:T(8,128)(2,1)}, u32[]{:S(2)}, u32[]{:S(2)}) collective-permute-start(bf16[2,4,64,512]{3,2,1,0:T(8,128)(2,1)} %get-tuple-element.195), channel_id=1, source_target_pairs={{0,3},{1,2},{2,1},{3,0},{4,7},{5,6},{6,5},{7,4},{8,11},{9,10},{10,... | collective-permute-start | bytes 1572872 | tf_op jit(solution)/shard_map/ppermute | solution.py:19
  364.0 26.0 %copy-start.3 = (bf16[256,1024]{1,0:T(8,128)(2,1)S(1)}, bf16[256,1024]{1,0:T(8,128)(2,1)}, u32[]{:S(2)}) copy-start(bf16[256,1024]{1,0:T(8,128)(2,1)} %get-tuple-element.199.dq_ref) | copy-start | bytes 1572868
  365.2 24.8 %collective-permute-start.35 = (bf16[4,64,512]{2,1,0:T(8,128)(2,1)S(1)}, bf16[4,64,512]{2,1,0:T(8,128)(2,1)S(1)}, u32[]{:S(2)}, u32[]{:S(2)}) collective-permute-start(bf16[4,64,512]{2,1,0:T(8,128)(2,1)S(1)} %get-tuple-element.224), channel_id=1, source_target_pairs={{4,0},{8,4},{12,8},{5,1},{9,5},{13,9},{6,2},{10,6},{14,10},{7,3},{... | collective-permute-start | bytes 786440 | tf_op jit(solution)/shard_map/ppermute | solution.py:24
  390.7 5.9 %collective-permute-start.37 = (bf16[256,256]{1,0:T(8,128)(2,1)S(1)}, bf16[256,256]{1,0:T(8,128)(2,1)S(1)}, u32[]{:S(2)}, u32[]{:S(2)}) collective-permute-start(bf16[256,256]{1,0:T(8,128)(2,1)S(1)} %get-tuple-element.239), channel_id=1, source_target_pairs={{0,1},{1,0},{2,3},{3,2},{4,5},{5,4},{6,7},{7,6},{8,9},{9,8},{10,11... | collective-permute-start | bytes 393224 | tf_op jit(solution)/shard_map/ppermute | solution.py:19
  391.5 26.1 %copy-start.36 = (f32[1,1152]{1,0:T(1,128)S(1)}, f32[1,1152]{1,0:T(1,128)}, u32[]{:S(2)}) copy-start(f32[1,1152]{1,0:T(1,128)} %get-tuple-element.214) | copy-start | bytes 13828
  391.5 26.2 %copy-start.38 = (f32[1,1152]{1,0:T(1,128)S(1)}, f32[1,1152]{1,0:T(1,128)}, u32[]{:S(2)}) copy-start(f32[1,1152]{1,0:T(1,128)} %get-tuple-element.212) | copy-start | bytes 13828
  391.5 26.3 %copy-start.37 = (f32[1,1152]{1,0:T(1,128)S(1)}, f32[1,1152]{1,0:T(1,128)}, u32[]{:S(2)}) copy-start(f32[1,1152]{1,0:T(1,128)} %get-tuple-element.213) | copy-start | bytes 13828
  391.5 26.5 %copy-start.40 = (f32[4,1,256]{2,1,0:T(1,128)S(1)}, f32[4,1,256]{2,1,0:T(1,128)}, u32[]{:S(2)}) copy-start(f32[4,1,256]{2,1,0:T(1,128)} %get-tuple-element.215) | copy-start | bytes 12292
  391.5 22.1 %collective-permute-start.36 = (bf16[4,64,512]{2,1,0:T(8,128)(2,1)S(1)}, bf16[4,64,512]{2,1,0:T(8,128)(2,1)S(1)}, u32[]{:S(2)}, u32[]{:S(2)}) collective-permute-start(bf16[4,64,512]{2,1,0:T(8,128)(2,1)S(1)} %fusion.5), channel_id=1, source_target_pairs={{4,0},{8,4},{12,8},{5,1},{9,5},{13,9},{6,2},{10,6},{14,10},{7,3},{... | collective-permute-start | bytes 786440 | tf_op jit(solution)/shard_map/ppermute | solution.py:24
  393.0 30.6 %collective-permute-start.40 = (bf16[576,256]{1,0:T(8,128)(2,1)S(1)}, bf16[576,256]{1,0:T(8,128)(2,1)S(1)}, u32[]{:S(2)}, u32[]{:S(2)}) collective-permute-start(bf16[576,256]{1,0:T(8,128)(2,1)S(1)} %get-tuple-element.230), channel_id=1, source_target_pairs={{0,1},{1,0},{2,3},{3,2},{4,5},{5,4},{6,7},{7,6},{8,9},{9,8},{10,11... | collective-permute-start | bytes 884744 | tf_op jit(solution)/shard_map/ppermute | solution.py:19
  394.6 29.0 %collective-permute-start.41 = (bf16[576,256]{1,0:T(8,128)(2,1)S(1)}, bf16[576,256]{1,0:T(8,128)(2,1)S(1)}, u32[]{:S(2)}, u32[]{:S(2)}) collective-permute-start(bf16[576,256]{1,0:T(8,128)(2,1)S(1)} %get-tuple-element.232), channel_id=1, source_target_pairs={{0,2},{1,3},{2,0},{3,1},{4,6},{5,7},{6,4},{7,5},{8,10},{9,11},{10,... | collective-permute-start | bytes 884744 | tf_op jit(solution)/shard_map/ppermute | solution.py:19
  395.8 27.8 %collective-permute-start.42 = (bf16[576,256]{1,0:T(8,128)(2,1)S(1)}, bf16[576,256]{1,0:T(8,128)(2,1)S(1)}, u32[]{:S(2)}, u32[]{:S(2)}) collective-permute-start(bf16[576,256]{1,0:T(8,128)(2,1)S(1)} %get-tuple-element.231), channel_id=1, source_target_pairs={{0,3},{1,2},{2,1},{3,0},{4,7},{5,6},{6,5},{7,4},{8,11},{9,10},{10,... | collective-permute-start | bytes 884744 | tf_op jit(solution)/shard_map/ppermute | solution.py:19
  396.6 22.9 %copy-start.33 = (bf16[256,256]{1,0:T(8,128)(2,1)}, bf16[256,256]{1,0:T(8,128)(2,1)S(1)}, u32[]{:S(2)}) copy-start(bf16[256,256]{1,0:T(8,128)(2,1)S(1)} %collective-permute-done.37.refs_5_) | copy-start | bytes 393220
  396.6 21.5 %collective-permute-start.38 = (bf16[256,256]{1,0:T(8,128)(2,1)S(1)}, bf16[256,256]{1,0:T(8,128)(2,1)S(1)}, u32[]{:S(2)}, u32[]{:S(2)}) collective-permute-start(bf16[256,256]{1,0:T(8,128)(2,1)S(1)} %get-tuple-element.238), channel_id=1, source_target_pairs={{0,2},{1,3},{2,0},{3,1},{4,6},{5,7},{6,4},{7,5},{8,10},{9,11},{10,... | collective-permute-start | bytes 393224 | tf_op jit(solution)/shard_map/ppermute | solution.py:19
  413.7 5.9 %collective-permute-start.39 = (bf16[256,256]{1,0:T(8,128)(2,1)S(1)}, bf16[256,256]{1,0:T(8,128)(2,1)S(1)}, u32[]{:S(2)}, u32[]{:S(2)}) collective-permute-start(bf16[256,256]{1,0:T(8,128)(2,1)S(1)} %get-tuple-element.237), channel_id=1, source_target_pairs={{0,3},{1,2},{2,1},{3,0},{4,7},{5,6},{6,5},{7,4},{8,11},{9,10},{10,... | collective-permute-start | bytes 393224 | tf_op jit(solution)/shard_map/ppermute | solution.py:19
  435.6 1.2 collective-permute-start.45
  435.7 1.7 collective-permute-start.43
  436.2 2.3 collective-permute-start.44
  441.0 34.3 %all-to-all-start.1 = ((bf16[4,146,1024]{2,1,0:T(8,128)(2,1)}), bf16[4,146,1024]{2,1,0:T(8,128)(2,1)S(1)}, u32[]{:S(2)}, u32[]{:S(2)}) async-start(bf16[4,146,1024]{2,1,0:T(8,128)(2,1)} %pad_maximum_fusion.1), calls=%async_computation.1 | async-start | bytes 2490368 | tf_op jit(solution)/shard_map/all_to_all | solution.py:28
  475.8 6.9 %collective-permute-start.46 = (bf16[147,512]{1,0:T(8,128)(2,1)S(1)}, bf16[147,512]{1,0:T(8,128)(2,1)S(1)}, u32[]{:S(2)}, u32[]{:S(2)}) collective-permute-start(bf16[147,512]{1,0:T(8,128)(2,1)S(1)} %pad_maximum_fusion.5), channel_id=1, source_target_pairs={{0,1},{1,0},{2,3},{3,2},{4,5},{5,4},{6,7},{7,6},{8,9},{9,8},{10,11... | collective-permute-start | bytes 451592 | tf_op jit(solution)/shard_map/ppermute | solution.py:19
  478.3 8.3 %collective-permute-start.47 = (bf16[147,512]{1,0:T(8,128)(2,1)S(1)}, bf16[147,512]{1,0:T(8,128)(2,1)S(1)}, u32[]{:S(2)}, u32[]{:S(2)}) collective-permute-start(bf16[147,512]{1,0:T(8,128)(2,1)S(1)} %pad_maximum_fusion.5), channel_id=1, source_target_pairs={{0,2},{1,3},{2,0},{3,1},{4,6},{5,7},{6,4},{7,5},{8,10},{9,11},{10,... | collective-permute-start | bytes 451592 | tf_op jit(solution)/shard_map/ppermute | solution.py:19
  478.7 8.0 %collective-permute-start.48 = (bf16[147,512]{1,0:T(8,128)(2,1)S(1)}, bf16[147,512]{1,0:T(8,128)(2,1)S(1)}, u32[]{:S(2)}, u32[]{:S(2)}) collective-permute-start(bf16[147,512]{1,0:T(8,128)(2,1)S(1)} %pad_maximum_fusion.5), channel_id=1, source_target_pairs={{0,3},{1,2},{2,1},{3,0},{4,7},{5,6},{6,5},{7,4},{8,11},{9,10},{10,... | collective-permute-start | bytes 451592 | tf_op jit(solution)/shard_map/ppermute | solution.py:19
  (42 other events, 205.0 us)
Sparse Core Ops, SparseCore 0:
  10.2 33.9 all-gather.2
  45.8 119.6 all-gather.4
  262.6 46.4 reduce-scatter.4
  327.9 90.5 reduce-scatter.2

commit v3 on v2

--- a/solution.py
+++ b/solution.py
@@ -82,7 +82,8 @@
 
 VMEM = pl.BlockSpec(memory_space=pltpu.VMEM)
 SMEM = pl.BlockSpec(memory_space=pltpu.SMEM)
-ROOM = pltpu.CompilerParams(vmem_limit_bytes=60 * 1024 * 1024)
+ROOM = pltpu.CompilerParams(vmem_limit_bytes=28 * 1024 * 1024)
+ALL = pltpu.CompilerParams(vmem_limit_bytes=60 * 1024 * 1024)
 
 
 def cost(multiply_adds, *arrays):
@@ -423,7 +424,7 @@
         out_specs=[whole] * chunks + [strip] * results,
         out_shape=[struct((count, width), dtype)] * chunks + [struct((chunks * count, units), LOW)] * results,
         scratch_shapes=[pltpu.VMEM((chunks * count, width), F32)],
-        compiler_params=ROOM,
+        compiler_params=ALL,
         cost_estimate=cost(3 * chunks * count * width * units, *rows, weights, *saved),
         name=name,
     )(*rows, weights, weights, weights, *saved)
@@ -462,7 +463,11 @@
     datt_ref[...] = mm(low, out_ref[...]).astype(LOW)
 
 
-def finish_kernel(core_ref, raw_ref, cos_ref, sin_ref, gain_key_ref, dq_ref, q_ref, kv_ref, dhid_ref, x_ref, gain_ref, normed_ref, *refs):
+def pull_kernel(left_ref, right_ref, out_ref):
+    out_ref[...] = mm_t(left_ref[...], right_ref[...])
+
+
+def finish_kernel(core_ref, raw_ref, cos_ref, sin_ref, gain_key_ref, pulled_ref, kv_ref, dhid_ref, x_ref, gain_ref, normed_ref, *refs):
     parts, (din_ref, dgain_ref, dgain_key_ref, send_ref, own_ref, sums) = refs[:-6], refs[-6:]
     head = raw_ref.shape[1]
     d_kv = sum(r[...].astype(F32) for r in parts)
@@ -477,7 +482,7 @@
     core = core_ref[0]
     own_ref[...] = sums[pl.ds(pl.multiple_of(core * half, half), half), :].astype(LOW)
     send_ref[...] = sums[pl.ds(pl.multiple_of((1 - core) * half, half), half), :].astype(LOW)
-    d_normed = mm_t(dq_ref[...], q_ref[...]) + mm_t(low, kv_ref[...])
+    d_normed = pulled_ref[...] + mm_t(low, kv_ref[...])
     x = x_ref[...].astype(F32)
     d_x, d_gain = rms_back(d_normed, x, inverse_rms(x), gain_ref[...])
     dgain_ref[...] = column_sum(d_gain)
@@ -519,7 +524,7 @@
         out_specs=[out] * (2 * sets),
         out_shape=[struct((height // 2, width), LOW)] * (2 * sets),
         scratch_shapes=[pltpu.VMEM((height, chunks * rows), LOW), pltpu.VMEM((sets, height, step), F32)],
-        compiler_params=ROOM,
+        compiler_params=ALL if chunks > 1 else ROOM,
         cost_estimate=cost(sets * chunks * rows * height * width, *[v for v, _ in lefts], struct((height, sets * width), LOW)),
         name="weight_grad",
     )(core.reshape(1), *[v for v, _ in lefts], *[v for v, _ in rights])
@@ -644,14 +649,15 @@
         if g == 1:
             rows[0] = after(rows[0], done[0][0][0])
         if g == 2:
-            (down_halves,) = weight_grad(f, own, [(after(v, done[1][0][0]) if p == 2 else v, 0) for p, v in enumerate(d_outs)], acts)
-            down_sum = pair_sum((down_halves[1], swap(down_halves[0], "fsdp", 1)))
-            rows[0] = after(rows[0], down_sum)
+            rows[0] = after(rows[0], done[1][0][0])
         done.append(ffn_call(ffn_back_kernel, "ffn_back", rows, weights, (slopes[g], curves[g]), 2, LOW if g else F32))
+    last = done[-1][0][-1]
+    (down_halves,) = weight_grad(f, own, [(v if p else after(v, last), 0) for p, v in enumerate(d_outs)], acts)
+    down_sum = pair_sum((down_halves[1], swap(down_halves[0], "fsdp", 1)))
     (grad_down,) = scatter_ctx(down_sum)
     parts = [done[place[p][0]][0][place[p][1]] for p in range(T)]
     d_gates, d_ups = [[(done[place[p][0]][1][i], place[p][1]) for p in range(T)] for i in range(2)]
-    first_in = after(ffn_ins[0], parts[-1])
+    first_in = after(ffn_ins[0], down_sum)
     gate_halves, up_halves = weight_grad(f, own, [(v, 0) for v in [first_in] + ffn_ins[1:]], d_gates, d_ups)
 
     parts = [after(v, *gate_halves, *up_halves) if p == 0 else v for p, v in enumerate(from_tp(parts))]
@@ -659,6 +665,7 @@
         middle_kernel,
         out_shape=[token, token_low, struct((own, wide), LOW), gain_row, gain_row],
         compiler_params=ROOM,
+        cost_estimate=cost(300 * own * wide * width_model, out_full),
         name="middle",
     )(d_result, hidden, branch, out_full, g_pre_ffn, g_post_attn, *parts)
     assert halo * block_rows == WIN
@@ -669,6 +676,7 @@
     (out_halves,) = weight_grad(f, own, [(d_branch, 0)], [(attended, 0)])
     out_sum = collect_core(*out_halves)
     out_low = out_sum.astype(LOW)
+    d_attended = after(d_attended, *out_halves)
     d_query, dg_query, *d_pairs = pl.pallas_call(
         functools.partial(attend_back_kernel, heads, T, halo + 1),
         grid=(seqs,),
@@ -677,45 +685,36 @@
         + [pl.BlockSpec((halo + (p == 0), 1, sub, 2 * head_width), lambda s: (0, s, 0, 0)) for p in range(T)],
         out_shape=[struct((own, wide), LOW), struct((seqs, 1, head_width), F32)]
         + [struct((halo + (p == 0), seqs, sub, 2 * head_width), F32 if p == 0 else LOW) for p in range(T)],
-        compiler_params=ROOM,
+        compiler_params=ALL,
         name="attend_back",
     )(t.reshape(1), qinfo, kinfo, q_raw, g_query, cos_own, sin_own, q_rot, lse, d_attended, *kv_rows)
-    d_blocks = [d_pairs[0][b] for b in range(halo + 1)]
+    d_own = after(d_pairs[0], out_low)
+    d_blocks = [d_own[b] for b in range(halo + 1)]
     for p in range(1, T):
-        got = after(swap(d_pairs[p], "tp", p), out_low).astype(F32)
+        got = swap(d_pairs[p], "tp", p).astype(F32)
         for b in range(1, halo):
             d_blocks[b] = d_blocks[b] + got[b - 1]
         later = (t ^ p) > t
         d_blocks[0] = d_blocks[0] + jnp.where(later, got[halo - 1], 0.0)
         d_blocks[halo] = d_blocks[halo] + jnp.where(later, 0.0, got[halo - 1])
     d_kv = d_blocks[halo]
+    d_query_late, out_low = after(d_query, d_kv.astype(LOW)), after(out_low, d_kv.astype(LOW))
     for d in range(halo, 0, -1):
         come = shifted(d_kv.astype(LOW), "ctx", -1)
-        if d == halo:
-            d_query_late, out_low = after(d_query, come), after(out_low, come)
         if d > 1:
             d_kv = d_blocks[d - 1] + come.astype(F32)
     d_kv = [d_blocks[0], come]
-    out_head = out_sum[:, :head_width]
-    for p in range(1, T):
-        out_head = out_head + swap(out_low[:, p * head_width : (p + 1) * head_width], "tp", p).astype(F32)
-    head_of = lambda p: d_query_late[:, p * head_width : (p + 1) * head_width]
-    normed_late = after(normed, d_kv[1])
-    (q_halves,) = weight_grad(
-        f, own, [(normed_late, p) for p in range(T)], [(swap(head_of(p), "tp", p) if p else head_of(p), 0) for p in range(T)]
-    )
-    out_low = out_head.astype(LOW)
-    d_kv[0] = after(d_kv[0], *q_halves, out_low)
-    own_rows = lambda table: jnp.tile(table, (seqs, 1))
-    grad_input, dg_input, dg_key, *kv_halves = pl.pallas_call(
-        finish_kernel,
-        in_specs=[SMEM] + [VMEM] * (11 + len(d_kv)),
-        out_shape=[token, gain_row, struct((1, head_width), F32)] + [struct((half, 2 * head_width), LOW)] * 2,
-        scratch_shapes=[pltpu.VMEM((2 * half, 2 * head_width), F32)],
-        compiler_params=ROOM,
-        name="finish",
-    )(f.reshape(1), key_own, own_rows(cos_own), own_rows(sin_own), g_key, d_query, q_full, kv_full, d_hidden, x_own, g_input,
-      normed_own, *[v.reshape(own, 2 * head_width) for v in d_kv])
+    head = lambda v, p: v[:, p * head_width : (p + 1) * head_width]
+    heads_sent = [jnp.concatenate([head(d_query_late, p), head(out_low, p)], axis=0) for p in range(1, T)]
+    heads_here = [swap(v, "tp", p + 1) for p, v in enumerate(heads_sent)]
+    out_head = head(out_sum, 0)
+    for v in heads_here:
+        out_head = out_head + v[own:].astype(F32)
+    normed_late = after(normed, come)
+    (q_halves,) = weight_grad(f, own, [(normed_late, p) for p in range(T)], [(head(d_query, 0), 0)] + [(v, 0) for v in heads_here])
+    pulled = pl.pallas_call(
+        pull_kernel, out_shape=token, compiler_params=ROOM, name="pull"
+    )(d_query, q_full)
 
     def pack(values, wide):
         top = lax.reduce_precision(values, 8, 7)
@@ -727,28 +726,47 @@
         flat = rows.reshape(-1)
         return flat[:n] + flat[n : 2 * n]
 
-    sums = [dg_input, dg_post_attn, dg_pre_ffn, dg_post_ffn]
-    small = [jnp.sum(dg_query, axis=(0, 1)), dg_key]
-    extra = [v.reshape(F * C, piece) for v in sums] + [v.reshape(F * C, gain_piece) for v in small]
-    extra = jnp.concatenate(extra + [jnp.broadcast_to(error[:, :1], (F * C, 1))], axis=1).reshape(F, C, -1)
-    n = extra.shape[2]
-    extra = lax.dynamic_index_in_dim(extra, f, 0, False) + swap(lax.dynamic_index_in_dim(extra, f ^ 1, 0, False), "fsdp", 1)
-    q_low = collect_core(after(q_halves[0], dg_key), q_halves[1]).astype(LOW)
-    grads = jnp.concatenate([q_low, out_low, collect_core(*kv_halves).astype(LOW)], axis=1)
-    grads = jnp.concatenate([grads.reshape(C, piece, grads.shape[1]), pack(extra, grads.shape[1])], axis=1)
-    grads = jnp.sum(exchange(grads, "ctx").astype(F32), axis=0)
-    grad_query, grad_out = grads[:piece, :head_width], grads[:piece, head_width : 2 * head_width]
-    kv_low = grads[:piece, 2 * head_width :]
-    kv_low = jnp.concatenate([kv_low.astype(LOW), pack(unpack(grads[piece:], n)[None], kv_low.shape[1])[0]], axis=0)
-    kv_low = lax.optimization_barrier(kv_low)
-    totals = {p: (swap(kv_low, "tp", p) if p else kv_low).astype(F32) for p in range(T)}
+    def core_rows(values):
+        rows = jnp.concatenate([v.reshape(F * C, -1) for v in values], axis=1).reshape(F, C, -1)
+        return lax.dynamic_index_in_dim(rows, f, 0, False) + swap(lax.dynamic_index_in_dim(rows, f ^ 1, 0, False), "fsdp", 1)
+
+    def owner_sums(weight_sums, rows):
+        wide = weight_sums.shape[1]
+        sent = jnp.concatenate([weight_sums.reshape(C, piece, wide), pack(rows, wide)], axis=1)
+        sums = jnp.sum(exchange(sent, "ctx").astype(F32), axis=0)
+        return sums[:piece], unpack(sums[piece:], rows.shape[1])
+
+    early = core_rows(
+        [dg_post_attn, dg_pre_ffn, dg_post_ffn, jnp.sum(dg_query, axis=(0, 1)), jnp.broadcast_to(error[:, :1], (F * C, 1))]
+    )
+    both_heads = jnp.concatenate([collect_core(*q_halves).astype(LOW), out_head.astype(LOW)], axis=1)
+    d_kv[0] = after(d_kv[0], both_heads, pulled)
+    own_rows = lambda table: jnp.tile(table, (seqs, 1))
+    grad_input, dg_input, dg_key, *kv_halves = pl.pallas_call(
+        finish_kernel,
+        in_specs=[SMEM] + [VMEM] * (10 + len(d_kv)),
+        out_shape=[token, gain_row, struct((1, head_width), F32)] + [struct((half, 2 * head_width), LOW)] * 2,
+        scratch_shapes=[pltpu.VMEM((2 * half, 2 * head_width), F32)],
+        compiler_params=ROOM,
+        name="finish",
+    )(f.reshape(1), key_own, own_rows(cos_own), own_rows(sin_own), g_key, pulled, kv_full, d_hidden, x_own, g_input,
+      normed_own, *[v.reshape(own, 2 * head_width) for v in d_kv])
+    late = core_rows([dg_input, dg_key])
+    sums = jnp.concatenate([both_heads, collect_core(*kv_halves).astype(LOW)], axis=1)
+    sums, total = owner_sums(sums, jnp.concatenate([early, late], axis=1))
+    grad_query, grad_out = sums[:, :head_width], sums[:, head_width : 2 * head_width]
+    grad_kv = sums[:, 2 * head_width :]
+    low = jnp.concatenate([grad_kv.astype(LOW), pack(total[None], 2 * head_width)[0]], axis=0)
+    low = lax.optimization_barrier(low)
+    totals = {p: (swap(low, "tp", p) if p else low).astype(F32) for p in range(T)}
     bit = 1
     while bit < T:
         totals = {p: totals[p] + totals[p ^ bit] for p in totals if not p & bit}
         bit *= 2
-    grad_kv, total = totals[0][:piece], unpack(totals[0][piece:], n)
-    loss = total[-1] / (2.0 * width_model * count)
-    at = 4 * piece
+    grad_kv, total = totals[0][:piece], unpack(totals[0][piece:], total.shape[0])
+    early, late = total[: early.shape[1]], total[early.shape[1] :]
+    loss = early[-1] / (2.0 * width_model * count)
+    at = 3 * piece
     return (
         output.reshape(seqs, sub, width_model),
         loss,
@@ -760,12 +778,12 @@
         grad_gate,
         grad_up,
         grad_down.T,
-        total[:piece],
-        total[at : at + gain_piece],
-        total[at + gain_piece : at + 2 * gain_piece],
-        total[piece : 2 * piece],
-        total[2 * piece : 3 * piece],
-        total[3 * piece : 4 * piece],
+        late[:piece],
+        early[at : at + gain_piece],
+        late[piece:],
+        early[:piece],
+        early[piece : 2 * piece],
+        early[2 * piece : at],
     )
 
 

time: 506 us -> 483 us (0.955)
  Pallas kernels: 160 us -> 132 us
  local copies, waits for them, and re-layouts: 31.4 us -> 57.9 us
  waiting for transfers between devices: 203 us -> 182 us
    unnamed x108 -> x210, local copies, waits for them, and re-layouts: 9.14 us -> 35.2 us
    ppermute x45 -> x43, waiting for transfers between devices: 105 us -> 87.3 us  [swap(): lax.ppermute(values, axis, [(i, i ^ bits) for i in range(lax.axis_size(ax...]
    pallas_call x2, Pallas kernels: 10.3 us -> 3.94 us  [pair_sum(): pl.pallas_call(pair_sum_kernel, grid=(rows // step,), in_specs=[pl.BlockS...]
    ppermute x45 -> x43, starting transfers between devices: 43.3 us -> 38.2 us  [swap(): lax.ppermute(values, axis, [(i, i ^ bits) for i in range(lax.axis_size(ax...]
  transfers between devices with their start and end apart: 55 -> 53, of which waited for: 27 -> 24; matrix products, arithmetic and copies ran while one was open for 9% -> 10% of each run, Pallas kernels for 28% -> 22%
where the time goes in v3:
time: 483 us; the launch traced here: 477 us
  waiting for transfers between devices  182 us (38%)
  Pallas kernels  132 us (27%)
  starting transfers between devices  58.8 us (12%)
  local copies, waits for them, and re-layouts  57.9 us (12%)
  other arithmetic  26.2 us (5%)
  between operations  18.6 us (4%)
    ppermute x43, waiting for transfers between devices, swap(): lax.ppermute(values, axis, [(i, i ^ bits) for i in range(lax.axis_size(ax...  87.3 us
    pallas_call x6, Pallas kernels, ffn_call(): pl.pallas_call(functools.partial(kernel, units, chunks), grid=(pl.cdiv(un...  64.7 us
    ppermute x4, waiting for transfers between devices, shifted(): lax.ppermute(values, axis, [(i, i + by) for i in range(size) if 0 <= i +...  52.8 us
    ppermute x43, starting transfers between devices, swap(): lax.ppermute(values, axis, [(i, i ^ bits) for i in range(lax.axis_size(ax...  38.2 us
    unnamed x210, local copies, waits for them, and re-layouts  35.2 us
    pallas_call x4, Pallas kernels, weight_grad(): pl.pallas_call(functools.partial(weight_grad_kernel, chunks, sets), grid=...  32.8 us
    all_to_all x2, waiting for transfers between devices, exchange(): return lax.all_to_all(values, axes, 0, 0, tiled=True)  28 us
    ppermute x4, starting transfers between devices, shifted(): lax.ppermute(values, axis, [(i, i + by) for i in range(size) if 0 <= i +...  10.6 us
  transfers between devices with their start and end apart: 53, of which 24 were waited for; matrix products, arithmetic and copies ran while one was open for 10% of the time, Pallas kernels for 22%

profile of v3, /device:TPU:0, one launch (start us, length us, event | category | flops | bytes accessed | tf_op | source)
XLA Modules:
  0.0 477.2 jit_solution(9485790846020138215)
XLA Ops:
  9.4 2.6 pad_maximum_fusion
  14.2 6.3 %all-to-all-start = ((bf16[8,2,832]{2,1,0:T(2,128)(2,1)}), bf16[8,2,832]{2,1,0:T(2,128)(2,1)S(1)}, u32[]{:S(2)}, u32[]{:S(2)}) async-start(bf16[8,2,832]{2,1,0:T(2,128)(2,1)} %reshape.325), calls=%async_computation | async-start | bytes 57344 | tf_op jit(solution)/shard_map/all_to_all | solution.py:28
  35.7 1.7 copy-done.13
  40.5 3.6 all-gather.3.cloned.1.call-done
  45.7 2.4 collective-permute-start.2
  51.9 2.8 project_keys.1
  57.4 3.2 collective-permute-start.8
  60.6 2.3 collective-permute-done.2.refs_3_
  62.9 12.1 %collective-permute-done.1.refs_2_ = bf16[576,512]{1,0:T(8,128)(2,1)} collective-permute-done((bf16[576,512]{1,0:T(8,128)(2,1)S(1)}, bf16[576,512]{1,0:T(8,128)(2,1)}, u32[]{:S(2)}, u32[]{:S(2)}) %collective-permute-start.1) | collective-permute-done | bytes 589856 | tf_op jit(solution)/shard_map/ppermute | solution.py:19
  75.6 4.1 collective-permute-start.12
  79.8 11.3 %collective-permute-done.12.refs_5_ = bf16[4,64,512]{2,1,0:T(8,128)(2,1)} collective-permute-done((bf16[4,64,512]{2,1,0:T(8,128)(2,1)}, bf16[4,64,512]{2,1,0:T(8,128)(2,1)}, u32[]{:S(2)}, u32[]{:S(2)}) %collective-permute-start.12) | collective-permute-done | bytes 262176 | tf_op jit(solution)/shard_map/ppermute | solution.py:24
  98.8 2.8 assemble.1
  101.6 4.4 collective-permute-done.10.refs_3_
  106.1 1.6 collective-permute-start.15
  107.7 2.0 fusion.25.q_ref
  109.8 4.9 %collective-permute-done.13.refs_6_ = bf16[4,64,512]{2,1,0:T(8,128)(2,1)S(1)} collective-permute-done((bf16[4,64,512]{2,1,0:T(8,128)(2,1)}, bf16[4,64,512]{2,1,0:T(8,128)(2,1)S(1)}, u32[]{:S(2)}, u32[]{:S(2)}) %collective-permute-start.13) | collective-permute-done | bytes 262176 | tf_op jit(solution)/shard_map/ppermute | solution.py:19
  114.7 4.2 collective-permute-done.15.refs_8_
  118.9 4.9 %attend.1 = (bf16[256,1024]{1,0:T(8,128)(2,1)S(1)}, bf16[256,1024]{1,0:T(8,128)(2,1)S(1)}, f32[4,256,1]{2,1,0:T(8,128)S(1)}) custom-call(s32[4,64,2]{2,1,0:T(8,128)S(1)} %copy-done.31, s32[4,2,768]{2,1,0:T(2,128)S(1)} %copy-done.54, f32[256,1024]{1,0:T(8,128)S(1)} %fusion.25.q_ref, f32[1,256]{1,0:T(1,128)S(1)} %copy-done.61, f32[64,256]{1,0:T(8,128)S(1)} %copy-done.32, ...), custom_call_target="tpu_custom_call" | custom-call | flops 402653184 | bytes 4194304 | tf_op jit(solution)/shard_map/attend/pallas_call | solution.py:603
  129.4 1.5 collective-permute-start.19
  132.3 22.2 %collective-permute-done.18.refs_0_.refs_2_ = bf16[256,1152]{1,0:T(8,128)(2,1)S(1)} collective-permute-done((bf16[256,1152]{1,0:T(8,128)(2,1)S(1)}, bf16[256,1152]{1,0:T(8,128)(2,1)S(1)}, u32[]{:S(2)}, u32[]{:S(2)}) %collective-permute-start.18) | collective-permute-done | bytes 589856 | tf_op jit(solution)/shard_map/ppermute | solution.py:19
  155.4 10.0 %all-gather.5.cloned.1.call-done.refs_1_.refs_2_.refs_3_.refs_4_ = bf16[3,1152,1728]{2,1,0:T(8,128)(2,1)} async-done(((bf16[3,144,1728]{2,1,0:T(8,128)(2,1)}), bf16[3,1152,1728]{2,1,0:T(8,128)(2,1)}) %all-gather.5.cloned.1.call-update) | async-done | bytes 11943952 | tf_op jit(solution)/shard_map/all_gather | solution.py:552
  165.4 13.1 %ffn.5 = (bf16[256,1152]{1,0:T(8,128)(2,1)}, bf16[256,1152]{1,0:T(8,128)(2,1)}, bf16[512,1728]{1,0:T(8,128)(2,1)}, bf16[512,1728]{1,0:T(8,128)(2,1)}, bf16[512,1728]{1,0:T(8,128)(2,1)}) custom-call(bf16[256,1152]{1,0:T(8,128)(2,1)} %copy-done.85, bf16[256,1152]{1,0:T(8,128)(2,1)} %collective-permute-done.19.refs_1_.refs_3_, ...), custom_call_target="tpu_custom_call" | custom-call | flops 6115295232 | bytes 13123584 | tf_op jit(solution)/shard_map/ffn/pallas_call | solution.py:418
  178.5 1.8 collective-permute-start.20
  181.7 9.0 %ffn.4 = (bf16[256,1152]{1,0:T(8,128)(2,1)}, bf16[256,1728]{1,0:T(8,128)(2,1)}, bf16[256,1728]{1,0:T(8,128)(2,1)}, bf16[256,1728]{1,0:T(8,128)(2,1)}) custom-call(bf16[256,1152]{1,0:T(8,128)(2,1)} %collective-permute-done.16.refs_0_.refs_1_, bf16[3,1152,1728]{2,1,0:T(8,128)(2,1)} %all-gather.5.cloned.1.call-done.refs_1_.refs_2_.refs_3_.refs_4_, ...), custom_call_target="tpu_custom_call" | custom-call | flops 3057647616 | bytes 12533760 | tf_op jit(solution)/shard_map/ffn/pallas_call | solution.py:418
  192.7 9.6 %ffn.3 = (f32[256,1152]{1,0:T(8,128)}, bf16[256,1728]{1,0:T(8,128)(2,1)}, bf16[256,1728]{1,0:T(8,128)(2,1)}, bf16[256,1728]{1,0:T(8,128)(2,1)}) custom-call(bf16[256,1152]{1,0:T(8,128)(2,1)} %copy-done.41, bf16[3,1152,1728]{2,1,0:T(8,128)(2,1)} %all-gather.5.cloned.1.call-done.refs_1_.refs_2_.refs_3_.refs_4_, ...), custom_call_target="tpu_custom_call" | custom-call | flops 3057647616 | bytes 12533760 | tf_op jit(solution)/shard_map/ffn/pallas_call | solution.py:418
  202.3 4.4 collective-permute-done.20.refs_2_
  209.2 3.4 loss.1
  214.8 1.5 collective-permute-start.23
  218.3 9.3 %ffn_back.3 = (f32[256,1152]{1,0:T(8,128)}, bf16[256,1728]{1,0:T(8,128)(2,1)}, bf16[256,1728]{1,0:T(8,128)(2,1)}) custom-call(bf16[256,1152]{1,0:T(8,128)(2,1)} %get-tuple-element.160.refs_0_, bf16[3,1152,1728]{2,1,0:T(8,128)(2,1)} %all-gather.5.cloned.1.call-done.refs_1_.refs_2_.refs_3_.refs_4_, ...), custom_call_target="tpu_custom_call" | custom-call | flops 3057647616 | bytes 14303232 | tf_op jit(solution)/shard_map/ffn_back/pallas_call | solution.py:418
  227.6 3.7 collective-permute-done.23.refs_0_.refs_1_
  232.1 9.1 %ffn_back.4 = (bf16[256,1152]{1,0:T(8,128)(2,1)}, bf16[256,1728]{1,0:T(8,128)(2,1)}, bf16[256,1728]{1,0:T(8,128)(2,1)}) custom-call(bf16[256,1152]{1,0:T(8,128)(2,1)} %copy-done.86, bf16[3,1152,1728]{2,1,0:T(8,128)(2,1)} %all-gather.5.cloned.1.call-done.refs_1_.refs_2_.refs_3_.refs_4_, ...), custom_call_target="tpu_custom_call" | custom-call | flops 3057647616 | bytes 14303232 | tf_op jit(solution)/shard_map/ffn_back/pallas_call | solution.py:418
  241.1 1.7 collective-permute-done.22.refs_0_.refs_2_
  243.9 14.6 %ffn_back.5 = (bf16[256,1152]{1,0:T(8,128)(2,1)}, bf16[256,1152]{1,0:T(8,128)(2,1)}, bf16[512,1728]{1,0:T(8,128)(2,1)}, bf16[512,1728]{1,0:T(8,128)(2,1)}) custom-call(bf16[256,1152]{1,0:T(8,128)(2,1)} %copy-done.87, bf16[256,1152]{1,0:T(8,128)(2,1)} %copy-done.88, bf16[3,1152,1728]{2,1,0:T(8,128)(2,1)} %all-gather.5.cloned.1.call-done.refs_1_.refs_2_.refs_3_.refs_4_, ...), custom_call_target="tpu_custom_call" | custom-call | flops 6115295232 | bytes 16662528 | tf_op jit(solution)/shard_map/ffn_back/pallas_call | solution.py:418
  258.5 10.7 %weight_grad.4 = (bf16[576,1728]{1,0:T(8,128)(2,1)}, bf16[576,1728]{1,0:T(8,128)(2,1)}) custom-call(s32[1]{0:T(128)} %bitcast.8.core_ref, bf16[256,1152]{1,0:T(8,128)(2,1)} %get-tuple-element.160.refs_0_, bf16[256,1152]{1,0:T(8,128)(2,1)} %copy-done.86, bf16[256,1152]{1,0:T(8,128)(2,1)} %copy-done.87, bf16[256,1152]{1,0:T(8,128)(2,1)} %copy-done.88, ...), custom_call_target="tpu_custom_call" | custom-call | flops 4076863488 | bytes 6340608 | tf_op jit(solution)/shard_map/weight_grad/pallas_call | solution.py:518
  269.2 1.5 collective-permute-start.28
  270.8 1.5 collective-permute-start.26
  273.6 1.6 copy-done.18
  277.1 15.7 %weight_grad.5 = (bf16[576,1728]{1,0:T(8,128)(2,1)}, bf16[576,1728]{1,0:T(8,128)(2,1)}, bf16[576,1728]{1,0:T(8,128)(2,1)}, bf16[576,1728]{1,0:T(8,128)(2,1)}) custom-call(s32[1]{0:T(128)} %bitcast.8.core_ref, bf16[256,1152]{1,0:T(8,128)(2,1)} %copy-done.41, bf16[256,1152]{1,0:T(8,128)(2,1)} %collective-permute-done.16.refs_0_.refs_1_, ...), custom_call_target="tpu_custom_call" | custom-call | flops 8153726976 | bytes 10321920 | tf_op jit(solution)/shard_map/weight_grad/pallas_call | solution.py:518
  292.8 6.1 %collective-permute-done.27.refs_2_ = bf16[256,1152]{1,0:T(8,128)(2,1)} collective-permute-done((bf16[256,1152]{1,0:T(8,128)(2,1)}, bf16[256,1152]{1,0:T(8,128)(2,1)}, u32[]{:S(2)}, u32[]{:S(2)}) %collective-permute-start.27) | collective-permute-done | bytes 589856 | tf_op jit(solution)/shard_map/ppermute | solution.py:19
  304.7 3.6 middle.1
  308.3 2.9 weight_grad.6
  312.3 1.6 copy-done.20
  313.9 3.4 pair_sum.3
  317.3 2.0 copy-done.4
  319.3 7.1 %attend_back.1 = (bf16[256,1024]{1,0:T(8,128)(2,1)}, f32[4,1,256]{2,1,0:T(1,128)}, f32[3,4,64,512]{3,2,1,0:T(8,128)}, bf16[2,4,64,512]{3,2,1,0:T(8,128)(2,1)}, b...) custom-call(s32[1]{0:T(128)} %bitcast.4.place_ref, s32[4,64,2]{2,1,0:T(8,128)} %copy.35.qinfo_ref, ...), custom_call_target="tpu_custom_call" | custom-call | tf_op jit(solution)/shard_map/attend_back/pallas_call | solution.py:680
  331.7 3.9 convert_add_fusion
  338.5 3.1 collective-permute-done.32
  344.1 9.2 %collective-permute-done.34 = bf16[2,4,64,512]{3,2,1,0:T(8,128)(2,1)S(1)} collective-permute-done((bf16[2,4,64,512]{3,2,1,0:T(8,128)(2,1)}, bf16[2,4,64,512]{3,2,1,0:T(8,128)(2,1)S(1)}, u32[]{:S(2)}, u32[]{:S(2)}) %collective-permute-start.34) | collective-permute-done | bytes 524320 | tf_op jit(solution)/shard_map/ppermute | solution.py:19
  355.3 2.2 collective-permute-start.37
  357.6 1.5 collective-permute-start.38
  359.2 19.4 %collective-permute-done.35 = bf16[4,64,512]{2,1,0:T(8,128)(2,1)S(1)} collective-permute-done((bf16[4,64,512]{2,1,0:T(8,128)(2,1)S(1)}, bf16[4,64,512]{2,1,0:T(8,128)(2,1)S(1)}, u32[]{:S(2)}, u32[]{:S(2)}) %collective-permute-start.35) | collective-permute-done | bytes 262176 | tf_op jit(solution)/shard_map/ppermute | solution.py:24
  379.0 1.8 collective-permute-start.36
  380.8 2.4 fusion.2
  383.2 22.1 %collective-permute-done.36 = bf16[4,64,512]{2,1,0:T(8,128)(2,1)S(1)} collective-permute-done((bf16[4,64,512]{2,1,0:T(8,128)(2,1)S(1)}, bf16[4,64,512]{2,1,0:T(8,128)(2,1)S(1)}, u32[]{:S(2)}, u32[]{:S(2)}) %collective-permute-start.36) | collective-permute-done | bytes 262176 | tf_op jit(solution)/shard_map/ppermute | solution.py:24
  405.4 2.5 finish.1
  410.2 3.5 weight_grad.7
  418.1 3.5 all-to-all-start.1
  422.3 2.1 convert_bitcast_fusion
  424.4 28.0 %all-to-all-done.1 = bf16[4,146,1024]{2,1,0:T(8,128)(2,1)S(1)} async-done(((bf16[4,146,1024]{2,1,0:T(8,128)(2,1)}), bf16[4,146,1024]{2,1,0:T(8,128)(2,1)S(1)}, u32[]{:S(2)}, u32[]{:S(2)}) %all-to-all-start.1) | async-done | bytes 1196064 | tf_op jit(solution)/shard_map/all_to_all | solution.py:28
  452.9 1.5 collective-permute-start.44
  454.5 1.9 collective-permute-start.46
  457.2 2.2 collective-permute-done.44
  459.4 3.5 collective-permute-done.45
  466.4 1.5 convert_element_type.143
  (385 shorter events, 92.8 us)
Async XLA Ops:
  7.2 184.7 %copy-start = (bf16[4,256,1152]{2,1,0:T(8,128)(2,1)S(1)}, bf16[4,256,1152]{2,1,0:T(8,128)(2,1)}, u32[]{:S(2)}) copy-start(bf16[4,256,1152]{2,1,0:T(8,128)(2,1)} %param.17) | copy-start | bytes 7077892
  7.2 36.9 %all-gather.3.cloned.1.call-start = ((), (), s32[]{:S(2)}) async-start(), calls=%async_computation.4 | async-start | bytes 1474560 | tf_op jit(solution)/shard_map/all_gather | solution.py:551
  9.2 156.1 %all-gather.5.cloned.1.call-start = ((), (), s32[]{:S(2)}) async-start(), calls=%async_computation.5 | async-start | bytes 13934592 | tf_op jit(solution)/shard_map/all_gather | solution.py:552
  14.2 12.8 %all-to-all-start = ((bf16[8,2,832]{2,1,0:T(2,128)(2,1)}), bf16[8,2,832]{2,1,0:T(2,128)(2,1)S(1)}, u32[]{:S(2)}, u32[]{:S(2)}) async-start(bf16[8,2,832]{2,1,0:T(2,128)(2,1)} %reshape.325), calls=%async_computation | async-start | bytes 57344 | tf_op jit(solution)/shard_map/all_to_all | solution.py:28
  20.5 401.8 %reduce-scatter.5.cloned.1.call-start = ((), (), s32[]{:S(2)}) async-start(), calls=%async_computation.7 | async-start | bytes 2580480 | tf_op jit(solution)/shard_map/reduce_scatter | solution.py:643
  32.2 93.2 %copy-start.57 = (f32[1,1152]{1,0:T(1,128)}, f32[1,1152]{1,0:T(1,128)S(1)}, u32[]{:S(2)}) copy-start(f32[1,1152]{1,0:T(1,128)S(1)} %reshape.274.gain_attn_ref) | copy-start | bytes 13828
  33.0 92.4 %copy-start.59 = (f32[1,1152]{1,0:T(1,128)}, f32[1,1152]{1,0:T(1,128)S(1)}, u32[]{:S(2)}) copy-start(f32[1,1152]{1,0:T(1,128)S(1)} %reshape.275.gain_ffn_ref) | copy-start | bytes 13828
  45.6 3.6 collective-permute-start.3
  45.7 17.2 %collective-permute-start.2 = (bf16[576,512]{1,0:T(8,128)(2,1)S(1)}, bf16[576,512]{1,0:T(8,128)(2,1)}, u32[]{:S(2)}, u32[]{:S(2)}) collective-permute-start(bf16[576,512]{1,0:T(8,128)(2,1)S(1)} %get-tuple-element.123.refs_0_), channel_id=1, source_target_pairs={{0,3},{1,2},{2,1},{3,0},{4,7},{5,6},{6,5},{7,4},{8,11},{9,10},{10,... | collective-permute-start | bytes 1769480 | tf_op jit(solution)/shard_map/ppermute | solution.py:19
  48.1 26.9 %collective-permute-start.1 = (bf16[576,512]{1,0:T(8,128)(2,1)S(1)}, bf16[576,512]{1,0:T(8,128)(2,1)}, u32[]{:S(2)}, u32[]{:S(2)}) collective-permute-start(bf16[576,512]{1,0:T(8,128)(2,1)S(1)} %get-tuple-element.123.refs_0_), channel_id=1, source_target_pairs={{0,2},{1,3},{2,0},{3,1},{4,6},{5,7},{6,4},{7,5},{8,10},{9,11},{10,... | collective-permute-start | bytes 1769480 | tf_op jit(solution)/shard_map/ppermute | solution.py:19
  48.7 26.4 %collective-permute-start = (bf16[576,512]{1,0:T(8,128)(2,1)S(1)}, bf16[576,512]{1,0:T(8,128)(2,1)}, u32[]{:S(2)}, u32[]{:S(2)}) collective-permute-start(bf16[576,512]{1,0:T(8,128)(2,1)S(1)} %get-tuple-element.123.refs_0_), channel_id=1, source_target_pairs={{0,1},{1,0},{2,3},{3,2},{4,5},{5,4},{6,7},{7,6},{8,9},{9,8},{10,11... | collective-permute-start | bytes 1769480 | tf_op jit(solution)/shard_map/ppermute | solution.py:19
  57.4 18.2 %collective-permute-start.8 = (bf16[4,64,512]{2,1,0:T(8,128)(2,1)S(1)}, bf16[4,64,512]{2,1,0:T(8,128)(2,1)}, u32[]{:S(2)}, u32[]{:S(2)}) collective-permute-start(bf16[4,64,512]{2,1,0:T(8,128)(2,1)S(1)} %get-tuple-element.122), channel_id=1, source_target_pairs={{0,4},{4,8},{8,12},{1,5},{5,9},{9,13},{2,6},{6,10},{10,14},{3,7},{... | collective-permute-start | bytes 786440 | tf_op jit(solution)/shard_map/ppermute | solution.py:24
  62.9 31.1 %collective-permute-start.7 = (bf16[576,512]{1,0:T(8,128)(2,1)}, bf16[576,512]{1,0:T(8,128)(2,1)}, u32[]{:S(2)}, u32[]{:S(2)}) collective-permute-start(bf16[576,512]{1,0:T(8,128)(2,1)} %collective-permute-done.2.refs_3_), channel_id=1, source_target_pairs={{0,16},{16,0},{1,17},{17,1},{2,18},{18,2},{3,19},{19,3},{4,20},{20... | collective-permute-start | bytes 1769480 | tf_op jit(solution)/shard_map/ppermute | solution.py:19
  75.1 20.4 %collective-permute-start.6 = (bf16[576,512]{1,0:T(8,128)(2,1)}, bf16[576,512]{1,0:T(8,128)(2,1)}, u32[]{:S(2)}, u32[]{:S(2)}) collective-permute-start(bf16[576,512]{1,0:T(8,128)(2,1)} %collective-permute-done.1.refs_2_), channel_id=1, source_target_pairs={{0,16},{16,0},{1,17},{17,1},{2,18},{18,2},{3,19},{19,3},{4,20},{20... | collective-permute-start | bytes 1769480 | tf_op jit(solution)/shard_map/ppermute | solution.py:19
  75.1 20.9 %collective-permute-start.5 = (bf16[576,512]{1,0:T(8,128)(2,1)}, bf16[576,512]{1,0:T(8,128)(2,1)}, u32[]{:S(2)}, u32[]{:S(2)}) collective-permute-start(bf16[576,512]{1,0:T(8,128)(2,1)} %collective-permute-done.refs_1_), channel_id=1, source_target_pairs={{0,16},{16,0},{1,17},{17,1},{2,18},{18,2},{3,19},{19,3},{4,20},{20... | collective-permute-start | bytes 1769480 | tf_op jit(solution)/shard_map/ppermute | solution.py:19
  75.6 21.9 %collective-permute-start.4 = (bf16[576,512]{1,0:T(8,128)(2,1)S(1)}, bf16[576,512]{1,0:T(8,128)(2,1)}, u32[]{:S(2)}, u32[]{:S(2)}) collective-permute-start(bf16[576,512]{1,0:T(8,128)(2,1)S(1)} %get-tuple-element.123.refs_0_), channel_id=1, source_target_pairs={{0,16},{16,0},{1,17},{17,1},{2,18},{18,2},{3,19},{19,3},{4,20},{20... | collective-permute-start | bytes 1769480 | tf_op jit(solution)/shard_map/ppermute | solution.py:19
  75.6 15.4 %collective-permute-start.12 = (bf16[4,64,512]{2,1,0:T(8,128)(2,1)}, bf16[4,64,512]{2,1,0:T(8,128)(2,1)}, u32[]{:S(2)}, u32[]{:S(2)}) collective-permute-start(bf16[4,64,512]{2,1,0:T(8,128)(2,1)} %collective-permute-done.8.refs_1_), channel_id=1, source_target_pairs={{0,4},{4,8},{8,12},{1,5},{5,9},{9,13},{2,6},{6,10},{10,14},{3,7},{... | collective-permute-start | bytes 786440 | tf_op jit(solution)/shard_map/ppermute | solution.py:24
  91.1 15.0 %collective-permute-start.10 = (bf16[4,64,512]{2,1,0:T(8,128)(2,1)}, bf16[4,64,512]{2,1,0:T(8,128)(2,1)}, u32[]{:S(2)}, u32[]{:S(2)}) collective-permute-start(bf16[4,64,512]{2,1,0:T(8,128)(2,1)} %collective-permute-done.8.refs_1_), channel_id=1, source_target_pairs={{0,2},{1,3},{2,0},{3,1},{4,6},{5,7},{6,4},{7,5},{8,10},{9,11},{10,... | collective-permute-start | bytes 786440 | tf_op jit(solution)/shard_map/ppermute | solution.py:19
  94.0 15.7 %collective-permute-start.11 = (bf16[4,64,512]{2,1,0:T(8,128)(2,1)}, bf16[4,64,512]{2,1,0:T(8,128)(2,1)S(1)}, u32[]{:S(2)}, u32[]{:S(2)}) collective-permute-start(bf16[4,64,512]{2,1,0:T(8,128)(2,1)} %collective-permute-done.8.refs_1_), channel_id=1, source_target_pairs={{0,3},{1,2},{2,1},{3,0},{4,7},{5,6},{6,5},{7,4},{8,11},{9,10},{10,... | collective-permute-start | bytes 786440 | tf_op jit(solution)/shard_map/ppermute | solution.py:19
  95.5 14.3 %collective-permute-start.9 = (bf16[4,64,512]{2,1,0:T(8,128)(2,1)}, bf16[4,64,512]{2,1,0:T(8,128)(2,1)S(1)}, u32[]{:S(2)}, u32[]{:S(2)}) collective-permute-start(bf16[4,64,512]{2,1,0:T(8,128)(2,1)} %collective-permute-done.8.refs_1_), channel_id=1, source_target_pairs={{0,1},{1,0},{2,3},{3,2},{4,5},{5,4},{6,7},{7,6},{8,9},{9,8},{10,11... | collective-permute-start | bytes 786440 | tf_op jit(solution)/shard_map/ppermute | solution.py:19
  96.0 18.7 %collective-permute-start.13 = (bf16[4,64,512]{2,1,0:T(8,128)(2,1)}, bf16[4,64,512]{2,1,0:T(8,128)(2,1)S(1)}, u32[]{:S(2)}, u32[]{:S(2)}) collective-permute-start(bf16[4,64,512]{2,1,0:T(8,128)(2,1)} %collective-permute-done.12.refs_5_), channel_id=1, source_target_pairs={{0,1},{1,0},{2,3},{3,2},{4,5},{5,4},{6,7},{7,6},{8,9},{9,8},{10,11... | collective-permute-start | bytes 786440 | tf_op jit(solution)/shard_map/ppermute | solution.py:19
  97.5 17.2 %collective-permute-start.14 = (bf16[4,64,512]{2,1,0:T(8,128)(2,1)}, bf16[4,64,512]{2,1,0:T(8,128)(2,1)S(1)}, u32[]{:S(2)}, u32[]{:S(2)}) collective-permute-start(bf16[4,64,512]{2,1,0:T(8,128)(2,1)} %collective-permute-done.12.refs_5_), channel_id=1, source_target_pairs={{0,2},{1,3},{2,0},{3,1},{4,6},{5,7},{6,4},{7,5},{8,10},{9,11},{10,... | collective-permute-start | bytes 786440 | tf_op jit(solution)/shard_map/ppermute | solution.py:19
  106.1 12.8 %collective-permute-start.15 = (bf16[4,64,512]{2,1,0:T(8,128)(2,1)}, bf16[4,64,512]{2,1,0:T(8,128)(2,1)S(1)}, u32[]{:S(2)}, u32[]{:S(2)}) collective-permute-start(bf16[4,64,512]{2,1,0:T(8,128)(2,1)} %collective-permute-done.12.refs_5_), channel_id=1, source_target_pairs={{0,3},{1,2},{2,1},{3,0},{4,7},{5,6},{6,5},{7,4},{8,11},{9,10},{10,... | collective-permute-start | bytes 786440 | tf_op jit(solution)/shard_map/ppermute | solution.py:19
  125.5 29.1 %copy-start.42 = (bf16[256,1024]{1,0:T(8,128)(2,1)}, bf16[256,1024]{1,0:T(8,128)(2,1)S(1)}, u32[]{:S(2)}) copy-start(bf16[256,1024]{1,0:T(8,128)(2,1)S(1)} %get-tuple-element.132.att_ref.refs_1_) | copy-start | bytes 1572868
  128.8 49.7 %copy-start.41 = (bf16[256,1152]{1,0:T(8,128)(2,1)}, bf16[256,1152]{1,0:T(8,128)(2,1)S(1)}, u32[]{:S(2)}) copy-start(bf16[256,1152]{1,0:T(8,128)(2,1)S(1)} %get-tuple-element.166.refs_0_) | copy-start | bytes 1769476
  128.8 25.7 %collective-permute-start.18 = (bf16[256,1152]{1,0:T(8,128)(2,1)S(1)}, bf16[256,1152]{1,0:T(8,128)(2,1)S(1)}, u32[]{:S(2)}, u32[]{:S(2)}) collective-permute-start(bf16[256,1152]{1,0:T(8,128)(2,1)S(1)} %get-tuple-element.166.refs_0_), channel_id=1, source_target_pairs={{0,2},{1,3},{2,0},{3,1},{4,6},{5,7},{6,4},{7,5},{8,10},{9,11},{10,... | collective-permute-start | bytes 1769480 | tf_op jit(solution)/shard_map/ppermute | solution.py:19
  129.4 26.0 %collective-permute-start.19 = (bf16[256,1152]{1,0:T(8,128)(2,1)S(1)}, bf16[256,1152]{1,0:T(8,128)(2,1)}, u32[]{:S(2)}, u32[]{:S(2)}) collective-permute-start(bf16[256,1152]{1,0:T(8,128)(2,1)S(1)} %get-tuple-element.166.refs_0_), channel_id=1, source_target_pairs={{0,3},{1,2},{2,1},{3,0},{4,7},{5,6},{6,5},{7,4},{8,11},{9,10},{10,... | collective-permute-start | bytes 1769480 | tf_op jit(solution)/shard_map/ppermute | solution.py:19
  130.9 50.8 %collective-permute-start.16 = (bf16[256,1152]{1,0:T(8,128)(2,1)S(1)}, bf16[256,1152]{1,0:T(8,128)(2,1)}, u32[]{:S(2)}, u32[]{:S(2)}) collective-permute-start(bf16[256,1152]{1,0:T(8,128)(2,1)S(1)} %get-tuple-element.166.refs_0_), channel_id=1, source_target_pairs={{0,1},{1,0},{2,3},{3,2},{4,5},{5,4},{6,7},{7,6},{8,9},{9,8},{10,11... | collective-permute-start | bytes 1769480 | tf_op jit(solution)/shard_map/ppermute | solution.py:19
  178.5 28.3 %collective-permute-start.20 = (bf16[256,1152]{1,0:T(8,128)(2,1)}, bf16[256,1152]{1,0:T(8,128)(2,1)}, u32[]{:S(2)}, u32[]{:S(2)}) collective-permute-start(bf16[256,1152]{1,0:T(8,128)(2,1)} %get-tuple-element.141), channel_id=1, source_target_pairs={{0,2},{1,3},{2,0},{3,1},{4,6},{5,7},{6,4},{7,5},{8,10},{9,11},{10,... | collective-permute-start | bytes 1769480 | tf_op jit(solution)/shard_map/ppermute | solution.py:19
  180.2 26.5 %collective-permute-start.21 = (bf16[256,1152]{1,0:T(8,128)(2,1)}, bf16[256,1152]{1,0:T(8,128)(2,1)}, u32[]{:S(2)}, u32[]{:S(2)}) collective-permute-start(bf16[256,1152]{1,0:T(8,128)(2,1)} %get-tuple-element.142), channel_id=1, source_target_pairs={{0,3},{1,2},{2,1},{3,0},{4,7},{5,6},{6,5},{7,4},{8,11},{9,10},{10,... | collective-permute-start | bytes 1769480 | tf_op jit(solution)/shard_map/ppermute | solution.py:19
  190.7 17.2 %collective-permute-start.17 = (bf16[256,1152]{1,0:T(8,128)(2,1)}, bf16[256,1152]{1,0:T(8,128)(2,1)}, u32[]{:S(2)}, u32[]{:S(2)}) collective-permute-start(bf16[256,1152]{1,0:T(8,128)(2,1)} %get-tuple-element.140), channel_id=1, source_target_pairs={{0,1},{1,0},{2,3},{3,2},{4,5},{5,4},{6,7},{7,6},{8,9},{9,8},{10,11... | collective-permute-start | bytes 1769480 | tf_op jit(solution)/shard_map/ppermute | solution.py:19
  214.8 16.5 %collective-permute-start.23 = (bf16[256,1152]{1,0:T(8,128)(2,1)}, bf16[256,1152]{1,0:T(8,128)(2,1)S(1)}, u32[]{:S(2)}, u32[]{:S(2)}) collective-permute-start(bf16[256,1152]{1,0:T(8,128)(2,1)} %get-tuple-element.160.refs_0_), channel_id=1, source_target_pairs={{0,1},{1,0},{2,3},{3,2},{4,5},{5,4},{6,7},{7,6},{8,9},{9,8},{10,11... | collective-permute-start | bytes 1769480 | tf_op jit(solution)/shard_map/ppermute | solution.py:19
  216.3 26.5 %collective-permute-start.22 = (bf16[256,1152]{1,0:T(8,128)(2,1)}, bf16[256,1152]{1,0:T(8,128)(2,1)S(1)}, u32[]{:S(2)}, u32[]{:S(2)}) collective-permute-start(bf16[256,1152]{1,0:T(8,128)(2,1)} %get-tuple-element.160.refs_0_), channel_id=1, source_target_pairs={{0,2},{1,3},{2,0},{3,1},{4,6},{5,7},{6,4},{7,5},{8,10},{9,11},{10,... | collective-permute-start | bytes 1769480 | tf_op jit(solution)/shard_map/ppermute | solution.py:19
  217.8 25.0 %collective-permute-start.24 = (bf16[256,1152]{1,0:T(8,128)(2,1)}, bf16[256,1152]{1,0:T(8,128)(2,1)S(1)}, u32[]{:S(2)}, u32[]{:S(2)}) collective-permute-start(bf16[256,1152]{1,0:T(8,128)(2,1)} %get-tuple-element.160.refs_0_), channel_id=1, source_target_pairs={{0,3},{1,2},{2,1},{3,0},{4,7},{5,6},{6,5},{7,4},{8,11},{9,10},{10,... | collective-permute-start | bytes 1769480 | tf_op jit(solution)/shard_map/ppermute | solution.py:19
  269.2 4.3 collective-permute-start.25
  269.2 29.6 %collective-permute-start.28 = (bf16[256,1152]{1,0:T(8,128)(2,1)}, bf16[256,1152]{1,0:T(8,128)(2,1)}, u32[]{:S(2)}, u32[]{:S(2)}) collective-permute-start(bf16[256,1152]{1,0:T(8,128)(2,1)} %get-tuple-element.159), channel_id=1, source_target_pairs={{0,3},{1,2},{2,1},{3,0},{4,7},{5,6},{6,5},{7,4},{8,11},{9,10},{10,... | collective-permute-start | bytes 1769480 | tf_op jit(solution)/shard_map/ppermute | solution.py:19
  270.8 28.1 %collective-permute-start.26 = (bf16[256,1152]{1,0:T(8,128)(2,1)}, bf16[256,1152]{1,0:T(8,128)(2,1)}, u32[]{:S(2)}, u32[]{:S(2)}) collective-permute-start(bf16[256,1152]{1,0:T(8,128)(2,1)} %get-tuple-element.155), channel_id=1, source_target_pairs={{0,1},{1,0},{2,3},{3,2},{4,5},{5,4},{6,7},{7,6},{8,9},{9,8},{10,11... | collective-permute-start | bytes 1769480 | tf_op jit(solution)/shard_map/ppermute | solution.py:19
  272.3 26.6 %collective-permute-start.27 = (bf16[256,1152]{1,0:T(8,128)(2,1)}, bf16[256,1152]{1,0:T(8,128)(2,1)}, u32[]{:S(2)}, u32[]{:S(2)}) collective-permute-start(bf16[256,1152]{1,0:T(8,128)(2,1)} %get-tuple-element.178), channel_id=1, source_target_pairs={{0,2},{1,3},{2,0},{3,1},{4,6},{5,7},{6,4},{7,5},{8,10},{9,11},{10,... | collective-permute-start | bytes 1769480 | tf_op jit(solution)/shard_map/ppermute | solution.py:19
  277.0 189.4 %reduce-scatter.3.cloned.1.call-start = ((), (), s32[]{:S(2)}) async-start(), calls=%async_computation.6 | async-start | bytes 5160960 | tf_op jit(solution)/shard_map/reduce_scatter | solution.py:643
  298.9 13.3 %collective-permute-start.30 = (bf16[576,1728]{1,0:T(8,128)(2,1)}, bf16[576,1728]{1,0:T(8,128)(2,1)}, u32[]{:S(2)}, u32[]{:S(2)}) collective-permute-start(bf16[576,1728]{1,0:T(8,128)(2,1)} %get-tuple-element.183), channel_id=1, source_target_pairs={{0,16},{16,0},{1,17},{17,1},{2,18},{18,2},{3,19},{19,3},{4,20},{20... | collective-permute-start | bytes 5971976 | tf_op jit(solution)/shard_map/ppermute | solution.py:19
  298.9 13.4 %collective-permute-start.29 = (bf16[576,1728]{1,0:T(8,128)(2,1)}, bf16[576,1728]{1,0:T(8,128)(2,1)}, u32[]{:S(2)}, u32[]{:S(2)}) collective-permute-start(bf16[576,1728]{1,0:T(8,128)(2,1)} %get-tuple-element.180), channel_id=1, source_target_pairs={{0,16},{16,0},{1,17},{17,1},{2,18},{18,2},{3,19},{19,3},{4,20},{20... | collective-permute-start | bytes 5971976 | tf_op jit(solution)/shard_map/ppermute | solution.py:19
  312.2 19.4 %collective-permute-start.31 = (bf16[576,1024]{1,0:T(8,128)(2,1)}, bf16[576,1024]{1,0:T(8,128)(2,1)}, u32[]{:S(2)}, u32[]{:S(2)}) collective-permute-start(bf16[576,1024]{1,0:T(8,128)(2,1)} %get-tuple-element.186), channel_id=1, source_target_pairs={{0,16},{16,0},{1,17},{17,1},{2,18},{18,2},{3,19},{19,3},{4,20},{20... | collective-permute-start | bytes 3538952 | tf_op jit(solution)/shard_map/ppermute | solution.py:19
  326.5 15.1 %collective-permute-start.32 = (bf16[2,4,64,512]{3,2,1,0:T(8,128)(2,1)}, bf16[2,4,64,512]{3,2,1,0:T(8,128)(2,1)}, u32[]{:S(2)}, u32[]{:S(2)}) collective-permute-start(bf16[2,4,64,512]{3,2,1,0:T(8,128)(2,1)} %get-tuple-element.191), channel_id=1, source_target_pairs={{0,1},{1,0},{2,3},{3,2},{4,5},{5,4},{6,7},{7,6},{8,9},{9,8},{10,11... | collective-permute-start | bytes 1572872 | tf_op jit(solution)/shard_map/ppermute | solution.py:19
  327.5 15.2 %collective-permute-start.33 = (bf16[2,4,64,512]{3,2,1,0:T(8,128)(2,1)}, bf16[2,4,64,512]{3,2,1,0:T(8,128)(2,1)}, u32[]{:S(2)}, u32[]{:S(2)}) collective-permute-start(bf16[2,4,64,512]{3,2,1,0:T(8,128)(2,1)} %get-tuple-element.192), channel_id=1, source_target_pairs={{0,2},{1,3},{2,0},{3,1},{4,6},{5,7},{6,4},{7,5},{8,10},{9,11},{10,... | collective-permute-start | bytes 1572872 | tf_op jit(solution)/shard_map/ppermute | solution.py:19
  328.6 24.7 %collective-permute-start.34 = (bf16[2,4,64,512]{3,2,1,0:T(8,128)(2,1)}, bf16[2,4,64,512]{3,2,1,0:T(8,128)(2,1)S(1)}, u32[]{:S(2)}, u32[]{:S(2)}) collective-permute-start(bf16[2,4,64,512]{3,2,1,0:T(8,128)(2,1)} %get-tuple-element.193), channel_id=1, source_target_pairs={{0,3},{1,2},{2,1},{3,0},{4,7},{5,6},{6,5},{7,4},{8,11},{9,10},{10,... | collective-permute-start | bytes 1572872 | tf_op jit(solution)/shard_map/ppermute | solution.py:19
  338.4 20.8 %collective-permute-start.42 = (f32[4,465]{1,0:T(4,128)S(1)}, f32[4,465]{1,0:T(4,128)S(1)}, u32[]{:S(2)}, u32[]{:S(2)}) collective-permute-start(f32[4,465]{1,0:T(4,128)S(1)} %dynamic-slice_bitcast_fusion), channel_id=1, source_target_pairs={{0,16},{16,0},{1,17},{17,1},{2,18},{18,2},{3,19},{19,3},{4,20},{20... | collective-permute-start | bytes 22328 | tf_op jit(solution)/shard_map/ppermute | solution.py:19
  353.7 24.9 %collective-permute-start.35 = (bf16[4,64,512]{2,1,0:T(8,128)(2,1)S(1)}, bf16[4,64,512]{2,1,0:T(8,128)(2,1)S(1)}, u32[]{:S(2)}, u32[]{:S(2)}) collective-permute-start(bf16[4,64,512]{2,1,0:T(8,128)(2,1)S(1)} %get-tuple-element.220), channel_id=1, source_target_pairs={{4,0},{8,4},{12,8},{5,1},{9,5},{13,9},{6,2},{10,6},{14,10},{7,3},{... | collective-permute-start | bytes 786440 | tf_op jit(solution)/shard_map/ppermute | solution.py:24
  355.3 25.4 %collective-permute-start.37 = (bf16[832,256]{1,0:T(8,128)(2,1)S(1)}, bf16[832,256]{1,0:T(8,128)(2,1)S(1)}, u32[]{:S(2)}, u32[]{:S(2)}) collective-permute-start(bf16[832,256]{1,0:T(8,128)(2,1)S(1)} %pad_maximum_fusion.3), channel_id=1, source_target_pairs={{0,1},{1,0},{2,3},{3,2},{4,5},{5,4},{6,7},{7,6},{8,9},{9,8},{10,11... | collective-permute-start | bytes 1277960 | tf_op jit(solution)/shard_map/ppermute | solution.py:19
  357.6 23.2 %collective-permute-start.38 = (bf16[832,256]{1,0:T(8,128)(2,1)S(1)}, bf16[832,256]{1,0:T(8,128)(2,1)S(1)}, u32[]{:S(2)}, u32[]{:S(2)}) collective-permute-start(bf16[832,256]{1,0:T(8,128)(2,1)S(1)} %pad_maximum_fusion.4), channel_id=1, source_target_pairs={{0,2},{1,3},{2,0},{3,1},{4,6},{5,7},{6,4},{7,5},{8,10},{9,11},{10,... | collective-permute-start | bytes 1277960 | tf_op jit(solution)/shard_map/ppermute | solution.py:19
  359.1 21.7 %collective-permute-start.39 = (bf16[832,256]{1,0:T(8,128)(2,1)S(1)}, bf16[832,256]{1,0:T(8,128)(2,1)S(1)}, u32[]{:S(2)}, u32[]{:S(2)}) collective-permute-start(bf16[832,256]{1,0:T(8,128)(2,1)S(1)} %pad_maximum_fusion.5), channel_id=1, source_target_pairs={{0,3},{1,2},{2,1},{3,0},{4,7},{5,6},{6,5},{7,4},{8,11},{9,10},{10,... | collective-permute-start | bytes 1277960 | tf_op jit(solution)/shard_map/ppermute | solution.py:19
  359.2 46.0 %copy-start.33 = (f32[64,256]{1,0:T(8,128)S(1)}, f32[64,256]{1,0:T(8,128)}, u32[]{:S(2)}) copy-start(f32[64,256]{1,0:T(8,128)} %slice.218.cos_ref) | copy-start | bytes 196612
  359.2 46.1 %copy-start.35 = (f32[64,256]{1,0:T(8,128)S(1)}, f32[64,256]{1,0:T(8,128)}, u32[]{:S(2)}) copy-start(f32[64,256]{1,0:T(8,128)} %slice.219.sin_ref) | copy-start | bytes 196612
  378.6 26.7 %copy-start.24 = (f32[256,1152]{1,0:T(8,128)S(1)}, f32[256,1152]{1,0:T(8,128)}, u32[]{:S(2)}) copy-start(f32[256,1152]{1,0:T(8,128)} %copy-done.23) | copy-start | bytes 3538948
  378.6 26.7 %copy-start.53 = (f32[256,256]{1,0:T(8,128)S(1)}, f32[256,256]{1,0:T(8,128)}, u32[]{:S(2)}) copy-start(f32[256,256]{1,0:T(8,128)} %copy-done.52) | copy-start | bytes 786436
  378.9 26.4 %copy-start.10 = (f32[256,1152]{1,0:T(8,128)S(1)}, f32[256,1152]{1,0:T(8,128)}, u32[]{:S(2)}) copy-start(f32[256,1152]{1,0:T(8,128)} %copy-done.9) | copy-start | bytes 3538948
  378.9 26.4 %copy-start.22 = (bf16[1152,512]{1,0:T(8,128)(2,1)S(1)}, bf16[1152,512]{1,0:T(8,128)(2,1)}, u32[]{:S(2)}) copy-start(bf16[1152,512]{1,0:T(8,128)(2,1)} %copy-done.21) | copy-start | bytes 3538948
  379.0 26.3 %collective-permute-start.36 = (bf16[4,64,512]{2,1,0:T(8,128)(2,1)S(1)}, bf16[4,64,512]{2,1,0:T(8,128)(2,1)S(1)}, u32[]{:S(2)}, u32[]{:S(2)}) collective-permute-start(bf16[4,64,512]{2,1,0:T(8,128)(2,1)S(1)} %fusion.5), channel_id=1, source_target_pairs={{4,0},{8,4},{12,8},{5,1},{9,5},{13,9},{6,2},{10,6},{14,10},{7,3},{... | collective-permute-start | bytes 786440 | tf_op jit(solution)/shard_map/ppermute | solution.py:24
  410.1 4.1 collective-permute-start.43
  413.6 1.9 collective-permute-start.40
  414.1 2.5 collective-permute-start.41
  418.1 34.3 %all-to-all-start.1 = ((bf16[4,146,1024]{2,1,0:T(8,128)(2,1)}), bf16[4,146,1024]{2,1,0:T(8,128)(2,1)S(1)}, u32[]{:S(2)}, u32[]{:S(2)}) async-start(bf16[4,146,1024]{2,1,0:T(8,128)(2,1)} %pad_maximum_fusion.1), calls=%async_computation.1 | async-start | bytes 2490368 | tf_op jit(solution)/shard_map/all_to_all | solution.py:28
  452.9 6.5 %collective-permute-start.44 = (bf16[147,512]{1,0:T(8,128)(2,1)S(1)}, bf16[147,512]{1,0:T(8,128)(2,1)S(1)}, u32[]{:S(2)}, u32[]{:S(2)}) collective-permute-start(bf16[147,512]{1,0:T(8,128)(2,1)S(1)} %pad_maximum_fusion.8), channel_id=1, source_target_pairs={{0,1},{1,0},{2,3},{3,2},{4,5},{5,4},{6,7},{7,6},{8,9},{9,8},{10,11... | collective-permute-start | bytes 451592 | tf_op jit(solution)/shard_map/ppermute | solution.py:19
  454.4 8.5 %collective-permute-start.45 = (bf16[147,512]{1,0:T(8,128)(2,1)S(1)}, bf16[147,512]{1,0:T(8,128)(2,1)S(1)}, u32[]{:S(2)}, u32[]{:S(2)}) collective-permute-start(bf16[147,512]{1,0:T(8,128)(2,1)S(1)} %pad_maximum_fusion.8), channel_id=1, source_target_pairs={{0,2},{1,3},{2,0},{3,1},{4,6},{5,7},{6,4},{7,5},{8,10},{9,11},{10,... | collective-permute-start | bytes 451592 | tf_op jit(solution)/shard_map/ppermute | solution.py:19
  454.5 8.5 %collective-permute-start.46 = (bf16[147,512]{1,0:T(8,128)(2,1)S(1)}, bf16[147,512]{1,0:T(8,128)(2,1)S(1)}, u32[]{:S(2)}, u32[]{:S(2)}) collective-permute-start(bf16[147,512]{1,0:T(8,128)(2,1)S(1)} %pad_maximum_fusion.8), channel_id=1, source_target_pairs={{0,3},{1,2},{2,1},{3,0},{4,7},{5,6},{6,5},{7,4},{8,11},{9,10},{10,... | collective-permute-start | bytes 451592 | tf_op jit(solution)/shard_map/ppermute | solution.py:19
  (91 other events, 592.8 us)
Sparse Core Ops, SparseCore 0:
  10.2 33.8 all-gather.2
  45.7 119.5 all-gather.4
  277.1 46.3 reduce-scatter.4
  325.9 86.1 reduce-scatter.2

commit v4 on v3

--- a/solution.py
+++ b/solution.py
@@ -276,15 +276,16 @@
     d_keys = t_mm(d_scores, rows)
     d_vals = t_mm(probs.astype(LOW), douts)
     per = kv_refs[0].shape[2]
+    own_ref, side_refs, middle_refs = dkv_refs[0], dkv_refs[1:chunks], dkv_refs[chunks:]
     for part, at in ((d_keys, 0), (d_vals, width)):
         piece = lambda b, p: part[(b * chunks + p) * per : (b * chunks + p + 1) * per]
         for b in range(blocks):
-            dkv_refs[0][b, 0, :, at : at + width] = piece(b, 0)
+            own_ref[b, 0, :, at : at + width] = piece(b, 0)
         for p in range(1, chunks):
             earlier = (place_ref[0] ^ p) < place_ref[0]
             for b in range(1, blocks - 1):
-                dkv_refs[p][b - 1, 0, :, at : at + width] = piece(b, p).astype(LOW)
-            dkv_refs[p][blocks - 2, 0, :, at : at + width] = jnp.where(earlier, piece(0, p), piece(blocks - 1, p)).astype(LOW)
+                middle_refs[p - 1][b - 1, 0, :, at : at + width] = piece(b, p).astype(LOW)
+            side_refs[p - 1][0, :, at : at + width] = jnp.where(earlier, piece(0, p), piece(blocks - 1, p)).astype(LOW)
     gain_sum = jnp.zeros((1, width), F32)
     for h, q in enumerate(heads_of(q_ref[...], heads)):
         e = d_rows[h * count : (h + 1) * count] * scale
@@ -311,7 +312,7 @@
         in_specs=[pl.BlockSpec((step, width), lambda j: (j, 0))] * len(arrays),
         out_specs=pl.BlockSpec((len(pairs), step, width), lambda j: (0, j, 0)),
         out_shape=struct((len(pairs), rows, width), LOW),
-        compiler_params=ROOM,
+        compiler_params=ALL,
         name="pair_sum",
     )(*arrays)
 
@@ -492,7 +493,7 @@
 def weight_grad_kernel(chunks, sets, core_ref, *refs):
     lefts, refs = refs[:chunks], refs[chunks:]
     rights, refs = refs[: chunks * sets], refs[chunks * sets :]
-    outs, (turned, sums) = refs[: 2 * sets], refs[2 * sets :]
+    outs, turned = refs[: 2 * sets], refs[2 * sets]
     rows = lefts[0].shape[0]
     half = outs[0].shape[0]
 
@@ -504,13 +505,13 @@
     core = core_ref[0]
     for i in range(sets):
         right = jnp.concatenate([r[...] for r in rights[i * chunks : (i + 1) * chunks]], axis=0)
-        sums[i] = mm(turned[...], right)
         for place, out in ((1 - core, outs[2 * i]), (core, outs[2 * i + 1])):
-            out[...] = sums[i, pl.ds(pl.multiple_of(place * half, half), half), :].astype(LOW)
-
-
-def weight_grad(core, rows, lefts, *rights, step=256):
+            out[...] = mm(turned[pl.ds(pl.multiple_of(place * half, half), half), :], right).astype(LOW)
+
+
+def weight_grad(core, rows, lefts, *rights):
     chunks, sets = len(lefts), len(rights)
+    step = 896 if sets == 1 and rights[0][0][0].shape[1] > 1024 else 256
     height = lefts[0][0].shape[1]
     width = rights[0][0][0].shape[1]
     rights = [pair for group in rights for pair in group]
@@ -523,9 +524,9 @@
         + [pl.BlockSpec((rows, step), lambda j, at=at: (at, j)) for _, at in rights],
         out_specs=[out] * (2 * sets),
         out_shape=[struct((height // 2, width), LOW)] * (2 * sets),
-        scratch_shapes=[pltpu.VMEM((height, chunks * rows), LOW), pltpu.VMEM((sets, height, step), F32)],
-        compiler_params=ALL if chunks > 1 else ROOM,
-        cost_estimate=cost(sets * chunks * rows * height * width, *[v for v, _ in lefts], struct((height, sets * width), LOW)),
+        scratch_shapes=[pltpu.VMEM((height, chunks * rows), LOW)],
+        compiler_params=ALL,
+        cost_estimate=None if width < height else cost(sets * chunks * rows * height * width, *[v for v, _ in lefts], struct((height, sets * width), LOW)),
         name="weight_grad",
     )(core.reshape(1), *[v for v, _ in lefts], *[v for v, _ in rights])
     return [flat[2 * i : 2 * i + 2] for i in range(sets)]
@@ -630,7 +631,7 @@
         loss_kernel,
         in_specs=[SMEM] + [VMEM] * (4 + T),
         out_shape=[token_low, token, token_low, gain_row, struct((1, 128), F32)],
-        compiler_params=ROOM,
+        compiler_params=ALL,
         cost_estimate=cost(own, *parts, *parts),
         name="loss",
     )((all_tokens / count).reshape(1), hidden, target_own, valid_own, g_post_ffn, *from_tp(parts))
@@ -664,7 +665,7 @@
     d_hidden, d_branch, d_attended, dg_pre_ffn, dg_post_attn = pl.pallas_call(
         middle_kernel,
         out_shape=[token, token_low, struct((own, wide), LOW), gain_row, gain_row],
-        compiler_params=ROOM,
+        compiler_params=ALL,
         cost_estimate=cost(300 * own * wide * width_model, out_full),
         name="middle",
     )(d_result, hidden, branch, out_full, g_pre_ffn, g_post_attn, *parts)
@@ -682,9 +683,12 @@
         grid=(seqs,),
         in_specs=[SMEM] + [specs[k] for k in ("qinfo", "kinfo", "q", "gain", "table", "table", "q", "lse", "q")] + kv_specs,
         out_specs=[specs["q"], specs["dgain"]]
-        + [pl.BlockSpec((halo + (p == 0), 1, sub, 2 * head_width), lambda s: (0, s, 0, 0)) for p in range(T)],
-        out_shape=[struct((own, wide), LOW), struct((seqs, 1, head_width), F32)]
-        + [struct((halo + (p == 0), seqs, sub, 2 * head_width), F32 if p == 0 else LOW) for p in range(T)],
+        + [pl.BlockSpec((halo + 1, 1, sub, 2 * head_width), lambda s: (0, s, 0, 0))]
+        + [specs["far"]] * (T - 1)
+        + [pl.BlockSpec((halo - 1, 1, sub, 2 * head_width), lambda s: (0, s, 0, 0))] * (T - 1),
+        out_shape=[struct((own, wide), LOW), struct((seqs, 1, head_width), F32), struct((halo + 1, seqs, sub, 2 * head_width), F32)]
+        + [struct((seqs, sub, 2 * head_width), LOW)] * (T - 1)
+        + [struct((halo - 1, seqs, sub, 2 * head_width), LOW)] * (T - 1),
         compiler_params=ALL,
         name="attend_back",
     )(t.reshape(1), qinfo, kinfo, q_raw, g_query, cos_own, sin_own, q_rot, lse, d_attended, *kv_rows)
@@ -692,17 +696,19 @@
     d_blocks = [d_own[b] for b in range(halo + 1)]
     for p in range(1, T):
         got = swap(d_pairs[p], "tp", p).astype(F32)
+        later = (t ^ p) > t
+        d_blocks[0] = d_blocks[0] + jnp.where(later, got, 0.0)
+        d_blocks[halo] = d_blocks[halo] + jnp.where(later, 0.0, got)
+    d_kv = d_blocks[halo].astype(LOW)
+    for p in range(1, T):
+        middle = swap(after(d_pairs[T - 1 + p], d_kv), "tp", p)
         for b in range(1, halo):
-            d_blocks[b] = d_blocks[b] + got[b - 1]
-        later = (t ^ p) > t
-        d_blocks[0] = d_blocks[0] + jnp.where(later, got[halo - 1], 0.0)
-        d_blocks[halo] = d_blocks[halo] + jnp.where(later, 0.0, got[halo - 1])
-    d_kv = d_blocks[halo]
-    d_query_late, out_low = after(d_query, d_kv.astype(LOW)), after(out_low, d_kv.astype(LOW))
+            d_blocks[b] = d_blocks[b] + middle[b - 1].astype(F32)
+    d_query_late, out_low = after(d_query, middle), after(out_low, middle)
     for d in range(halo, 0, -1):
-        come = shifted(d_kv.astype(LOW), "ctx", -1)
+        come = shifted(d_kv, "ctx", -1)
         if d > 1:
-            d_kv = d_blocks[d - 1] + come.astype(F32)
+            d_kv = (d_blocks[d - 1] + come.astype(F32)).astype(LOW)
     d_kv = [d_blocks[0], come]
     head = lambda v, p: v[:, p * head_width : (p + 1) * head_width]
     heads_sent = [jnp.concatenate([head(d_query_late, p), head(out_low, p)], axis=0) for p in range(1, T)]
@@ -757,7 +763,7 @@
     grad_query, grad_out = sums[:, :head_width], sums[:, head_width : 2 * head_width]
     grad_kv = sums[:, 2 * head_width :]
     low = jnp.concatenate([grad_kv.astype(LOW), pack(total[None], 2 * head_width)[0]], axis=0)
-    low = lax.optimization_barrier(low)
+    low, grad_gate, grad_up, grad_down = lax.optimization_barrier((low, grad_gate, grad_up, grad_down))
     totals = {p: (swap(low, "tp", p) if p else low).astype(F32) for p in range(T)}
     bit = 1
     while bit < T:

time: 483 us -> 468 us (0.969)
  waiting for transfers between devices: 182 us -> 159 us
  Pallas kernels: 132 us -> 142 us
  local copies, waits for them, and re-layouts: 57.9 us -> 51.1 us
    ppermute x4, waiting for transfers between devices: 52.8 us -> 37.2 us  [shifted(): lax.ppermute(values, axis, [(i, i + by) for i in range(size) if 0 <= i +...]
    unnamed x210 -> x164, local copies, waits for them, and re-layouts: 35.2 us -> 23.1 us
    ppermute x43 -> x46, waiting for transfers between devices: 87.3 us -> 80.7 us  [swap(): lax.ppermute(values, axis, [(i, i ^ bits) for i in range(lax.axis_size(ax...]
    pallas_call x2, Pallas kernels: 3.94 us -> 10.3 us  [pair_sum(): pl.pallas_call(pair_sum_kernel, grid=(rows // step,), in_specs=[pl.BlockS...]
    ppermute x43 -> x46, starting transfers between devices: 38.2 us -> 41.4 us  [swap(): lax.ppermute(values, axis, [(i, i ^ bits) for i in range(lax.axis_size(ax...]
  transfers between devices with their start and end apart: 53 -> 56, of which waited for: 24 -> 26; matrix products, arithmetic and copies ran while one was open for 10% -> 11% of each run, Pallas kernels for 22% -> 24%
where the time goes in v4:
time: 468 us; the launch traced here: 463 us
  waiting for transfers between devices  159 us (34%)
  Pallas kernels  142 us (30%)
  starting transfers between devices  63.3 us (14%)
  local copies, waits for them, and re-layouts  51.1 us (11%)
  other arithmetic  27.3 us (6%)
  between operations  18.3 us (4%)
    ppermute x46, waiting for transfers between devices, swap(): lax.ppermute(values, axis, [(i, i ^ bits) for i in range(lax.axis_size(ax...  80.7 us
    pallas_call x6, Pallas kernels, ffn_call(): pl.pallas_call(functools.partial(kernel, units, chunks), grid=(pl.cdiv(un...  65 us
    ppermute x46, starting transfers between devices, swap(): lax.ppermute(values, axis, [(i, i ^ bits) for i in range(lax.axis_size(ax...  41.4 us
    ppermute x4, waiting for transfers between devices, shifted(): lax.ppermute(values, axis, [(i, i + by) for i in range(size) if 0 <= i +...  37.2 us
    pallas_call x4, Pallas kernels, weight_grad(): pl.pallas_call(functools.partial(weight_grad_kernel, chunks, sets), grid=...  32.1 us
    all_to_all x2, waiting for transfers between devices, exchange(): return lax.all_to_all(values, axes, 0, 0, tiled=True)  27.7 us
    unnamed x164, local copies, waits for them, and re-layouts  23.1 us
    all_to_all x2, starting transfers between devices, exchange(): return lax.all_to_all(values, axes, 0, 0, tiled=True)  11.7 us
  transfers between devices with their start and end apart: 56, of which 26 were waited for; matrix products, arithmetic and copies ran while one was open for 11% of the time, Pallas kernels for 24%

profile of v4, /device:TPU:0, one launch (start us, length us, event | category | flops | bytes accessed | tf_op | source)
XLA Modules:
  0.0 463.2 jit_solution(3265624839999207204)
XLA Ops:
  9.4 2.4 pad_maximum_fusion
  14.0 6.3 %all-to-all-start = ((bf16[8,2,832]{2,1,0:T(2,128)(2,1)}), bf16[8,2,832]{2,1,0:T(2,128)(2,1)S(1)}, u32[]{:S(2)}, u32[]{:S(2)}) async-start(bf16[8,2,832]{2,1,0:T(2,128)(2,1)} %reshape.303), calls=%async_computation | async-start | bytes 57344 | tf_op jit(solution)/shard_map/all_to_all | solution.py:28
  35.5 1.7 copy-done.11
  40.4 3.8 all-gather.3.cloned.1.call-done
  45.7 2.4 collective-permute-start.2
  51.9 2.8 project_keys.1
  57.4 3.2 collective-permute-start.8
  60.6 2.3 collective-permute-done.2.refs_3_
  63.0 12.1 %collective-permute-done.1.refs_2_ = bf16[576,512]{1,0:T(8,128)(2,1)} collective-permute-done((bf16[576,512]{1,0:T(8,128)(2,1)S(1)}, bf16[576,512]{1,0:T(8,128)(2,1)}, u32[]{:S(2)}, u32[]{:S(2)}) %collective-permute-start.1) | collective-permute-done | bytes 589856 | tf_op jit(solution)/shard_map/ppermute | solution.py:19
  75.7 4.1 collective-permute-start.12
  79.7 11.3 %collective-permute-done.12.refs_5_ = bf16[4,64,512]{2,1,0:T(8,128)(2,1)} collective-permute-done((bf16[4,64,512]{2,1,0:T(8,128)(2,1)}, bf16[4,64,512]{2,1,0:T(8,128)(2,1)}, u32[]{:S(2)}, u32[]{:S(2)}) %collective-permute-start.12) | collective-permute-done | bytes 262176 | tf_op jit(solution)/shard_map/ppermute | solution.py:24
  91.1 1.5 collective-permute-start.10
  96.0 1.5 collective-permute-start.13
  98.8 2.8 assemble.1
  101.6 4.5 collective-permute-done.10.refs_3_
  106.0 1.6 collective-permute-start.15
  107.7 2.0 fusion.29.q_ref
  109.8 4.9 %collective-permute-done.13.refs_6_ = bf16[4,64,512]{2,1,0:T(8,128)(2,1)S(1)} collective-permute-done((bf16[4,64,512]{2,1,0:T(8,128)(2,1)}, bf16[4,64,512]{2,1,0:T(8,128)(2,1)S(1)}, u32[]{:S(2)}, u32[]{:S(2)}) %collective-permute-start.13) | collective-permute-done | bytes 262176 | tf_op jit(solution)/shard_map/ppermute | solution.py:19
  114.7 4.2 collective-permute-done.15.refs_8_
  119.0 4.9 %attend.1 = (bf16[256,1024]{1,0:T(8,128)(2,1)S(1)}, bf16[256,1024]{1,0:T(8,128)(2,1)S(1)}, f32[4,256,1]{2,1,0:T(8,128)S(1)}) custom-call(s32[4,64,2]{2,1,0:T(8,128)S(1)} %copy-done.21, s32[4,2,768]{2,1,0:T(2,128)S(1)} %copy-done.42, f32[256,1024]{1,0:T(8,128)S(1)} %fusion.29.q_ref, f32[1,256]{1,0:T(1,128)S(1)} %copy-done.47, f32[64,256]{1,0:T(8,128)S(1)} %copy-done.22, ...), custom_call_target="tpu_custom_call" | custom-call | flops 402653184 | bytes 4194304 | tf_op jit(solution)/shard_map/attend/pallas_call | solution.py:604
  129.4 1.5 collective-permute-start.19
  132.3 22.3 %collective-permute-done.18.refs_0_.refs_2_ = bf16[256,1152]{1,0:T(8,128)(2,1)S(1)} collective-permute-done((bf16[256,1152]{1,0:T(8,128)(2,1)S(1)}, bf16[256,1152]{1,0:T(8,128)(2,1)S(1)}, u32[]{:S(2)}, u32[]{:S(2)}) %collective-permute-start.18) | collective-permute-done | bytes 589856 | tf_op jit(solution)/shard_map/ppermute | solution.py:19
  155.5 9.9 %all-gather.5.cloned.1.call-done.refs_1_.refs_2_.refs_3_.refs_4_ = bf16[3,1152,1728]{2,1,0:T(8,128)(2,1)} async-done(((bf16[3,144,1728]{2,1,0:T(8,128)(2,1)}), bf16[3,1152,1728]{2,1,0:T(8,128)(2,1)}) %all-gather.5.cloned.1.call-update) | async-done | bytes 11943952 | tf_op jit(solution)/shard_map/all_gather | solution.py:553
  165.4 13.1 %ffn.5 = (bf16[256,1152]{1,0:T(8,128)(2,1)}, bf16[256,1152]{1,0:T(8,128)(2,1)}, bf16[512,1728]{1,0:T(8,128)(2,1)}, bf16[512,1728]{1,0:T(8,128)(2,1)}, bf16[512,1728]{1,0:T(8,128)(2,1)}) custom-call(bf16[256,1152]{1,0:T(8,128)(2,1)} %copy-done.57, bf16[256,1152]{1,0:T(8,128)(2,1)} %collective-permute-done.19.refs_1_.refs_3_, ...), custom_call_target="tpu_custom_call" | custom-call | flops 6115295232 | bytes 13123584 | tf_op jit(solution)/shard_map/ffn/pallas_call | solution.py:419
  178.5 1.8 collective-permute-start.20
  181.7 9.1 %ffn.4 = (bf16[256,1152]{1,0:T(8,128)(2,1)}, bf16[256,1728]{1,0:T(8,128)(2,1)}, bf16[256,1728]{1,0:T(8,128)(2,1)}, bf16[256,1728]{1,0:T(8,128)(2,1)}) custom-call(bf16[256,1152]{1,0:T(8,128)(2,1)} %collective-permute-done.16.refs_0_.refs_1_, bf16[3,1152,1728]{2,1,0:T(8,128)(2,1)} %all-gather.5.cloned.1.call-done.refs_1_.refs_2_.refs_3_.refs_4_, ...), custom_call_target="tpu_custom_call" | custom-call | flops 3057647616 | bytes 12533760 | tf_op jit(solution)/shard_map/ffn/pallas_call | solution.py:419
  194.1 9.4 %ffn.3 = (f32[256,1152]{1,0:T(8,128)}, bf16[256,1728]{1,0:T(8,128)(2,1)}, bf16[256,1728]{1,0:T(8,128)(2,1)}, bf16[256,1728]{1,0:T(8,128)(2,1)}) custom-call(bf16[256,1152]{1,0:T(8,128)(2,1)} %copy-done.33, bf16[3,1152,1728]{2,1,0:T(8,128)(2,1)} %all-gather.5.cloned.1.call-done.refs_1_.refs_2_.refs_3_.refs_4_, ...), custom_call_target="tpu_custom_call" | custom-call | flops 3057647616 | bytes 12533760 | tf_op jit(solution)/shard_map/ffn/pallas_call | solution.py:419
  203.6 3.2 collective-permute-done.20.refs_2_
  208.7 4.6 loss.1
  213.3 1.5 collective-permute-start.23
  214.8 1.5 collective-permute-start.22
  216.8 9.3 %ffn_back.3 = (f32[256,1152]{1,0:T(8,128)}, bf16[256,1728]{1,0:T(8,128)(2,1)}, bf16[256,1728]{1,0:T(8,128)(2,1)}) custom-call(bf16[256,1152]{1,0:T(8,128)(2,1)} %get-tuple-element.170.refs_0_, bf16[3,1152,1728]{2,1,0:T(8,128)(2,1)} %all-gather.5.cloned.1.call-done.refs_1_.refs_2_.refs_3_.refs_4_, ...), custom_call_target="tpu_custom_call" | custom-call | flops 3057647616 | bytes 14303232 | tf_op jit(solution)/shard_map/ffn_back/pallas_call | solution.py:419
  226.1 3.7 collective-permute-done.23.refs_0_.refs_1_
  230.6 9.1 %ffn_back.4 = (bf16[256,1152]{1,0:T(8,128)(2,1)}, bf16[256,1728]{1,0:T(8,128)(2,1)}, bf16[256,1728]{1,0:T(8,128)(2,1)}) custom-call(bf16[256,1152]{1,0:T(8,128)(2,1)} %copy-done.58, bf16[3,1152,1728]{2,1,0:T(8,128)(2,1)} %all-gather.5.cloned.1.call-done.refs_1_.refs_2_.refs_3_.refs_4_, ...), custom_call_target="tpu_custom_call" | custom-call | flops 3057647616 | bytes 14303232 | tf_op jit(solution)/shard_map/ffn_back/pallas_call | solution.py:419
  239.7 1.8 collective-permute-done.22.refs_0_.refs_2_
  242.5 15.0 %ffn_back.5 = (bf16[256,1152]{1,0:T(8,128)(2,1)}, bf16[256,1152]{1,0:T(8,128)(2,1)}, bf16[512,1728]{1,0:T(8,128)(2,1)}, bf16[512,1728]{1,0:T(8,128)(2,1)}) custom-call(bf16[256,1152]{1,0:T(8,128)(2,1)} %copy-done.59, bf16[256,1152]{1,0:T(8,128)(2,1)} %copy-done.60, bf16[3,1152,1728]{2,1,0:T(8,128)(2,1)} %all-gather.5.cloned.1.call-done.refs_1_.refs_2_.refs_3_.refs_4_, ...), custom_call_target="tpu_custom_call" | custom-call | flops 6115295232 | bytes 16662528 | tf_op jit(solution)/shard_map/ffn_back/pallas_call | solution.py:419
  257.5 9.4 %weight_grad.4 = (bf16[576,1728]{1,0:T(8,128)(2,1)}, bf16[576,1728]{1,0:T(8,128)(2,1)}) custom-call(s32[1]{0:T(128)} %bitcast.8.core_ref, bf16[256,1152]{1,0:T(8,128)(2,1)} %get-tuple-element.170.refs_0_, bf16[256,1152]{1,0:T(8,128)(2,1)} %copy-done.58, bf16[256,1152]{1,0:T(8,128)(2,1)} %copy-done.59, bf16[256,1152]{1,0:T(8,128)(2,1)} %copy-done.60, ...), custom_call_target="tpu_custom_call" | custom-call | flops 4076863488 | bytes 6340608 | tf_op jit(solution)/shard_map/weight_grad/pallas_call | solution.py:519
  266.9 1.5 collective-permute-start.28
  268.4 1.5 collective-permute-start.26
  272.5 4.4 pair_sum.2
  277.0 14.1 %weight_grad.5 = (bf16[576,1728]{1,0:T(8,128)(2,1)}, bf16[576,1728]{1,0:T(8,128)(2,1)}, bf16[576,1728]{1,0:T(8,128)(2,1)}, bf16[576,1728]{1,0:T(8,128)(2,1)}) custom-call(s32[1]{0:T(128)} %bitcast.8.core_ref, bf16[256,1152]{1,0:T(8,128)(2,1)} %copy-done.33, bf16[256,1152]{1,0:T(8,128)(2,1)} %collective-permute-done.16.refs_0_.refs_1_, ...), custom_call_target="tpu_custom_call" | custom-call | flops 8153726976 | bytes 10321920 | tf_op jit(solution)/shard_map/weight_grad/pallas_call | solution.py:519
  291.1 5.4 %collective-permute-done.27.refs_2_ = bf16[256,1152]{1,0:T(8,128)(2,1)} collective-permute-done((bf16[256,1152]{1,0:T(8,128)(2,1)}, bf16[256,1152]{1,0:T(8,128)(2,1)}, u32[]{:S(2)}, u32[]{:S(2)}) %collective-permute-start.27) | collective-permute-done | bytes 589856 | tf_op jit(solution)/shard_map/ppermute | solution.py:19
  297.1 6.5 %middle.1 = (f32[256,1152]{1,0:T(8,128)}, bf16[256,1152]{1,0:T(8,128)(2,1)}, bf16[256,1024]{1,0:T(8,128)(2,1)}, f32[1,1152]{1,0:T(1,128)}, f32[1,1152]{1,0:T(1,128)}) custom-call(f32[256,1152]{1,0:T(8,128)} %get-tuple-element.156.dres_ref, f32[256,1152]{1,0:T(8,128)} %copy-done.20, f32[256,1152]{1,0:T(8,128)} %copy-done.50, bf16[1152,1024]{1,0:T(8,128)(2,1)} %bitcast.85, ...), custom_call_target="tpu_custom_call" | custom-call | flops 181193932800 | bytes 2359296 | tf_op jit(solution)/shard_map/middle/pallas_call | solution.py:665
  304.0 5.9 %pair_sum.3 = bf16[2,576,1728]{2,1,0:T(8,128)(2,1)} custom-call(bf16[576,1728]{1,0:T(8,128)(2,1)} %get-tuple-element.184.refs_0_, bf16[576,1728]{1,0:T(8,128)(2,1)} %collective-permute-done.29.refs_1_, bf16[576,1728]{1,0:T(8,128)(2,1)} %get-tuple-element.186.refs_2_, bf16[576,1728]{1,0:T(8,128)(2,1)} %collective-permute-done.30.refs_3_), custom_call_target="tpu_custom_call" | custom-call | tf_op jit(solution)/shard_map/pair_sum/pallas_call | solution.py:309
  309.9 4.6 weight_grad.6
  314.7 7.2 %attend_back.1 = (bf16[256,1024]{1,0:T(8,128)(2,1)}, f32[4,1,256]{2,1,0:T(1,128)}, f32[3,4,64,512]{3,2,1,0:T(8,128)}, bf16[4,64,512]{2,1,0:T(8,128)(2,1)}, bf16[...) custom-call(s32[1]{0:T(128)} %bitcast.4.place_ref, ...), custom_call_target="tpu_custom_call" | custom-call | tf_op jit(solution)/shard_map/attend_back/pallas_call | solution.py:681
  325.4 2.4 convert_add_fusion
  327.8 3.5 collective-permute-done.32
  331.3 4.5 collective-permute-done.33
  338.3 1.8 collective-permute-start.37
  347.2 1.6 slice.158.refs_4_
  354.7 11.9 %collective-permute-done.38 = bf16[4,64,512]{2,1,0:T(8,128)(2,1)} collective-permute-done((bf16[4,64,512]{2,1,0:T(8,128)(2,1)}, bf16[4,64,512]{2,1,0:T(8,128)(2,1)}, u32[]{:S(2)}, u32[]{:S(2)}) %collective-permute-start.38) | collective-permute-done | bytes 262176 | tf_op jit(solution)/shard_map/ppermute | solution.py:24
  366.6 1.6 fusion.10
  368.2 1.5 collective-permute-start.39
  375.8 13.9 %collective-permute-done.39 = bf16[4,64,512]{2,1,0:T(8,128)(2,1)S(1)} collective-permute-done((bf16[4,64,512]{2,1,0:T(8,128)(2,1)S(1)}, bf16[4,64,512]{2,1,0:T(8,128)(2,1)S(1)}, u32[]{:S(2)}, u32[]{:S(2)}) %collective-permute-start.39) | collective-permute-done | bytes 262176 | tf_op jit(solution)/shard_map/ppermute | solution.py:24
  389.9 2.5 finish.1
  396.8 4.0 weight_grad.7
  401.1 1.5 fusion.2
  404.3 5.4 %all-to-all-start.1 = ((bf16[4,146,1024]{2,1,0:T(8,128)(2,1)}), bf16[4,146,1024]{2,1,0:T(8,128)(2,1)S(1)}, u32[]{:S(2)}, u32[]{:S(2)}) async-start(bf16[4,146,1024]{2,1,0:T(8,128)(2,1)} %pad_maximum_fusion.1), calls=%async_computation.1 | async-start | bytes 2490368 | tf_op jit(solution)/shard_map/all_to_all | solution.py:28
  410.3 2.1 bitcast_convert_fusion
  412.4 27.7 %all-to-all-done.1 = bf16[4,146,1024]{2,1,0:T(8,128)(2,1)S(1)} async-done(((bf16[4,146,1024]{2,1,0:T(8,128)(2,1)}), bf16[4,146,1024]{2,1,0:T(8,128)(2,1)S(1)}, u32[]{:S(2)}, u32[]{:S(2)}) %all-to-all-start.1) | async-done | bytes 1196064 | tf_op jit(solution)/shard_map/all_to_all | solution.py:28
  444.6 2.3 collective-permute-start.49
  447.6 2.6 collective-permute-done.47
  450.2 1.8 collective-permute-done.48
  (342 shorter events, 95.1 us)
Async XLA Ops:
  7.2 184.7 %copy-start = (bf16[4,256,1152]{2,1,0:T(8,128)(2,1)S(1)}, bf16[4,256,1152]{2,1,0:T(8,128)(2,1)}, u32[]{:S(2)}) copy-start(bf16[4,256,1152]{2,1,0:T(8,128)(2,1)} %param.17) | copy-start | bytes 7077892
  7.2 36.9 %all-gather.3.cloned.1.call-start = ((), (), s32[]{:S(2)}) async-start(), calls=%async_computation.4 | async-start | bytes 1474560 | tf_op jit(solution)/shard_map/all_gather | solution.py:552
  9.2 156.2 %all-gather.5.cloned.1.call-start = ((), (), s32[]{:S(2)}) async-start(), calls=%async_computation.5 | async-start | bytes 13934592 | tf_op jit(solution)/shard_map/all_gather | solution.py:553
  14.0 12.8 %all-to-all-start = ((bf16[8,2,832]{2,1,0:T(2,128)(2,1)}), bf16[8,2,832]{2,1,0:T(2,128)(2,1)S(1)}, u32[]{:S(2)}, u32[]{:S(2)}) async-start(bf16[8,2,832]{2,1,0:T(2,128)(2,1)} %reshape.303), calls=%async_computation | async-start | bytes 57344 | tf_op jit(solution)/shard_map/all_to_all | solution.py:28
  20.4 390.0 %reduce-scatter.5.cloned.1.call-start = ((), (), s32[]{:S(2)}) async-start(), calls=%async_computation.7 | async-start | bytes 2580480 | tf_op jit(solution)/shard_map/reduce_scatter | solution.py:644
  32.1 93.5 %copy-start.45 = (f32[1,1152]{1,0:T(1,128)}, f32[1,1152]{1,0:T(1,128)S(1)}, u32[]{:S(2)}) copy-start(f32[1,1152]{1,0:T(1,128)S(1)} %reshape.252.gain_attn_ref) | copy-start | bytes 13828
  32.9 92.7 %copy-start.46 = (f32[1,1152]{1,0:T(1,128)}, f32[1,1152]{1,0:T(1,128)S(1)}, u32[]{:S(2)}) copy-start(f32[1,1152]{1,0:T(1,128)S(1)} %reshape.253.gain_ffn_ref) | copy-start | bytes 13828
  45.6 3.6 collective-permute-start.3
  45.7 17.2 %collective-permute-start.2 = (bf16[576,512]{1,0:T(8,128)(2,1)S(1)}, bf16[576,512]{1,0:T(8,128)(2,1)}, u32[]{:S(2)}, u32[]{:S(2)}) collective-permute-start(bf16[576,512]{1,0:T(8,128)(2,1)S(1)} %get-tuple-element.133.refs_0_), channel_id=1, source_target_pairs={{0,3},{1,2},{2,1},{3,0},{4,7},{5,6},{6,5},{7,4},{8,11},{9,10},{10,... | collective-permute-start | bytes 1769480 | tf_op jit(solution)/shard_map/ppermute | solution.py:19
  48.1 27.0 %collective-permute-start.1 = (bf16[576,512]{1,0:T(8,128)(2,1)S(1)}, bf16[576,512]{1,0:T(8,128)(2,1)}, u32[]{:S(2)}, u32[]{:S(2)}) collective-permute-start(bf16[576,512]{1,0:T(8,128)(2,1)S(1)} %get-tuple-element.133.refs_0_), channel_id=1, source_target_pairs={{0,2},{1,3},{2,0},{3,1},{4,6},{5,7},{6,4},{7,5},{8,10},{9,11},{10,... | collective-permute-start | bytes 1769480 | tf_op jit(solution)/shard_map/ppermute | solution.py:19
  48.7 26.4 %collective-permute-start = (bf16[576,512]{1,0:T(8,128)(2,1)S(1)}, bf16[576,512]{1,0:T(8,128)(2,1)}, u32[]{:S(2)}, u32[]{:S(2)}) collective-permute-start(bf16[576,512]{1,0:T(8,128)(2,1)S(1)} %get-tuple-element.133.refs_0_), channel_id=1, source_target_pairs={{0,1},{1,0},{2,3},{3,2},{4,5},{5,4},{6,7},{7,6},{8,9},{9,8},{10,11... | collective-permute-start | bytes 1769480 | tf_op jit(solution)/shard_map/ppermute | solution.py:19
  57.4 18.3 %collective-permute-start.8 = (bf16[4,64,512]{2,1,0:T(8,128)(2,1)S(1)}, bf16[4,64,512]{2,1,0:T(8,128)(2,1)}, u32[]{:S(2)}, u32[]{:S(2)}) collective-permute-start(bf16[4,64,512]{2,1,0:T(8,128)(2,1)S(1)} %get-tuple-element.132), channel_id=1, source_target_pairs={{0,4},{4,8},{8,12},{1,5},{5,9},{9,13},{2,6},{6,10},{10,14},{3,7},{... | collective-permute-start | bytes 786440 | tf_op jit(solution)/shard_map/ppermute | solution.py:24
  62.9 31.1 %collective-permute-start.7 = (bf16[576,512]{1,0:T(8,128)(2,1)}, bf16[576,512]{1,0:T(8,128)(2,1)}, u32[]{:S(2)}, u32[]{:S(2)}) collective-permute-start(bf16[576,512]{1,0:T(8,128)(2,1)} %collective-permute-done.2.refs_3_), channel_id=1, source_target_pairs={{0,16},{16,0},{1,17},{17,1},{2,18},{18,2},{3,19},{19,3},{4,20},{20... | collective-permute-start | bytes 1769480 | tf_op jit(solution)/shard_map/ppermute | solution.py:19
  75.1 20.4 %collective-permute-start.6 = (bf16[576,512]{1,0:T(8,128)(2,1)}, bf16[576,512]{1,0:T(8,128)(2,1)}, u32[]{:S(2)}, u32[]{:S(2)}) collective-permute-start(bf16[576,512]{1,0:T(8,128)(2,1)} %collective-permute-done.1.refs_2_), channel_id=1, source_target_pairs={{0,16},{16,0},{1,17},{17,1},{2,18},{18,2},{3,19},{19,3},{4,20},{20... | collective-permute-start | bytes 1769480 | tf_op jit(solution)/shard_map/ppermute | solution.py:19
  75.1 20.9 %collective-permute-start.5 = (bf16[576,512]{1,0:T(8,128)(2,1)}, bf16[576,512]{1,0:T(8,128)(2,1)}, u32[]{:S(2)}, u32[]{:S(2)}) collective-permute-start(bf16[576,512]{1,0:T(8,128)(2,1)} %collective-permute-done.refs_1_), channel_id=1, source_target_pairs={{0,16},{16,0},{1,17},{17,1},{2,18},{18,2},{3,19},{19,3},{4,20},{20... | collective-permute-start | bytes 1769480 | tf_op jit(solution)/shard_map/ppermute | solution.py:19
  75.6 21.9 %collective-permute-start.4 = (bf16[576,512]{1,0:T(8,128)(2,1)S(1)}, bf16[576,512]{1,0:T(8,128)(2,1)}, u32[]{:S(2)}, u32[]{:S(2)}) collective-permute-start(bf16[576,512]{1,0:T(8,128)(2,1)S(1)} %get-tuple-element.133.refs_0_), channel_id=1, source_target_pairs={{0,16},{16,0},{1,17},{17,1},{2,18},{18,2},{3,19},{19,3},{4,20},{20... | collective-permute-start | bytes 1769480 | tf_op jit(solution)/shard_map/ppermute | solution.py:19
  75.7 15.4 %collective-permute-start.12 = (bf16[4,64,512]{2,1,0:T(8,128)(2,1)}, bf16[4,64,512]{2,1,0:T(8,128)(2,1)}, u32[]{:S(2)}, u32[]{:S(2)}) collective-permute-start(bf16[4,64,512]{2,1,0:T(8,128)(2,1)} %collective-permute-done.8.refs_1_), channel_id=1, source_target_pairs={{0,4},{4,8},{8,12},{1,5},{5,9},{9,13},{2,6},{6,10},{10,14},{3,7},{... | collective-permute-start | bytes 786440 | tf_op jit(solution)/shard_map/ppermute | solution.py:24
  91.1 15.0 %collective-permute-start.10 = (bf16[4,64,512]{2,1,0:T(8,128)(2,1)}, bf16[4,64,512]{2,1,0:T(8,128)(2,1)}, u32[]{:S(2)}, u32[]{:S(2)}) collective-permute-start(bf16[4,64,512]{2,1,0:T(8,128)(2,1)} %collective-permute-done.8.refs_1_), channel_id=1, source_target_pairs={{0,2},{1,3},{2,0},{3,1},{4,6},{5,7},{6,4},{7,5},{8,10},{9,11},{10,... | collective-permute-start | bytes 786440 | tf_op jit(solution)/shard_map/ppermute | solution.py:19
  94.0 15.7 %collective-permute-start.11 = (bf16[4,64,512]{2,1,0:T(8,128)(2,1)}, bf16[4,64,512]{2,1,0:T(8,128)(2,1)S(1)}, u32[]{:S(2)}, u32[]{:S(2)}) collective-permute-start(bf16[4,64,512]{2,1,0:T(8,128)(2,1)} %collective-permute-done.8.refs_1_), channel_id=1, source_target_pairs={{0,3},{1,2},{2,1},{3,0},{4,7},{5,6},{6,5},{7,4},{8,11},{9,10},{10,... | collective-permute-start | bytes 786440 | tf_op jit(solution)/shard_map/ppermute | solution.py:19
  95.5 14.3 %collective-permute-start.9 = (bf16[4,64,512]{2,1,0:T(8,128)(2,1)}, bf16[4,64,512]{2,1,0:T(8,128)(2,1)S(1)}, u32[]{:S(2)}, u32[]{:S(2)}) collective-permute-start(bf16[4,64,512]{2,1,0:T(8,128)(2,1)} %collective-permute-done.8.refs_1_), channel_id=1, source_target_pairs={{0,1},{1,0},{2,3},{3,2},{4,5},{5,4},{6,7},{7,6},{8,9},{9,8},{10,11... | collective-permute-start | bytes 786440 | tf_op jit(solution)/shard_map/ppermute | solution.py:19
  96.0 18.7 %collective-permute-start.13 = (bf16[4,64,512]{2,1,0:T(8,128)(2,1)}, bf16[4,64,512]{2,1,0:T(8,128)(2,1)S(1)}, u32[]{:S(2)}, u32[]{:S(2)}) collective-permute-start(bf16[4,64,512]{2,1,0:T(8,128)(2,1)} %collective-permute-done.12.refs_5_), channel_id=1, source_target_pairs={{0,1},{1,0},{2,3},{3,2},{4,5},{5,4},{6,7},{7,6},{8,9},{9,8},{10,11... | collective-permute-start | bytes 786440 | tf_op jit(solution)/shard_map/ppermute | solution.py:19
  97.5 17.2 %collective-permute-start.14 = (bf16[4,64,512]{2,1,0:T(8,128)(2,1)}, bf16[4,64,512]{2,1,0:T(8,128)(2,1)S(1)}, u32[]{:S(2)}, u32[]{:S(2)}) collective-permute-start(bf16[4,64,512]{2,1,0:T(8,128)(2,1)} %collective-permute-done.12.refs_5_), channel_id=1, source_target_pairs={{0,2},{1,3},{2,0},{3,1},{4,6},{5,7},{6,4},{7,5},{8,10},{9,11},{10,... | collective-permute-start | bytes 786440 | tf_op jit(solution)/shard_map/ppermute | solution.py:19
  101.6 23.9 %copy-start.12 = (bf16[2,576,1024]{2,1,0:T(8,128)(2,1)}, bf16[2,576,1024]{2,1,0:T(8,128)(2,1)S(1)}, u32[]{:S(2)}) copy-start(bf16[2,576,1024]{2,1,0:T(8,128)(2,1)S(1)} %get-tuple-element.143) | copy-start | bytes 7077892
  106.0 12.9 %collective-permute-start.15 = (bf16[4,64,512]{2,1,0:T(8,128)(2,1)}, bf16[4,64,512]{2,1,0:T(8,128)(2,1)S(1)}, u32[]{:S(2)}, u32[]{:S(2)}) collective-permute-start(bf16[4,64,512]{2,1,0:T(8,128)(2,1)} %collective-permute-done.12.refs_5_), channel_id=1, source_target_pairs={{0,3},{1,2},{2,1},{3,0},{4,7},{5,6},{6,5},{7,4},{8,11},{9,10},{10,... | collective-permute-start | bytes 786440 | tf_op jit(solution)/shard_map/ppermute | solution.py:19
  128.8 49.6 %copy-start.33 = (bf16[256,1152]{1,0:T(8,128)(2,1)}, bf16[256,1152]{1,0:T(8,128)(2,1)S(1)}, u32[]{:S(2)}) copy-start(bf16[256,1152]{1,0:T(8,128)(2,1)S(1)} %get-tuple-element.176.refs_0_) | copy-start | bytes 1769476
  128.8 25.8 %collective-permute-start.18 = (bf16[256,1152]{1,0:T(8,128)(2,1)S(1)}, bf16[256,1152]{1,0:T(8,128)(2,1)S(1)}, u32[]{:S(2)}, u32[]{:S(2)}) collective-permute-start(bf16[256,1152]{1,0:T(8,128)(2,1)S(1)} %get-tuple-element.176.refs_0_), channel_id=1, source_target_pairs={{0,2},{1,3},{2,0},{3,1},{4,6},{5,7},{6,4},{7,5},{8,10},{9,11},{10,... | collective-permute-start | bytes 1769480 | tf_op jit(solution)/shard_map/ppermute | solution.py:19
  129.4 26.1 %collective-permute-start.19 = (bf16[256,1152]{1,0:T(8,128)(2,1)S(1)}, bf16[256,1152]{1,0:T(8,128)(2,1)}, u32[]{:S(2)}, u32[]{:S(2)}) collective-permute-start(bf16[256,1152]{1,0:T(8,128)(2,1)S(1)} %get-tuple-element.176.refs_0_), channel_id=1, source_target_pairs={{0,3},{1,2},{2,1},{3,0},{4,7},{5,6},{6,5},{7,4},{8,11},{9,10},{10,... | collective-permute-start | bytes 1769480 | tf_op jit(solution)/shard_map/ppermute | solution.py:19
  130.9 50.8 %collective-permute-start.16 = (bf16[256,1152]{1,0:T(8,128)(2,1)S(1)}, bf16[256,1152]{1,0:T(8,128)(2,1)}, u32[]{:S(2)}, u32[]{:S(2)}) collective-permute-start(bf16[256,1152]{1,0:T(8,128)(2,1)S(1)} %get-tuple-element.176.refs_0_), channel_id=1, source_target_pairs={{0,1},{1,0},{2,3},{3,2},{4,5},{5,4},{6,7},{7,6},{8,9},{9,8},{10,11... | collective-permute-start | bytes 1769480 | tf_op jit(solution)/shard_map/ppermute | solution.py:19
  178.5 28.3 %collective-permute-start.20 = (bf16[256,1152]{1,0:T(8,128)(2,1)}, bf16[256,1152]{1,0:T(8,128)(2,1)}, u32[]{:S(2)}, u32[]{:S(2)}) collective-permute-start(bf16[256,1152]{1,0:T(8,128)(2,1)} %get-tuple-element.151), channel_id=1, source_target_pairs={{0,2},{1,3},{2,0},{3,1},{4,6},{5,7},{6,4},{7,5},{8,10},{9,11},{10,... | collective-permute-start | bytes 1769480 | tf_op jit(solution)/shard_map/ppermute | solution.py:19
  180.2 26.5 %collective-permute-start.21 = (bf16[256,1152]{1,0:T(8,128)(2,1)}, bf16[256,1152]{1,0:T(8,128)(2,1)}, u32[]{:S(2)}, u32[]{:S(2)}) collective-permute-start(bf16[256,1152]{1,0:T(8,128)(2,1)} %get-tuple-element.152), channel_id=1, source_target_pairs={{0,3},{1,2},{2,1},{3,0},{4,7},{5,6},{6,5},{7,4},{8,11},{9,10},{10,... | collective-permute-start | bytes 1769480 | tf_op jit(solution)/shard_map/ppermute | solution.py:19
  190.8 17.1 %collective-permute-start.17 = (bf16[256,1152]{1,0:T(8,128)(2,1)}, bf16[256,1152]{1,0:T(8,128)(2,1)S(1)}, u32[]{:S(2)}, u32[]{:S(2)}) collective-permute-start(bf16[256,1152]{1,0:T(8,128)(2,1)} %get-tuple-element.150), channel_id=1, source_target_pairs={{0,1},{1,0},{2,3},{3,2},{4,5},{5,4},{6,7},{7,6},{8,9},{9,8},{10,11... | collective-permute-start | bytes 1769480 | tf_op jit(solution)/shard_map/ppermute | solution.py:19
  213.3 16.5 %collective-permute-start.23 = (bf16[256,1152]{1,0:T(8,128)(2,1)}, bf16[256,1152]{1,0:T(8,128)(2,1)S(1)}, u32[]{:S(2)}, u32[]{:S(2)}) collective-permute-start(bf16[256,1152]{1,0:T(8,128)(2,1)} %get-tuple-element.170.refs_0_), channel_id=1, source_target_pairs={{0,1},{1,0},{2,3},{3,2},{4,5},{5,4},{6,7},{7,6},{8,9},{9,8},{10,11... | collective-permute-start | bytes 1769480 | tf_op jit(solution)/shard_map/ppermute | solution.py:19
  214.8 26.6 %collective-permute-start.22 = (bf16[256,1152]{1,0:T(8,128)(2,1)}, bf16[256,1152]{1,0:T(8,128)(2,1)S(1)}, u32[]{:S(2)}, u32[]{:S(2)}) collective-permute-start(bf16[256,1152]{1,0:T(8,128)(2,1)} %get-tuple-element.170.refs_0_), channel_id=1, source_target_pairs={{0,2},{1,3},{2,0},{3,1},{4,6},{5,7},{6,4},{7,5},{8,10},{9,11},{10,... | collective-permute-start | bytes 1769480 | tf_op jit(solution)/shard_map/ppermute | solution.py:19
  216.3 25.1 %collective-permute-start.24 = (bf16[256,1152]{1,0:T(8,128)(2,1)}, bf16[256,1152]{1,0:T(8,128)(2,1)S(1)}, u32[]{:S(2)}, u32[]{:S(2)}) collective-permute-start(bf16[256,1152]{1,0:T(8,128)(2,1)} %get-tuple-element.170.refs_0_), channel_id=1, source_target_pairs={{0,3},{1,2},{2,1},{3,0},{4,7},{5,6},{6,5},{7,4},{8,11},{9,10},{10,... | collective-permute-start | bytes 1769480 | tf_op jit(solution)/shard_map/ppermute | solution.py:19
  266.9 4.3 collective-permute-start.25
  266.9 29.6 %collective-permute-start.28 = (bf16[256,1152]{1,0:T(8,128)(2,1)}, bf16[256,1152]{1,0:T(8,128)(2,1)}, u32[]{:S(2)}, u32[]{:S(2)}) collective-permute-start(bf16[256,1152]{1,0:T(8,128)(2,1)} %get-tuple-element.169), channel_id=1, source_target_pairs={{0,3},{1,2},{2,1},{3,0},{4,7},{5,6},{6,5},{7,4},{8,11},{9,10},{10,... | collective-permute-start | bytes 1769480 | tf_op jit(solution)/shard_map/ppermute | solution.py:19
  268.4 28.1 %collective-permute-start.26 = (bf16[256,1152]{1,0:T(8,128)(2,1)S(1)}, bf16[256,1152]{1,0:T(8,128)(2,1)}, u32[]{:S(2)}, u32[]{:S(2)}) collective-permute-start(bf16[256,1152]{1,0:T(8,128)(2,1)S(1)} %copy-done.78), channel_id=1, source_target_pairs={{0,1},{1,0},{2,3},{3,2},{4,5},{5,4},{6,7},{7,6},{8,9},{9,8},{10,11... | collective-permute-start | bytes 1769480 | tf_op jit(solution)/shard_map/ppermute | solution.py:19
  269.9 26.6 %collective-permute-start.27 = (bf16[256,1152]{1,0:T(8,128)(2,1)}, bf16[256,1152]{1,0:T(8,128)(2,1)}, u32[]{:S(2)}, u32[]{:S(2)}) collective-permute-start(bf16[256,1152]{1,0:T(8,128)(2,1)} %get-tuple-element.188), channel_id=1, source_target_pairs={{0,2},{1,3},{2,0},{3,1},{4,6},{5,7},{6,4},{7,5},{8,10},{9,11},{10,... | collective-permute-start | bytes 1769480 | tf_op jit(solution)/shard_map/ppermute | solution.py:19
  276.9 163.6 %reduce-scatter.3.cloned.1.call-start = ((), (), s32[]{:S(2)}) async-start(), calls=%async_computation.6 | async-start | bytes 5160960 | tf_op jit(solution)/shard_map/reduce_scatter | solution.py:644
  296.5 7.0 %collective-permute-start.30 = (bf16[576,1728]{1,0:T(8,128)(2,1)}, bf16[576,1728]{1,0:T(8,128)(2,1)}, u32[]{:S(2)}, u32[]{:S(2)}) collective-permute-start(bf16[576,1728]{1,0:T(8,128)(2,1)} %get-tuple-element.193), channel_id=1, source_target_pairs={{0,16},{16,0},{1,17},{17,1},{2,18},{18,2},{3,19},{19,3},{4,20},{20... | collective-permute-start | bytes 5971976 | tf_op jit(solution)/shard_map/ppermute | solution.py:19
  296.6 7.4 %collective-permute-start.29 = (bf16[576,1728]{1,0:T(8,128)(2,1)}, bf16[576,1728]{1,0:T(8,128)(2,1)}, u32[]{:S(2)}, u32[]{:S(2)}) collective-permute-start(bf16[576,1728]{1,0:T(8,128)(2,1)} %get-tuple-element.190), channel_id=1, source_target_pairs={{0,16},{16,0},{1,17},{17,1},{2,18},{18,2},{3,19},{19,3},{4,20},{20... | collective-permute-start | bytes 5971976 | tf_op jit(solution)/shard_map/ppermute | solution.py:19
  314.5 10.9 %collective-permute-start.31 = (bf16[576,1024]{1,0:T(8,128)(2,1)}, bf16[576,1024]{1,0:T(8,128)(2,1)S(1)}, u32[]{:S(2)}, u32[]{:S(2)}) collective-permute-start(bf16[576,1024]{1,0:T(8,128)(2,1)} %get-tuple-element.196), channel_id=1, source_target_pairs={{0,16},{16,0},{1,17},{17,1},{2,18},{18,2},{3,19},{19,3},{4,20},{20... | collective-permute-start | bytes 3538952 | tf_op jit(solution)/shard_map/ppermute | solution.py:19
  321.8 9.4 %collective-permute-start.32 = (bf16[4,64,512]{2,1,0:T(8,128)(2,1)}, bf16[4,64,512]{2,1,0:T(8,128)(2,1)S(1)}, u32[]{:S(2)}, u32[]{:S(2)}) collective-permute-start(bf16[4,64,512]{2,1,0:T(8,128)(2,1)} %get-tuple-element.202), channel_id=1, source_target_pairs={{0,1},{1,0},{2,3},{3,2},{4,5},{5,4},{6,7},{7,6},{8,9},{9,8},{10,11... | collective-permute-start | bytes 786440 | tf_op jit(solution)/shard_map/ppermute | solution.py:19
  322.9 12.9 %collective-permute-start.33 = (bf16[4,64,512]{2,1,0:T(8,128)(2,1)}, bf16[4,64,512]{2,1,0:T(8,128)(2,1)S(1)}, u32[]{:S(2)}, u32[]{:S(2)}) collective-permute-start(bf16[4,64,512]{2,1,0:T(8,128)(2,1)} %get-tuple-element.203), channel_id=1, source_target_pairs={{0,2},{1,3},{2,0},{3,1},{4,6},{5,7},{6,4},{7,5},{8,10},{9,11},{10,... | collective-permute-start | bytes 786440 | tf_op jit(solution)/shard_map/ppermute | solution.py:19
  324.0 13.2 %collective-permute-start.34 = (bf16[4,64,512]{2,1,0:T(8,128)(2,1)}, bf16[4,64,512]{2,1,0:T(8,128)(2,1)S(1)}, u32[]{:S(2)}, u32[]{:S(2)}) collective-permute-start(bf16[4,64,512]{2,1,0:T(8,128)(2,1)} %get-tuple-element.204), channel_id=1, source_target_pairs={{0,3},{1,2},{2,1},{3,0},{4,7},{5,6},{6,5},{7,4},{8,11},{9,10},{10,... | collective-permute-start | bytes 786440 | tf_op jit(solution)/shard_map/ppermute | solution.py:19
  327.8 20.9 %copy-start.5 = (bf16[2,576,1024]{2,1,0:T(8,128)(2,1)S(1)}, bf16[2,576,1024]{2,1,0:T(8,128)(2,1)}, u32[]{:S(2)}) copy-start(bf16[2,576,1024]{2,1,0:T(8,128)(2,1)} %copy-done.4) | copy-start | bytes 7077892
  338.3 16.3 %collective-permute-start.37 = (bf16[1,4,64,512]{3,2,1,0:T(8,128)(2,1)}, bf16[1,4,64,512]{3,2,1,0:T(8,128)(2,1)}, u32[]{:S(2)}, u32[]{:S(2)}) collective-permute-start(bf16[1,4,64,512]{3,2,1,0:T(8,128)(2,1)} %get-tuple-element.209), channel_id=1, source_target_pairs={{0,3},{1,2},{2,1},{3,0},{4,7},{5,6},{6,5},{7,4},{8,11},{9,10},{10,... | collective-permute-start | bytes 786440 | tf_op jit(solution)/shard_map/ppermute | solution.py:19
  340.1 14.6 %collective-permute-start.35 = (bf16[1,4,64,512]{3,2,1,0:T(8,128)(2,1)}, bf16[1,4,64,512]{3,2,1,0:T(8,128)(2,1)}, u32[]{:S(2)}, u32[]{:S(2)}) collective-permute-start(bf16[1,4,64,512]{3,2,1,0:T(8,128)(2,1)} %get-tuple-element.205), channel_id=1, source_target_pairs={{0,1},{1,0},{2,3},{3,2},{4,5},{5,4},{6,7},{7,6},{8,9},{9,8},{10,11... | collective-permute-start | bytes 786440 | tf_op jit(solution)/shard_map/ppermute | solution.py:19
  340.7 13.9 %collective-permute-start.36 = (bf16[1,4,64,512]{3,2,1,0:T(8,128)(2,1)}, bf16[1,4,64,512]{3,2,1,0:T(8,128)(2,1)}, u32[]{:S(2)}, u32[]{:S(2)}) collective-permute-start(bf16[1,4,64,512]{3,2,1,0:T(8,128)(2,1)} %get-tuple-element.207), channel_id=1, source_target_pairs={{0,2},{1,3},{2,0},{3,1},{4,6},{5,7},{6,4},{7,5},{8,10},{9,11},{10,... | collective-permute-start | bytes 786440 | tf_op jit(solution)/shard_map/ppermute | solution.py:19
  341.8 24.8 %collective-permute-start.38 = (bf16[4,64,512]{2,1,0:T(8,128)(2,1)}, bf16[4,64,512]{2,1,0:T(8,128)(2,1)}, u32[]{:S(2)}, u32[]{:S(2)}) collective-permute-start(bf16[4,64,512]{2,1,0:T(8,128)(2,1)} %get-tuple-element.242), channel_id=1, source_target_pairs={{4,0},{8,4},{12,8},{5,1},{9,5},{13,9},{6,2},{10,6},{14,10},{7,3},{... | collective-permute-start | bytes 786440 | tf_op jit(solution)/shard_map/ppermute | solution.py:24
  354.7 40.8 %collective-permute-start.45 = (f32[4,465]{1,0:T(4,128)}, f32[4,465]{1,0:T(4,128)}, u32[]{:S(2)}, u32[]{:S(2)}) collective-permute-start(f32[4,465]{1,0:T(4,128)} %dynamic-slice_bitcast_fusion), channel_id=1, source_target_pairs={{0,16},{16,0},{1,17},{17,1},{2,18},{18,2},{3,19},{19,3},{4,20},{20... | collective-permute-start | bytes 22328 | tf_op jit(solution)/shard_map/ppermute | solution.py:19
  368.2 21.5 %collective-permute-start.39 = (bf16[4,64,512]{2,1,0:T(8,128)(2,1)S(1)}, bf16[4,64,512]{2,1,0:T(8,128)(2,1)S(1)}, u32[]{:S(2)}, u32[]{:S(2)}) collective-permute-start(bf16[4,64,512]{2,1,0:T(8,128)(2,1)S(1)} %fusion.10), channel_id=1, source_target_pairs={{4,0},{8,4},{12,8},{5,1},{9,5},{13,9},{6,2},{10,6},{14,10},{7,3},{... | collective-permute-start | bytes 786440 | tf_op jit(solution)/shard_map/ppermute | solution.py:24
  369.8 20.0 %copy-start.25 = (f32[64,256]{1,0:T(8,128)S(1)}, f32[64,256]{1,0:T(8,128)}, u32[]{:S(2)}) copy-start(f32[64,256]{1,0:T(8,128)} %slice.192.sin_ref) | copy-start | bytes 196612
  369.8 20.0 %copy-start.19 = (f32[256,1152]{1,0:T(8,128)S(1)}, f32[256,1152]{1,0:T(8,128)}, u32[]{:S(2)}) copy-start(f32[256,1152]{1,0:T(8,128)} %get-tuple-element.218.dhid_ref) | copy-start | bytes 3538948
  370.7 26.1 %collective-permute-start.40 = (bf16[832,256]{1,0:T(8,128)(2,1)}, bf16[832,256]{1,0:T(8,128)(2,1)}, u32[]{:S(2)}, u32[]{:S(2)}) collective-permute-start(bf16[832,256]{1,0:T(8,128)(2,1)} %pad_maximum_fusion.3), channel_id=1, source_target_pairs={{0,1},{1,0},{2,3},{3,2},{4,5},{5,4},{6,7},{7,6},{8,9},{9,8},{10,11... | collective-permute-start | bytes 1277960 | tf_op jit(solution)/shard_map/ppermute | solution.py:19
  372.6 24.2 %collective-permute-start.41 = (bf16[832,256]{1,0:T(8,128)(2,1)}, bf16[832,256]{1,0:T(8,128)(2,1)}, u32[]{:S(2)}, u32[]{:S(2)}) collective-permute-start(bf16[832,256]{1,0:T(8,128)(2,1)} %pad_maximum_fusion.4), channel_id=1, source_target_pairs={{0,2},{1,3},{2,0},{3,1},{4,6},{5,7},{6,4},{7,5},{8,10},{9,11},{10,... | collective-permute-start | bytes 1277960 | tf_op jit(solution)/shard_map/ppermute | solution.py:19
  374.8 22.0 %collective-permute-start.42 = (bf16[832,256]{1,0:T(8,128)(2,1)}, bf16[832,256]{1,0:T(8,128)(2,1)}, u32[]{:S(2)}, u32[]{:S(2)}) collective-permute-start(bf16[832,256]{1,0:T(8,128)(2,1)} %pad_maximum_fusion.5), channel_id=1, source_target_pairs={{0,3},{1,2},{2,1},{3,0},{4,7},{5,6},{6,5},{7,4},{8,11},{9,10},{10,... | collective-permute-start | bytes 1277960 | tf_op jit(solution)/shard_map/ppermute | solution.py:19
  395.4 1.2 collective-permute-start.46
  396.2 6.6 %collective-permute-start.44 = (bf16[576,512]{1,0:T(8,128)(2,1)}, bf16[576,512]{1,0:T(8,128)(2,1)S(1)}, u32[]{:S(2)}, u32[]{:S(2)}) collective-permute-start(bf16[576,512]{1,0:T(8,128)(2,1)} %copy-done.51), channel_id=1, source_target_pairs={{0,16},{16,0},{1,17},{17,1},{2,18},{18,2},{3,19},{19,3},{4,20},{20... | collective-permute-start | bytes 1769480 | tf_op jit(solution)/shard_map/ppermute | solution.py:19
  400.8 1.8 collective-permute-start.43
  404.3 35.8 %all-to-all-start.1 = ((bf16[4,146,1024]{2,1,0:T(8,128)(2,1)}), bf16[4,146,1024]{2,1,0:T(8,128)(2,1)S(1)}, u32[]{:S(2)}, u32[]{:S(2)}) async-start(bf16[4,146,1024]{2,1,0:T(8,128)(2,1)} %pad_maximum_fusion.1), calls=%async_computation.1 | async-start | bytes 2490368 | tf_op jit(solution)/shard_map/all_to_all | solution.py:28
  443.4 6.8 %collective-permute-start.47 = (bf16[147,512]{1,0:T(8,128)(2,1)S(1)}, bf16[147,512]{1,0:T(8,128)(2,1)S(1)}, u32[]{:S(2)}, u32[]{:S(2)}) collective-permute-start(bf16[147,512]{1,0:T(8,128)(2,1)S(1)} %pad_maximum_fusion.8), channel_id=1, source_target_pairs={{0,1},{1,0},{2,3},{3,2},{4,5},{5,4},{6,7},{7,6},{8,9},{9,8},{10,11... | collective-permute-start | bytes 451592 | tf_op jit(solution)/shard_map/ppermute | solution.py:19
  443.4 8.6 %collective-permute-start.48 = (bf16[147,512]{1,0:T(8,128)(2,1)S(1)}, bf16[147,512]{1,0:T(8,128)(2,1)S(1)}, u32[]{:S(2)}, u32[]{:S(2)}) collective-permute-start(bf16[147,512]{1,0:T(8,128)(2,1)S(1)} %pad_maximum_fusion.8), channel_id=1, source_target_pairs={{0,2},{1,3},{2,0},{3,1},{4,6},{5,7},{6,4},{7,5},{8,10},{9,11},{10,... | collective-permute-start | bytes 451592 | tf_op jit(solution)/shard_map/ppermute | solution.py:19
  444.6 7.4 %collective-permute-start.49 = (bf16[147,512]{1,0:T(8,128)(2,1)S(1)}, bf16[147,512]{1,0:T(8,128)(2,1)S(1)}, u32[]{:S(2)}, u32[]{:S(2)}) collective-permute-start(bf16[147,512]{1,0:T(8,128)(2,1)S(1)} %pad_maximum_fusion.8), channel_id=1, source_target_pairs={{0,3},{1,2},{2,1},{3,0},{4,7},{5,6},{6,5},{7,4},{8,11},{9,10},{10,... | collective-permute-start | bytes 451592 | tf_op jit(solution)/shard_map/ppermute | solution.py:19
  (71 other events, 520.4 us)
Sparse Core Ops, SparseCore 0:
  10.2 33.9 all-gather.2
  45.8 119.5 all-gather.4
  277.1 46.1 reduce-scatter.4
  325.6 86.2 reduce-scatter.2

commit v5 on v4

--- a/solution.py
+++ b/solution.py
@@ -468,8 +468,8 @@
     out_ref[...] = mm_t(left_ref[...], right_ref[...])
 
 
-def finish_kernel(core_ref, raw_ref, cos_ref, sin_ref, gain_key_ref, pulled_ref, kv_ref, dhid_ref, x_ref, gain_ref, normed_ref, *refs):
-    parts, (din_ref, dgain_ref, dgain_key_ref, send_ref, own_ref, sums) = refs[:-6], refs[-6:]
+def finish_kernel(chunks, place_ref, raw_ref, cos_ref, sin_ref, gain_key_ref, pulled_ref, kv_ref, dhid_ref, x_ref, gain_ref, normed_ref, *refs):
+    parts, (din_ref, dgain_ref, dgain_key_ref, send_ref, own_ref, sums, turned) = refs[:-7], refs[-7:]
     head = raw_ref.shape[1]
     d_kv = sum(r[...].astype(F32) for r in parts)
     key = raw_ref[...]
@@ -478,9 +478,12 @@
     d_key, d_gain = rms_back(e, key, inverse_rms(key), gain_key_ref[...])
     dgain_key_ref[...] = column_sum(d_gain)
     low = jnp.concatenate([d_key.astype(LOW), d_kv[:, head:].astype(LOW)], axis=1)
-    sums[...] = mm(normed_ref[...].T, low)
+    turned[...] = low
+    part = low.shape[1] // chunks
+    ordered = [turned[:, pl.ds(pl.multiple_of((place_ref[1] ^ p) * part, part), part)] for p in range(chunks)]
+    sums[...] = mm(normed_ref[...].T, jnp.concatenate(ordered, axis=1))
     half = own_ref.shape[0]
-    core = core_ref[0]
+    core = place_ref[0]
     own_ref[...] = sums[pl.ds(pl.multiple_of(core * half, half), half), :].astype(LOW)
     send_ref[...] = sums[pl.ds(pl.multiple_of((1 - core) * half, half), half), :].astype(LOW)
     d_normed = pulled_ref[...] + mm_t(low, kv_ref[...])
@@ -704,7 +707,7 @@
         middle = swap(after(d_pairs[T - 1 + p], d_kv), "tp", p)
         for b in range(1, halo):
             d_blocks[b] = d_blocks[b] + middle[b - 1].astype(F32)
-    d_query_late, out_low = after(d_query, middle), after(out_low, middle)
+    d_query_late, out_low = after(d_query, d_kv), after(out_low, d_kv)
     for d in range(halo, 0, -1):
         come = shifted(d_kv, "ctx", -1)
         if d > 1:
@@ -736,10 +739,10 @@
         rows = jnp.concatenate([v.reshape(F * C, -1) for v in values], axis=1).reshape(F, C, -1)
         return lax.dynamic_index_in_dim(rows, f, 0, False) + swap(lax.dynamic_index_in_dim(rows, f ^ 1, 0, False), "fsdp", 1)
 
-    def owner_sums(weight_sums, rows):
+    def owner_sums(weight_sums, rows, *earlier):
         wide = weight_sums.shape[1]
         sent = jnp.concatenate([weight_sums.reshape(C, piece, wide), pack(rows, wide)], axis=1)
-        sums = jnp.sum(exchange(sent, "ctx").astype(F32), axis=0)
+        sums = jnp.sum(after(exchange(sent, "ctx"), *earlier).astype(F32), axis=0)
         return sums[:piece], unpack(sums[piece:], rows.shape[1])
 
     early = core_rows(
@@ -749,27 +752,36 @@
     d_kv[0] = after(d_kv[0], both_heads, pulled)
     own_rows = lambda table: jnp.tile(table, (seqs, 1))
     grad_input, dg_input, dg_key, *kv_halves = pl.pallas_call(
-        finish_kernel,
+        functools.partial(finish_kernel, T),
         in_specs=[SMEM] + [VMEM] * (10 + len(d_kv)),
         out_shape=[token, gain_row, struct((1, head_width), F32)] + [struct((half, 2 * head_width), LOW)] * 2,
-        scratch_shapes=[pltpu.VMEM((2 * half, 2 * head_width), F32)],
+        scratch_shapes=[pltpu.VMEM((2 * half, 2 * head_width), F32), pltpu.VMEM((own, 2 * head_width), LOW)],
         compiler_params=ROOM,
         name="finish",
-    )(f.reshape(1), key_own, own_rows(cos_own), own_rows(sin_own), g_key, pulled, kv_full, d_hidden, x_own, g_input,
+    )(jnp.stack([f, t]), key_own, own_rows(cos_own), own_rows(sin_own), g_key, pulled, kv_full, d_hidden, x_own, g_input,
       normed_own, *[v.reshape(own, 2 * head_width) for v in d_kv])
     late = core_rows([dg_input, dg_key])
-    sums = jnp.concatenate([both_heads, collect_core(*kv_halves).astype(LOW)], axis=1)
-    sums, total = owner_sums(sums, jnp.concatenate([early, late], axis=1))
+    part = 2 * head_width // T
+    kv_sum = collect_core(*kv_halves)
+    kv_low = kv_sum.astype(LOW)
+    kv_part = kv_sum[:, :part]
+    for p in range(1, T):
+        kv_part = kv_part + swap(kv_low[:, p * part : (p + 1) * part], "tp", p).astype(F32)
+    sums = jnp.concatenate([both_heads, kv_part.astype(LOW)], axis=1)
+    sums, total = owner_sums(sums, jnp.concatenate([early, late], axis=1), grad_gate, grad_up)
     grad_query, grad_out = sums[:, :head_width], sums[:, head_width : 2 * head_width]
-    grad_kv = sums[:, 2 * head_width :]
-    low = jnp.concatenate([grad_kv.astype(LOW), pack(total[None], 2 * head_width)[0]], axis=0)
-    low, grad_gate, grad_up, grad_down = lax.optimization_barrier((low, grad_gate, grad_up, grad_down))
-    totals = {p: (swap(low, "tp", p) if p else low).astype(F32) for p in range(T)}
+    n = total.shape[0]
+    rows = -(-n // part)
+    mine = jnp.concatenate([sums[:, 2 * head_width :], jnp.pad(total, (0, rows * part - n)).reshape(rows, part)], axis=0)
+    pieces = [swap(mine, "tp", p) if p else mine for p in range(T)]
+    whole = jnp.stack(pieces)
+    grad_kv = jnp.concatenate([lax.dynamic_index_in_dim(whole, t ^ p, 0, False)[:piece] for p in range(T)], axis=1)
+    totals = {p: v[piece:] for p, v in enumerate(pieces)}
     bit = 1
     while bit < T:
         totals = {p: totals[p] + totals[p ^ bit] for p in totals if not p & bit}
         bit *= 2
-    grad_kv, total = totals[0][:piece], unpack(totals[0][piece:], total.shape[0])
+    total = totals[0].reshape(-1)[:n]
     early, late = total[: early.shape[1]], total[early.shape[1] :]
     loss = early[-1] / (2.0 * width_model * count)
     at = 3 * piece

time: 468 us -> 462 us (0.987)
  local copies, waits for them, and re-layouts: 51.1 us -> 43.8 us
    all_to_all x2, waiting for transfers between devices: 27.7 us -> 14.2 us  [exchange(): return lax.all_to_all(values, axes, 0, 0, tiled=True)]
    ppermute x46 -> x49, waiting for transfers between devices: 80.7 us -> 93.7 us  [swap(): lax.ppermute(values, axis, [(i, i ^ bits) for i in range(lax.axis_size(ax...]
    unnamed x164 -> x148, local copies, waits for them, and re-layouts: 23.1 us -> 19.3 us
    ppermute x46 -> x49, starting transfers between devices: 41.4 us -> 43.8 us  [swap(): lax.ppermute(values, axis, [(i, i ^ bits) for i in range(lax.axis_size(ax...]
  transfers between devices with their start and end apart: 56 -> 59, of which waited for: 26 -> 31; matrix products, arithmetic and copies ran while one was open for 11% -> 11% of each run, Pallas kernels for 24% -> 25%
where the time goes in v5:
time: 462 us; the launch traced here: 457 us
  waiting for transfers between devices  157 us (34%)
  Pallas kernels  143 us (31%)
  starting transfers between devices  64.6 us (14%)
  local copies, waits for them, and re-layouts  43.8 us (9%)
  other arithmetic  28.5 us (6%)
  between operations  18.3 us (4%)
    ppermute x49, waiting for transfers between devices, swap(): lax.ppermute(values, axis, [(i, i ^ bits) for i in range(lax.axis_size(ax...  93.7 us
    pallas_call x6, Pallas kernels, ffn_call(): pl.pallas_call(functools.partial(kernel, units, chunks), grid=(pl.cdiv(un...  64.9 us
    ppermute x49, starting transfers between devices, swap(): lax.ppermute(values, axis, [(i, i ^ bits) for i in range(lax.axis_size(ax...  43.8 us
    ppermute x4, waiting for transfers between devices, shifted(): lax.ppermute(values, axis, [(i, i + by) for i in range(size) if 0 <= i +...  35.5 us
    pallas_call x4, Pallas kernels, weight_grad(): pl.pallas_call(functools.partial(weight_grad_kernel, chunks, sets), grid=...  32.1 us
    unnamed x148, local copies, waits for them, and re-layouts  19.3 us
    all_to_all x2, waiting for transfers between devices, exchange(): return lax.all_to_all(values, axes, 0, 0, tiled=True)  14.2 us
    all_to_all x2, starting transfers between devices, exchange(): return lax.all_to_all(values, axes, 0, 0, tiled=True)  10.5 us
  transfers between devices with their start and end apart: 59, of which 31 were waited for; matrix products, arithmetic and copies ran while one was open for 11% of the time, Pallas kernels for 25%

profile of v5, /device:TPU:0, one launch (start us, length us, event | category | flops | bytes accessed | tf_op | source)
XLA Modules:
  0.0 457.1 jit_solution(6585383823002103635)
XLA Ops:
  9.4 2.6 pad_maximum_fusion
  14.2 6.3 %all-to-all-start = ((bf16[8,2,832]{2,1,0:T(2,128)(2,1)}), bf16[8,2,832]{2,1,0:T(2,128)(2,1)S(1)}, u32[]{:S(2)}, u32[]{:S(2)}) async-start(bf16[8,2,832]{2,1,0:T(2,128)(2,1)} %reshape.269), calls=%async_computation | async-start | bytes 57344 | tf_op jit(solution)/shard_map/all_to_all | solution.py:28
  35.7 1.7 copy-done.9
  40.6 3.6 all-gather.3.cloned.1.call-done
  45.7 2.4 collective-permute-start.2
  51.9 2.8 project_keys.1
  57.4 3.3 collective-permute-start.8
  60.6 2.3 collective-permute-done.2.refs_3_
  62.9 12.1 %collective-permute-done.1.refs_2_ = bf16[576,512]{1,0:T(8,128)(2,1)} collective-permute-done((bf16[576,512]{1,0:T(8,128)(2,1)S(1)}, bf16[576,512]{1,0:T(8,128)(2,1)}, u32[]{:S(2)}, u32[]{:S(2)}) %collective-permute-start.1) | collective-permute-done | bytes 589856 | tf_op jit(solution)/shard_map/ppermute | solution.py:19
  75.6 4.1 collective-permute-start.12
  79.7 11.3 %collective-permute-done.12.refs_5_ = bf16[4,64,512]{2,1,0:T(8,128)(2,1)} collective-permute-done((bf16[4,64,512]{2,1,0:T(8,128)(2,1)}, bf16[4,64,512]{2,1,0:T(8,128)(2,1)}, u32[]{:S(2)}, u32[]{:S(2)}) %collective-permute-start.12) | collective-permute-done | bytes 262176 | tf_op jit(solution)/shard_map/ppermute | solution.py:24
  98.7 2.8 assemble.1
  101.6 4.5 collective-permute-done.10.refs_3_
  106.1 1.6 collective-permute-start.15
  107.7 2.0 fusion.33.q_ref
  109.8 4.9 %collective-permute-done.13.refs_6_ = bf16[4,64,512]{2,1,0:T(8,128)(2,1)S(1)} collective-permute-done((bf16[4,64,512]{2,1,0:T(8,128)(2,1)}, bf16[4,64,512]{2,1,0:T(8,128)(2,1)S(1)}, u32[]{:S(2)}, u32[]{:S(2)}) %collective-permute-start.13) | collective-permute-done | bytes 262176 | tf_op jit(solution)/shard_map/ppermute | solution.py:19
  114.7 4.2 collective-permute-done.15.refs_8_
  118.9 4.9 %attend.1 = (bf16[256,1024]{1,0:T(8,128)(2,1)S(1)}, bf16[256,1024]{1,0:T(8,128)(2,1)S(1)}, f32[4,256,1]{2,1,0:T(8,128)S(1)}) custom-call(s32[4,64,2]{2,1,0:T(8,128)S(1)} %copy-done.18, s32[4,2,768]{2,1,0:T(2,128)S(1)} %copy-done.37, f32[256,1024]{1,0:T(8,128)S(1)} %fusion.33.q_ref, f32[1,256]{1,0:T(1,128)S(1)} %copy-done.42, f32[64,256]{1,0:T(8,128)S(1)} %copy-done.19, ...), custom_call_target="tpu_custom_call" | custom-call | flops 402653184 | bytes 4194304 | tf_op jit(solution)/shard_map/attend/pallas_call | solution.py:607
  129.4 1.5 collective-permute-start.19
  132.3 22.3 %collective-permute-done.18.refs_0_.refs_2_ = bf16[256,1152]{1,0:T(8,128)(2,1)S(1)} collective-permute-done((bf16[256,1152]{1,0:T(8,128)(2,1)S(1)}, bf16[256,1152]{1,0:T(8,128)(2,1)S(1)}, u32[]{:S(2)}, u32[]{:S(2)}) %collective-permute-start.18) | collective-permute-done | bytes 589856 | tf_op jit(solution)/shard_map/ppermute | solution.py:19
  155.5 9.9 %all-gather.5.cloned.1.call-done.refs_1_.refs_2_.refs_3_.refs_4_ = bf16[3,1152,1728]{2,1,0:T(8,128)(2,1)} async-done(((bf16[3,144,1728]{2,1,0:T(8,128)(2,1)}), bf16[3,1152,1728]{2,1,0:T(8,128)(2,1)}) %all-gather.5.cloned.1.call-update) | async-done | bytes 11943952 | tf_op jit(solution)/shard_map/all_gather | solution.py:556
  165.4 13.0 %ffn.5 = (bf16[256,1152]{1,0:T(8,128)(2,1)}, bf16[256,1152]{1,0:T(8,128)(2,1)}, bf16[512,1728]{1,0:T(8,128)(2,1)}, bf16[512,1728]{1,0:T(8,128)(2,1)}, bf16[512,1728]{1,0:T(8,128)(2,1)}) custom-call(bf16[256,1152]{1,0:T(8,128)(2,1)} %copy-done.49, bf16[256,1152]{1,0:T(8,128)(2,1)} %collective-permute-done.19.refs_1_.refs_3_, ...), custom_call_target="tpu_custom_call" | custom-call | flops 6115295232 | bytes 13123584 | tf_op jit(solution)/shard_map/ffn/pallas_call | solution.py:419
  178.4 1.8 collective-permute-start.20
  181.6 9.1 %ffn.4 = (bf16[256,1152]{1,0:T(8,128)(2,1)}, bf16[256,1728]{1,0:T(8,128)(2,1)}, bf16[256,1728]{1,0:T(8,128)(2,1)}, bf16[256,1728]{1,0:T(8,128)(2,1)}) custom-call(bf16[256,1152]{1,0:T(8,128)(2,1)} %collective-permute-done.16.refs_0_.refs_1_, bf16[3,1152,1728]{2,1,0:T(8,128)(2,1)} %all-gather.5.cloned.1.call-done.refs_1_.refs_2_.refs_3_.refs_4_, ...), custom_call_target="tpu_custom_call" | custom-call | flops 3057647616 | bytes 12533760 | tf_op jit(solution)/shard_map/ffn/pallas_call | solution.py:419
  194.1 9.4 %ffn.3 = (f32[256,1152]{1,0:T(8,128)}, bf16[256,1728]{1,0:T(8,128)(2,1)}, bf16[256,1728]{1,0:T(8,128)(2,1)}, bf16[256,1728]{1,0:T(8,128)(2,1)}) custom-call(bf16[256,1152]{1,0:T(8,128)(2,1)} %copy-done.28, bf16[3,1152,1728]{2,1,0:T(8,128)(2,1)} %all-gather.5.cloned.1.call-done.refs_1_.refs_2_.refs_3_.refs_4_, ...), custom_call_target="tpu_custom_call" | custom-call | flops 3057647616 | bytes 12533760 | tf_op jit(solution)/shard_map/ffn/pallas_call | solution.py:419
  203.5 3.1 collective-permute-done.20.refs_2_
  208.6 4.6 %loss.1 = (bf16[256,1152]{1,0:T(8,128)(2,1)}, f32[256,1152]{1,0:T(8,128)}, bf16[256,1152]{1,0:T(8,128)(2,1)}, f32[1,1152]{1,0:T(1,128)}, f32[1,128]{1,0:T(1,128)}) custom-call(f32[1]{0:T(128)} %bitcast.factor_ref, f32[256,1152]{1,0:T(8,128)} %copy-done.17, bf16[256,1152]{1,0:T(8,128)(2,1)} %bitcast.106, f32[256,1]{1,0:T(8,128)} %reshape.242.valid_ref, ...), custom_call_target="tpu_custom_call" | custom-call | flops 512 | bytes 5898240 | tf_op jit(solution)/shard_map/loss/pallas_call | solution.py:633
  213.2 1.5 collective-permute-start.23
  216.7 9.4 %ffn_back.3 = (f32[256,1152]{1,0:T(8,128)}, bf16[256,1728]{1,0:T(8,128)(2,1)}, bf16[256,1728]{1,0:T(8,128)(2,1)}) custom-call(bf16[256,1152]{1,0:T(8,128)(2,1)} %get-tuple-element.167.refs_0_, bf16[3,1152,1728]{2,1,0:T(8,128)(2,1)} %all-gather.5.cloned.1.call-done.refs_1_.refs_2_.refs_3_.refs_4_, ...), custom_call_target="tpu_custom_call" | custom-call | flops 3057647616 | bytes 14303232 | tf_op jit(solution)/shard_map/ffn_back/pallas_call | solution.py:419
  226.1 3.6 collective-permute-done.23.refs_0_.refs_1_
  230.5 9.1 %ffn_back.4 = (bf16[256,1152]{1,0:T(8,128)(2,1)}, bf16[256,1728]{1,0:T(8,128)(2,1)}, bf16[256,1728]{1,0:T(8,128)(2,1)}) custom-call(bf16[256,1152]{1,0:T(8,128)(2,1)} %copy-done.50, bf16[3,1152,1728]{2,1,0:T(8,128)(2,1)} %all-gather.5.cloned.1.call-done.refs_1_.refs_2_.refs_3_.refs_4_, ...), custom_call_target="tpu_custom_call" | custom-call | flops 3057647616 | bytes 14303232 | tf_op jit(solution)/shard_map/ffn_back/pallas_call | solution.py:419
  239.6 1.8 collective-permute-done.22.refs_0_.refs_2_
  242.4 15.0 %ffn_back.5 = (bf16[256,1152]{1,0:T(8,128)(2,1)}, bf16[256,1152]{1,0:T(8,128)(2,1)}, bf16[512,1728]{1,0:T(8,128)(2,1)}, bf16[512,1728]{1,0:T(8,128)(2,1)}) custom-call(bf16[256,1152]{1,0:T(8,128)(2,1)} %copy-done.51, bf16[256,1152]{1,0:T(8,128)(2,1)} %copy-done.52, bf16[3,1152,1728]{2,1,0:T(8,128)(2,1)} %all-gather.5.cloned.1.call-done.refs_1_.refs_2_.refs_3_.refs_4_, ...), custom_call_target="tpu_custom_call" | custom-call | flops 6115295232 | bytes 16662528 | tf_op jit(solution)/shard_map/ffn_back/pallas_call | solution.py:419
  257.4 9.4 %weight_grad.4 = (bf16[576,1728]{1,0:T(8,128)(2,1)}, bf16[576,1728]{1,0:T(8,128)(2,1)}) custom-call(s32[1]{0:T(128)} %bitcast.8.core_ref, bf16[256,1152]{1,0:T(8,128)(2,1)} %get-tuple-element.167.refs_0_, bf16[256,1152]{1,0:T(8,128)(2,1)} %copy-done.50, bf16[256,1152]{1,0:T(8,128)(2,1)} %copy-done.51, bf16[256,1152]{1,0:T(8,128)(2,1)} %copy-done.52, ...), custom_call_target="tpu_custom_call" | custom-call | flops 4076863488 | bytes 6340608 | tf_op jit(solution)/shard_map/weight_grad/pallas_call | solution.py:522
  266.8 1.5 collective-permute-start.28
  272.4 4.4 pair_sum.2
  276.8 14.1 %weight_grad.5 = (bf16[576,1728]{1,0:T(8,128)(2,1)}, bf16[576,1728]{1,0:T(8,128)(2,1)}, bf16[576,1728]{1,0:T(8,128)(2,1)}, bf16[576,1728]{1,0:T(8,128)(2,1)}) custom-call(s32[1]{0:T(128)} %bitcast.8.core_ref, bf16[256,1152]{1,0:T(8,128)(2,1)} %copy-done.28, bf16[256,1152]{1,0:T(8,128)(2,1)} %collective-permute-done.16.refs_0_.refs_1_, ...), custom_call_target="tpu_custom_call" | custom-call | flops 8153726976 | bytes 10321920 | tf_op jit(solution)/shard_map/weight_grad/pallas_call | solution.py:522
  290.9 5.4 %collective-permute-done.27.refs_2_ = bf16[256,1152]{1,0:T(8,128)(2,1)} collective-permute-done((bf16[256,1152]{1,0:T(8,128)(2,1)}, bf16[256,1152]{1,0:T(8,128)(2,1)}, u32[]{:S(2)}, u32[]{:S(2)}) %collective-permute-start.27) | collective-permute-done | bytes 589856 | tf_op jit(solution)/shard_map/ppermute | solution.py:19
  296.9 6.4 %middle.1 = (f32[256,1152]{1,0:T(8,128)}, bf16[256,1152]{1,0:T(8,128)(2,1)}, bf16[256,1024]{1,0:T(8,128)(2,1)}, f32[1,1152]{1,0:T(1,128)}, f32[1,1152]{1,0:T(1,128)}) custom-call(f32[256,1152]{1,0:T(8,128)} %get-tuple-element.153.dres_ref, f32[256,1152]{1,0:T(8,128)} %copy-done.17, f32[256,1152]{1,0:T(8,128)} %copy-done.45, bf16[1152,1024]{1,0:T(8,128)(2,1)} %bitcast.101, ...), custom_call_target="tpu_custom_call" | custom-call | flops 181193932800 | bytes 2359296 | tf_op jit(solution)/shard_map/middle/pallas_call | solution.py:668
  303.8 5.9 %pair_sum.3 = bf16[2,576,1728]{2,1,0:T(8,128)(2,1)} custom-call(bf16[576,1728]{1,0:T(8,128)(2,1)} %get-tuple-element.181.refs_0_, bf16[576,1728]{1,0:T(8,128)(2,1)} %collective-permute-done.29.refs_1_, bf16[576,1728]{1,0:T(8,128)(2,1)} %get-tuple-element.183.refs_2_, bf16[576,1728]{1,0:T(8,128)(2,1)} %collective-permute-done.30.refs_3_), custom_call_target="tpu_custom_call" | custom-call | tf_op jit(solution)/shard_map/pair_sum/pallas_call | solution.py:309
  309.8 4.6 %weight_grad.6 = (bf16[576,1024]{1,0:T(8,128)(2,1)}, bf16[576,1024]{1,0:T(8,128)(2,1)}) custom-call(s32[1]{0:T(128)} %bitcast.8.core_ref, bf16[256,1152]{1,0:T(8,128)(2,1)} %get-tuple-element.188.refs_0_, bf16[256,1024]{1,0:T(8,128)(2,1)} %copy-done.11), custom_call_target="tpu_custom_call" | custom-call | tf_op jit(solution)/shard_map/weight_grad/pallas_call | solution.py:522
  314.9 7.2 %attend_back.1 = (bf16[256,1024]{1,0:T(8,128)(2,1)}, f32[4,1,256]{2,1,0:T(1,128)}, f32[3,4,64,512]{3,2,1,0:T(8,128)}, bf16[4,64,512]{2,1,0:T(8,128)(2,1)}, bf16[...) custom-call(s32[1]{0:T(128)} %bitcast.4.place_ref, ...), custom_call_target="tpu_custom_call" | custom-call | tf_op jit(solution)/shard_map/attend_back/pallas_call | solution.py:684
  325.7 3.3 convert_add_fusion
  329.3 2.2 collective-permute-done.32
  332.0 5.6 %collective-permute-done.34 = bf16[4,64,512]{2,1,0:T(8,128)(2,1)} collective-permute-done((bf16[4,64,512]{2,1,0:T(8,128)(2,1)}, bf16[4,64,512]{2,1,0:T(8,128)(2,1)}, u32[]{:S(2)}, u32[]{:S(2)}) %collective-permute-start.34) | collective-permute-done | bytes 262176 | tf_op jit(solution)/shard_map/ppermute | solution.py:19
  337.6 1.5 fusion.6
  346.5 3.5 collective-permute-done.35
  350.8 2.4 collective-permute-done.36
  353.2 2.7 collective-permute-done.37
  357.3 5.9 %collective-permute-done.38 = bf16[4,64,512]{2,1,0:T(8,128)(2,1)S(1)} collective-permute-done((bf16[4,64,512]{2,1,0:T(8,128)(2,1)S(1)}, bf16[4,64,512]{2,1,0:T(8,128)(2,1)S(1)}, u32[]{:S(2)}, u32[]{:S(2)}) %collective-permute-start.38) | collective-permute-done | bytes 262176 | tf_op jit(solution)/shard_map/ppermute | solution.py:24
  363.2 1.9 fusion.10
  367.9 1.6 slice.191.refs_4_
  370.4 18.3 %collective-permute-done.39 = bf16[4,64,512]{2,1,0:T(8,128)(2,1)} collective-permute-done((bf16[4,64,512]{2,1,0:T(8,128)(2,1)}, bf16[4,64,512]{2,1,0:T(8,128)(2,1)}, u32[]{:S(2)}, u32[]{:S(2)}) %collective-permute-start.39) | collective-permute-done | bytes 262176 | tf_op jit(solution)/shard_map/ppermute | solution.py:24
  388.8 3.6 finish.1
  394.4 1.5 fusion.2
  395.9 4.0 weight_grad.7
  401.9 1.6 collective-permute-start.46
  404.1 3.1 collective-permute-done.45
  407.2 3.8 collective-permute-done.46
  412.1 4.2 all-to-all-start.1
  417.0 2.1 convert_bitcast_fusion
  421.9 14.2 %all-to-all-done.1 = bf16[4,147,640]{2,1,0:T(8,128)(2,1)} async-done(((bf16[4,147,640]{2,1,0:T(8,128)(2,1)}), bf16[4,147,640]{2,1,0:T(8,128)(2,1)}, u32[]{:S(2)}, u32[]{:S(2)}) %all-to-all-start.1) | async-done | bytes 752672 | tf_op jit(solution)/shard_map/all_to_all | solution.py:28
  437.7 1.8 collective-permute-start.50
  442.3 1.6 collective-permute-done.51
  (334 shorter events, 97.0 us)
Async XLA Ops:
  7.2 184.7 %copy-start = (bf16[4,256,1152]{2,1,0:T(8,128)(2,1)S(1)}, bf16[4,256,1152]{2,1,0:T(8,128)(2,1)}, u32[]{:S(2)}) copy-start(bf16[4,256,1152]{2,1,0:T(8,128)(2,1)} %param.17) | copy-start | bytes 7077892
  7.2 36.9 %all-gather.3.cloned.1.call-start = ((), (), s32[]{:S(2)}) async-start(), calls=%async_computation.4 | async-start | bytes 1474560 | tf_op jit(solution)/shard_map/all_gather | solution.py:555
  9.2 156.1 %all-gather.5.cloned.1.call-start = ((), (), s32[]{:S(2)}) async-start(), calls=%async_computation.5 | async-start | bytes 13934592 | tf_op jit(solution)/shard_map/all_gather | solution.py:556
  14.2 12.8 %all-to-all-start = ((bf16[8,2,832]{2,1,0:T(2,128)(2,1)}), bf16[8,2,832]{2,1,0:T(2,128)(2,1)S(1)}, u32[]{:S(2)}, u32[]{:S(2)}) async-start(bf16[8,2,832]{2,1,0:T(2,128)(2,1)} %reshape.269), calls=%async_computation | async-start | bytes 57344 | tf_op jit(solution)/shard_map/all_to_all | solution.py:28
  20.5 396.5 %reduce-scatter.5.cloned.1.call-start = ((), (), s32[]{:S(2)}) async-start(), calls=%async_computation.7 | async-start | bytes 2580480 | tf_op jit(solution)/shard_map/reduce_scatter | solution.py:647
  32.2 93.3 %copy-start.40 = (f32[1,1152]{1,0:T(1,128)}, f32[1,1152]{1,0:T(1,128)S(1)}, u32[]{:S(2)}) copy-start(f32[1,1152]{1,0:T(1,128)S(1)} %reshape.218.gain_attn_ref) | copy-start | bytes 13828
  33.0 92.5 %copy-start.41 = (f32[1,1152]{1,0:T(1,128)}, f32[1,1152]{1,0:T(1,128)S(1)}, u32[]{:S(2)}) copy-start(f32[1,1152]{1,0:T(1,128)S(1)} %reshape.219.gain_ffn_ref) | copy-start | bytes 13828
  45.6 3.6 collective-permute-start.3
  45.7 17.2 %collective-permute-start.2 = (bf16[576,512]{1,0:T(8,128)(2,1)S(1)}, bf16[576,512]{1,0:T(8,128)(2,1)}, u32[]{:S(2)}, u32[]{:S(2)}) collective-permute-start(bf16[576,512]{1,0:T(8,128)(2,1)S(1)} %get-tuple-element.130.refs_0_), channel_id=1, source_target_pairs={{0,3},{1,2},{2,1},{3,0},{4,7},{5,6},{6,5},{7,4},{8,11},{9,10},{10,... | collective-permute-start | bytes 1769480 | tf_op jit(solution)/shard_map/ppermute | solution.py:19
  48.1 26.9 %collective-permute-start.1 = (bf16[576,512]{1,0:T(8,128)(2,1)S(1)}, bf16[576,512]{1,0:T(8,128)(2,1)}, u32[]{:S(2)}, u32[]{:S(2)}) collective-permute-start(bf16[576,512]{1,0:T(8,128)(2,1)S(1)} %get-tuple-element.130.refs_0_), channel_id=1, source_target_pairs={{0,2},{1,3},{2,0},{3,1},{4,6},{5,7},{6,4},{7,5},{8,10},{9,11},{10,... | collective-permute-start | bytes 1769480 | tf_op jit(solution)/shard_map/ppermute | solution.py:19
  48.7 26.4 %collective-permute-start = (bf16[576,512]{1,0:T(8,128)(2,1)S(1)}, bf16[576,512]{1,0:T(8,128)(2,1)}, u32[]{:S(2)}, u32[]{:S(2)}) collective-permute-start(bf16[576,512]{1,0:T(8,128)(2,1)S(1)} %get-tuple-element.130.refs_0_), channel_id=1, source_target_pairs={{0,1},{1,0},{2,3},{3,2},{4,5},{5,4},{6,7},{7,6},{8,9},{9,8},{10,11... | collective-permute-start | bytes 1769480 | tf_op jit(solution)/shard_map/ppermute | solution.py:19
  57.4 18.3 %collective-permute-start.8 = (bf16[4,64,512]{2,1,0:T(8,128)(2,1)S(1)}, bf16[4,64,512]{2,1,0:T(8,128)(2,1)}, u32[]{:S(2)}, u32[]{:S(2)}) collective-permute-start(bf16[4,64,512]{2,1,0:T(8,128)(2,1)S(1)} %get-tuple-element.129), channel_id=1, source_target_pairs={{0,4},{4,8},{8,12},{1,5},{5,9},{9,13},{2,6},{6,10},{10,14},{3,7},{... | collective-permute-start | bytes 786440 | tf_op jit(solution)/shard_map/ppermute | solution.py:24
  62.9 31.1 %collective-permute-start.7 = (bf16[576,512]{1,0:T(8,128)(2,1)}, bf16[576,512]{1,0:T(8,128)(2,1)}, u32[]{:S(2)}, u32[]{:S(2)}) collective-permute-start(bf16[576,512]{1,0:T(8,128)(2,1)} %collective-permute-done.2.refs_3_), channel_id=1, source_target_pairs={{0,16},{16,0},{1,17},{17,1},{2,18},{18,2},{3,19},{19,3},{4,20},{20... | collective-permute-start | bytes 1769480 | tf_op jit(solution)/shard_map/ppermute | solution.py:19
  75.1 20.4 %collective-permute-start.6 = (bf16[576,512]{1,0:T(8,128)(2,1)}, bf16[576,512]{1,0:T(8,128)(2,1)}, u32[]{:S(2)}, u32[]{:S(2)}) collective-permute-start(bf16[576,512]{1,0:T(8,128)(2,1)} %collective-permute-done.1.refs_2_), channel_id=1, source_target_pairs={{0,16},{16,0},{1,17},{17,1},{2,18},{18,2},{3,19},{19,3},{4,20},{20... | collective-permute-start | bytes 1769480 | tf_op jit(solution)/shard_map/ppermute | solution.py:19
  75.1 20.9 %collective-permute-start.5 = (bf16[576,512]{1,0:T(8,128)(2,1)}, bf16[576,512]{1,0:T(8,128)(2,1)}, u32[]{:S(2)}, u32[]{:S(2)}) collective-permute-start(bf16[576,512]{1,0:T(8,128)(2,1)} %collective-permute-done.refs_1_), channel_id=1, source_target_pairs={{0,16},{16,0},{1,17},{17,1},{2,18},{18,2},{3,19},{19,3},{4,20},{20... | collective-permute-start | bytes 1769480 | tf_op jit(solution)/shard_map/ppermute | solution.py:19
  75.6 21.9 %collective-permute-start.4 = (bf16[576,512]{1,0:T(8,128)(2,1)S(1)}, bf16[576,512]{1,0:T(8,128)(2,1)}, u32[]{:S(2)}, u32[]{:S(2)}) collective-permute-start(bf16[576,512]{1,0:T(8,128)(2,1)S(1)} %get-tuple-element.130.refs_0_), channel_id=1, source_target_pairs={{0,16},{16,0},{1,17},{17,1},{2,18},{18,2},{3,19},{19,3},{4,20},{20... | collective-permute-start | bytes 1769480 | tf_op jit(solution)/shard_map/ppermute | solution.py:19
  75.6 15.4 %collective-permute-start.12 = (bf16[4,64,512]{2,1,0:T(8,128)(2,1)}, bf16[4,64,512]{2,1,0:T(8,128)(2,1)}, u32[]{:S(2)}, u32[]{:S(2)}) collective-permute-start(bf16[4,64,512]{2,1,0:T(8,128)(2,1)} %collective-permute-done.8.refs_1_), channel_id=1, source_target_pairs={{0,4},{4,8},{8,12},{1,5},{5,9},{9,13},{2,6},{6,10},{10,14},{3,7},{... | collective-permute-start | bytes 786440 | tf_op jit(solution)/shard_map/ppermute | solution.py:24
  91.1 15.0 %collective-permute-start.10 = (bf16[4,64,512]{2,1,0:T(8,128)(2,1)}, bf16[4,64,512]{2,1,0:T(8,128)(2,1)}, u32[]{:S(2)}, u32[]{:S(2)}) collective-permute-start(bf16[4,64,512]{2,1,0:T(8,128)(2,1)} %collective-permute-done.8.refs_1_), channel_id=1, source_target_pairs={{0,2},{1,3},{2,0},{3,1},{4,6},{5,7},{6,4},{7,5},{8,10},{9,11},{10,... | collective-permute-start | bytes 786440 | tf_op jit(solution)/shard_map/ppermute | solution.py:19
  94.0 15.7 %collective-permute-start.11 = (bf16[4,64,512]{2,1,0:T(8,128)(2,1)}, bf16[4,64,512]{2,1,0:T(8,128)(2,1)S(1)}, u32[]{:S(2)}, u32[]{:S(2)}) collective-permute-start(bf16[4,64,512]{2,1,0:T(8,128)(2,1)} %collective-permute-done.8.refs_1_), channel_id=1, source_target_pairs={{0,3},{1,2},{2,1},{3,0},{4,7},{5,6},{6,5},{7,4},{8,11},{9,10},{10,... | collective-permute-start | bytes 786440 | tf_op jit(solution)/shard_map/ppermute | solution.py:19
  95.4 14.3 %collective-permute-start.9 = (bf16[4,64,512]{2,1,0:T(8,128)(2,1)}, bf16[4,64,512]{2,1,0:T(8,128)(2,1)S(1)}, u32[]{:S(2)}, u32[]{:S(2)}) collective-permute-start(bf16[4,64,512]{2,1,0:T(8,128)(2,1)} %collective-permute-done.8.refs_1_), channel_id=1, source_target_pairs={{0,1},{1,0},{2,3},{3,2},{4,5},{5,4},{6,7},{7,6},{8,9},{9,8},{10,11... | collective-permute-start | bytes 786440 | tf_op jit(solution)/shard_map/ppermute | solution.py:19
  96.0 18.7 %collective-permute-start.13 = (bf16[4,64,512]{2,1,0:T(8,128)(2,1)}, bf16[4,64,512]{2,1,0:T(8,128)(2,1)S(1)}, u32[]{:S(2)}, u32[]{:S(2)}) collective-permute-start(bf16[4,64,512]{2,1,0:T(8,128)(2,1)} %collective-permute-done.12.refs_5_), channel_id=1, source_target_pairs={{0,1},{1,0},{2,3},{3,2},{4,5},{5,4},{6,7},{7,6},{8,9},{9,8},{10,11... | collective-permute-start | bytes 786440 | tf_op jit(solution)/shard_map/ppermute | solution.py:19
  97.5 17.2 %collective-permute-start.14 = (bf16[4,64,512]{2,1,0:T(8,128)(2,1)}, bf16[4,64,512]{2,1,0:T(8,128)(2,1)S(1)}, u32[]{:S(2)}, u32[]{:S(2)}) collective-permute-start(bf16[4,64,512]{2,1,0:T(8,128)(2,1)} %collective-permute-done.12.refs_5_), channel_id=1, source_target_pairs={{0,2},{1,3},{2,0},{3,1},{4,6},{5,7},{6,4},{7,5},{8,10},{9,11},{10,... | collective-permute-start | bytes 786440 | tf_op jit(solution)/shard_map/ppermute | solution.py:19
  101.6 23.9 %copy-start.10 = (bf16[2,576,1024]{2,1,0:T(8,128)(2,1)}, bf16[2,576,1024]{2,1,0:T(8,128)(2,1)S(1)}, u32[]{:S(2)}) copy-start(bf16[2,576,1024]{2,1,0:T(8,128)(2,1)S(1)} %get-tuple-element.140) | copy-start | bytes 7077892
  106.1 12.8 %collective-permute-start.15 = (bf16[4,64,512]{2,1,0:T(8,128)(2,1)}, bf16[4,64,512]{2,1,0:T(8,128)(2,1)S(1)}, u32[]{:S(2)}, u32[]{:S(2)}) collective-permute-start(bf16[4,64,512]{2,1,0:T(8,128)(2,1)} %collective-permute-done.12.refs_5_), channel_id=1, source_target_pairs={{0,3},{1,2},{2,1},{3,0},{4,7},{5,6},{6,5},{7,4},{8,11},{9,10},{10,... | collective-permute-start | bytes 786440 | tf_op jit(solution)/shard_map/ppermute | solution.py:19
  128.8 49.6 %copy-start.28 = (bf16[256,1152]{1,0:T(8,128)(2,1)}, bf16[256,1152]{1,0:T(8,128)(2,1)S(1)}, u32[]{:S(2)}) copy-start(bf16[256,1152]{1,0:T(8,128)(2,1)S(1)} %get-tuple-element.173.refs_0_) | copy-start | bytes 1769476
  128.8 25.8 %collective-permute-start.18 = (bf16[256,1152]{1,0:T(8,128)(2,1)S(1)}, bf16[256,1152]{1,0:T(8,128)(2,1)S(1)}, u32[]{:S(2)}, u32[]{:S(2)}) collective-permute-start(bf16[256,1152]{1,0:T(8,128)(2,1)S(1)} %get-tuple-element.173.refs_0_), channel_id=1, source_target_pairs={{0,2},{1,3},{2,0},{3,1},{4,6},{5,7},{6,4},{7,5},{8,10},{9,11},{10,... | collective-permute-start | bytes 1769480 | tf_op jit(solution)/shard_map/ppermute | solution.py:19
  129.4 26.1 %collective-permute-start.19 = (bf16[256,1152]{1,0:T(8,128)(2,1)S(1)}, bf16[256,1152]{1,0:T(8,128)(2,1)}, u32[]{:S(2)}, u32[]{:S(2)}) collective-permute-start(bf16[256,1152]{1,0:T(8,128)(2,1)S(1)} %get-tuple-element.173.refs_0_), channel_id=1, source_target_pairs={{0,3},{1,2},{2,1},{3,0},{4,7},{5,6},{6,5},{7,4},{8,11},{9,10},{10,... | collective-permute-start | bytes 1769480 | tf_op jit(solution)/shard_map/ppermute | solution.py:19
  130.9 50.7 %collective-permute-start.16 = (bf16[256,1152]{1,0:T(8,128)(2,1)S(1)}, bf16[256,1152]{1,0:T(8,128)(2,1)}, u32[]{:S(2)}, u32[]{:S(2)}) collective-permute-start(bf16[256,1152]{1,0:T(8,128)(2,1)S(1)} %get-tuple-element.173.refs_0_), channel_id=1, source_target_pairs={{0,1},{1,0},{2,3},{3,2},{4,5},{5,4},{6,7},{7,6},{8,9},{9,8},{10,11... | collective-permute-start | bytes 1769480 | tf_op jit(solution)/shard_map/ppermute | solution.py:19
  178.4 28.3 %collective-permute-start.20 = (bf16[256,1152]{1,0:T(8,128)(2,1)}, bf16[256,1152]{1,0:T(8,128)(2,1)}, u32[]{:S(2)}, u32[]{:S(2)}) collective-permute-start(bf16[256,1152]{1,0:T(8,128)(2,1)} %get-tuple-element.148), channel_id=1, source_target_pairs={{0,2},{1,3},{2,0},{3,1},{4,6},{5,7},{6,4},{7,5},{8,10},{9,11},{10,... | collective-permute-start | bytes 1769480 | tf_op jit(solution)/shard_map/ppermute | solution.py:19
  180.2 26.5 %collective-permute-start.21 = (bf16[256,1152]{1,0:T(8,128)(2,1)}, bf16[256,1152]{1,0:T(8,128)(2,1)}, u32[]{:S(2)}, u32[]{:S(2)}) collective-permute-start(bf16[256,1152]{1,0:T(8,128)(2,1)} %get-tuple-element.149), channel_id=1, source_target_pairs={{0,3},{1,2},{2,1},{3,0},{4,7},{5,6},{6,5},{7,4},{8,11},{9,10},{10,... | collective-permute-start | bytes 1769480 | tf_op jit(solution)/shard_map/ppermute | solution.py:19
  190.7 17.1 %collective-permute-start.17 = (bf16[256,1152]{1,0:T(8,128)(2,1)}, bf16[256,1152]{1,0:T(8,128)(2,1)S(1)}, u32[]{:S(2)}, u32[]{:S(2)}) collective-permute-start(bf16[256,1152]{1,0:T(8,128)(2,1)} %get-tuple-element.147), channel_id=1, source_target_pairs={{0,1},{1,0},{2,3},{3,2},{4,5},{5,4},{6,7},{7,6},{8,9},{9,8},{10,11... | collective-permute-start | bytes 1769480 | tf_op jit(solution)/shard_map/ppermute | solution.py:19
  213.2 16.5 %collective-permute-start.23 = (bf16[256,1152]{1,0:T(8,128)(2,1)}, bf16[256,1152]{1,0:T(8,128)(2,1)S(1)}, u32[]{:S(2)}, u32[]{:S(2)}) collective-permute-start(bf16[256,1152]{1,0:T(8,128)(2,1)} %get-tuple-element.167.refs_0_), channel_id=1, source_target_pairs={{0,1},{1,0},{2,3},{3,2},{4,5},{5,4},{6,7},{7,6},{8,9},{9,8},{10,11... | collective-permute-start | bytes 1769480 | tf_op jit(solution)/shard_map/ppermute | solution.py:19
  214.8 26.6 %collective-permute-start.22 = (bf16[256,1152]{1,0:T(8,128)(2,1)}, bf16[256,1152]{1,0:T(8,128)(2,1)S(1)}, u32[]{:S(2)}, u32[]{:S(2)}) collective-permute-start(bf16[256,1152]{1,0:T(8,128)(2,1)} %get-tuple-element.167.refs_0_), channel_id=1, source_target_pairs={{0,2},{1,3},{2,0},{3,1},{4,6},{5,7},{6,4},{7,5},{8,10},{9,11},{10,... | collective-permute-start | bytes 1769480 | tf_op jit(solution)/shard_map/ppermute | solution.py:19
  216.3 25.1 %collective-permute-start.24 = (bf16[256,1152]{1,0:T(8,128)(2,1)}, bf16[256,1152]{1,0:T(8,128)(2,1)S(1)}, u32[]{:S(2)}, u32[]{:S(2)}) collective-permute-start(bf16[256,1152]{1,0:T(8,128)(2,1)} %get-tuple-element.167.refs_0_), channel_id=1, source_target_pairs={{0,3},{1,2},{2,1},{3,0},{4,7},{5,6},{6,5},{7,4},{8,11},{9,10},{10,... | collective-permute-start | bytes 1769480 | tf_op jit(solution)/shard_map/ppermute | solution.py:19
  266.7 4.3 collective-permute-start.25
  266.8 29.6 %collective-permute-start.28 = (bf16[256,1152]{1,0:T(8,128)(2,1)}, bf16[256,1152]{1,0:T(8,128)(2,1)}, u32[]{:S(2)}, u32[]{:S(2)}) collective-permute-start(bf16[256,1152]{1,0:T(8,128)(2,1)} %get-tuple-element.166), channel_id=1, source_target_pairs={{0,3},{1,2},{2,1},{3,0},{4,7},{5,6},{6,5},{7,4},{8,11},{9,10},{10,... | collective-permute-start | bytes 1769480 | tf_op jit(solution)/shard_map/ppermute | solution.py:19
  268.3 28.1 %collective-permute-start.26 = (bf16[256,1152]{1,0:T(8,128)(2,1)S(1)}, bf16[256,1152]{1,0:T(8,128)(2,1)}, u32[]{:S(2)}, u32[]{:S(2)}) collective-permute-start(bf16[256,1152]{1,0:T(8,128)(2,1)S(1)} %copy-done.71), channel_id=1, source_target_pairs={{0,1},{1,0},{2,3},{3,2},{4,5},{5,4},{6,7},{7,6},{8,9},{9,8},{10,11... | collective-permute-start | bytes 1769480 | tf_op jit(solution)/shard_map/ppermute | solution.py:19
  269.8 26.6 %collective-permute-start.27 = (bf16[256,1152]{1,0:T(8,128)(2,1)}, bf16[256,1152]{1,0:T(8,128)(2,1)}, u32[]{:S(2)}, u32[]{:S(2)}) collective-permute-start(bf16[256,1152]{1,0:T(8,128)(2,1)} %get-tuple-element.185), channel_id=1, source_target_pairs={{0,2},{1,3},{2,0},{3,1},{4,6},{5,7},{6,4},{7,5},{8,10},{9,11},{10,... | collective-permute-start | bytes 1769480 | tf_op jit(solution)/shard_map/ppermute | solution.py:19
  276.8 142.3 %reduce-scatter.3.cloned.1.call-start = ((), (), s32[]{:S(2)}) async-start(), calls=%async_computation.6 | async-start | bytes 5160960 | tf_op jit(solution)/shard_map/reduce_scatter | solution.py:647
  296.4 7.0 %collective-permute-start.30 = (bf16[576,1728]{1,0:T(8,128)(2,1)}, bf16[576,1728]{1,0:T(8,128)(2,1)}, u32[]{:S(2)}, u32[]{:S(2)}) collective-permute-start(bf16[576,1728]{1,0:T(8,128)(2,1)} %get-tuple-element.190), channel_id=1, source_target_pairs={{0,16},{16,0},{1,17},{17,1},{2,18},{18,2},{3,19},{19,3},{4,20},{20... | collective-permute-start | bytes 5971976 | tf_op jit(solution)/shard_map/ppermute | solution.py:19
  296.4 7.4 %collective-permute-start.29 = (bf16[576,1728]{1,0:T(8,128)(2,1)}, bf16[576,1728]{1,0:T(8,128)(2,1)}, u32[]{:S(2)}, u32[]{:S(2)}) collective-permute-start(bf16[576,1728]{1,0:T(8,128)(2,1)} %get-tuple-element.187), channel_id=1, source_target_pairs={{0,16},{16,0},{1,17},{17,1},{2,18},{18,2},{3,19},{19,3},{4,20},{20... | collective-permute-start | bytes 5971976 | tf_op jit(solution)/shard_map/ppermute | solution.py:19
  314.4 11.3 %collective-permute-start.31 = (bf16[576,1024]{1,0:T(8,128)(2,1)}, bf16[576,1024]{1,0:T(8,128)(2,1)}, u32[]{:S(2)}, u32[]{:S(2)}) collective-permute-start(bf16[576,1024]{1,0:T(8,128)(2,1)} %get-tuple-element.193), channel_id=1, source_target_pairs={{0,16},{16,0},{1,17},{17,1},{2,18},{18,2},{3,19},{19,3},{4,20},{20... | collective-permute-start | bytes 3538952 | tf_op jit(solution)/shard_map/ppermute | solution.py:19
  322.1 9.4 %collective-permute-start.32 = (bf16[4,64,512]{2,1,0:T(8,128)(2,1)}, bf16[4,64,512]{2,1,0:T(8,128)(2,1)S(1)}, u32[]{:S(2)}, u32[]{:S(2)}) collective-permute-start(bf16[4,64,512]{2,1,0:T(8,128)(2,1)} %get-tuple-element.199), channel_id=1, source_target_pairs={{0,1},{1,0},{2,3},{3,2},{4,5},{5,4},{6,7},{7,6},{8,9},{9,8},{10,11... | collective-permute-start | bytes 786440 | tf_op jit(solution)/shard_map/ppermute | solution.py:19
  323.1 8.9 %collective-permute-start.33 = (bf16[4,64,512]{2,1,0:T(8,128)(2,1)}, bf16[4,64,512]{2,1,0:T(8,128)(2,1)S(1)}, u32[]{:S(2)}, u32[]{:S(2)}) collective-permute-start(bf16[4,64,512]{2,1,0:T(8,128)(2,1)} %get-tuple-element.200), channel_id=1, source_target_pairs={{0,2},{1,3},{2,0},{3,1},{4,6},{5,7},{6,4},{7,5},{8,10},{9,11},{10,... | collective-permute-start | bytes 786440 | tf_op jit(solution)/shard_map/ppermute | solution.py:19
  324.3 13.3 %collective-permute-start.34 = (bf16[4,64,512]{2,1,0:T(8,128)(2,1)}, bf16[4,64,512]{2,1,0:T(8,128)(2,1)}, u32[]{:S(2)}, u32[]{:S(2)}) collective-permute-start(bf16[4,64,512]{2,1,0:T(8,128)(2,1)} %get-tuple-element.201), channel_id=1, source_target_pairs={{0,3},{1,2},{2,1},{3,0},{4,7},{5,6},{6,5},{7,4},{8,11},{9,10},{10,... | collective-permute-start | bytes 786440 | tf_op jit(solution)/shard_map/ppermute | solution.py:19
  329.2 41.2 %collective-permute-start.48 = (f32[4,465]{1,0:T(4,128)S(1)}, f32[4,465]{1,0:T(4,128)S(1)}, u32[]{:S(2)}, u32[]{:S(2)}) collective-permute-start(f32[4,465]{1,0:T(4,128)S(1)} %dynamic-slice_bitcast_fusion.4), channel_id=1, source_target_pairs={{0,16},{16,0},{1,17},{17,1},{2,18},{18,2},{3,19},{19,3},{4,20},{20... | collective-permute-start | bytes 22328 | tf_op jit(solution)/shard_map/ppermute | solution.py:19
  339.2 24.0 %collective-permute-start.38 = (bf16[4,64,512]{2,1,0:T(8,128)(2,1)S(1)}, bf16[4,64,512]{2,1,0:T(8,128)(2,1)S(1)}, u32[]{:S(2)}, u32[]{:S(2)}) collective-permute-start(bf16[4,64,512]{2,1,0:T(8,128)(2,1)S(1)} %get-tuple-element.236), channel_id=1, source_target_pairs={{4,0},{8,4},{12,8},{5,1},{9,5},{13,9},{6,2},{10,6},{14,10},{7,3},{... | collective-permute-start | bytes 786440 | tf_op jit(solution)/shard_map/ppermute | solution.py:24
  340.5 9.5 %collective-permute-start.35 = (bf16[1,4,64,512]{3,2,1,0:T(8,128)(2,1)}, bf16[1,4,64,512]{3,2,1,0:T(8,128)(2,1)S(1)}, u32[]{:S(2)}, u32[]{:S(2)}) collective-permute-start(bf16[1,4,64,512]{3,2,1,0:T(8,128)(2,1)} %get-tuple-element.202), channel_id=1, source_target_pairs={{0,1},{1,0},{2,3},{3,2},{4,5},{5,4},{6,7},{7,6},{8,9},{9,8},{10,11... | collective-permute-start | bytes 786440 | tf_op jit(solution)/shard_map/ppermute | solution.py:19
  341.3 11.9 %collective-permute-start.36 = (bf16[1,4,64,512]{3,2,1,0:T(8,128)(2,1)}, bf16[1,4,64,512]{3,2,1,0:T(8,128)(2,1)S(1)}, u32[]{:S(2)}, u32[]{:S(2)}) collective-permute-start(bf16[1,4,64,512]{3,2,1,0:T(8,128)(2,1)} %get-tuple-element.204), channel_id=1, source_target_pairs={{0,2},{1,3},{2,0},{3,1},{4,6},{5,7},{6,4},{7,5},{8,10},{9,11},{10,... | collective-permute-start | bytes 786440 | tf_op jit(solution)/shard_map/ppermute | solution.py:19
  342.7 13.1 %collective-permute-start.37 = (bf16[1,4,64,512]{3,2,1,0:T(8,128)(2,1)}, bf16[1,4,64,512]{3,2,1,0:T(8,128)(2,1)S(1)}, u32[]{:S(2)}, u32[]{:S(2)}) collective-permute-start(bf16[1,4,64,512]{3,2,1,0:T(8,128)(2,1)} %get-tuple-element.206), channel_id=1, source_target_pairs={{0,3},{1,2},{2,1},{3,0},{4,7},{5,6},{6,5},{7,4},{8,11},{9,10},{10,... | collective-permute-start | bytes 786440 | tf_op jit(solution)/shard_map/ppermute | solution.py:19
  350.0 44.4 %collective-permute-start.40 = (bf16[832,256]{1,0:T(8,128)(2,1)}, bf16[832,256]{1,0:T(8,128)(2,1)}, u32[]{:S(2)}, u32[]{:S(2)}) collective-permute-start(bf16[832,256]{1,0:T(8,128)(2,1)} %pad_maximum_fusion.3), channel_id=1, source_target_pairs={{0,1},{1,0},{2,3},{3,2},{4,5},{5,4},{6,7},{7,6},{8,9},{9,8},{10,11... | collective-permute-start | bytes 1277960 | tf_op jit(solution)/shard_map/ppermute | solution.py:19
  353.2 41.2 %collective-permute-start.41 = (bf16[832,256]{1,0:T(8,128)(2,1)}, bf16[832,256]{1,0:T(8,128)(2,1)}, u32[]{:S(2)}, u32[]{:S(2)}) collective-permute-start(bf16[832,256]{1,0:T(8,128)(2,1)} %pad_maximum_fusion.4), channel_id=1, source_target_pairs={{0,2},{1,3},{2,0},{3,1},{4,6},{5,7},{6,4},{7,5},{8,10},{9,11},{10,... | collective-permute-start | bytes 1277960 | tf_op jit(solution)/shard_map/ppermute | solution.py:19
  355.8 38.5 %collective-permute-start.42 = (bf16[832,256]{1,0:T(8,128)(2,1)}, bf16[832,256]{1,0:T(8,128)(2,1)}, u32[]{:S(2)}, u32[]{:S(2)}) collective-permute-start(bf16[832,256]{1,0:T(8,128)(2,1)} %pad_maximum_fusion.5), channel_id=1, source_target_pairs={{0,3},{1,2},{2,1},{3,0},{4,7},{5,6},{6,5},{7,4},{8,11},{9,10},{10,... | collective-permute-start | bytes 1277960 | tf_op jit(solution)/shard_map/ppermute | solution.py:19
  365.1 23.6 %collective-permute-start.39 = (bf16[4,64,512]{2,1,0:T(8,128)(2,1)}, bf16[4,64,512]{2,1,0:T(8,128)(2,1)}, u32[]{:S(2)}, u32[]{:S(2)}) collective-permute-start(bf16[4,64,512]{2,1,0:T(8,128)(2,1)} %fusion.10), channel_id=1, source_target_pairs={{4,0},{8,4},{12,8},{5,1},{9,5},{13,9},{6,2},{10,6},{14,10},{7,3},{... | collective-permute-start | bytes 786440 | tf_op jit(solution)/shard_map/ppermute | solution.py:24
  392.4 7.8 %collective-permute-start.44 = (bf16[576,512]{1,0:T(8,128)(2,1)S(1)}, bf16[576,512]{1,0:T(8,128)(2,1)S(1)}, u32[]{:S(2)}, u32[]{:S(2)}) collective-permute-start(bf16[576,512]{1,0:T(8,128)(2,1)S(1)} %get-tuple-element.218), channel_id=1, source_target_pairs={{0,16},{16,0},{1,17},{17,1},{2,18},{18,2},{3,19},{19,3},{4,20},{20... | collective-permute-start | bytes 1769480 | tf_op jit(solution)/shard_map/ppermute | solution.py:19
  393.9 6.1 %collective-permute-start.49 = (f32[4,176]{1,0:T(4,128)S(1)}, f32[4,176]{1,0:T(4,128)S(1)}, u32[]{:S(2)}, u32[]{:S(2)}) collective-permute-start(f32[4,176]{1,0:T(4,128)S(1)} %fusion.23), channel_id=1, source_target_pairs={{0,16},{16,0},{1,17},{17,1},{2,18},{18,2},{3,19},{19,3},{4,20},{20... | collective-permute-start | bytes 8456 | tf_op jit(solution)/shard_map/ppermute | solution.py:19
  399.9 4.2 collective-permute-start.43
  400.5 6.7 %collective-permute-start.45 = (bf16[576,128]{1,0:T(8,128)(2,1)S(1)}, bf16[576,128]{1,0:T(8,128)(2,1)S(1)}, u32[]{:S(2)}, u32[]{:S(2)}) collective-permute-start(bf16[576,128]{1,0:T(8,128)(2,1)S(1)} %get-tuple-element.247), channel_id=1, source_target_pairs={{0,1},{1,0},{2,3},{3,2},{4,5},{5,4},{6,7},{7,6},{8,9},{9,8},{10,11... | collective-permute-start | bytes 442376 | tf_op jit(solution)/shard_map/ppermute | solution.py:19
  401.9 9.1 %collective-permute-start.46 = (bf16[576,128]{1,0:T(8,128)(2,1)S(1)}, bf16[576,128]{1,0:T(8,128)(2,1)S(1)}, u32[]{:S(2)}, u32[]{:S(2)}) collective-permute-start(bf16[576,128]{1,0:T(8,128)(2,1)S(1)} %get-tuple-element.249), channel_id=1, source_target_pairs={{0,2},{1,3},{2,0},{3,1},{4,6},{5,7},{6,4},{7,5},{8,10},{9,11},{10,... | collective-permute-start | bytes 442376 | tf_op jit(solution)/shard_map/ppermute | solution.py:19
  403.6 7.5 %collective-permute-start.47 = (bf16[576,128]{1,0:T(8,128)(2,1)S(1)}, bf16[576,128]{1,0:T(8,128)(2,1)S(1)}, u32[]{:S(2)}, u32[]{:S(2)}) collective-permute-start(bf16[576,128]{1,0:T(8,128)(2,1)S(1)} %get-tuple-element.248), channel_id=1, source_target_pairs={{0,3},{1,2},{2,1},{3,0},{4,7},{5,6},{6,5},{7,4},{8,11},{9,10},{10,... | collective-permute-start | bytes 442376 | tf_op jit(solution)/shard_map/ppermute | solution.py:19
  412.1 24.0 %all-to-all-start.1 = ((bf16[4,147,640]{2,1,0:T(8,128)(2,1)}), bf16[4,147,640]{2,1,0:T(8,128)(2,1)}, u32[]{:S(2)}, u32[]{:S(2)}) async-start(bf16[4,147,640]{2,1,0:T(8,128)(2,1)} %pad_maximum_fusion.1), calls=%async_computation.1 | async-start | bytes 1556480 | tf_op jit(solution)/shard_map/all_to_all | solution.py:28
  437.7 4.6 %collective-permute-start.50 = (f32[150,128]{1,0:T(8,128)S(1)}, f32[150,128]{1,0:T(8,128)S(1)}, u32[]{:S(2)}, u32[]{:S(2)}) collective-permute-start(f32[150,128]{1,0:T(8,128)S(1)} %get-tuple-element.262), channel_id=1, source_target_pairs={{0,1},{1,0},{2,3},{3,2},{4,5},{5,4},{6,7},{7,6},{8,9},{9,8},{10,11... | collective-permute-start | bytes 230408 | tf_op jit(solution)/shard_map/ppermute | solution.py:19
  439.5 4.5 collective-permute-start.51
  440.0 5.3 %collective-permute-start.52 = (f32[150,128]{1,0:T(8,128)S(1)}, f32[150,128]{1,0:T(8,128)S(1)}, u32[]{:S(2)}, u32[]{:S(2)}) collective-permute-start(f32[150,128]{1,0:T(8,128)S(1)} %get-tuple-element.262), channel_id=1, source_target_pairs={{0,3},{1,2},{2,1},{3,0},{4,7},{5,6},{6,5},{7,4},{8,11},{9,10},{10,... | collective-permute-start | bytes 230408 | tf_op jit(solution)/shard_map/ppermute | solution.py:19
  (67 other events, 490.9 us)
Sparse Core Ops, SparseCore 0:
  10.2 33.8 all-gather.2
  45.7 119.5 all-gather.4
  276.9 46.3 reduce-scatter.4
  325.6 86.1 reduce-scatter.2

commit v6 on v5

--- a/solution.py
+++ b/solution.py
@@ -514,7 +514,8 @@
 
 def weight_grad(core, rows, lefts, *rights):
     chunks, sets = len(lefts), len(rights)
-    step = 896 if sets == 1 and rights[0][0][0].shape[1] > 1024 else 256
+    widest = rights[0][0][0].shape[1]
+    step = 256 if sets > 1 or widest < 1024 else 512 if widest == 1024 else 896
     height = lefts[0][0].shape[1]
     width = rights[0][0][0].shape[1]
     rights = [pair for group in rights for pair in group]

time: 462 us -> 462 us (level)
  no operation moved by 1% of the time
where the time goes in v6:
time: 462 us; the launch traced here: 457 us
  waiting for transfers between devices  158 us (34%)
  Pallas kernels  142 us (31%)
  starting transfers between devices  65.5 us (14%)
  local copies, waits for them, and re-layouts  43.7 us (9%)
  other arithmetic  28.5 us (6%)
  between operations  18.3 us (4%)
    ppermute x49, waiting for transfers between devices, swap(): lax.ppermute(values, axis, [(i, i ^ bits) for i in range(lax.axis_size(ax...  92.6 us
    pallas_call x6, Pallas kernels, ffn_call(): pl.pallas_call(functools.partial(kernel, units, chunks), grid=(pl.cdiv(un...  64.9 us
    ppermute x49, starting transfers between devices, swap(): lax.ppermute(values, axis, [(i, i ^ bits) for i in range(lax.axis_size(ax...  44.7 us
    ppermute x4, waiting for transfers between devices, shifted(): lax.ppermute(values, axis, [(i, i + by) for i in range(size) if 0 <= i +...  37 us
    pallas_call x4, Pallas kernels, weight_grad(): pl.pallas_call(functools.partial(weight_grad_kernel, chunks, sets), grid=...  30.7 us
    unnamed x148, local copies, waits for them, and re-layouts  19.3 us
    all_to_all x2, waiting for transfers between devices, exchange(): return lax.all_to_all(values, axes, 0, 0, tiled=True)  14.4 us
    all_to_all x2, starting transfers between devices, exchange(): return lax.all_to_all(values, axes, 0, 0, tiled=True)  10.5 us
  transfers between devices with their start and end apart: 59, of which 31 were waited for; matrix products, arithmetic and copies ran while one was open for 11% of the time, Pallas kernels for 25%

profile of v6, /device:TPU:0, one launch (start us, length us, event | category | flops | bytes accessed | tf_op | source)
XLA Modules:
  0.0 457.1 jit_solution(12881952519110937102)
XLA Ops:
  9.4 2.6 pad_maximum_fusion
  14.2 6.3 %all-to-all-start = ((bf16[8,2,832]{2,1,0:T(2,128)(2,1)}), bf16[8,2,832]{2,1,0:T(2,128)(2,1)S(1)}, u32[]{:S(2)}, u32[]{:S(2)}) async-start(bf16[8,2,832]{2,1,0:T(2,128)(2,1)} %reshape.269), calls=%async_computation | async-start | bytes 57344 | tf_op jit(solution)/shard_map/all_to_all | solution.py:28
  35.7 1.7 copy-done.9
  40.6 3.6 all-gather.3.cloned.1.call-done
  45.7 2.4 collective-permute-start.2
  51.9 2.8 project_keys.1
  57.4 3.3 collective-permute-start.8
  60.6 2.3 collective-permute-done.2.refs_3_
  62.9 12.1 %collective-permute-done.1.refs_2_ = bf16[576,512]{1,0:T(8,128)(2,1)} collective-permute-done((bf16[576,512]{1,0:T(8,128)(2,1)S(1)}, bf16[576,512]{1,0:T(8,128)(2,1)}, u32[]{:S(2)}, u32[]{:S(2)}) %collective-permute-start.1) | collective-permute-done | bytes 589856 | tf_op jit(solution)/shard_map/ppermute | solution.py:19
  75.6 4.1 collective-permute-start.12
  79.7 11.3 %collective-permute-done.12.refs_5_ = bf16[4,64,512]{2,1,0:T(8,128)(2,1)} collective-permute-done((bf16[4,64,512]{2,1,0:T(8,128)(2,1)}, bf16[4,64,512]{2,1,0:T(8,128)(2,1)}, u32[]{:S(2)}, u32[]{:S(2)}) %collective-permute-start.12) | collective-permute-done | bytes 262176 | tf_op jit(solution)/shard_map/ppermute | solution.py:24
  98.7 2.8 assemble.1
  101.6 4.5 collective-permute-done.10.refs_3_
  106.1 1.6 collective-permute-start.15
  107.7 2.0 fusion.33.q_ref
  109.8 4.9 %collective-permute-done.13.refs_6_ = bf16[4,64,512]{2,1,0:T(8,128)(2,1)S(1)} collective-permute-done((bf16[4,64,512]{2,1,0:T(8,128)(2,1)}, bf16[4,64,512]{2,1,0:T(8,128)(2,1)S(1)}, u32[]{:S(2)}, u32[]{:S(2)}) %collective-permute-start.13) | collective-permute-done | bytes 262176 | tf_op jit(solution)/shard_map/ppermute | solution.py:19
  114.7 4.2 collective-permute-done.15.refs_8_
  118.9 4.9 %attend.1 = (bf16[256,1024]{1,0:T(8,128)(2,1)S(1)}, bf16[256,1024]{1,0:T(8,128)(2,1)S(1)}, f32[4,256,1]{2,1,0:T(8,128)S(1)}) custom-call(s32[4,64,2]{2,1,0:T(8,128)S(1)} %copy-done.18, s32[4,2,768]{2,1,0:T(2,128)S(1)} %copy-done.37, f32[256,1024]{1,0:T(8,128)S(1)} %fusion.33.q_ref, f32[1,256]{1,0:T(1,128)S(1)} %copy-done.42, f32[64,256]{1,0:T(8,128)S(1)} %copy-done.19, ...), custom_call_target="tpu_custom_call" | custom-call | flops 402653184 | bytes 4194304 | tf_op jit(solution)/shard_map/attend/pallas_call | solution.py:608
  129.4 1.5 collective-permute-start.19
  132.3 22.3 %collective-permute-done.18.refs_0_.refs_2_ = bf16[256,1152]{1,0:T(8,128)(2,1)S(1)} collective-permute-done((bf16[256,1152]{1,0:T(8,128)(2,1)S(1)}, bf16[256,1152]{1,0:T(8,128)(2,1)S(1)}, u32[]{:S(2)}, u32[]{:S(2)}) %collective-permute-start.18) | collective-permute-done | bytes 589856 | tf_op jit(solution)/shard_map/ppermute | solution.py:19
  155.5 9.9 %all-gather.5.cloned.1.call-done.refs_1_.refs_2_.refs_3_.refs_4_ = bf16[3,1152,1728]{2,1,0:T(8,128)(2,1)} async-done(((bf16[3,144,1728]{2,1,0:T(8,128)(2,1)}), bf16[3,1152,1728]{2,1,0:T(8,128)(2,1)}) %all-gather.5.cloned.1.call-update) | async-done | bytes 11943952 | tf_op jit(solution)/shard_map/all_gather | solution.py:557
  165.4 13.0 %ffn.5 = (bf16[256,1152]{1,0:T(8,128)(2,1)}, bf16[256,1152]{1,0:T(8,128)(2,1)}, bf16[512,1728]{1,0:T(8,128)(2,1)}, bf16[512,1728]{1,0:T(8,128)(2,1)}, bf16[512,1728]{1,0:T(8,128)(2,1)}) custom-call(bf16[256,1152]{1,0:T(8,128)(2,1)} %copy-done.49, bf16[256,1152]{1,0:T(8,128)(2,1)} %collective-permute-done.19.refs_1_.refs_3_, ...), custom_call_target="tpu_custom_call" | custom-call | flops 6115295232 | bytes 13123584 | tf_op jit(solution)/shard_map/ffn/pallas_call | solution.py:419
  178.4 1.8 collective-permute-start.20
  181.6 9.1 %ffn.4 = (bf16[256,1152]{1,0:T(8,128)(2,1)}, bf16[256,1728]{1,0:T(8,128)(2,1)}, bf16[256,1728]{1,0:T(8,128)(2,1)}, bf16[256,1728]{1,0:T(8,128)(2,1)}) custom-call(bf16[256,1152]{1,0:T(8,128)(2,1)} %collective-permute-done.16.refs_0_.refs_1_, bf16[3,1152,1728]{2,1,0:T(8,128)(2,1)} %all-gather.5.cloned.1.call-done.refs_1_.refs_2_.refs_3_.refs_4_, ...), custom_call_target="tpu_custom_call" | custom-call | flops 3057647616 | bytes 12533760 | tf_op jit(solution)/shard_map/ffn/pallas_call | solution.py:419
  194.1 9.4 %ffn.3 = (f32[256,1152]{1,0:T(8,128)}, bf16[256,1728]{1,0:T(8,128)(2,1)}, bf16[256,1728]{1,0:T(8,128)(2,1)}, bf16[256,1728]{1,0:T(8,128)(2,1)}) custom-call(bf16[256,1152]{1,0:T(8,128)(2,1)} %copy-done.28, bf16[3,1152,1728]{2,1,0:T(8,128)(2,1)} %all-gather.5.cloned.1.call-done.refs_1_.refs_2_.refs_3_.refs_4_, ...), custom_call_target="tpu_custom_call" | custom-call | flops 3057647616 | bytes 12533760 | tf_op jit(solution)/shard_map/ffn/pallas_call | solution.py:419
  203.5 3.1 collective-permute-done.20.refs_2_
  208.6 4.6 %loss.1 = (bf16[256,1152]{1,0:T(8,128)(2,1)}, f32[256,1152]{1,0:T(8,128)}, bf16[256,1152]{1,0:T(8,128)(2,1)}, f32[1,1152]{1,0:T(1,128)}, f32[1,128]{1,0:T(1,128)}) custom-call(f32[1]{0:T(128)} %bitcast.factor_ref, f32[256,1152]{1,0:T(8,128)} %copy-done.17, bf16[256,1152]{1,0:T(8,128)(2,1)} %bitcast.106, f32[256,1]{1,0:T(8,128)} %reshape.242.valid_ref, ...), custom_call_target="tpu_custom_call" | custom-call | flops 512 | bytes 5898240 | tf_op jit(solution)/shard_map/loss/pallas_call | solution.py:634
  213.2 1.5 collective-permute-start.23
  214.8 1.5 collective-permute-start.22
  216.7 9.4 %ffn_back.3 = (f32[256,1152]{1,0:T(8,128)}, bf16[256,1728]{1,0:T(8,128)(2,1)}, bf16[256,1728]{1,0:T(8,128)(2,1)}) custom-call(bf16[256,1152]{1,0:T(8,128)(2,1)} %get-tuple-element.167.refs_0_, bf16[3,1152,1728]{2,1,0:T(8,128)(2,1)} %all-gather.5.cloned.1.call-done.refs_1_.refs_2_.refs_3_.refs_4_, ...), custom_call_target="tpu_custom_call" | custom-call | flops 3057647616 | bytes 14303232 | tf_op jit(solution)/shard_map/ffn_back/pallas_call | solution.py:419
  226.1 3.6 collective-permute-done.23.refs_0_.refs_1_
  230.5 9.1 %ffn_back.4 = (bf16[256,1152]{1,0:T(8,128)(2,1)}, bf16[256,1728]{1,0:T(8,128)(2,1)}, bf16[256,1728]{1,0:T(8,128)(2,1)}) custom-call(bf16[256,1152]{1,0:T(8,128)(2,1)} %copy-done.50, bf16[3,1152,1728]{2,1,0:T(8,128)(2,1)} %all-gather.5.cloned.1.call-done.refs_1_.refs_2_.refs_3_.refs_4_, ...), custom_call_target="tpu_custom_call" | custom-call | flops 3057647616 | bytes 14303232 | tf_op jit(solution)/shard_map/ffn_back/pallas_call | solution.py:419
  239.6 1.8 collective-permute-done.22.refs_0_.refs_2_
  242.4 15.0 %ffn_back.5 = (bf16[256,1152]{1,0:T(8,128)(2,1)}, bf16[256,1152]{1,0:T(8,128)(2,1)}, bf16[512,1728]{1,0:T(8,128)(2,1)}, bf16[512,1728]{1,0:T(8,128)(2,1)}) custom-call(bf16[256,1152]{1,0:T(8,128)(2,1)} %copy-done.51, bf16[256,1152]{1,0:T(8,128)(2,1)} %copy-done.52, bf16[3,1152,1728]{2,1,0:T(8,128)(2,1)} %all-gather.5.cloned.1.call-done.refs_1_.refs_2_.refs_3_.refs_4_, ...), custom_call_target="tpu_custom_call" | custom-call | flops 6115295232 | bytes 16662528 | tf_op jit(solution)/shard_map/ffn_back/pallas_call | solution.py:419
  257.4 9.4 %weight_grad.4 = (bf16[576,1728]{1,0:T(8,128)(2,1)}, bf16[576,1728]{1,0:T(8,128)(2,1)}) custom-call(s32[1]{0:T(128)} %bitcast.8.core_ref, bf16[256,1152]{1,0:T(8,128)(2,1)} %get-tuple-element.167.refs_0_, bf16[256,1152]{1,0:T(8,128)(2,1)} %copy-done.50, bf16[256,1152]{1,0:T(8,128)(2,1)} %copy-done.51, bf16[256,1152]{1,0:T(8,128)(2,1)} %copy-done.52, ...), custom_call_target="tpu_custom_call" | custom-call | flops 4076863488 | bytes 6340608 | tf_op jit(solution)/shard_map/weight_grad/pallas_call | solution.py:523
  266.8 1.5 collective-permute-start.28
  272.4 4.4 pair_sum.2
  276.8 14.1 %weight_grad.5 = (bf16[576,1728]{1,0:T(8,128)(2,1)}, bf16[576,1728]{1,0:T(8,128)(2,1)}, bf16[576,1728]{1,0:T(8,128)(2,1)}, bf16[576,1728]{1,0:T(8,128)(2,1)}) custom-call(s32[1]{0:T(128)} %bitcast.8.core_ref, bf16[256,1152]{1,0:T(8,128)(2,1)} %copy-done.28, bf16[256,1152]{1,0:T(8,128)(2,1)} %collective-permute-done.16.refs_0_.refs_1_, ...), custom_call_target="tpu_custom_call" | custom-call | flops 8153726976 | bytes 10321920 | tf_op jit(solution)/shard_map/weight_grad/pallas_call | solution.py:523
  290.9 5.4 %collective-permute-done.27.refs_2_ = bf16[256,1152]{1,0:T(8,128)(2,1)} collective-permute-done((bf16[256,1152]{1,0:T(8,128)(2,1)}, bf16[256,1152]{1,0:T(8,128)(2,1)}, u32[]{:S(2)}, u32[]{:S(2)}) %collective-permute-start.27) | collective-permute-done | bytes 589856 | tf_op jit(solution)/shard_map/ppermute | solution.py:19
  296.9 6.4 %middle.1 = (f32[256,1152]{1,0:T(8,128)}, bf16[256,1152]{1,0:T(8,128)(2,1)}, bf16[256,1024]{1,0:T(8,128)(2,1)}, f32[1,1152]{1,0:T(1,128)}, f32[1,1152]{1,0:T(1,128)}) custom-call(f32[256,1152]{1,0:T(8,128)} %get-tuple-element.153.dres_ref, f32[256,1152]{1,0:T(8,128)} %copy-done.17, f32[256,1152]{1,0:T(8,128)} %copy-done.45, bf16[1152,1024]{1,0:T(8,128)(2,1)} %bitcast.101, ...), custom_call_target="tpu_custom_call" | custom-call | flops 181193932800 | bytes 2359296 | tf_op jit(solution)/shard_map/middle/pallas_call | solution.py:669
  303.8 5.9 %pair_sum.3 = bf16[2,576,1728]{2,1,0:T(8,128)(2,1)} custom-call(bf16[576,1728]{1,0:T(8,128)(2,1)} %get-tuple-element.181.refs_0_, bf16[576,1728]{1,0:T(8,128)(2,1)} %collective-permute-done.29.refs_1_, bf16[576,1728]{1,0:T(8,128)(2,1)} %get-tuple-element.183.refs_2_, bf16[576,1728]{1,0:T(8,128)(2,1)} %collective-permute-done.30.refs_3_), custom_call_target="tpu_custom_call" | custom-call | tf_op jit(solution)/shard_map/pair_sum/pallas_call | solution.py:309
  309.8 3.3 weight_grad.6
  313.5 7.2 %attend_back.1 = (bf16[256,1024]{1,0:T(8,128)(2,1)}, f32[4,1,256]{2,1,0:T(1,128)}, f32[3,4,64,512]{3,2,1,0:T(8,128)}, bf16[4,64,512]{2,1,0:T(8,128)(2,1)}, bf16[...) custom-call(s32[1]{0:T(128)} %bitcast.4.place_ref, ...), custom_call_target="tpu_custom_call" | custom-call | tf_op jit(solution)/shard_map/attend_back/pallas_call | solution.py:685
  324.4 3.3 convert_add_fusion
  328.0 2.2 collective-permute-done.32
  330.2 4.5 collective-permute-done.33
  334.7 1.5 collective-permute-done.34
  336.2 1.5 fusion.6
  345.1 3.5 collective-permute-done.35
  349.4 2.7 collective-permute-done.36
  353.0 1.5 collective-permute-done.37
  355.9 6.4 %collective-permute-done.38 = bf16[4,64,512]{2,1,0:T(8,128)(2,1)S(1)} collective-permute-done((bf16[4,64,512]{2,1,0:T(8,128)(2,1)S(1)}, bf16[4,64,512]{2,1,0:T(8,128)(2,1)S(1)}, u32[]{:S(2)}, u32[]{:S(2)}) %collective-permute-start.38) | collective-permute-done | bytes 262176 | tf_op jit(solution)/shard_map/ppermute | solution.py:24
  362.3 1.9 fusion.10
  367.0 1.6 slice.191.refs_4_
  369.5 19.3 %collective-permute-done.39 = bf16[4,64,512]{2,1,0:T(8,128)(2,1)} collective-permute-done((bf16[4,64,512]{2,1,0:T(8,128)(2,1)}, bf16[4,64,512]{2,1,0:T(8,128)(2,1)}, u32[]{:S(2)}, u32[]{:S(2)}) %collective-permute-start.39) | collective-permute-done | bytes 262176 | tf_op jit(solution)/shard_map/ppermute | solution.py:24
  389.0 3.6 finish.1
  394.5 1.5 fusion.2
  396.0 4.0 weight_grad.7
  404.3 3.1 collective-permute-done.45
  407.3 3.8 collective-permute-done.46
  412.2 4.2 all-to-all-start.1
  417.1 2.1 convert_bitcast_fusion
  422.0 14.3 %all-to-all-done.1 = bf16[4,147,640]{2,1,0:T(8,128)(2,1)} async-done(((bf16[4,147,640]{2,1,0:T(8,128)(2,1)}), bf16[4,147,640]{2,1,0:T(8,128)(2,1)}, u32[]{:S(2)}, u32[]{:S(2)}) %all-to-all-start.1) | async-done | bytes 752672 | tf_op jit(solution)/shard_map/all_to_all | solution.py:28
  437.9 1.5 collective-permute-start.50
  (334 shorter events, 99.3 us)
Async XLA Ops:
  7.2 184.7 %copy-start = (bf16[4,256,1152]{2,1,0:T(8,128)(2,1)S(1)}, bf16[4,256,1152]{2,1,0:T(8,128)(2,1)}, u32[]{:S(2)}) copy-start(bf16[4,256,1152]{2,1,0:T(8,128)(2,1)} %param.17) | copy-start | bytes 7077892
  7.2 36.9 %all-gather.3.cloned.1.call-start = ((), (), s32[]{:S(2)}) async-start(), calls=%async_computation.4 | async-start | bytes 1474560 | tf_op jit(solution)/shard_map/all_gather | solution.py:556
  9.2 156.1 %all-gather.5.cloned.1.call-start = ((), (), s32[]{:S(2)}) async-start(), calls=%async_computation.5 | async-start | bytes 13934592 | tf_op jit(solution)/shard_map/all_gather | solution.py:557
  14.2 12.8 %all-to-all-start = ((bf16[8,2,832]{2,1,0:T(2,128)(2,1)}), bf16[8,2,832]{2,1,0:T(2,128)(2,1)S(1)}, u32[]{:S(2)}, u32[]{:S(2)}) async-start(bf16[8,2,832]{2,1,0:T(2,128)(2,1)} %reshape.269), calls=%async_computation | async-start | bytes 57344 | tf_op jit(solution)/shard_map/all_to_all | solution.py:28
  20.5 396.6 %reduce-scatter.5.cloned.1.call-start = ((), (), s32[]{:S(2)}) async-start(), calls=%async_computation.7 | async-start | bytes 2580480 | tf_op jit(solution)/shard_map/reduce_scatter | solution.py:648
  32.2 93.3 %copy-start.40 = (f32[1,1152]{1,0:T(1,128)}, f32[1,1152]{1,0:T(1,128)S(1)}, u32[]{:S(2)}) copy-start(f32[1,1152]{1,0:T(1,128)S(1)} %reshape.218.gain_attn_ref) | copy-start | bytes 13828
  33.0 92.5 %copy-start.41 = (f32[1,1152]{1,0:T(1,128)}, f32[1,1152]{1,0:T(1,128)S(1)}, u32[]{:S(2)}) copy-start(f32[1,1152]{1,0:T(1,128)S(1)} %reshape.219.gain_ffn_ref) | copy-start | bytes 13828
  45.6 3.6 collective-permute-start.3
  45.7 17.2 %collective-permute-start.2 = (bf16[576,512]{1,0:T(8,128)(2,1)S(1)}, bf16[576,512]{1,0:T(8,128)(2,1)}, u32[]{:S(2)}, u32[]{:S(2)}) collective-permute-start(bf16[576,512]{1,0:T(8,128)(2,1)S(1)} %get-tuple-element.130.refs_0_), channel_id=1, source_target_pairs={{0,3},{1,2},{2,1},{3,0},{4,7},{5,6},{6,5},{7,4},{8,11},{9,10},{10,... | collective-permute-start | bytes 1769480 | tf_op jit(solution)/shard_map/ppermute | solution.py:19
  48.1 26.9 %collective-permute-start.1 = (bf16[576,512]{1,0:T(8,128)(2,1)S(1)}, bf16[576,512]{1,0:T(8,128)(2,1)}, u32[]{:S(2)}, u32[]{:S(2)}) collective-permute-start(bf16[576,512]{1,0:T(8,128)(2,1)S(1)} %get-tuple-element.130.refs_0_), channel_id=1, source_target_pairs={{0,2},{1,3},{2,0},{3,1},{4,6},{5,7},{6,4},{7,5},{8,10},{9,11},{10,... | collective-permute-start | bytes 1769480 | tf_op jit(solution)/shard_map/ppermute | solution.py:19
  48.7 26.4 %collective-permute-start = (bf16[576,512]{1,0:T(8,128)(2,1)S(1)}, bf16[576,512]{1,0:T(8,128)(2,1)}, u32[]{:S(2)}, u32[]{:S(2)}) collective-permute-start(bf16[576,512]{1,0:T(8,128)(2,1)S(1)} %get-tuple-element.130.refs_0_), channel_id=1, source_target_pairs={{0,1},{1,0},{2,3},{3,2},{4,5},{5,4},{6,7},{7,6},{8,9},{9,8},{10,11... | collective-permute-start | bytes 1769480 | tf_op jit(solution)/shard_map/ppermute | solution.py:19
  57.4 18.3 %collective-permute-start.8 = (bf16[4,64,512]{2,1,0:T(8,128)(2,1)S(1)}, bf16[4,64,512]{2,1,0:T(8,128)(2,1)}, u32[]{:S(2)}, u32[]{:S(2)}) collective-permute-start(bf16[4,64,512]{2,1,0:T(8,128)(2,1)S(1)} %get-tuple-element.129), channel_id=1, source_target_pairs={{0,4},{4,8},{8,12},{1,5},{5,9},{9,13},{2,6},{6,10},{10,14},{3,7},{... | collective-permute-start | bytes 786440 | tf_op jit(solution)/shard_map/ppermute | solution.py:24
  62.9 31.1 %collective-permute-start.7 = (bf16[576,512]{1,0:T(8,128)(2,1)}, bf16[576,512]{1,0:T(8,128)(2,1)}, u32[]{:S(2)}, u32[]{:S(2)}) collective-permute-start(bf16[576,512]{1,0:T(8,128)(2,1)} %collective-permute-done.2.refs_3_), channel_id=1, source_target_pairs={{0,16},{16,0},{1,17},{17,1},{2,18},{18,2},{3,19},{19,3},{4,20},{20... | collective-permute-start | bytes 1769480 | tf_op jit(solution)/shard_map/ppermute | solution.py:19
  75.1 20.4 %collective-permute-start.6 = (bf16[576,512]{1,0:T(8,128)(2,1)}, bf16[576,512]{1,0:T(8,128)(2,1)}, u32[]{:S(2)}, u32[]{:S(2)}) collective-permute-start(bf16[576,512]{1,0:T(8,128)(2,1)} %collective-permute-done.1.refs_2_), channel_id=1, source_target_pairs={{0,16},{16,0},{1,17},{17,1},{2,18},{18,2},{3,19},{19,3},{4,20},{20... | collective-permute-start | bytes 1769480 | tf_op jit(solution)/shard_map/ppermute | solution.py:19
  75.1 20.9 %collective-permute-start.5 = (bf16[576,512]{1,0:T(8,128)(2,1)}, bf16[576,512]{1,0:T(8,128)(2,1)}, u32[]{:S(2)}, u32[]{:S(2)}) collective-permute-start(bf16[576,512]{1,0:T(8,128)(2,1)} %collective-permute-done.refs_1_), channel_id=1, source_target_pairs={{0,16},{16,0},{1,17},{17,1},{2,18},{18,2},{3,19},{19,3},{4,20},{20... | collective-permute-start | bytes 1769480 | tf_op jit(solution)/shard_map/ppermute | solution.py:19
  75.6 21.9 %collective-permute-start.4 = (bf16[576,512]{1,0:T(8,128)(2,1)S(1)}, bf16[576,512]{1,0:T(8,128)(2,1)}, u32[]{:S(2)}, u32[]{:S(2)}) collective-permute-start(bf16[576,512]{1,0:T(8,128)(2,1)S(1)} %get-tuple-element.130.refs_0_), channel_id=1, source_target_pairs={{0,16},{16,0},{1,17},{17,1},{2,18},{18,2},{3,19},{19,3},{4,20},{20... | collective-permute-start | bytes 1769480 | tf_op jit(solution)/shard_map/ppermute | solution.py:19
  75.6 15.4 %collective-permute-start.12 = (bf16[4,64,512]{2,1,0:T(8,128)(2,1)}, bf16[4,64,512]{2,1,0:T(8,128)(2,1)}, u32[]{:S(2)}, u32[]{:S(2)}) collective-permute-start(bf16[4,64,512]{2,1,0:T(8,128)(2,1)} %collective-permute-done.8.refs_1_), channel_id=1, source_target_pairs={{0,4},{4,8},{8,12},{1,5},{5,9},{9,13},{2,6},{6,10},{10,14},{3,7},{... | collective-permute-start | bytes 786440 | tf_op jit(solution)/shard_map/ppermute | solution.py:24
  91.1 15.0 %collective-permute-start.10 = (bf16[4,64,512]{2,1,0:T(8,128)(2,1)}, bf16[4,64,512]{2,1,0:T(8,128)(2,1)}, u32[]{:S(2)}, u32[]{:S(2)}) collective-permute-start(bf16[4,64,512]{2,1,0:T(8,128)(2,1)} %collective-permute-done.8.refs_1_), channel_id=1, source_target_pairs={{0,2},{1,3},{2,0},{3,1},{4,6},{5,7},{6,4},{7,5},{8,10},{9,11},{10,... | collective-permute-start | bytes 786440 | tf_op jit(solution)/shard_map/ppermute | solution.py:19
  94.0 15.7 %collective-permute-start.11 = (bf16[4,64,512]{2,1,0:T(8,128)(2,1)}, bf16[4,64,512]{2,1,0:T(8,128)(2,1)S(1)}, u32[]{:S(2)}, u32[]{:S(2)}) collective-permute-start(bf16[4,64,512]{2,1,0:T(8,128)(2,1)} %collective-permute-done.8.refs_1_), channel_id=1, source_target_pairs={{0,3},{1,2},{2,1},{3,0},{4,7},{5,6},{6,5},{7,4},{8,11},{9,10},{10,... | collective-permute-start | bytes 786440 | tf_op jit(solution)/shard_map/ppermute | solution.py:19
  95.4 14.3 %collective-permute-start.9 = (bf16[4,64,512]{2,1,0:T(8,128)(2,1)}, bf16[4,64,512]{2,1,0:T(8,128)(2,1)S(1)}, u32[]{:S(2)}, u32[]{:S(2)}) collective-permute-start(bf16[4,64,512]{2,1,0:T(8,128)(2,1)} %collective-permute-done.8.refs_1_), channel_id=1, source_target_pairs={{0,1},{1,0},{2,3},{3,2},{4,5},{5,4},{6,7},{7,6},{8,9},{9,8},{10,11... | collective-permute-start | bytes 786440 | tf_op jit(solution)/shard_map/ppermute | solution.py:19
  96.0 18.7 %collective-permute-start.13 = (bf16[4,64,512]{2,1,0:T(8,128)(2,1)}, bf16[4,64,512]{2,1,0:T(8,128)(2,1)S(1)}, u32[]{:S(2)}, u32[]{:S(2)}) collective-permute-start(bf16[4,64,512]{2,1,0:T(8,128)(2,1)} %collective-permute-done.12.refs_5_), channel_id=1, source_target_pairs={{0,1},{1,0},{2,3},{3,2},{4,5},{5,4},{6,7},{7,6},{8,9},{9,8},{10,11... | collective-permute-start | bytes 786440 | tf_op jit(solution)/shard_map/ppermute | solution.py:19
  97.5 17.2 %collective-permute-start.14 = (bf16[4,64,512]{2,1,0:T(8,128)(2,1)}, bf16[4,64,512]{2,1,0:T(8,128)(2,1)S(1)}, u32[]{:S(2)}, u32[]{:S(2)}) collective-permute-start(bf16[4,64,512]{2,1,0:T(8,128)(2,1)} %collective-permute-done.12.refs_5_), channel_id=1, source_target_pairs={{0,2},{1,3},{2,0},{3,1},{4,6},{5,7},{6,4},{7,5},{8,10},{9,11},{10,... | collective-permute-start | bytes 786440 | tf_op jit(solution)/shard_map/ppermute | solution.py:19
  101.6 23.9 %copy-start.10 = (bf16[2,576,1024]{2,1,0:T(8,128)(2,1)}, bf16[2,576,1024]{2,1,0:T(8,128)(2,1)S(1)}, u32[]{:S(2)}) copy-start(bf16[2,576,1024]{2,1,0:T(8,128)(2,1)S(1)} %get-tuple-element.140) | copy-start | bytes 7077892
  106.1 12.8 %collective-permute-start.15 = (bf16[4,64,512]{2,1,0:T(8,128)(2,1)}, bf16[4,64,512]{2,1,0:T(8,128)(2,1)S(1)}, u32[]{:S(2)}, u32[]{:S(2)}) collective-permute-start(bf16[4,64,512]{2,1,0:T(8,128)(2,1)} %collective-permute-done.12.refs_5_), channel_id=1, source_target_pairs={{0,3},{1,2},{2,1},{3,0},{4,7},{5,6},{6,5},{7,4},{8,11},{9,10},{10,... | collective-permute-start | bytes 786440 | tf_op jit(solution)/shard_map/ppermute | solution.py:19
  128.8 49.6 %copy-start.28 = (bf16[256,1152]{1,0:T(8,128)(2,1)}, bf16[256,1152]{1,0:T(8,128)(2,1)S(1)}, u32[]{:S(2)}) copy-start(bf16[256,1152]{1,0:T(8,128)(2,1)S(1)} %get-tuple-element.173.refs_0_) | copy-start | bytes 1769476
  128.8 25.8 %collective-permute-start.18 = (bf16[256,1152]{1,0:T(8,128)(2,1)S(1)}, bf16[256,1152]{1,0:T(8,128)(2,1)S(1)}, u32[]{:S(2)}, u32[]{:S(2)}) collective-permute-start(bf16[256,1152]{1,0:T(8,128)(2,1)S(1)} %get-tuple-element.173.refs_0_), channel_id=1, source_target_pairs={{0,2},{1,3},{2,0},{3,1},{4,6},{5,7},{6,4},{7,5},{8,10},{9,11},{10,... | collective-permute-start | bytes 1769480 | tf_op jit(solution)/shard_map/ppermute | solution.py:19
  129.4 26.1 %collective-permute-start.19 = (bf16[256,1152]{1,0:T(8,128)(2,1)S(1)}, bf16[256,1152]{1,0:T(8,128)(2,1)}, u32[]{:S(2)}, u32[]{:S(2)}) collective-permute-start(bf16[256,1152]{1,0:T(8,128)(2,1)S(1)} %get-tuple-element.173.refs_0_), channel_id=1, source_target_pairs={{0,3},{1,2},{2,1},{3,0},{4,7},{5,6},{6,5},{7,4},{8,11},{9,10},{10,... | collective-permute-start | bytes 1769480 | tf_op jit(solution)/shard_map/ppermute | solution.py:19
  130.9 50.7 %collective-permute-start.16 = (bf16[256,1152]{1,0:T(8,128)(2,1)S(1)}, bf16[256,1152]{1,0:T(8,128)(2,1)}, u32[]{:S(2)}, u32[]{:S(2)}) collective-permute-start(bf16[256,1152]{1,0:T(8,128)(2,1)S(1)} %get-tuple-element.173.refs_0_), channel_id=1, source_target_pairs={{0,1},{1,0},{2,3},{3,2},{4,5},{5,4},{6,7},{7,6},{8,9},{9,8},{10,11... | collective-permute-start | bytes 1769480 | tf_op jit(solution)/shard_map/ppermute | solution.py:19
  178.4 28.3 %collective-permute-start.20 = (bf16[256,1152]{1,0:T(8,128)(2,1)}, bf16[256,1152]{1,0:T(8,128)(2,1)}, u32[]{:S(2)}, u32[]{:S(2)}) collective-permute-start(bf16[256,1152]{1,0:T(8,128)(2,1)} %get-tuple-element.148), channel_id=1, source_target_pairs={{0,2},{1,3},{2,0},{3,1},{4,6},{5,7},{6,4},{7,5},{8,10},{9,11},{10,... | collective-permute-start | bytes 1769480 | tf_op jit(solution)/shard_map/ppermute | solution.py:19
  180.2 26.5 %collective-permute-start.21 = (bf16[256,1152]{1,0:T(8,128)(2,1)}, bf16[256,1152]{1,0:T(8,128)(2,1)}, u32[]{:S(2)}, u32[]{:S(2)}) collective-permute-start(bf16[256,1152]{1,0:T(8,128)(2,1)} %get-tuple-element.149), channel_id=1, source_target_pairs={{0,3},{1,2},{2,1},{3,0},{4,7},{5,6},{6,5},{7,4},{8,11},{9,10},{10,... | collective-permute-start | bytes 1769480 | tf_op jit(solution)/shard_map/ppermute | solution.py:19
  190.7 17.1 %collective-permute-start.17 = (bf16[256,1152]{1,0:T(8,128)(2,1)}, bf16[256,1152]{1,0:T(8,128)(2,1)S(1)}, u32[]{:S(2)}, u32[]{:S(2)}) collective-permute-start(bf16[256,1152]{1,0:T(8,128)(2,1)} %get-tuple-element.147), channel_id=1, source_target_pairs={{0,1},{1,0},{2,3},{3,2},{4,5},{5,4},{6,7},{7,6},{8,9},{9,8},{10,11... | collective-permute-start | bytes 1769480 | tf_op jit(solution)/shard_map/ppermute | solution.py:19
  213.2 16.5 %collective-permute-start.23 = (bf16[256,1152]{1,0:T(8,128)(2,1)}, bf16[256,1152]{1,0:T(8,128)(2,1)S(1)}, u32[]{:S(2)}, u32[]{:S(2)}) collective-permute-start(bf16[256,1152]{1,0:T(8,128)(2,1)} %get-tuple-element.167.refs_0_), channel_id=1, source_target_pairs={{0,1},{1,0},{2,3},{3,2},{4,5},{5,4},{6,7},{7,6},{8,9},{9,8},{10,11... | collective-permute-start | bytes 1769480 | tf_op jit(solution)/shard_map/ppermute | solution.py:19
  214.8 26.6 %collective-permute-start.22 = (bf16[256,1152]{1,0:T(8,128)(2,1)}, bf16[256,1152]{1,0:T(8,128)(2,1)S(1)}, u32[]{:S(2)}, u32[]{:S(2)}) collective-permute-start(bf16[256,1152]{1,0:T(8,128)(2,1)} %get-tuple-element.167.refs_0_), channel_id=1, source_target_pairs={{0,2},{1,3},{2,0},{3,1},{4,6},{5,7},{6,4},{7,5},{8,10},{9,11},{10,... | collective-permute-start | bytes 1769480 | tf_op jit(solution)/shard_map/ppermute | solution.py:19
  216.3 25.1 %collective-permute-start.24 = (bf16[256,1152]{1,0:T(8,128)(2,1)}, bf16[256,1152]{1,0:T(8,128)(2,1)S(1)}, u32[]{:S(2)}, u32[]{:S(2)}) collective-permute-start(bf16[256,1152]{1,0:T(8,128)(2,1)} %get-tuple-element.167.refs_0_), channel_id=1, source_target_pairs={{0,3},{1,2},{2,1},{3,0},{4,7},{5,6},{6,5},{7,4},{8,11},{9,10},{10,... | collective-permute-start | bytes 1769480 | tf_op jit(solution)/shard_map/ppermute | solution.py:19
  266.7 4.3 collective-permute-start.25
  266.8 29.6 %collective-permute-start.28 = (bf16[256,1152]{1,0:T(8,128)(2,1)}, bf16[256,1152]{1,0:T(8,128)(2,1)}, u32[]{:S(2)}, u32[]{:S(2)}) collective-permute-start(bf16[256,1152]{1,0:T(8,128)(2,1)} %get-tuple-element.166), channel_id=1, source_target_pairs={{0,3},{1,2},{2,1},{3,0},{4,7},{5,6},{6,5},{7,4},{8,11},{9,10},{10,... | collective-permute-start | bytes 1769480 | tf_op jit(solution)/shard_map/ppermute | solution.py:19
  268.3 28.1 %collective-permute-start.26 = (bf16[256,1152]{1,0:T(8,128)(2,1)S(1)}, bf16[256,1152]{1,0:T(8,128)(2,1)}, u32[]{:S(2)}, u32[]{:S(2)}) collective-permute-start(bf16[256,1152]{1,0:T(8,128)(2,1)S(1)} %copy-done.71), channel_id=1, source_target_pairs={{0,1},{1,0},{2,3},{3,2},{4,5},{5,4},{6,7},{7,6},{8,9},{9,8},{10,11... | collective-permute-start | bytes 1769480 | tf_op jit(solution)/shard_map/ppermute | solution.py:19
  269.8 26.6 %collective-permute-start.27 = (bf16[256,1152]{1,0:T(8,128)(2,1)}, bf16[256,1152]{1,0:T(8,128)(2,1)}, u32[]{:S(2)}, u32[]{:S(2)}) collective-permute-start(bf16[256,1152]{1,0:T(8,128)(2,1)} %get-tuple-element.185), channel_id=1, source_target_pairs={{0,2},{1,3},{2,0},{3,1},{4,6},{5,7},{6,4},{7,5},{8,10},{9,11},{10,... | collective-permute-start | bytes 1769480 | tf_op jit(solution)/shard_map/ppermute | solution.py:19
  276.8 142.4 %reduce-scatter.3.cloned.1.call-start = ((), (), s32[]{:S(2)}) async-start(), calls=%async_computation.6 | async-start | bytes 5160960 | tf_op jit(solution)/shard_map/reduce_scatter | solution.py:648
  296.4 7.0 %collective-permute-start.30 = (bf16[576,1728]{1,0:T(8,128)(2,1)}, bf16[576,1728]{1,0:T(8,128)(2,1)}, u32[]{:S(2)}, u32[]{:S(2)}) collective-permute-start(bf16[576,1728]{1,0:T(8,128)(2,1)} %get-tuple-element.190), channel_id=1, source_target_pairs={{0,16},{16,0},{1,17},{17,1},{2,18},{18,2},{3,19},{19,3},{4,20},{20... | collective-permute-start | bytes 5971976 | tf_op jit(solution)/shard_map/ppermute | solution.py:19
  296.4 7.4 %collective-permute-start.29 = (bf16[576,1728]{1,0:T(8,128)(2,1)}, bf16[576,1728]{1,0:T(8,128)(2,1)}, u32[]{:S(2)}, u32[]{:S(2)}) collective-permute-start(bf16[576,1728]{1,0:T(8,128)(2,1)} %get-tuple-element.187), channel_id=1, source_target_pairs={{0,16},{16,0},{1,17},{17,1},{2,18},{18,2},{3,19},{19,3},{4,20},{20... | collective-permute-start | bytes 5971976 | tf_op jit(solution)/shard_map/ppermute | solution.py:19
  313.0 11.3 %collective-permute-start.31 = (bf16[576,1024]{1,0:T(8,128)(2,1)}, bf16[576,1024]{1,0:T(8,128)(2,1)}, u32[]{:S(2)}, u32[]{:S(2)}) collective-permute-start(bf16[576,1024]{1,0:T(8,128)(2,1)} %get-tuple-element.193), channel_id=1, source_target_pairs={{0,16},{16,0},{1,17},{17,1},{2,18},{18,2},{3,19},{19,3},{4,20},{20... | collective-permute-start | bytes 3538952 | tf_op jit(solution)/shard_map/ppermute | solution.py:19
  320.8 9.4 %collective-permute-start.32 = (bf16[4,64,512]{2,1,0:T(8,128)(2,1)}, bf16[4,64,512]{2,1,0:T(8,128)(2,1)S(1)}, u32[]{:S(2)}, u32[]{:S(2)}) collective-permute-start(bf16[4,64,512]{2,1,0:T(8,128)(2,1)} %get-tuple-element.199), channel_id=1, source_target_pairs={{0,1},{1,0},{2,3},{3,2},{4,5},{5,4},{6,7},{7,6},{8,9},{9,8},{10,11... | collective-permute-start | bytes 786440 | tf_op jit(solution)/shard_map/ppermute | solution.py:19
  321.8 12.9 %collective-permute-start.33 = (bf16[4,64,512]{2,1,0:T(8,128)(2,1)}, bf16[4,64,512]{2,1,0:T(8,128)(2,1)S(1)}, u32[]{:S(2)}, u32[]{:S(2)}) collective-permute-start(bf16[4,64,512]{2,1,0:T(8,128)(2,1)} %get-tuple-element.200), channel_id=1, source_target_pairs={{0,2},{1,3},{2,0},{3,1},{4,6},{5,7},{6,4},{7,5},{8,10},{9,11},{10,... | collective-permute-start | bytes 786440 | tf_op jit(solution)/shard_map/ppermute | solution.py:19
  322.9 13.3 %collective-permute-start.34 = (bf16[4,64,512]{2,1,0:T(8,128)(2,1)}, bf16[4,64,512]{2,1,0:T(8,128)(2,1)}, u32[]{:S(2)}, u32[]{:S(2)}) collective-permute-start(bf16[4,64,512]{2,1,0:T(8,128)(2,1)} %get-tuple-element.201), channel_id=1, source_target_pairs={{0,3},{1,2},{2,1},{3,0},{4,7},{5,6},{6,5},{7,4},{8,11},{9,10},{10,... | collective-permute-start | bytes 786440 | tf_op jit(solution)/shard_map/ppermute | solution.py:19
  327.9 41.6 %collective-permute-start.48 = (f32[4,465]{1,0:T(4,128)S(1)}, f32[4,465]{1,0:T(4,128)S(1)}, u32[]{:S(2)}, u32[]{:S(2)}) collective-permute-start(f32[4,465]{1,0:T(4,128)S(1)} %dynamic-slice_bitcast_fusion.4), channel_id=1, source_target_pairs={{0,16},{16,0},{1,17},{17,1},{2,18},{18,2},{3,19},{19,3},{4,20},{20... | collective-permute-start | bytes 22328 | tf_op jit(solution)/shard_map/ppermute | solution.py:19
  337.8 24.5 %collective-permute-start.38 = (bf16[4,64,512]{2,1,0:T(8,128)(2,1)S(1)}, bf16[4,64,512]{2,1,0:T(8,128)(2,1)S(1)}, u32[]{:S(2)}, u32[]{:S(2)}) collective-permute-start(bf16[4,64,512]{2,1,0:T(8,128)(2,1)S(1)} %get-tuple-element.236), channel_id=1, source_target_pairs={{4,0},{8,4},{12,8},{5,1},{9,5},{13,9},{6,2},{10,6},{14,10},{7,3},{... | collective-permute-start | bytes 786440 | tf_op jit(solution)/shard_map/ppermute | solution.py:24
  339.1 9.5 %collective-permute-start.35 = (bf16[1,4,64,512]{3,2,1,0:T(8,128)(2,1)}, bf16[1,4,64,512]{3,2,1,0:T(8,128)(2,1)S(1)}, u32[]{:S(2)}, u32[]{:S(2)}) collective-permute-start(bf16[1,4,64,512]{3,2,1,0:T(8,128)(2,1)} %get-tuple-element.202), channel_id=1, source_target_pairs={{0,1},{1,0},{2,3},{3,2},{4,5},{5,4},{6,7},{7,6},{8,9},{9,8},{10,11... | collective-permute-start | bytes 786440 | tf_op jit(solution)/shard_map/ppermute | solution.py:19
  339.9 12.1 %collective-permute-start.36 = (bf16[1,4,64,512]{3,2,1,0:T(8,128)(2,1)}, bf16[1,4,64,512]{3,2,1,0:T(8,128)(2,1)S(1)}, u32[]{:S(2)}, u32[]{:S(2)}) collective-permute-start(bf16[1,4,64,512]{3,2,1,0:T(8,128)(2,1)} %get-tuple-element.204), channel_id=1, source_target_pairs={{0,2},{1,3},{2,0},{3,1},{4,6},{5,7},{6,4},{7,5},{8,10},{9,11},{10,... | collective-permute-start | bytes 786440 | tf_op jit(solution)/shard_map/ppermute | solution.py:19
  341.4 13.2 %collective-permute-start.37 = (bf16[1,4,64,512]{3,2,1,0:T(8,128)(2,1)}, bf16[1,4,64,512]{3,2,1,0:T(8,128)(2,1)S(1)}, u32[]{:S(2)}, u32[]{:S(2)}) collective-permute-start(bf16[1,4,64,512]{3,2,1,0:T(8,128)(2,1)} %get-tuple-element.206), channel_id=1, source_target_pairs={{0,3},{1,2},{2,1},{3,0},{4,7},{5,6},{6,5},{7,4},{8,11},{9,10},{10,... | collective-permute-start | bytes 786440 | tf_op jit(solution)/shard_map/ppermute | solution.py:19
  348.6 45.9 %collective-permute-start.40 = (bf16[832,256]{1,0:T(8,128)(2,1)}, bf16[832,256]{1,0:T(8,128)(2,1)}, u32[]{:S(2)}, u32[]{:S(2)}) collective-permute-start(bf16[832,256]{1,0:T(8,128)(2,1)} %pad_maximum_fusion.3), channel_id=1, source_target_pairs={{0,1},{1,0},{2,3},{3,2},{4,5},{5,4},{6,7},{7,6},{8,9},{9,8},{10,11... | collective-permute-start | bytes 1277960 | tf_op jit(solution)/shard_map/ppermute | solution.py:19
  352.1 42.5 %collective-permute-start.41 = (bf16[832,256]{1,0:T(8,128)(2,1)}, bf16[832,256]{1,0:T(8,128)(2,1)}, u32[]{:S(2)}, u32[]{:S(2)}) collective-permute-start(bf16[832,256]{1,0:T(8,128)(2,1)} %pad_maximum_fusion.4), channel_id=1, source_target_pairs={{0,2},{1,3},{2,0},{3,1},{4,6},{5,7},{6,4},{7,5},{8,10},{9,11},{10,... | collective-permute-start | bytes 1277960 | tf_op jit(solution)/shard_map/ppermute | solution.py:19
  354.5 40.0 %collective-permute-start.42 = (bf16[832,256]{1,0:T(8,128)(2,1)}, bf16[832,256]{1,0:T(8,128)(2,1)}, u32[]{:S(2)}, u32[]{:S(2)}) collective-permute-start(bf16[832,256]{1,0:T(8,128)(2,1)} %pad_maximum_fusion.5), channel_id=1, source_target_pairs={{0,3},{1,2},{2,1},{3,0},{4,7},{5,6},{6,5},{7,4},{8,11},{9,10},{10,... | collective-permute-start | bytes 1277960 | tf_op jit(solution)/shard_map/ppermute | solution.py:19
  364.2 24.6 %collective-permute-start.39 = (bf16[4,64,512]{2,1,0:T(8,128)(2,1)}, bf16[4,64,512]{2,1,0:T(8,128)(2,1)}, u32[]{:S(2)}, u32[]{:S(2)}) collective-permute-start(bf16[4,64,512]{2,1,0:T(8,128)(2,1)} %fusion.10), channel_id=1, source_target_pairs={{4,0},{8,4},{12,8},{5,1},{9,5},{13,9},{6,2},{10,6},{14,10},{7,3},{... | collective-permute-start | bytes 786440 | tf_op jit(solution)/shard_map/ppermute | solution.py:24
  392.5 7.8 %collective-permute-start.44 = (bf16[576,512]{1,0:T(8,128)(2,1)S(1)}, bf16[576,512]{1,0:T(8,128)(2,1)S(1)}, u32[]{:S(2)}, u32[]{:S(2)}) collective-permute-start(bf16[576,512]{1,0:T(8,128)(2,1)S(1)} %get-tuple-element.218), channel_id=1, source_target_pairs={{0,16},{16,0},{1,17},{17,1},{2,18},{18,2},{3,19},{19,3},{4,20},{20... | collective-permute-start | bytes 1769480 | tf_op jit(solution)/shard_map/ppermute | solution.py:19
  394.0 6.0 %collective-permute-start.49 = (f32[4,176]{1,0:T(4,128)S(1)}, f32[4,176]{1,0:T(4,128)S(1)}, u32[]{:S(2)}, u32[]{:S(2)}) collective-permute-start(f32[4,176]{1,0:T(4,128)S(1)} %fusion.23), channel_id=1, source_target_pairs={{0,16},{16,0},{1,17},{17,1},{2,18},{18,2},{3,19},{19,3},{4,20},{20... | collective-permute-start | bytes 8456 | tf_op jit(solution)/shard_map/ppermute | solution.py:19
  400.0 4.1 collective-permute-start.43
  400.6 6.7 %collective-permute-start.45 = (bf16[576,128]{1,0:T(8,128)(2,1)S(1)}, bf16[576,128]{1,0:T(8,128)(2,1)S(1)}, u32[]{:S(2)}, u32[]{:S(2)}) collective-permute-start(bf16[576,128]{1,0:T(8,128)(2,1)S(1)} %get-tuple-element.247), channel_id=1, source_target_pairs={{0,1},{1,0},{2,3},{3,2},{4,5},{5,4},{6,7},{7,6},{8,9},{9,8},{10,11... | collective-permute-start | bytes 442376 | tf_op jit(solution)/shard_map/ppermute | solution.py:19
  402.0 9.1 %collective-permute-start.46 = (bf16[576,128]{1,0:T(8,128)(2,1)S(1)}, bf16[576,128]{1,0:T(8,128)(2,1)S(1)}, u32[]{:S(2)}, u32[]{:S(2)}) collective-permute-start(bf16[576,128]{1,0:T(8,128)(2,1)S(1)} %get-tuple-element.249), channel_id=1, source_target_pairs={{0,2},{1,3},{2,0},{3,1},{4,6},{5,7},{6,4},{7,5},{8,10},{9,11},{10,... | collective-permute-start | bytes 442376 | tf_op jit(solution)/shard_map/ppermute | solution.py:19
  403.5 7.6 %collective-permute-start.47 = (bf16[576,128]{1,0:T(8,128)(2,1)S(1)}, bf16[576,128]{1,0:T(8,128)(2,1)S(1)}, u32[]{:S(2)}, u32[]{:S(2)}) collective-permute-start(bf16[576,128]{1,0:T(8,128)(2,1)S(1)} %get-tuple-element.248), channel_id=1, source_target_pairs={{0,3},{1,2},{2,1},{3,0},{4,7},{5,6},{6,5},{7,4},{8,11},{9,10},{10,... | collective-permute-start | bytes 442376 | tf_op jit(solution)/shard_map/ppermute | solution.py:19
  412.2 24.1 %all-to-all-start.1 = ((bf16[4,147,640]{2,1,0:T(8,128)(2,1)}), bf16[4,147,640]{2,1,0:T(8,128)(2,1)}, u32[]{:S(2)}, u32[]{:S(2)}) async-start(bf16[4,147,640]{2,1,0:T(8,128)(2,1)} %pad_maximum_fusion.1), calls=%async_computation.1 | async-start | bytes 1556480 | tf_op jit(solution)/shard_map/all_to_all | solution.py:28
  437.9 4.9 %collective-permute-start.50 = (f32[150,128]{1,0:T(8,128)S(1)}, f32[150,128]{1,0:T(8,128)S(1)}, u32[]{:S(2)}, u32[]{:S(2)}) collective-permute-start(f32[150,128]{1,0:T(8,128)S(1)} %get-tuple-element.262), channel_id=1, source_target_pairs={{0,1},{1,0},{2,3},{3,2},{4,5},{5,4},{6,7},{7,6},{8,9},{9,8},{10,11... | collective-permute-start | bytes 230408 | tf_op jit(solution)/shard_map/ppermute | solution.py:19
  439.4 4.6 %collective-permute-start.51 = (f32[150,128]{1,0:T(8,128)S(1)}, f32[150,128]{1,0:T(8,128)S(1)}, u32[]{:S(2)}, u32[]{:S(2)}) collective-permute-start(f32[150,128]{1,0:T(8,128)S(1)} %get-tuple-element.262), channel_id=1, source_target_pairs={{0,2},{1,3},{2,0},{3,1},{4,6},{5,7},{6,4},{7,5},{8,10},{9,11},{10,... | collective-permute-start | bytes 230408 | tf_op jit(solution)/shard_map/ppermute | solution.py:19
  440.1 5.3 %collective-permute-start.52 = (f32[150,128]{1,0:T(8,128)S(1)}, f32[150,128]{1,0:T(8,128)S(1)}, u32[]{:S(2)}, u32[]{:S(2)}) collective-permute-start(f32[150,128]{1,0:T(8,128)S(1)} %get-tuple-element.262), channel_id=1, source_target_pairs={{0,3},{1,2},{2,1},{3,0},{4,7},{5,6},{6,5},{7,4},{8,11},{9,10},{10,... | collective-permute-start | bytes 230408 | tf_op jit(solution)/shard_map/ppermute | solution.py:19
  (67 other events, 494.4 us)
Sparse Core Ops, SparseCore 0:
  10.2 33.8 all-gather.2
  45.7 119.5 all-gather.4
  276.9 46.3 reduce-scatter.4
  325.6 86.1 reduce-scatter.2

commit v7 on v6

--- a/solution.py
+++ b/solution.py
@@ -354,13 +354,19 @@
             block(rest)
 
 
+def add_up(ref, values):
+    @pl.when(pl.program_id(0) == 0)
+    def _():
+        ref[...] = values
+
+    @pl.when(pl.program_id(0) > 0)
+    def _():
+        ref[...] += values
+
+
 def ffn_kernel(units, chunks, *refs):
     rows_refs, (gate_ref, up_ref, down_ref) = refs[:chunks], refs[chunks : chunks + 3]
     part_refs, (act_ref, slope_ref, curve_ref, sums) = refs[chunks + 3 : 2 * chunks + 3], refs[2 * chunks + 3 :]
-
-    @pl.when(pl.program_id(0) == 0)
-    def _():
-        sums[...] = jnp.zeros_like(sums)
 
     def block(size):
         rows = jnp.concatenate([r[...] for r in rows_refs], axis=0)
@@ -375,7 +381,7 @@
         act_ref[:, :size] = act
         slope_ref[:, :size] = (slope * up).astype(LOW)
         curve_ref[:, :size] = curve.astype(LOW)
-        sums[...] += mm_t(act, down_ref[0, :, :size])
+        add_up(sums, mm_t(act, down_ref[0, :, :size]))
 
     for_blocks(units, act_ref.shape[1], block)
     split_rows(sums, part_refs)
@@ -392,10 +398,6 @@
 def ffn_back_kernel(units, chunks, *refs):
     rows_refs, (gate_ref, up_ref, down_ref, slope_ref, curve_ref) = refs[:chunks], refs[chunks : chunks + 5]
     part_refs, (dgate_ref, dup_ref, sums) = refs[chunks + 5 : 2 * chunks + 5], refs[2 * chunks + 5 :]
-
-    @pl.when(pl.program_id(0) == 0)
-    def _():
-        sums[...] = jnp.zeros_like(sums)
 
     def block(size):
         rows = jnp.concatenate([r[...] for r in rows_refs], axis=0)
@@ -404,7 +406,7 @@
         d_up = (d_act * curve_ref[:, :size].astype(F32)).astype(LOW)
         dgate_ref[:, :size] = d_gate
         dup_ref[:, :size] = d_up
-        sums[...] += mm_t(d_gate, gate_ref[0, :, :size]) + mm_t(d_up, up_ref[0, :, :size])
+        add_up(sums, mm_t(d_gate, gate_ref[0, :, :size]) + mm_t(d_up, up_ref[0, :, :size]))
 
     for_blocks(units, dgate_ref.shape[1], block)
     split_rows(sums, part_refs)

time: 462 us -> 464 us (level)
  no operation moved by 1% of the time
where the time goes in v7:
time: 464 us; the launch traced here: 458 us
  waiting for transfers between devices  156 us (34%)
  Pallas kernels  144 us (31%)
  starting transfers between devices  65.4 us (14%)
  local copies, waits for them, and re-layouts  43.7 us (9%)
  other arithmetic  28.5 us (6%)
  between operations  18.2 us (4%)
    ppermute x49, waiting for transfers between devices, swap(): lax.ppermute(values, axis, [(i, i ^ bits) for i in range(lax.axis_size(ax...  91.6 us
    pallas_call x6, Pallas kernels, ffn_call(): pl.pallas_call(functools.partial(kernel, units, chunks), grid=(pl.cdiv(un...  67.3 us
    ppermute x49, starting transfers between devices, swap(): lax.ppermute(values, axis, [(i, i ^ bits) for i in range(lax.axis_size(ax...  44.3 us
    ppermute x4, waiting for transfers between devices, shifted(): lax.ppermute(values, axis, [(i, i + by) for i in range(size) if 0 <= i +...  36.7 us
    pallas_call x4, Pallas kernels, weight_grad(): pl.pallas_call(functools.partial(weight_grad_kernel, chunks, sets), grid=...  30.9 us
    unnamed x148, local copies, waits for them, and re-layouts  19.3 us
    all_to_all x2, waiting for transfers between devices, exchange(): return lax.all_to_all(values, axes, 0, 0, tiled=True)  14.4 us
    all_to_all x2, starting transfers between devices, exchange(): return lax.all_to_all(values, axes, 0, 0, tiled=True)  10.5 us
  transfers between devices with their start and end apart: 59, of which 31 were waited for; matrix products, arithmetic and copies ran while one was open for 11% of the time, Pallas kernels for 25%

profile of v7, /device:TPU:0, one launch (start us, length us, event | category | flops | bytes accessed | tf_op | source)
XLA Modules:
  0.0 458.2 jit_solution(14604584907132968659)
XLA Ops:
  9.4 2.6 pad_maximum_fusion
  14.2 6.3 %all-to-all-start = ((bf16[8,2,832]{2,1,0:T(2,128)(2,1)}), bf16[8,2,832]{2,1,0:T(2,128)(2,1)S(1)}, u32[]{:S(2)}, u32[]{:S(2)}) async-start(bf16[8,2,832]{2,1,0:T(2,128)(2,1)} %reshape.269), calls=%async_computation | async-start | bytes 57344 | tf_op jit(solution)/shard_map/all_to_all | solution.py:28
  35.7 1.7 copy-done.9
  40.6 3.6 all-gather.3.cloned.1.call-done
  45.7 2.4 collective-permute-start.2
  51.9 2.8 project_keys.1
  57.4 3.3 collective-permute-start.8
  60.6 2.3 collective-permute-done.2.refs_3_
  62.9 12.1 %collective-permute-done.1.refs_2_ = bf16[576,512]{1,0:T(8,128)(2,1)} collective-permute-done((bf16[576,512]{1,0:T(8,128)(2,1)S(1)}, bf16[576,512]{1,0:T(8,128)(2,1)}, u32[]{:S(2)}, u32[]{:S(2)}) %collective-permute-start.1) | collective-permute-done | bytes 589856 | tf_op jit(solution)/shard_map/ppermute | solution.py:19
  75.6 4.4 collective-permute-start.12
  80.1 11.0 %collective-permute-done.12.refs_5_ = bf16[4,64,512]{2,1,0:T(8,128)(2,1)} collective-permute-done((bf16[4,64,512]{2,1,0:T(8,128)(2,1)}, bf16[4,64,512]{2,1,0:T(8,128)(2,1)}, u32[]{:S(2)}, u32[]{:S(2)}) %collective-permute-start.12) | collective-permute-done | bytes 262176 | tf_op jit(solution)/shard_map/ppermute | solution.py:24
  98.7 2.8 assemble.1
  101.6 4.5 collective-permute-done.10.refs_3_
  106.1 1.6 collective-permute-start.15
  107.7 2.0 fusion.33.q_ref
  109.8 4.9 %collective-permute-done.13.refs_6_ = bf16[4,64,512]{2,1,0:T(8,128)(2,1)S(1)} collective-permute-done((bf16[4,64,512]{2,1,0:T(8,128)(2,1)}, bf16[4,64,512]{2,1,0:T(8,128)(2,1)S(1)}, u32[]{:S(2)}, u32[]{:S(2)}) %collective-permute-start.13) | collective-permute-done | bytes 262176 | tf_op jit(solution)/shard_map/ppermute | solution.py:19
  114.7 4.2 collective-permute-done.15.refs_8_
  118.9 4.9 %attend.1 = (bf16[256,1024]{1,0:T(8,128)(2,1)S(1)}, bf16[256,1024]{1,0:T(8,128)(2,1)S(1)}, f32[4,256,1]{2,1,0:T(8,128)S(1)}) custom-call(s32[4,64,2]{2,1,0:T(8,128)S(1)} %copy-done.18, s32[4,2,768]{2,1,0:T(2,128)S(1)} %copy-done.37, f32[256,1024]{1,0:T(8,128)S(1)} %fusion.33.q_ref, f32[1,256]{1,0:T(1,128)S(1)} %copy-done.42, f32[64,256]{1,0:T(8,128)S(1)} %copy-done.19, ...), custom_call_target="tpu_custom_call" | custom-call | flops 402653184 | bytes 4194304 | tf_op jit(solution)/shard_map/attend/pallas_call | solution.py:610
  129.4 1.5 collective-permute-start.19
  132.3 22.3 %collective-permute-done.18.refs_0_.refs_2_ = bf16[256,1152]{1,0:T(8,128)(2,1)S(1)} collective-permute-done((bf16[256,1152]{1,0:T(8,128)(2,1)S(1)}, bf16[256,1152]{1,0:T(8,128)(2,1)S(1)}, u32[]{:S(2)}, u32[]{:S(2)}) %collective-permute-start.18) | collective-permute-done | bytes 589856 | tf_op jit(solution)/shard_map/ppermute | solution.py:19
  155.5 9.9 %all-gather.5.cloned.1.call-done.refs_1_.refs_2_.refs_3_.refs_4_ = bf16[3,1152,1728]{2,1,0:T(8,128)(2,1)} async-done(((bf16[3,144,1728]{2,1,0:T(8,128)(2,1)}), bf16[3,1152,1728]{2,1,0:T(8,128)(2,1)}) %all-gather.5.cloned.1.call-update) | async-done | bytes 11943952 | tf_op jit(solution)/shard_map/all_gather | solution.py:559
  165.4 13.7 %ffn.5 = (bf16[256,1152]{1,0:T(8,128)(2,1)}, bf16[256,1152]{1,0:T(8,128)(2,1)}, bf16[512,1728]{1,0:T(8,128)(2,1)}, bf16[512,1728]{1,0:T(8,128)(2,1)}, bf16[512,1728]{1,0:T(8,128)(2,1)}) custom-call(bf16[256,1152]{1,0:T(8,128)(2,1)} %copy-done.49, bf16[256,1152]{1,0:T(8,128)(2,1)} %collective-permute-done.19.refs_1_.refs_3_, ...), custom_call_target="tpu_custom_call" | custom-call | flops 6115295232 | bytes 13123584 | tf_op jit(solution)/shard_map/ffn/pallas_call | solution.py:421
  179.1 1.8 collective-permute-start.20
  182.3 9.5 %ffn.4 = (bf16[256,1152]{1,0:T(8,128)(2,1)}, bf16[256,1728]{1,0:T(8,128)(2,1)}, bf16[256,1728]{1,0:T(8,128)(2,1)}, bf16[256,1728]{1,0:T(8,128)(2,1)}) custom-call(bf16[256,1152]{1,0:T(8,128)(2,1)} %collective-permute-done.16.refs_0_.refs_1_, bf16[3,1152,1728]{2,1,0:T(8,128)(2,1)} %all-gather.5.cloned.1.call-done.refs_1_.refs_2_.refs_3_.refs_4_, ...), custom_call_target="tpu_custom_call" | custom-call | flops 3057647616 | bytes 12533760 | tf_op jit(solution)/shard_map/ffn/pallas_call | solution.py:421
  195.2 9.4 %ffn.3 = (f32[256,1152]{1,0:T(8,128)}, bf16[256,1728]{1,0:T(8,128)(2,1)}, bf16[256,1728]{1,0:T(8,128)(2,1)}, bf16[256,1728]{1,0:T(8,128)(2,1)}) custom-call(bf16[256,1152]{1,0:T(8,128)(2,1)} %copy-done.28, bf16[3,1152,1728]{2,1,0:T(8,128)(2,1)} %all-gather.5.cloned.1.call-done.refs_1_.refs_2_.refs_3_.refs_4_, ...), custom_call_target="tpu_custom_call" | custom-call | flops 3057647616 | bytes 12533760 | tf_op jit(solution)/shard_map/ffn/pallas_call | solution.py:421
  204.6 2.7 collective-permute-done.20.refs_2_
  209.3 4.6 loss.1
  213.9 1.5 collective-permute-start.23
  215.4 1.5 collective-permute-start.22
  217.4 9.7 %ffn_back.3 = (f32[256,1152]{1,0:T(8,128)}, bf16[256,1728]{1,0:T(8,128)(2,1)}, bf16[256,1728]{1,0:T(8,128)(2,1)}) custom-call(bf16[256,1152]{1,0:T(8,128)(2,1)} %get-tuple-element.167.refs_0_, bf16[3,1152,1728]{2,1,0:T(8,128)(2,1)} %all-gather.5.cloned.1.call-done.refs_1_.refs_2_.refs_3_.refs_4_, ...), custom_call_target="tpu_custom_call" | custom-call | flops 3057647616 | bytes 14303232 | tf_op jit(solution)/shard_map/ffn_back/pallas_call | solution.py:421
  227.1 3.3 collective-permute-done.23.refs_0_.refs_1_
  231.2 9.6 %ffn_back.4 = (bf16[256,1152]{1,0:T(8,128)(2,1)}, bf16[256,1728]{1,0:T(8,128)(2,1)}, bf16[256,1728]{1,0:T(8,128)(2,1)}) custom-call(bf16[256,1152]{1,0:T(8,128)(2,1)} %copy-done.50, bf16[3,1152,1728]{2,1,0:T(8,128)(2,1)} %all-gather.5.cloned.1.call-done.refs_1_.refs_2_.refs_3_.refs_4_, ...), custom_call_target="tpu_custom_call" | custom-call | flops 3057647616 | bytes 14303232 | tf_op jit(solution)/shard_map/ffn_back/pallas_call | solution.py:421
  243.1 15.4 %ffn_back.5 = (bf16[256,1152]{1,0:T(8,128)(2,1)}, bf16[256,1152]{1,0:T(8,128)(2,1)}, bf16[512,1728]{1,0:T(8,128)(2,1)}, bf16[512,1728]{1,0:T(8,128)(2,1)}) custom-call(bf16[256,1152]{1,0:T(8,128)(2,1)} %copy-done.51, bf16[256,1152]{1,0:T(8,128)(2,1)} %copy-done.52, bf16[3,1152,1728]{2,1,0:T(8,128)(2,1)} %all-gather.5.cloned.1.call-done.refs_1_.refs_2_.refs_3_.refs_4_, ...), custom_call_target="tpu_custom_call" | custom-call | flops 6115295232 | bytes 16662528 | tf_op jit(solution)/shard_map/ffn_back/pallas_call | solution.py:421
  258.5 9.4 %weight_grad.4 = (bf16[576,1728]{1,0:T(8,128)(2,1)}, bf16[576,1728]{1,0:T(8,128)(2,1)}) custom-call(s32[1]{0:T(128)} %bitcast.8.core_ref, bf16[256,1152]{1,0:T(8,128)(2,1)} %get-tuple-element.167.refs_0_, bf16[256,1152]{1,0:T(8,128)(2,1)} %copy-done.50, bf16[256,1152]{1,0:T(8,128)(2,1)} %copy-done.51, bf16[256,1152]{1,0:T(8,128)(2,1)} %copy-done.52, ...), custom_call_target="tpu_custom_call" | custom-call | flops 4076863488 | bytes 6340608 | tf_op jit(solution)/shard_map/weight_grad/pallas_call | solution.py:525
  267.9 1.5 collective-permute-start.28
  273.5 4.4 pair_sum.2
  278.0 14.3 %weight_grad.5 = (bf16[576,1728]{1,0:T(8,128)(2,1)}, bf16[576,1728]{1,0:T(8,128)(2,1)}, bf16[576,1728]{1,0:T(8,128)(2,1)}, bf16[576,1728]{1,0:T(8,128)(2,1)}) custom-call(s32[1]{0:T(128)} %bitcast.8.core_ref, bf16[256,1152]{1,0:T(8,128)(2,1)} %copy-done.28, bf16[256,1152]{1,0:T(8,128)(2,1)} %collective-permute-done.16.refs_0_.refs_1_, ...), custom_call_target="tpu_custom_call" | custom-call | flops 8153726976 | bytes 10321920 | tf_op jit(solution)/shard_map/weight_grad/pallas_call | solution.py:525
  292.3 5.2 %collective-permute-done.27.refs_2_ = bf16[256,1152]{1,0:T(8,128)(2,1)} collective-permute-done((bf16[256,1152]{1,0:T(8,128)(2,1)}, bf16[256,1152]{1,0:T(8,128)(2,1)}, u32[]{:S(2)}, u32[]{:S(2)}) %collective-permute-start.27) | collective-permute-done | bytes 589856 | tf_op jit(solution)/shard_map/ppermute | solution.py:19
  298.1 6.5 %middle.1 = (f32[256,1152]{1,0:T(8,128)}, bf16[256,1152]{1,0:T(8,128)(2,1)}, bf16[256,1024]{1,0:T(8,128)(2,1)}, f32[1,1152]{1,0:T(1,128)}, f32[1,1152]{1,0:T(1,128)}) custom-call(f32[256,1152]{1,0:T(8,128)} %get-tuple-element.153.dres_ref, f32[256,1152]{1,0:T(8,128)} %copy-done.17, f32[256,1152]{1,0:T(8,128)} %copy-done.45, bf16[1152,1024]{1,0:T(8,128)(2,1)} %bitcast.101, ...), custom_call_target="tpu_custom_call" | custom-call | flops 181193932800 | bytes 2359296 | tf_op jit(solution)/shard_map/middle/pallas_call | solution.py:671
  305.0 5.9 %pair_sum.3 = bf16[2,576,1728]{2,1,0:T(8,128)(2,1)} custom-call(bf16[576,1728]{1,0:T(8,128)(2,1)} %get-tuple-element.181.refs_0_, bf16[576,1728]{1,0:T(8,128)(2,1)} %collective-permute-done.29.refs_1_, bf16[576,1728]{1,0:T(8,128)(2,1)} %get-tuple-element.183.refs_2_, bf16[576,1728]{1,0:T(8,128)(2,1)} %collective-permute-done.30.refs_3_), custom_call_target="tpu_custom_call" | custom-call | tf_op jit(solution)/shard_map/pair_sum/pallas_call | solution.py:309
  310.9 3.3 weight_grad.6
  314.7 7.2 %attend_back.1 = (bf16[256,1024]{1,0:T(8,128)(2,1)}, f32[4,1,256]{2,1,0:T(1,128)}, f32[3,4,64,512]{3,2,1,0:T(8,128)}, bf16[4,64,512]{2,1,0:T(8,128)(2,1)}, bf16[...) custom-call(s32[1]{0:T(128)} %bitcast.4.place_ref, ...), custom_call_target="tpu_custom_call" | custom-call | tf_op jit(solution)/shard_map/attend_back/pallas_call | solution.py:687
  325.5 3.3 convert_add_fusion
  329.1 2.2 collective-permute-done.32
  331.3 4.5 collective-permute-done.33
  335.9 1.5 collective-permute-done.34
  337.4 1.5 fusion.6
  346.3 3.5 collective-permute-done.35
  350.5 3.1 collective-permute-done.36
  354.1 1.6 collective-permute-done.37
  357.1 6.4 %collective-permute-done.38 = bf16[4,64,512]{2,1,0:T(8,128)(2,1)S(1)} collective-permute-done((bf16[4,64,512]{2,1,0:T(8,128)(2,1)S(1)}, bf16[4,64,512]{2,1,0:T(8,128)(2,1)S(1)}, u32[]{:S(2)}, u32[]{:S(2)}) %collective-permute-start.38) | collective-permute-done | bytes 262176 | tf_op jit(solution)/shard_map/ppermute | solution.py:24
  363.5 1.9 fusion.10
  368.1 1.6 slice.191.refs_4_
  370.6 19.3 %collective-permute-done.39 = bf16[4,64,512]{2,1,0:T(8,128)(2,1)} collective-permute-done((bf16[4,64,512]{2,1,0:T(8,128)(2,1)}, bf16[4,64,512]{2,1,0:T(8,128)(2,1)}, u32[]{:S(2)}, u32[]{:S(2)}) %collective-permute-start.39) | collective-permute-done | bytes 262176 | tf_op jit(solution)/shard_map/ppermute | solution.py:24
  390.1 3.6 finish.1
  395.6 1.5 fusion.2
  397.1 4.0 weight_grad.7
  403.1 1.5 collective-permute-start.46
  405.4 3.1 collective-permute-done.45
  408.5 3.8 collective-permute-done.46
  413.3 4.2 all-to-all-start.1
  418.2 2.1 convert_bitcast_fusion
  423.1 14.4 %all-to-all-done.1 = bf16[4,147,640]{2,1,0:T(8,128)(2,1)} async-done(((bf16[4,147,640]{2,1,0:T(8,128)(2,1)}), bf16[4,147,640]{2,1,0:T(8,128)(2,1)}, u32[]{:S(2)}, u32[]{:S(2)}) %all-to-all-start.1) | async-done | bytes 752672 | tf_op jit(solution)/shard_map/all_to_all | solution.py:28
  439.0 1.5 collective-permute-start.50
  (334 shorter events, 98.5 us)
Async XLA Ops:
  7.2 185.7 %copy-start = (bf16[4,256,1152]{2,1,0:T(8,128)(2,1)S(1)}, bf16[4,256,1152]{2,1,0:T(8,128)(2,1)}, u32[]{:S(2)}) copy-start(bf16[4,256,1152]{2,1,0:T(8,128)(2,1)} %param.17) | copy-start | bytes 7077892
  7.2 36.9 %all-gather.3.cloned.1.call-start = ((), (), s32[]{:S(2)}) async-start(), calls=%async_computation.4 | async-start | bytes 1474560 | tf_op jit(solution)/shard_map/all_gather | solution.py:558
  9.2 156.1 %all-gather.5.cloned.1.call-start = ((), (), s32[]{:S(2)}) async-start(), calls=%async_computation.5 | async-start | bytes 13934592 | tf_op jit(solution)/shard_map/all_gather | solution.py:559
  14.2 12.8 %all-to-all-start = ((bf16[8,2,832]{2,1,0:T(2,128)(2,1)}), bf16[8,2,832]{2,1,0:T(2,128)(2,1)S(1)}, u32[]{:S(2)}, u32[]{:S(2)}) async-start(bf16[8,2,832]{2,1,0:T(2,128)(2,1)} %reshape.269), calls=%async_computation | async-start | bytes 57344 | tf_op jit(solution)/shard_map/all_to_all | solution.py:28
  20.5 397.7 %reduce-scatter.5.cloned.1.call-start = ((), (), s32[]{:S(2)}) async-start(), calls=%async_computation.7 | async-start | bytes 2580480 | tf_op jit(solution)/shard_map/reduce_scatter | solution.py:650
  32.2 93.3 %copy-start.40 = (f32[1,1152]{1,0:T(1,128)}, f32[1,1152]{1,0:T(1,128)S(1)}, u32[]{:S(2)}) copy-start(f32[1,1152]{1,0:T(1,128)S(1)} %reshape.218.gain_attn_ref) | copy-start | bytes 13828
  33.0 92.5 %copy-start.41 = (f32[1,1152]{1,0:T(1,128)}, f32[1,1152]{1,0:T(1,128)S(1)}, u32[]{:S(2)}) copy-start(f32[1,1152]{1,0:T(1,128)S(1)} %reshape.219.gain_ffn_ref) | copy-start | bytes 13828
  45.6 3.6 collective-permute-start.3
  45.7 17.2 %collective-permute-start.2 = (bf16[576,512]{1,0:T(8,128)(2,1)S(1)}, bf16[576,512]{1,0:T(8,128)(2,1)}, u32[]{:S(2)}, u32[]{:S(2)}) collective-permute-start(bf16[576,512]{1,0:T(8,128)(2,1)S(1)} %get-tuple-element.130.refs_0_), channel_id=1, source_target_pairs={{0,3},{1,2},{2,1},{3,0},{4,7},{5,6},{6,5},{7,4},{8,11},{9,10},{10,... | collective-permute-start | bytes 1769480 | tf_op jit(solution)/shard_map/ppermute | solution.py:19
  48.1 26.9 %collective-permute-start.1 = (bf16[576,512]{1,0:T(8,128)(2,1)S(1)}, bf16[576,512]{1,0:T(8,128)(2,1)}, u32[]{:S(2)}, u32[]{:S(2)}) collective-permute-start(bf16[576,512]{1,0:T(8,128)(2,1)S(1)} %get-tuple-element.130.refs_0_), channel_id=1, source_target_pairs={{0,2},{1,3},{2,0},{3,1},{4,6},{5,7},{6,4},{7,5},{8,10},{9,11},{10,... | collective-permute-start | bytes 1769480 | tf_op jit(solution)/shard_map/ppermute | solution.py:19
  48.7 26.4 %collective-permute-start = (bf16[576,512]{1,0:T(8,128)(2,1)S(1)}, bf16[576,512]{1,0:T(8,128)(2,1)}, u32[]{:S(2)}, u32[]{:S(2)}) collective-permute-start(bf16[576,512]{1,0:T(8,128)(2,1)S(1)} %get-tuple-element.130.refs_0_), channel_id=1, source_target_pairs={{0,1},{1,0},{2,3},{3,2},{4,5},{5,4},{6,7},{7,6},{8,9},{9,8},{10,11... | collective-permute-start | bytes 1769480 | tf_op jit(solution)/shard_map/ppermute | solution.py:19
  57.4 18.3 %collective-permute-start.8 = (bf16[4,64,512]{2,1,0:T(8,128)(2,1)S(1)}, bf16[4,64,512]{2,1,0:T(8,128)(2,1)}, u32[]{:S(2)}, u32[]{:S(2)}) collective-permute-start(bf16[4,64,512]{2,1,0:T(8,128)(2,1)S(1)} %get-tuple-element.129), channel_id=1, source_target_pairs={{0,4},{4,8},{8,12},{1,5},{5,9},{9,13},{2,6},{6,10},{10,14},{3,7},{... | collective-permute-start | bytes 786440 | tf_op jit(solution)/shard_map/ppermute | solution.py:24
  62.9 31.1 %collective-permute-start.7 = (bf16[576,512]{1,0:T(8,128)(2,1)}, bf16[576,512]{1,0:T(8,128)(2,1)}, u32[]{:S(2)}, u32[]{:S(2)}) collective-permute-start(bf16[576,512]{1,0:T(8,128)(2,1)} %collective-permute-done.2.refs_3_), channel_id=1, source_target_pairs={{0,16},{16,0},{1,17},{17,1},{2,18},{18,2},{3,19},{19,3},{4,20},{20... | collective-permute-start | bytes 1769480 | tf_op jit(solution)/shard_map/ppermute | solution.py:19
  75.1 20.4 %collective-permute-start.6 = (bf16[576,512]{1,0:T(8,128)(2,1)}, bf16[576,512]{1,0:T(8,128)(2,1)}, u32[]{:S(2)}, u32[]{:S(2)}) collective-permute-start(bf16[576,512]{1,0:T(8,128)(2,1)} %collective-permute-done.1.refs_2_), channel_id=1, source_target_pairs={{0,16},{16,0},{1,17},{17,1},{2,18},{18,2},{3,19},{19,3},{4,20},{20... | collective-permute-start | bytes 1769480 | tf_op jit(solution)/shard_map/ppermute | solution.py:19
  75.1 20.9 %collective-permute-start.5 = (bf16[576,512]{1,0:T(8,128)(2,1)}, bf16[576,512]{1,0:T(8,128)(2,1)}, u32[]{:S(2)}, u32[]{:S(2)}) collective-permute-start(bf16[576,512]{1,0:T(8,128)(2,1)} %collective-permute-done.refs_1_), channel_id=1, source_target_pairs={{0,16},{16,0},{1,17},{17,1},{2,18},{18,2},{3,19},{19,3},{4,20},{20... | collective-permute-start | bytes 1769480 | tf_op jit(solution)/shard_map/ppermute | solution.py:19
  75.6 21.9 %collective-permute-start.4 = (bf16[576,512]{1,0:T(8,128)(2,1)S(1)}, bf16[576,512]{1,0:T(8,128)(2,1)}, u32[]{:S(2)}, u32[]{:S(2)}) collective-permute-start(bf16[576,512]{1,0:T(8,128)(2,1)S(1)} %get-tuple-element.130.refs_0_), channel_id=1, source_target_pairs={{0,16},{16,0},{1,17},{17,1},{2,18},{18,2},{3,19},{19,3},{4,20},{20... | collective-permute-start | bytes 1769480 | tf_op jit(solution)/shard_map/ppermute | solution.py:19
  75.6 15.4 %collective-permute-start.12 = (bf16[4,64,512]{2,1,0:T(8,128)(2,1)}, bf16[4,64,512]{2,1,0:T(8,128)(2,1)}, u32[]{:S(2)}, u32[]{:S(2)}) collective-permute-start(bf16[4,64,512]{2,1,0:T(8,128)(2,1)} %collective-permute-done.8.refs_1_), channel_id=1, source_target_pairs={{0,4},{4,8},{8,12},{1,5},{5,9},{9,13},{2,6},{6,10},{10,14},{3,7},{... | collective-permute-start | bytes 786440 | tf_op jit(solution)/shard_map/ppermute | solution.py:24
  91.1 15.0 %collective-permute-start.10 = (bf16[4,64,512]{2,1,0:T(8,128)(2,1)}, bf16[4,64,512]{2,1,0:T(8,128)(2,1)}, u32[]{:S(2)}, u32[]{:S(2)}) collective-permute-start(bf16[4,64,512]{2,1,0:T(8,128)(2,1)} %collective-permute-done.8.refs_1_), channel_id=1, source_target_pairs={{0,2},{1,3},{2,0},{3,1},{4,6},{5,7},{6,4},{7,5},{8,10},{9,11},{10,... | collective-permute-start | bytes 786440 | tf_op jit(solution)/shard_map/ppermute | solution.py:19
  94.0 15.8 %collective-permute-start.11 = (bf16[4,64,512]{2,1,0:T(8,128)(2,1)}, bf16[4,64,512]{2,1,0:T(8,128)(2,1)S(1)}, u32[]{:S(2)}, u32[]{:S(2)}) collective-permute-start(bf16[4,64,512]{2,1,0:T(8,128)(2,1)} %collective-permute-done.8.refs_1_), channel_id=1, source_target_pairs={{0,3},{1,2},{2,1},{3,0},{4,7},{5,6},{6,5},{7,4},{8,11},{9,10},{10,... | collective-permute-start | bytes 786440 | tf_op jit(solution)/shard_map/ppermute | solution.py:19
  95.5 14.3 %collective-permute-start.9 = (bf16[4,64,512]{2,1,0:T(8,128)(2,1)}, bf16[4,64,512]{2,1,0:T(8,128)(2,1)S(1)}, u32[]{:S(2)}, u32[]{:S(2)}) collective-permute-start(bf16[4,64,512]{2,1,0:T(8,128)(2,1)} %collective-permute-done.8.refs_1_), channel_id=1, source_target_pairs={{0,1},{1,0},{2,3},{3,2},{4,5},{5,4},{6,7},{7,6},{8,9},{9,8},{10,11... | collective-permute-start | bytes 786440 | tf_op jit(solution)/shard_map/ppermute | solution.py:19
  96.0 18.7 %collective-permute-start.13 = (bf16[4,64,512]{2,1,0:T(8,128)(2,1)}, bf16[4,64,512]{2,1,0:T(8,128)(2,1)S(1)}, u32[]{:S(2)}, u32[]{:S(2)}) collective-permute-start(bf16[4,64,512]{2,1,0:T(8,128)(2,1)} %collective-permute-done.12.refs_5_), channel_id=1, source_target_pairs={{0,1},{1,0},{2,3},{3,2},{4,5},{5,4},{6,7},{7,6},{8,9},{9,8},{10,11... | collective-permute-start | bytes 786440 | tf_op jit(solution)/shard_map/ppermute | solution.py:19
  97.5 17.2 %collective-permute-start.14 = (bf16[4,64,512]{2,1,0:T(8,128)(2,1)}, bf16[4,64,512]{2,1,0:T(8,128)(2,1)S(1)}, u32[]{:S(2)}, u32[]{:S(2)}) collective-permute-start(bf16[4,64,512]{2,1,0:T(8,128)(2,1)} %collective-permute-done.12.refs_5_), channel_id=1, source_target_pairs={{0,2},{1,3},{2,0},{3,1},{4,6},{5,7},{6,4},{7,5},{8,10},{9,11},{10,... | collective-permute-start | bytes 786440 | tf_op jit(solution)/shard_map/ppermute | solution.py:19
  101.6 23.9 %copy-start.10 = (bf16[2,576,1024]{2,1,0:T(8,128)(2,1)}, bf16[2,576,1024]{2,1,0:T(8,128)(2,1)S(1)}, u32[]{:S(2)}) copy-start(bf16[2,576,1024]{2,1,0:T(8,128)(2,1)S(1)} %get-tuple-element.140) | copy-start | bytes 7077892
  106.1 12.8 %collective-permute-start.15 = (bf16[4,64,512]{2,1,0:T(8,128)(2,1)}, bf16[4,64,512]{2,1,0:T(8,128)(2,1)S(1)}, u32[]{:S(2)}, u32[]{:S(2)}) collective-permute-start(bf16[4,64,512]{2,1,0:T(8,128)(2,1)} %collective-permute-done.12.refs_5_), channel_id=1, source_target_pairs={{0,3},{1,2},{2,1},{3,0},{4,7},{5,6},{6,5},{7,4},{8,11},{9,10},{10,... | collective-permute-start | bytes 786440 | tf_op jit(solution)/shard_map/ppermute | solution.py:19
  128.8 50.3 %copy-start.28 = (bf16[256,1152]{1,0:T(8,128)(2,1)}, bf16[256,1152]{1,0:T(8,128)(2,1)S(1)}, u32[]{:S(2)}) copy-start(bf16[256,1152]{1,0:T(8,128)(2,1)S(1)} %get-tuple-element.173.refs_0_) | copy-start | bytes 1769476
  128.8 25.8 %collective-permute-start.18 = (bf16[256,1152]{1,0:T(8,128)(2,1)S(1)}, bf16[256,1152]{1,0:T(8,128)(2,1)S(1)}, u32[]{:S(2)}, u32[]{:S(2)}) collective-permute-start(bf16[256,1152]{1,0:T(8,128)(2,1)S(1)} %get-tuple-element.173.refs_0_), channel_id=1, source_target_pairs={{0,2},{1,3},{2,0},{3,1},{4,6},{5,7},{6,4},{7,5},{8,10},{9,11},{10,... | collective-permute-start | bytes 1769480 | tf_op jit(solution)/shard_map/ppermute | solution.py:19
  129.4 26.1 %collective-permute-start.19 = (bf16[256,1152]{1,0:T(8,128)(2,1)S(1)}, bf16[256,1152]{1,0:T(8,128)(2,1)}, u32[]{:S(2)}, u32[]{:S(2)}) collective-permute-start(bf16[256,1152]{1,0:T(8,128)(2,1)S(1)} %get-tuple-element.173.refs_0_), channel_id=1, source_target_pairs={{0,3},{1,2},{2,1},{3,0},{4,7},{5,6},{6,5},{7,4},{8,11},{9,10},{10,... | collective-permute-start | bytes 1769480 | tf_op jit(solution)/shard_map/ppermute | solution.py:19
  130.9 51.4 %collective-permute-start.16 = (bf16[256,1152]{1,0:T(8,128)(2,1)S(1)}, bf16[256,1152]{1,0:T(8,128)(2,1)}, u32[]{:S(2)}, u32[]{:S(2)}) collective-permute-start(bf16[256,1152]{1,0:T(8,128)(2,1)S(1)} %get-tuple-element.173.refs_0_), channel_id=1, source_target_pairs={{0,1},{1,0},{2,3},{3,2},{4,5},{5,4},{6,7},{7,6},{8,9},{9,8},{10,11... | collective-permute-start | bytes 1769480 | tf_op jit(solution)/shard_map/ppermute | solution.py:19
  179.1 28.3 %collective-permute-start.20 = (bf16[256,1152]{1,0:T(8,128)(2,1)}, bf16[256,1152]{1,0:T(8,128)(2,1)}, u32[]{:S(2)}, u32[]{:S(2)}) collective-permute-start(bf16[256,1152]{1,0:T(8,128)(2,1)} %get-tuple-element.148), channel_id=1, source_target_pairs={{0,2},{1,3},{2,0},{3,1},{4,6},{5,7},{6,4},{7,5},{8,10},{9,11},{10,... | collective-permute-start | bytes 1769480 | tf_op jit(solution)/shard_map/ppermute | solution.py:19
  180.9 26.5 %collective-permute-start.21 = (bf16[256,1152]{1,0:T(8,128)(2,1)}, bf16[256,1152]{1,0:T(8,128)(2,1)}, u32[]{:S(2)}, u32[]{:S(2)}) collective-permute-start(bf16[256,1152]{1,0:T(8,128)(2,1)} %get-tuple-element.149), channel_id=1, source_target_pairs={{0,3},{1,2},{2,1},{3,0},{4,7},{5,6},{6,5},{7,4},{8,11},{9,10},{10,... | collective-permute-start | bytes 1769480 | tf_op jit(solution)/shard_map/ppermute | solution.py:19
  191.8 16.7 %collective-permute-start.17 = (bf16[256,1152]{1,0:T(8,128)(2,1)}, bf16[256,1152]{1,0:T(8,128)(2,1)S(1)}, u32[]{:S(2)}, u32[]{:S(2)}) collective-permute-start(bf16[256,1152]{1,0:T(8,128)(2,1)} %get-tuple-element.147), channel_id=1, source_target_pairs={{0,1},{1,0},{2,3},{3,2},{4,5},{5,4},{6,7},{7,6},{8,9},{9,8},{10,11... | collective-permute-start | bytes 1769480 | tf_op jit(solution)/shard_map/ppermute | solution.py:19
  213.9 16.5 %collective-permute-start.23 = (bf16[256,1152]{1,0:T(8,128)(2,1)}, bf16[256,1152]{1,0:T(8,128)(2,1)S(1)}, u32[]{:S(2)}, u32[]{:S(2)}) collective-permute-start(bf16[256,1152]{1,0:T(8,128)(2,1)} %get-tuple-element.167.refs_0_), channel_id=1, source_target_pairs={{0,1},{1,0},{2,3},{3,2},{4,5},{5,4},{6,7},{7,6},{8,9},{9,8},{10,11... | collective-permute-start | bytes 1769480 | tf_op jit(solution)/shard_map/ppermute | solution.py:19
  215.4 26.6 %collective-permute-start.22 = (bf16[256,1152]{1,0:T(8,128)(2,1)}, bf16[256,1152]{1,0:T(8,128)(2,1)S(1)}, u32[]{:S(2)}, u32[]{:S(2)}) collective-permute-start(bf16[256,1152]{1,0:T(8,128)(2,1)} %get-tuple-element.167.refs_0_), channel_id=1, source_target_pairs={{0,2},{1,3},{2,0},{3,1},{4,6},{5,7},{6,4},{7,5},{8,10},{9,11},{10,... | collective-permute-start | bytes 1769480 | tf_op jit(solution)/shard_map/ppermute | solution.py:19
  216.9 25.1 %collective-permute-start.24 = (bf16[256,1152]{1,0:T(8,128)(2,1)}, bf16[256,1152]{1,0:T(8,128)(2,1)S(1)}, u32[]{:S(2)}, u32[]{:S(2)}) collective-permute-start(bf16[256,1152]{1,0:T(8,128)(2,1)} %get-tuple-element.167.refs_0_), channel_id=1, source_target_pairs={{0,3},{1,2},{2,1},{3,0},{4,7},{5,6},{6,5},{7,4},{8,11},{9,10},{10,... | collective-permute-start | bytes 1769480 | tf_op jit(solution)/shard_map/ppermute | solution.py:19
  267.9 4.3 collective-permute-start.25
  267.9 29.6 %collective-permute-start.28 = (bf16[256,1152]{1,0:T(8,128)(2,1)}, bf16[256,1152]{1,0:T(8,128)(2,1)}, u32[]{:S(2)}, u32[]{:S(2)}) collective-permute-start(bf16[256,1152]{1,0:T(8,128)(2,1)} %get-tuple-element.166), channel_id=1, source_target_pairs={{0,3},{1,2},{2,1},{3,0},{4,7},{5,6},{6,5},{7,4},{8,11},{9,10},{10,... | collective-permute-start | bytes 1769480 | tf_op jit(solution)/shard_map/ppermute | solution.py:19
  269.4 28.1 %collective-permute-start.26 = (bf16[256,1152]{1,0:T(8,128)(2,1)S(1)}, bf16[256,1152]{1,0:T(8,128)(2,1)}, u32[]{:S(2)}, u32[]{:S(2)}) collective-permute-start(bf16[256,1152]{1,0:T(8,128)(2,1)S(1)} %copy-done.71), channel_id=1, source_target_pairs={{0,1},{1,0},{2,3},{3,2},{4,5},{5,4},{6,7},{7,6},{8,9},{9,8},{10,11... | collective-permute-start | bytes 1769480 | tf_op jit(solution)/shard_map/ppermute | solution.py:19
  270.9 26.6 %collective-permute-start.27 = (bf16[256,1152]{1,0:T(8,128)(2,1)}, bf16[256,1152]{1,0:T(8,128)(2,1)}, u32[]{:S(2)}, u32[]{:S(2)}) collective-permute-start(bf16[256,1152]{1,0:T(8,128)(2,1)} %get-tuple-element.185), channel_id=1, source_target_pairs={{0,2},{1,3},{2,0},{3,1},{4,6},{5,7},{6,4},{7,5},{8,10},{9,11},{10,... | collective-permute-start | bytes 1769480 | tf_op jit(solution)/shard_map/ppermute | solution.py:19
  277.9 142.3 %reduce-scatter.3.cloned.1.call-start = ((), (), s32[]{:S(2)}) async-start(), calls=%async_computation.6 | async-start | bytes 5160960 | tf_op jit(solution)/shard_map/reduce_scatter | solution.py:650
  297.6 7.0 %collective-permute-start.30 = (bf16[576,1728]{1,0:T(8,128)(2,1)}, bf16[576,1728]{1,0:T(8,128)(2,1)}, u32[]{:S(2)}, u32[]{:S(2)}) collective-permute-start(bf16[576,1728]{1,0:T(8,128)(2,1)} %get-tuple-element.190), channel_id=1, source_target_pairs={{0,16},{16,0},{1,17},{17,1},{2,18},{18,2},{3,19},{19,3},{4,20},{20... | collective-permute-start | bytes 5971976 | tf_op jit(solution)/shard_map/ppermute | solution.py:19
  297.6 7.4 %collective-permute-start.29 = (bf16[576,1728]{1,0:T(8,128)(2,1)}, bf16[576,1728]{1,0:T(8,128)(2,1)}, u32[]{:S(2)}, u32[]{:S(2)}) collective-permute-start(bf16[576,1728]{1,0:T(8,128)(2,1)} %get-tuple-element.187), channel_id=1, source_target_pairs={{0,16},{16,0},{1,17},{17,1},{2,18},{18,2},{3,19},{19,3},{4,20},{20... | collective-permute-start | bytes 5971976 | tf_op jit(solution)/shard_map/ppermute | solution.py:19
  314.2 11.3 %collective-permute-start.31 = (bf16[576,1024]{1,0:T(8,128)(2,1)}, bf16[576,1024]{1,0:T(8,128)(2,1)}, u32[]{:S(2)}, u32[]{:S(2)}) collective-permute-start(bf16[576,1024]{1,0:T(8,128)(2,1)} %get-tuple-element.193), channel_id=1, source_target_pairs={{0,16},{16,0},{1,17},{17,1},{2,18},{18,2},{3,19},{19,3},{4,20},{20... | collective-permute-start | bytes 3538952 | tf_op jit(solution)/shard_map/ppermute | solution.py:19
  321.9 9.4 %collective-permute-start.32 = (bf16[4,64,512]{2,1,0:T(8,128)(2,1)}, bf16[4,64,512]{2,1,0:T(8,128)(2,1)S(1)}, u32[]{:S(2)}, u32[]{:S(2)}) collective-permute-start(bf16[4,64,512]{2,1,0:T(8,128)(2,1)} %get-tuple-element.199), channel_id=1, source_target_pairs={{0,1},{1,0},{2,3},{3,2},{4,5},{5,4},{6,7},{7,6},{8,9},{9,8},{10,11... | collective-permute-start | bytes 786440 | tf_op jit(solution)/shard_map/ppermute | solution.py:19
  322.9 12.9 %collective-permute-start.33 = (bf16[4,64,512]{2,1,0:T(8,128)(2,1)}, bf16[4,64,512]{2,1,0:T(8,128)(2,1)S(1)}, u32[]{:S(2)}, u32[]{:S(2)}) collective-permute-start(bf16[4,64,512]{2,1,0:T(8,128)(2,1)} %get-tuple-element.200), channel_id=1, source_target_pairs={{0,2},{1,3},{2,0},{3,1},{4,6},{5,7},{6,4},{7,5},{8,10},{9,11},{10,... | collective-permute-start | bytes 786440 | tf_op jit(solution)/shard_map/ppermute | solution.py:19
  324.0 13.4 %collective-permute-start.34 = (bf16[4,64,512]{2,1,0:T(8,128)(2,1)}, bf16[4,64,512]{2,1,0:T(8,128)(2,1)}, u32[]{:S(2)}, u32[]{:S(2)}) collective-permute-start(bf16[4,64,512]{2,1,0:T(8,128)(2,1)} %get-tuple-element.201), channel_id=1, source_target_pairs={{0,3},{1,2},{2,1},{3,0},{4,7},{5,6},{6,5},{7,4},{8,11},{9,10},{10,... | collective-permute-start | bytes 786440 | tf_op jit(solution)/shard_map/ppermute | solution.py:19
  329.1 41.5 %collective-permute-start.48 = (f32[4,465]{1,0:T(4,128)S(1)}, f32[4,465]{1,0:T(4,128)S(1)}, u32[]{:S(2)}, u32[]{:S(2)}) collective-permute-start(f32[4,465]{1,0:T(4,128)S(1)} %dynamic-slice_bitcast_fusion.4), channel_id=1, source_target_pairs={{0,16},{16,0},{1,17},{17,1},{2,18},{18,2},{3,19},{19,3},{4,20},{20... | collective-permute-start | bytes 22328 | tf_op jit(solution)/shard_map/ppermute | solution.py:19
  338.9 24.5 %collective-permute-start.38 = (bf16[4,64,512]{2,1,0:T(8,128)(2,1)S(1)}, bf16[4,64,512]{2,1,0:T(8,128)(2,1)S(1)}, u32[]{:S(2)}, u32[]{:S(2)}) collective-permute-start(bf16[4,64,512]{2,1,0:T(8,128)(2,1)S(1)} %get-tuple-element.236), channel_id=1, source_target_pairs={{4,0},{8,4},{12,8},{5,1},{9,5},{13,9},{6,2},{10,6},{14,10},{7,3},{... | collective-permute-start | bytes 786440 | tf_op jit(solution)/shard_map/ppermute | solution.py:24
  340.2 9.5 %collective-permute-start.35 = (bf16[1,4,64,512]{3,2,1,0:T(8,128)(2,1)}, bf16[1,4,64,512]{3,2,1,0:T(8,128)(2,1)S(1)}, u32[]{:S(2)}, u32[]{:S(2)}) collective-permute-start(bf16[1,4,64,512]{3,2,1,0:T(8,128)(2,1)} %get-tuple-element.202), channel_id=1, source_target_pairs={{0,1},{1,0},{2,3},{3,2},{4,5},{5,4},{6,7},{7,6},{8,9},{9,8},{10,11... | collective-permute-start | bytes 786440 | tf_op jit(solution)/shard_map/ppermute | solution.py:19
  341.1 12.5 %collective-permute-start.36 = (bf16[1,4,64,512]{3,2,1,0:T(8,128)(2,1)}, bf16[1,4,64,512]{3,2,1,0:T(8,128)(2,1)S(1)}, u32[]{:S(2)}, u32[]{:S(2)}) collective-permute-start(bf16[1,4,64,512]{3,2,1,0:T(8,128)(2,1)} %get-tuple-element.204), channel_id=1, source_target_pairs={{0,2},{1,3},{2,0},{3,1},{4,6},{5,7},{6,4},{7,5},{8,10},{9,11},{10,... | collective-permute-start | bytes 786440 | tf_op jit(solution)/shard_map/ppermute | solution.py:19
  342.5 13.2 %collective-permute-start.37 = (bf16[1,4,64,512]{3,2,1,0:T(8,128)(2,1)}, bf16[1,4,64,512]{3,2,1,0:T(8,128)(2,1)S(1)}, u32[]{:S(2)}, u32[]{:S(2)}) collective-permute-start(bf16[1,4,64,512]{3,2,1,0:T(8,128)(2,1)} %get-tuple-element.206), channel_id=1, source_target_pairs={{0,3},{1,2},{2,1},{3,0},{4,7},{5,6},{6,5},{7,4},{8,11},{9,10},{10,... | collective-permute-start | bytes 786440 | tf_op jit(solution)/shard_map/ppermute | solution.py:19
  349.7 45.9 %collective-permute-start.40 = (bf16[832,256]{1,0:T(8,128)(2,1)}, bf16[832,256]{1,0:T(8,128)(2,1)}, u32[]{:S(2)}, u32[]{:S(2)}) collective-permute-start(bf16[832,256]{1,0:T(8,128)(2,1)} %pad_maximum_fusion.3), channel_id=1, source_target_pairs={{0,1},{1,0},{2,3},{3,2},{4,5},{5,4},{6,7},{7,6},{8,9},{9,8},{10,11... | collective-permute-start | bytes 1277960 | tf_op jit(solution)/shard_map/ppermute | solution.py:19
  353.6 42.0 %collective-permute-start.41 = (bf16[832,256]{1,0:T(8,128)(2,1)}, bf16[832,256]{1,0:T(8,128)(2,1)}, u32[]{:S(2)}, u32[]{:S(2)}) collective-permute-start(bf16[832,256]{1,0:T(8,128)(2,1)} %pad_maximum_fusion.4), channel_id=1, source_target_pairs={{0,2},{1,3},{2,0},{3,1},{4,6},{5,7},{6,4},{7,5},{8,10},{9,11},{10,... | collective-permute-start | bytes 1277960 | tf_op jit(solution)/shard_map/ppermute | solution.py:19
  355.7 40.0 %collective-permute-start.42 = (bf16[832,256]{1,0:T(8,128)(2,1)}, bf16[832,256]{1,0:T(8,128)(2,1)}, u32[]{:S(2)}, u32[]{:S(2)}) collective-permute-start(bf16[832,256]{1,0:T(8,128)(2,1)} %pad_maximum_fusion.5), channel_id=1, source_target_pairs={{0,3},{1,2},{2,1},{3,0},{4,7},{5,6},{6,5},{7,4},{8,11},{9,10},{10,... | collective-permute-start | bytes 1277960 | tf_op jit(solution)/shard_map/ppermute | solution.py:19
  365.4 24.6 %collective-permute-start.39 = (bf16[4,64,512]{2,1,0:T(8,128)(2,1)}, bf16[4,64,512]{2,1,0:T(8,128)(2,1)}, u32[]{:S(2)}, u32[]{:S(2)}) collective-permute-start(bf16[4,64,512]{2,1,0:T(8,128)(2,1)} %fusion.10), channel_id=1, source_target_pairs={{4,0},{8,4},{12,8},{5,1},{9,5},{13,9},{6,2},{10,6},{14,10},{7,3},{... | collective-permute-start | bytes 786440 | tf_op jit(solution)/shard_map/ppermute | solution.py:24
  393.7 7.8 %collective-permute-start.44 = (bf16[576,512]{1,0:T(8,128)(2,1)S(1)}, bf16[576,512]{1,0:T(8,128)(2,1)S(1)}, u32[]{:S(2)}, u32[]{:S(2)}) collective-permute-start(bf16[576,512]{1,0:T(8,128)(2,1)S(1)} %get-tuple-element.218), channel_id=1, source_target_pairs={{0,16},{16,0},{1,17},{17,1},{2,18},{18,2},{3,19},{19,3},{4,20},{20... | collective-permute-start | bytes 1769480 | tf_op jit(solution)/shard_map/ppermute | solution.py:19
  395.1 6.1 %collective-permute-start.49 = (f32[4,176]{1,0:T(4,128)S(1)}, f32[4,176]{1,0:T(4,128)S(1)}, u32[]{:S(2)}, u32[]{:S(2)}) collective-permute-start(f32[4,176]{1,0:T(4,128)S(1)} %fusion.23), channel_id=1, source_target_pairs={{0,16},{16,0},{1,17},{17,1},{2,18},{18,2},{3,19},{19,3},{4,20},{20... | collective-permute-start | bytes 8456 | tf_op jit(solution)/shard_map/ppermute | solution.py:19
  401.2 4.1 collective-permute-start.43
  401.7 6.7 %collective-permute-start.45 = (bf16[576,128]{1,0:T(8,128)(2,1)S(1)}, bf16[576,128]{1,0:T(8,128)(2,1)S(1)}, u32[]{:S(2)}, u32[]{:S(2)}) collective-permute-start(bf16[576,128]{1,0:T(8,128)(2,1)S(1)} %get-tuple-element.247), channel_id=1, source_target_pairs={{0,1},{1,0},{2,3},{3,2},{4,5},{5,4},{6,7},{7,6},{8,9},{9,8},{10,11... | collective-permute-start | bytes 442376 | tf_op jit(solution)/shard_map/ppermute | solution.py:19
  403.1 9.1 %collective-permute-start.46 = (bf16[576,128]{1,0:T(8,128)(2,1)S(1)}, bf16[576,128]{1,0:T(8,128)(2,1)S(1)}, u32[]{:S(2)}, u32[]{:S(2)}) collective-permute-start(bf16[576,128]{1,0:T(8,128)(2,1)S(1)} %get-tuple-element.249), channel_id=1, source_target_pairs={{0,2},{1,3},{2,0},{3,1},{4,6},{5,7},{6,4},{7,5},{8,10},{9,11},{10,... | collective-permute-start | bytes 442376 | tf_op jit(solution)/shard_map/ppermute | solution.py:19
  404.6 7.6 %collective-permute-start.47 = (bf16[576,128]{1,0:T(8,128)(2,1)S(1)}, bf16[576,128]{1,0:T(8,128)(2,1)S(1)}, u32[]{:S(2)}, u32[]{:S(2)}) collective-permute-start(bf16[576,128]{1,0:T(8,128)(2,1)S(1)} %get-tuple-element.248), channel_id=1, source_target_pairs={{0,3},{1,2},{2,1},{3,0},{4,7},{5,6},{6,5},{7,4},{8,11},{9,10},{10,... | collective-permute-start | bytes 442376 | tf_op jit(solution)/shard_map/ppermute | solution.py:19
  413.3 24.2 %all-to-all-start.1 = ((bf16[4,147,640]{2,1,0:T(8,128)(2,1)}), bf16[4,147,640]{2,1,0:T(8,128)(2,1)}, u32[]{:S(2)}, u32[]{:S(2)}) async-start(bf16[4,147,640]{2,1,0:T(8,128)(2,1)} %pad_maximum_fusion.1), calls=%async_computation.1 | async-start | bytes 1556480 | tf_op jit(solution)/shard_map/all_to_all | solution.py:28
  439.0 4.9 %collective-permute-start.50 = (f32[150,128]{1,0:T(8,128)S(1)}, f32[150,128]{1,0:T(8,128)S(1)}, u32[]{:S(2)}, u32[]{:S(2)}) collective-permute-start(f32[150,128]{1,0:T(8,128)S(1)} %get-tuple-element.262), channel_id=1, source_target_pairs={{0,1},{1,0},{2,3},{3,2},{4,5},{5,4},{6,7},{7,6},{8,9},{9,8},{10,11... | collective-permute-start | bytes 230408 | tf_op jit(solution)/shard_map/ppermute | solution.py:19
  440.6 4.6 collective-permute-start.51
  441.2 5.3 %collective-permute-start.52 = (f32[150,128]{1,0:T(8,128)S(1)}, f32[150,128]{1,0:T(8,128)S(1)}, u32[]{:S(2)}, u32[]{:S(2)}) collective-permute-start(f32[150,128]{1,0:T(8,128)S(1)} %get-tuple-element.262), channel_id=1, source_target_pairs={{0,3},{1,2},{2,1},{3,0},{4,7},{5,6},{6,5},{7,4},{8,11},{9,10},{10,... | collective-permute-start | bytes 230408 | tf_op jit(solution)/shard_map/ppermute | solution.py:19
  (67 other events, 495.2 us)
Sparse Core Ops, SparseCore 0:
  10.2 33.8 all-gather.2
  45.7 119.5 all-gather.4
  278.1 46.2 reduce-scatter.4
  326.7 86.1 reduce-scatter.2

commit v8 on v6

--- a/solution.py
+++ b/solution.py
@@ -280,7 +280,7 @@
     for part, at in ((d_keys, 0), (d_vals, width)):
         piece = lambda b, p: part[(b * chunks + p) * per : (b * chunks + p + 1) * per]
         for b in range(blocks):
-            own_ref[b, 0, :, at : at + width] = piece(b, 0)
+            own_ref[b, 0, :, at : at + width] = piece(b, 0).astype(LOW)
         for p in range(1, chunks):
             earlier = (place_ref[0] ^ p) < place_ref[0]
             for b in range(1, blocks - 1):
@@ -515,7 +515,7 @@
 def weight_grad(core, rows, lefts, *rights):
     chunks, sets = len(lefts), len(rights)
     widest = rights[0][0][0].shape[1]
-    step = 256 if sets > 1 or widest < 1024 else 512 if widest == 1024 else 896
+    step = 256 if sets > 1 or widest < 1024 else 1024 if widest == 1024 else 896
     height = lefts[0][0].shape[1]
     width = rights[0][0][0].shape[1]
     rights = [pair for group in rights for pair in group]
@@ -690,14 +690,14 @@
         + [pl.BlockSpec((halo + 1, 1, sub, 2 * head_width), lambda s: (0, s, 0, 0))]
         + [specs["far"]] * (T - 1)
         + [pl.BlockSpec((halo - 1, 1, sub, 2 * head_width), lambda s: (0, s, 0, 0))] * (T - 1),
-        out_shape=[struct((own, wide), LOW), struct((seqs, 1, head_width), F32), struct((halo + 1, seqs, sub, 2 * head_width), F32)]
+        out_shape=[struct((own, wide), LOW), struct((seqs, 1, head_width), F32), struct((halo + 1, seqs, sub, 2 * head_width), LOW)]
         + [struct((seqs, sub, 2 * head_width), LOW)] * (T - 1)
         + [struct((halo - 1, seqs, sub, 2 * head_width), LOW)] * (T - 1),
         compiler_params=ALL,
         name="attend_back",
     )(t.reshape(1), qinfo, kinfo, q_raw, g_query, cos_own, sin_own, q_rot, lse, d_attended, *kv_rows)
     d_own = after(d_pairs[0], out_low)
-    d_blocks = [d_own[b] for b in range(halo + 1)]
+    d_blocks = [d_own[b].astype(F32) for b in range(halo + 1)]
     for p in range(1, T):
         got = swap(d_pairs[p], "tp", p).astype(F32)
         later = (t ^ p) > t

time: 462 us -> 462 us (level)
  no operation moved by 1% of the time
where the time goes in v8:
time: 462 us; the launch traced here: 457 us
  waiting for transfers between devices  158 us (34%)
  Pallas kernels  141 us (31%)
  starting transfers between devices  65.1 us (14%)
  local copies, waits for them, and re-layouts  44.4 us (10%)
  other arithmetic  28.2 us (6%)
  between operations  18.2 us (4%)
    ppermute x49, waiting for transfers between devices, swap(): lax.ppermute(values, axis, [(i, i ^ bits) for i in range(lax.axis_size(ax...  93.1 us
    pallas_call x6, Pallas kernels, ffn_call(): pl.pallas_call(functools.partial(kernel, units, chunks), grid=(pl.cdiv(un...  64.9 us
    ppermute x49, starting transfers between devices, swap(): lax.ppermute(values, axis, [(i, i ^ bits) for i in range(lax.axis_size(ax...  44.3 us
    ppermute x4, waiting for transfers between devices, shifted(): lax.ppermute(values, axis, [(i, i + by) for i in range(size) if 0 <= i +...  37.3 us
    pallas_call x4, Pallas kernels, weight_grad(): pl.pallas_call(functools.partial(weight_grad_kernel, chunks, sets), grid=...  30.8 us
    unnamed x148, local copies, waits for them, and re-layouts  20 us
    all_to_all x2, waiting for transfers between devices, exchange(): return lax.all_to_all(values, axes, 0, 0, tiled=True)  14.3 us
    all_to_all x2, starting transfers between devices, exchange(): return lax.all_to_all(values, axes, 0, 0, tiled=True)  10.5 us
  transfers between devices with their start and end apart: 59, of which 31 were waited for; matrix products, arithmetic and copies ran while one was open for 11% of the time, Pallas kernels for 25%

profile of v8, /device:TPU:0, one launch (start us, length us, event | category | flops | bytes accessed | tf_op | source)
XLA Modules:
  0.0 457.0 jit_solution(5641529028365144868)
XLA Ops:
  9.3 2.6 pad_maximum_fusion
  14.7 6.3 %all-to-all-start = ((bf16[8,2,832]{2,1,0:T(2,128)(2,1)}), bf16[8,2,832]{2,1,0:T(2,128)(2,1)S(1)}, u32[]{:S(2)}, u32[]{:S(2)}) async-start(bf16[8,2,832]{2,1,0:T(2,128)(2,1)} %reshape.276), calls=%async_computation | async-start | bytes 57344 | tf_op jit(solution)/shard_map/all_to_all | solution.py:28
  36.2 1.7 copy-done.9
  41.1 3.0 all-gather.3.cloned.1.call-done
  45.7 2.4 collective-permute-start.2
  51.9 2.8 project_keys.1
  57.4 3.3 collective-permute-start.8
  60.6 2.3 collective-permute-done.2.refs_3_
  62.9 12.1 %collective-permute-done.1.refs_2_ = bf16[576,512]{1,0:T(8,128)(2,1)} collective-permute-done((bf16[576,512]{1,0:T(8,128)(2,1)S(1)}, bf16[576,512]{1,0:T(8,128)(2,1)}, u32[]{:S(2)}, u32[]{:S(2)}) %collective-permute-start.1) | collective-permute-done | bytes 589856 | tf_op jit(solution)/shard_map/ppermute | solution.py:19
  75.6 4.1 collective-permute-start.12
  79.7 11.3 %collective-permute-done.12.refs_5_ = bf16[4,64,512]{2,1,0:T(8,128)(2,1)} collective-permute-done((bf16[4,64,512]{2,1,0:T(8,128)(2,1)}, bf16[4,64,512]{2,1,0:T(8,128)(2,1)}, u32[]{:S(2)}, u32[]{:S(2)}) %collective-permute-start.12) | collective-permute-done | bytes 262176 | tf_op jit(solution)/shard_map/ppermute | solution.py:24
  98.7 2.8 assemble.1
  101.6 4.5 collective-permute-done.10.refs_3_
  106.1 1.6 collective-permute-start.15
  107.7 2.0 fusion.33.q_ref
  109.8 4.9 %collective-permute-done.13.refs_6_ = bf16[4,64,512]{2,1,0:T(8,128)(2,1)S(1)} collective-permute-done((bf16[4,64,512]{2,1,0:T(8,128)(2,1)}, bf16[4,64,512]{2,1,0:T(8,128)(2,1)S(1)}, u32[]{:S(2)}, u32[]{:S(2)}) %collective-permute-start.13) | collective-permute-done | bytes 262176 | tf_op jit(solution)/shard_map/ppermute | solution.py:19
  114.7 4.2 collective-permute-done.15.refs_8_
  118.9 4.9 %attend.1 = (bf16[256,1024]{1,0:T(8,128)(2,1)S(1)}, bf16[256,1024]{1,0:T(8,128)(2,1)S(1)}, f32[4,256,1]{2,1,0:T(8,128)S(1)}) custom-call(s32[4,64,2]{2,1,0:T(8,128)S(1)} %copy-done.18, s32[4,2,768]{2,1,0:T(2,128)S(1)} %copy-done.37, f32[256,1024]{1,0:T(8,128)S(1)} %fusion.33.q_ref, f32[1,256]{1,0:T(1,128)S(1)} %copy-done.42, f32[64,256]{1,0:T(8,128)S(1)} %copy-done.19, ...), custom_call_target="tpu_custom_call" | custom-call | flops 402653184 | bytes 4194304 | tf_op jit(solution)/shard_map/attend/pallas_call | solution.py:608
  129.4 1.5 collective-permute-start.19
  132.3 22.3 %collective-permute-done.18.refs_0_.refs_2_ = bf16[256,1152]{1,0:T(8,128)(2,1)S(1)} collective-permute-done((bf16[256,1152]{1,0:T(8,128)(2,1)S(1)}, bf16[256,1152]{1,0:T(8,128)(2,1)S(1)}, u32[]{:S(2)}, u32[]{:S(2)}) %collective-permute-start.18) | collective-permute-done | bytes 589856 | tf_op jit(solution)/shard_map/ppermute | solution.py:19
  155.5 9.9 %all-gather.5.cloned.1.call-done.refs_1_.refs_2_.refs_3_.refs_4_ = bf16[3,1152,1728]{2,1,0:T(8,128)(2,1)} async-done(((bf16[3,144,1728]{2,1,0:T(8,128)(2,1)}), bf16[3,1152,1728]{2,1,0:T(8,128)(2,1)}) %all-gather.5.cloned.1.call-update) | async-done | bytes 11943952 | tf_op jit(solution)/shard_map/all_gather | solution.py:557
  165.4 13.0 %ffn.5 = (bf16[256,1152]{1,0:T(8,128)(2,1)}, bf16[256,1152]{1,0:T(8,128)(2,1)}, bf16[512,1728]{1,0:T(8,128)(2,1)}, bf16[512,1728]{1,0:T(8,128)(2,1)}, bf16[512,1728]{1,0:T(8,128)(2,1)}) custom-call(bf16[256,1152]{1,0:T(8,128)(2,1)} %copy-done.49, bf16[256,1152]{1,0:T(8,128)(2,1)} %collective-permute-done.19.refs_1_.refs_3_, ...), custom_call_target="tpu_custom_call" | custom-call | flops 6115295232 | bytes 13123584 | tf_op jit(solution)/shard_map/ffn/pallas_call | solution.py:419
  178.4 1.8 collective-permute-start.20
  181.6 9.1 %ffn.4 = (bf16[256,1152]{1,0:T(8,128)(2,1)}, bf16[256,1728]{1,0:T(8,128)(2,1)}, bf16[256,1728]{1,0:T(8,128)(2,1)}, bf16[256,1728]{1,0:T(8,128)(2,1)}) custom-call(bf16[256,1152]{1,0:T(8,128)(2,1)} %collective-permute-done.16.refs_0_.refs_1_, bf16[3,1152,1728]{2,1,0:T(8,128)(2,1)} %all-gather.5.cloned.1.call-done.refs_1_.refs_2_.refs_3_.refs_4_, ...), custom_call_target="tpu_custom_call" | custom-call | flops 3057647616 | bytes 12533760 | tf_op jit(solution)/shard_map/ffn/pallas_call | solution.py:419
  194.1 9.4 %ffn.3 = (f32[256,1152]{1,0:T(8,128)}, bf16[256,1728]{1,0:T(8,128)(2,1)}, bf16[256,1728]{1,0:T(8,128)(2,1)}, bf16[256,1728]{1,0:T(8,128)(2,1)}) custom-call(bf16[256,1152]{1,0:T(8,128)(2,1)} %copy-done.28, bf16[3,1152,1728]{2,1,0:T(8,128)(2,1)} %all-gather.5.cloned.1.call-done.refs_1_.refs_2_.refs_3_.refs_4_, ...), custom_call_target="tpu_custom_call" | custom-call | flops 3057647616 | bytes 12533760 | tf_op jit(solution)/shard_map/ffn/pallas_call | solution.py:419
  203.5 3.1 collective-permute-done.20.refs_2_
  208.6 4.6 %loss.1 = (bf16[256,1152]{1,0:T(8,128)(2,1)}, f32[256,1152]{1,0:T(8,128)}, bf16[256,1152]{1,0:T(8,128)(2,1)}, f32[1,1152]{1,0:T(1,128)}, f32[1,128]{1,0:T(1,128)}) custom-call(f32[1]{0:T(128)} %bitcast.factor_ref, f32[256,1152]{1,0:T(8,128)} %copy-done.17, bf16[256,1152]{1,0:T(8,128)(2,1)} %bitcast.108, f32[256,1]{1,0:T(8,128)} %reshape.249.valid_ref, ...), custom_call_target="tpu_custom_call" | custom-call | flops 512 | bytes 5898240 | tf_op jit(solution)/shard_map/loss/pallas_call | solution.py:634
  213.2 1.5 collective-permute-start.23
  216.7 9.4 %ffn_back.3 = (f32[256,1152]{1,0:T(8,128)}, bf16[256,1728]{1,0:T(8,128)(2,1)}, bf16[256,1728]{1,0:T(8,128)(2,1)}) custom-call(bf16[256,1152]{1,0:T(8,128)(2,1)} %get-tuple-element.167.refs_0_, bf16[3,1152,1728]{2,1,0:T(8,128)(2,1)} %all-gather.5.cloned.1.call-done.refs_1_.refs_2_.refs_3_.refs_4_, ...), custom_call_target="tpu_custom_call" | custom-call | flops 3057647616 | bytes 14303232 | tf_op jit(solution)/shard_map/ffn_back/pallas_call | solution.py:419
  226.1 3.6 collective-permute-done.23.refs_0_.refs_1_
  230.5 9.1 %ffn_back.4 = (bf16[256,1152]{1,0:T(8,128)(2,1)}, bf16[256,1728]{1,0:T(8,128)(2,1)}, bf16[256,1728]{1,0:T(8,128)(2,1)}) custom-call(bf16[256,1152]{1,0:T(8,128)(2,1)} %copy-done.50, bf16[3,1152,1728]{2,1,0:T(8,128)(2,1)} %all-gather.5.cloned.1.call-done.refs_1_.refs_2_.refs_3_.refs_4_, ...), custom_call_target="tpu_custom_call" | custom-call | flops 3057647616 | bytes 14303232 | tf_op jit(solution)/shard_map/ffn_back/pallas_call | solution.py:419
  239.6 1.8 collective-permute-done.22.refs_0_.refs_2_
  242.4 15.0 %ffn_back.5 = (bf16[256,1152]{1,0:T(8,128)(2,1)}, bf16[256,1152]{1,0:T(8,128)(2,1)}, bf16[512,1728]{1,0:T(8,128)(2,1)}, bf16[512,1728]{1,0:T(8,128)(2,1)}) custom-call(bf16[256,1152]{1,0:T(8,128)(2,1)} %copy-done.51, bf16[256,1152]{1,0:T(8,128)(2,1)} %copy-done.52, bf16[3,1152,1728]{2,1,0:T(8,128)(2,1)} %all-gather.5.cloned.1.call-done.refs_1_.refs_2_.refs_3_.refs_4_, ...), custom_call_target="tpu_custom_call" | custom-call | flops 6115295232 | bytes 16662528 | tf_op jit(solution)/shard_map/ffn_back/pallas_call | solution.py:419
  257.4 9.4 %weight_grad.4 = (bf16[576,1728]{1,0:T(8,128)(2,1)}, bf16[576,1728]{1,0:T(8,128)(2,1)}) custom-call(s32[1]{0:T(128)} %bitcast.8.core_ref, bf16[256,1152]{1,0:T(8,128)(2,1)} %get-tuple-element.167.refs_0_, bf16[256,1152]{1,0:T(8,128)(2,1)} %copy-done.50, bf16[256,1152]{1,0:T(8,128)(2,1)} %copy-done.51, bf16[256,1152]{1,0:T(8,128)(2,1)} %copy-done.52, ...), custom_call_target="tpu_custom_call" | custom-call | flops 4076863488 | bytes 6340608 | tf_op jit(solution)/shard_map/weight_grad/pallas_call | solution.py:523
  266.8 1.5 collective-permute-start.28
  272.4 4.4 pair_sum.2
  276.8 14.1 %weight_grad.5 = (bf16[576,1728]{1,0:T(8,128)(2,1)}, bf16[576,1728]{1,0:T(8,128)(2,1)}, bf16[576,1728]{1,0:T(8,128)(2,1)}, bf16[576,1728]{1,0:T(8,128)(2,1)}) custom-call(s32[1]{0:T(128)} %bitcast.8.core_ref, bf16[256,1152]{1,0:T(8,128)(2,1)} %copy-done.28, bf16[256,1152]{1,0:T(8,128)(2,1)} %collective-permute-done.16.refs_0_.refs_1_, ...), custom_call_target="tpu_custom_call" | custom-call | flops 8153726976 | bytes 10321920 | tf_op jit(solution)/shard_map/weight_grad/pallas_call | solution.py:523
  290.9 5.4 %collective-permute-done.27.refs_2_ = bf16[256,1152]{1,0:T(8,128)(2,1)} collective-permute-done((bf16[256,1152]{1,0:T(8,128)(2,1)}, bf16[256,1152]{1,0:T(8,128)(2,1)}, u32[]{:S(2)}, u32[]{:S(2)}) %collective-permute-start.27) | collective-permute-done | bytes 589856 | tf_op jit(solution)/shard_map/ppermute | solution.py:19
  296.9 6.4 %middle.1 = (f32[256,1152]{1,0:T(8,128)}, bf16[256,1152]{1,0:T(8,128)(2,1)}, bf16[256,1024]{1,0:T(8,128)(2,1)}, f32[1,1152]{1,0:T(1,128)}, f32[1,1152]{1,0:T(1,128)}) custom-call(f32[256,1152]{1,0:T(8,128)} %get-tuple-element.153.dres_ref, f32[256,1152]{1,0:T(8,128)} %copy-done.17, f32[256,1152]{1,0:T(8,128)} %copy-done.45, bf16[1152,1024]{1,0:T(8,128)(2,1)} %bitcast.103, ...), custom_call_target="tpu_custom_call" | custom-call | flops 181193932800 | bytes 2359296 | tf_op jit(solution)/shard_map/middle/pallas_call | solution.py:669
  303.8 5.9 %pair_sum.3 = bf16[2,576,1728]{2,1,0:T(8,128)(2,1)} custom-call(bf16[576,1728]{1,0:T(8,128)(2,1)} %get-tuple-element.181.refs_0_, bf16[576,1728]{1,0:T(8,128)(2,1)} %collective-permute-done.29.refs_1_, bf16[576,1728]{1,0:T(8,128)(2,1)} %get-tuple-element.183.refs_2_, bf16[576,1728]{1,0:T(8,128)(2,1)} %collective-permute-done.30.refs_3_), custom_call_target="tpu_custom_call" | custom-call | tf_op jit(solution)/shard_map/pair_sum/pallas_call | solution.py:309
  309.8 3.3 weight_grad.6
  313.6 7.1 %attend_back.1 = (bf16[256,1024]{1,0:T(8,128)(2,1)}, f32[4,1,256]{2,1,0:T(1,128)}, bf16[3,4,64,512]{3,2,1,0:T(8,128)(2,1)}, bf16[4,64,512]{2,1,0:T(8,128)(2,1)},...) custom-call(s32[1]{0:T(128)} %bitcast.4.place_ref, ...), custom_call_target="tpu_custom_call" | custom-call | tf_op jit(solution)/shard_map/attend_back/pallas_call | solution.py:685
  324.3 3.3 convert_add_fusion
  327.9 2.2 collective-permute-done.32
  330.1 4.5 collective-permute-done.33
  334.6 1.5 collective-permute-done.34
  344.9 3.5 collective-permute-done.35
  349.1 3.1 collective-permute-done.36
  352.7 1.6 collective-permute-done.37
  355.7 6.4 %collective-permute-done.38 = bf16[4,64,512]{2,1,0:T(8,128)(2,1)S(1)} collective-permute-done((bf16[4,64,512]{2,1,0:T(8,128)(2,1)S(1)}, bf16[4,64,512]{2,1,0:T(8,128)(2,1)S(1)}, u32[]{:S(2)}, u32[]{:S(2)}) %collective-permute-start.38) | collective-permute-done | bytes 262176 | tf_op jit(solution)/shard_map/ppermute | solution.py:24
  362.1 1.8 fusion.10
  366.6 1.6 slice.191.refs_4_
  369.2 19.6 %collective-permute-done.39 = bf16[4,64,512]{2,1,0:T(8,128)(2,1)} collective-permute-done((bf16[4,64,512]{2,1,0:T(8,128)(2,1)}, bf16[4,64,512]{2,1,0:T(8,128)(2,1)}, u32[]{:S(2)}, u32[]{:S(2)}) %collective-permute-start.39) | collective-permute-done | bytes 262176 | tf_op jit(solution)/shard_map/ppermute | solution.py:24
  388.9 3.6 finish.1
  394.4 1.5 fusion.2
  395.9 4.0 weight_grad.7
  402.0 2.1 collective-permute-start.47
  404.2 3.1 collective-permute-done.45
  407.3 3.7 collective-permute-done.46
  412.1 4.2 all-to-all-start.1
  417.0 2.1 convert_bitcast_fusion
  421.8 14.3 %all-to-all-done.1 = bf16[4,147,640]{2,1,0:T(8,128)(2,1)} async-done(((bf16[4,147,640]{2,1,0:T(8,128)(2,1)}), bf16[4,147,640]{2,1,0:T(8,128)(2,1)}, u32[]{:S(2)}, u32[]{:S(2)}) %all-to-all-start.1) | async-done | bytes 752672 | tf_op jit(solution)/shard_map/all_to_all | solution.py:28
  438.0 1.9 collective-permute-start.51
  442.9 2.3 collective-permute-done.52
  (334 shorter events, 97.6 us)
Async XLA Ops:
  7.2 184.7 %copy-start = (bf16[4,256,1152]{2,1,0:T(8,128)(2,1)S(1)}, bf16[4,256,1152]{2,1,0:T(8,128)(2,1)}, u32[]{:S(2)}) copy-start(bf16[4,256,1152]{2,1,0:T(8,128)(2,1)} %param.17) | copy-start | bytes 7077892
  7.2 36.9 %all-gather.3.cloned.1.call-start = ((), (), s32[]{:S(2)}) async-start(), calls=%async_computation.4 | async-start | bytes 1474560 | tf_op jit(solution)/shard_map/all_gather | solution.py:556
  9.2 156.1 %all-gather.5.cloned.1.call-start = ((), (), s32[]{:S(2)}) async-start(), calls=%async_computation.5 | async-start | bytes 13934592 | tf_op jit(solution)/shard_map/all_gather | solution.py:557
  14.7 12.8 %all-to-all-start = ((bf16[8,2,832]{2,1,0:T(2,128)(2,1)}), bf16[8,2,832]{2,1,0:T(2,128)(2,1)S(1)}, u32[]{:S(2)}, u32[]{:S(2)}) async-start(bf16[8,2,832]{2,1,0:T(2,128)(2,1)} %reshape.276), calls=%async_computation | async-start | bytes 57344 | tf_op jit(solution)/shard_map/all_to_all | solution.py:28
  21.1 395.9 %reduce-scatter.5.cloned.1.call-start = ((), (), s32[]{:S(2)}) async-start(), calls=%async_computation.7 | async-start | bytes 2580480 | tf_op jit(solution)/shard_map/reduce_scatter | solution.py:648
  32.7 92.8 %copy-start.40 = (f32[1,1152]{1,0:T(1,128)}, f32[1,1152]{1,0:T(1,128)S(1)}, u32[]{:S(2)}) copy-start(f32[1,1152]{1,0:T(1,128)S(1)} %reshape.223.gain_attn_ref) | copy-start | bytes 13828
  33.5 92.0 %copy-start.41 = (f32[1,1152]{1,0:T(1,128)}, f32[1,1152]{1,0:T(1,128)S(1)}, u32[]{:S(2)}) copy-start(f32[1,1152]{1,0:T(1,128)S(1)} %reshape.224.gain_ffn_ref) | copy-start | bytes 13828
  45.6 3.6 collective-permute-start.3
  45.7 17.2 %collective-permute-start.2 = (bf16[576,512]{1,0:T(8,128)(2,1)S(1)}, bf16[576,512]{1,0:T(8,128)(2,1)}, u32[]{:S(2)}, u32[]{:S(2)}) collective-permute-start(bf16[576,512]{1,0:T(8,128)(2,1)S(1)} %get-tuple-element.130.refs_0_), channel_id=1, source_target_pairs={{0,3},{1,2},{2,1},{3,0},{4,7},{5,6},{6,5},{7,4},{8,11},{9,10},{10,... | collective-permute-start | bytes 1769480 | tf_op jit(solution)/shard_map/ppermute | solution.py:19
  48.1 26.9 %collective-permute-start.1 = (bf16[576,512]{1,0:T(8,128)(2,1)S(1)}, bf16[576,512]{1,0:T(8,128)(2,1)}, u32[]{:S(2)}, u32[]{:S(2)}) collective-permute-start(bf16[576,512]{1,0:T(8,128)(2,1)S(1)} %get-tuple-element.130.refs_0_), channel_id=1, source_target_pairs={{0,2},{1,3},{2,0},{3,1},{4,6},{5,7},{6,4},{7,5},{8,10},{9,11},{10,... | collective-permute-start | bytes 1769480 | tf_op jit(solution)/shard_map/ppermute | solution.py:19
  48.7 26.4 %collective-permute-start = (bf16[576,512]{1,0:T(8,128)(2,1)S(1)}, bf16[576,512]{1,0:T(8,128)(2,1)}, u32[]{:S(2)}, u32[]{:S(2)}) collective-permute-start(bf16[576,512]{1,0:T(8,128)(2,1)S(1)} %get-tuple-element.130.refs_0_), channel_id=1, source_target_pairs={{0,1},{1,0},{2,3},{3,2},{4,5},{5,4},{6,7},{7,6},{8,9},{9,8},{10,11... | collective-permute-start | bytes 1769480 | tf_op jit(solution)/shard_map/ppermute | solution.py:19
  57.4 18.3 %collective-permute-start.8 = (bf16[4,64,512]{2,1,0:T(8,128)(2,1)S(1)}, bf16[4,64,512]{2,1,0:T(8,128)(2,1)}, u32[]{:S(2)}, u32[]{:S(2)}) collective-permute-start(bf16[4,64,512]{2,1,0:T(8,128)(2,1)S(1)} %get-tuple-element.129), channel_id=1, source_target_pairs={{0,4},{4,8},{8,12},{1,5},{5,9},{9,13},{2,6},{6,10},{10,14},{3,7},{... | collective-permute-start | bytes 786440 | tf_op jit(solution)/shard_map/ppermute | solution.py:24
  62.9 31.1 %collective-permute-start.7 = (bf16[576,512]{1,0:T(8,128)(2,1)}, bf16[576,512]{1,0:T(8,128)(2,1)}, u32[]{:S(2)}, u32[]{:S(2)}) collective-permute-start(bf16[576,512]{1,0:T(8,128)(2,1)} %collective-permute-done.2.refs_3_), channel_id=1, source_target_pairs={{0,16},{16,0},{1,17},{17,1},{2,18},{18,2},{3,19},{19,3},{4,20},{20... | collective-permute-start | bytes 1769480 | tf_op jit(solution)/shard_map/ppermute | solution.py:19
  75.1 20.4 %collective-permute-start.6 = (bf16[576,512]{1,0:T(8,128)(2,1)}, bf16[576,512]{1,0:T(8,128)(2,1)}, u32[]{:S(2)}, u32[]{:S(2)}) collective-permute-start(bf16[576,512]{1,0:T(8,128)(2,1)} %collective-permute-done.1.refs_2_), channel_id=1, source_target_pairs={{0,16},{16,0},{1,17},{17,1},{2,18},{18,2},{3,19},{19,3},{4,20},{20... | collective-permute-start | bytes 1769480 | tf_op jit(solution)/shard_map/ppermute | solution.py:19
  75.1 20.9 %collective-permute-start.5 = (bf16[576,512]{1,0:T(8,128)(2,1)}, bf16[576,512]{1,0:T(8,128)(2,1)}, u32[]{:S(2)}, u32[]{:S(2)}) collective-permute-start(bf16[576,512]{1,0:T(8,128)(2,1)} %collective-permute-done.refs_1_), channel_id=1, source_target_pairs={{0,16},{16,0},{1,17},{17,1},{2,18},{18,2},{3,19},{19,3},{4,20},{20... | collective-permute-start | bytes 1769480 | tf_op jit(solution)/shard_map/ppermute | solution.py:19
  75.6 21.9 %collective-permute-start.4 = (bf16[576,512]{1,0:T(8,128)(2,1)S(1)}, bf16[576,512]{1,0:T(8,128)(2,1)}, u32[]{:S(2)}, u32[]{:S(2)}) collective-permute-start(bf16[576,512]{1,0:T(8,128)(2,1)S(1)} %get-tuple-element.130.refs_0_), channel_id=1, source_target_pairs={{0,16},{16,0},{1,17},{17,1},{2,18},{18,2},{3,19},{19,3},{4,20},{20... | collective-permute-start | bytes 1769480 | tf_op jit(solution)/shard_map/ppermute | solution.py:19
  75.6 15.4 %collective-permute-start.12 = (bf16[4,64,512]{2,1,0:T(8,128)(2,1)}, bf16[4,64,512]{2,1,0:T(8,128)(2,1)}, u32[]{:S(2)}, u32[]{:S(2)}) collective-permute-start(bf16[4,64,512]{2,1,0:T(8,128)(2,1)} %collective-permute-done.8.refs_1_), channel_id=1, source_target_pairs={{0,4},{4,8},{8,12},{1,5},{5,9},{9,13},{2,6},{6,10},{10,14},{3,7},{... | collective-permute-start | bytes 786440 | tf_op jit(solution)/shard_map/ppermute | solution.py:24
  91.1 15.0 %collective-permute-start.10 = (bf16[4,64,512]{2,1,0:T(8,128)(2,1)}, bf16[4,64,512]{2,1,0:T(8,128)(2,1)}, u32[]{:S(2)}, u32[]{:S(2)}) collective-permute-start(bf16[4,64,512]{2,1,0:T(8,128)(2,1)} %collective-permute-done.8.refs_1_), channel_id=1, source_target_pairs={{0,2},{1,3},{2,0},{3,1},{4,6},{5,7},{6,4},{7,5},{8,10},{9,11},{10,... | collective-permute-start | bytes 786440 | tf_op jit(solution)/shard_map/ppermute | solution.py:19
  94.0 15.7 %collective-permute-start.11 = (bf16[4,64,512]{2,1,0:T(8,128)(2,1)}, bf16[4,64,512]{2,1,0:T(8,128)(2,1)S(1)}, u32[]{:S(2)}, u32[]{:S(2)}) collective-permute-start(bf16[4,64,512]{2,1,0:T(8,128)(2,1)} %collective-permute-done.8.refs_1_), channel_id=1, source_target_pairs={{0,3},{1,2},{2,1},{3,0},{4,7},{5,6},{6,5},{7,4},{8,11},{9,10},{10,... | collective-permute-start | bytes 786440 | tf_op jit(solution)/shard_map/ppermute | solution.py:19
  95.4 14.3 %collective-permute-start.9 = (bf16[4,64,512]{2,1,0:T(8,128)(2,1)}, bf16[4,64,512]{2,1,0:T(8,128)(2,1)S(1)}, u32[]{:S(2)}, u32[]{:S(2)}) collective-permute-start(bf16[4,64,512]{2,1,0:T(8,128)(2,1)} %collective-permute-done.8.refs_1_), channel_id=1, source_target_pairs={{0,1},{1,0},{2,3},{3,2},{4,5},{5,4},{6,7},{7,6},{8,9},{9,8},{10,11... | collective-permute-start | bytes 786440 | tf_op jit(solution)/shard_map/ppermute | solution.py:19
  96.0 18.7 %collective-permute-start.13 = (bf16[4,64,512]{2,1,0:T(8,128)(2,1)}, bf16[4,64,512]{2,1,0:T(8,128)(2,1)S(1)}, u32[]{:S(2)}, u32[]{:S(2)}) collective-permute-start(bf16[4,64,512]{2,1,0:T(8,128)(2,1)} %collective-permute-done.12.refs_5_), channel_id=1, source_target_pairs={{0,1},{1,0},{2,3},{3,2},{4,5},{5,4},{6,7},{7,6},{8,9},{9,8},{10,11... | collective-permute-start | bytes 786440 | tf_op jit(solution)/shard_map/ppermute | solution.py:19
  97.5 17.2 %collective-permute-start.14 = (bf16[4,64,512]{2,1,0:T(8,128)(2,1)}, bf16[4,64,512]{2,1,0:T(8,128)(2,1)S(1)}, u32[]{:S(2)}, u32[]{:S(2)}) collective-permute-start(bf16[4,64,512]{2,1,0:T(8,128)(2,1)} %collective-permute-done.12.refs_5_), channel_id=1, source_target_pairs={{0,2},{1,3},{2,0},{3,1},{4,6},{5,7},{6,4},{7,5},{8,10},{9,11},{10,... | collective-permute-start | bytes 786440 | tf_op jit(solution)/shard_map/ppermute | solution.py:19
  101.6 23.9 %copy-start.10 = (bf16[2,576,1024]{2,1,0:T(8,128)(2,1)}, bf16[2,576,1024]{2,1,0:T(8,128)(2,1)S(1)}, u32[]{:S(2)}) copy-start(bf16[2,576,1024]{2,1,0:T(8,128)(2,1)S(1)} %get-tuple-element.140) | copy-start | bytes 7077892
  106.1 12.8 %collective-permute-start.15 = (bf16[4,64,512]{2,1,0:T(8,128)(2,1)}, bf16[4,64,512]{2,1,0:T(8,128)(2,1)S(1)}, u32[]{:S(2)}, u32[]{:S(2)}) collective-permute-start(bf16[4,64,512]{2,1,0:T(8,128)(2,1)} %collective-permute-done.12.refs_5_), channel_id=1, source_target_pairs={{0,3},{1,2},{2,1},{3,0},{4,7},{5,6},{6,5},{7,4},{8,11},{9,10},{10,... | collective-permute-start | bytes 786440 | tf_op jit(solution)/shard_map/ppermute | solution.py:19
  128.8 49.6 %copy-start.28 = (bf16[256,1152]{1,0:T(8,128)(2,1)}, bf16[256,1152]{1,0:T(8,128)(2,1)S(1)}, u32[]{:S(2)}) copy-start(bf16[256,1152]{1,0:T(8,128)(2,1)S(1)} %get-tuple-element.173.refs_0_) | copy-start | bytes 1769476
  128.8 25.8 %collective-permute-start.18 = (bf16[256,1152]{1,0:T(8,128)(2,1)S(1)}, bf16[256,1152]{1,0:T(8,128)(2,1)S(1)}, u32[]{:S(2)}, u32[]{:S(2)}) collective-permute-start(bf16[256,1152]{1,0:T(8,128)(2,1)S(1)} %get-tuple-element.173.refs_0_), channel_id=1, source_target_pairs={{0,2},{1,3},{2,0},{3,1},{4,6},{5,7},{6,4},{7,5},{8,10},{9,11},{10,... | collective-permute-start | bytes 1769480 | tf_op jit(solution)/shard_map/ppermute | solution.py:19
  129.4 26.1 %collective-permute-start.19 = (bf16[256,1152]{1,0:T(8,128)(2,1)S(1)}, bf16[256,1152]{1,0:T(8,128)(2,1)}, u32[]{:S(2)}, u32[]{:S(2)}) collective-permute-start(bf16[256,1152]{1,0:T(8,128)(2,1)S(1)} %get-tuple-element.173.refs_0_), channel_id=1, source_target_pairs={{0,3},{1,2},{2,1},{3,0},{4,7},{5,6},{6,5},{7,4},{8,11},{9,10},{10,... | collective-permute-start | bytes 1769480 | tf_op jit(solution)/shard_map/ppermute | solution.py:19
  130.9 50.7 %collective-permute-start.16 = (bf16[256,1152]{1,0:T(8,128)(2,1)S(1)}, bf16[256,1152]{1,0:T(8,128)(2,1)}, u32[]{:S(2)}, u32[]{:S(2)}) collective-permute-start(bf16[256,1152]{1,0:T(8,128)(2,1)S(1)} %get-tuple-element.173.refs_0_), channel_id=1, source_target_pairs={{0,1},{1,0},{2,3},{3,2},{4,5},{5,4},{6,7},{7,6},{8,9},{9,8},{10,11... | collective-permute-start | bytes 1769480 | tf_op jit(solution)/shard_map/ppermute | solution.py:19
  178.4 28.3 %collective-permute-start.20 = (bf16[256,1152]{1,0:T(8,128)(2,1)}, bf16[256,1152]{1,0:T(8,128)(2,1)}, u32[]{:S(2)}, u32[]{:S(2)}) collective-permute-start(bf16[256,1152]{1,0:T(8,128)(2,1)} %get-tuple-element.148), channel_id=1, source_target_pairs={{0,2},{1,3},{2,0},{3,1},{4,6},{5,7},{6,4},{7,5},{8,10},{9,11},{10,... | collective-permute-start | bytes 1769480 | tf_op jit(solution)/shard_map/ppermute | solution.py:19
  180.2 26.5 %collective-permute-start.21 = (bf16[256,1152]{1,0:T(8,128)(2,1)}, bf16[256,1152]{1,0:T(8,128)(2,1)}, u32[]{:S(2)}, u32[]{:S(2)}) collective-permute-start(bf16[256,1152]{1,0:T(8,128)(2,1)} %get-tuple-element.149), channel_id=1, source_target_pairs={{0,3},{1,2},{2,1},{3,0},{4,7},{5,6},{6,5},{7,4},{8,11},{9,10},{10,... | collective-permute-start | bytes 1769480 | tf_op jit(solution)/shard_map/ppermute | solution.py:19
  190.7 17.1 %collective-permute-start.17 = (bf16[256,1152]{1,0:T(8,128)(2,1)}, bf16[256,1152]{1,0:T(8,128)(2,1)S(1)}, u32[]{:S(2)}, u32[]{:S(2)}) collective-permute-start(bf16[256,1152]{1,0:T(8,128)(2,1)} %get-tuple-element.147), channel_id=1, source_target_pairs={{0,1},{1,0},{2,3},{3,2},{4,5},{5,4},{6,7},{7,6},{8,9},{9,8},{10,11... | collective-permute-start | bytes 1769480 | tf_op jit(solution)/shard_map/ppermute | solution.py:19
  213.2 16.5 %collective-permute-start.23 = (bf16[256,1152]{1,0:T(8,128)(2,1)}, bf16[256,1152]{1,0:T(8,128)(2,1)S(1)}, u32[]{:S(2)}, u32[]{:S(2)}) collective-permute-start(bf16[256,1152]{1,0:T(8,128)(2,1)} %get-tuple-element.167.refs_0_), channel_id=1, source_target_pairs={{0,1},{1,0},{2,3},{3,2},{4,5},{5,4},{6,7},{7,6},{8,9},{9,8},{10,11... | collective-permute-start | bytes 1769480 | tf_op jit(solution)/shard_map/ppermute | solution.py:19
  214.8 26.6 %collective-permute-start.22 = (bf16[256,1152]{1,0:T(8,128)(2,1)}, bf16[256,1152]{1,0:T(8,128)(2,1)S(1)}, u32[]{:S(2)}, u32[]{:S(2)}) collective-permute-start(bf16[256,1152]{1,0:T(8,128)(2,1)} %get-tuple-element.167.refs_0_), channel_id=1, source_target_pairs={{0,2},{1,3},{2,0},{3,1},{4,6},{5,7},{6,4},{7,5},{8,10},{9,11},{10,... | collective-permute-start | bytes 1769480 | tf_op jit(solution)/shard_map/ppermute | solution.py:19
  216.3 25.1 %collective-permute-start.24 = (bf16[256,1152]{1,0:T(8,128)(2,1)}, bf16[256,1152]{1,0:T(8,128)(2,1)S(1)}, u32[]{:S(2)}, u32[]{:S(2)}) collective-permute-start(bf16[256,1152]{1,0:T(8,128)(2,1)} %get-tuple-element.167.refs_0_), channel_id=1, source_target_pairs={{0,3},{1,2},{2,1},{3,0},{4,7},{5,6},{6,5},{7,4},{8,11},{9,10},{10,... | collective-permute-start | bytes 1769480 | tf_op jit(solution)/shard_map/ppermute | solution.py:19
  266.7 4.3 collective-permute-start.25
  266.8 29.6 %collective-permute-start.28 = (bf16[256,1152]{1,0:T(8,128)(2,1)}, bf16[256,1152]{1,0:T(8,128)(2,1)}, u32[]{:S(2)}, u32[]{:S(2)}) collective-permute-start(bf16[256,1152]{1,0:T(8,128)(2,1)} %get-tuple-element.166), channel_id=1, source_target_pairs={{0,3},{1,2},{2,1},{3,0},{4,7},{5,6},{6,5},{7,4},{8,11},{9,10},{10,... | collective-permute-start | bytes 1769480 | tf_op jit(solution)/shard_map/ppermute | solution.py:19
  268.3 28.1 %collective-permute-start.26 = (bf16[256,1152]{1,0:T(8,128)(2,1)S(1)}, bf16[256,1152]{1,0:T(8,128)(2,1)}, u32[]{:S(2)}, u32[]{:S(2)}) collective-permute-start(bf16[256,1152]{1,0:T(8,128)(2,1)S(1)} %copy-done.71), channel_id=1, source_target_pairs={{0,1},{1,0},{2,3},{3,2},{4,5},{5,4},{6,7},{7,6},{8,9},{9,8},{10,11... | collective-permute-start | bytes 1769480 | tf_op jit(solution)/shard_map/ppermute | solution.py:19
  269.8 26.6 %collective-permute-start.27 = (bf16[256,1152]{1,0:T(8,128)(2,1)}, bf16[256,1152]{1,0:T(8,128)(2,1)}, u32[]{:S(2)}, u32[]{:S(2)}) collective-permute-start(bf16[256,1152]{1,0:T(8,128)(2,1)} %get-tuple-element.185), channel_id=1, source_target_pairs={{0,2},{1,3},{2,0},{3,1},{4,6},{5,7},{6,4},{7,5},{8,10},{9,11},{10,... | collective-permute-start | bytes 1769480 | tf_op jit(solution)/shard_map/ppermute | solution.py:19
  276.8 142.3 %reduce-scatter.3.cloned.1.call-start = ((), (), s32[]{:S(2)}) async-start(), calls=%async_computation.6 | async-start | bytes 5160960 | tf_op jit(solution)/shard_map/reduce_scatter | solution.py:648
  296.4 7.0 %collective-permute-start.30 = (bf16[576,1728]{1,0:T(8,128)(2,1)}, bf16[576,1728]{1,0:T(8,128)(2,1)}, u32[]{:S(2)}, u32[]{:S(2)}) collective-permute-start(bf16[576,1728]{1,0:T(8,128)(2,1)} %get-tuple-element.190), channel_id=1, source_target_pairs={{0,16},{16,0},{1,17},{17,1},{2,18},{18,2},{3,19},{19,3},{4,20},{20... | collective-permute-start | bytes 5971976 | tf_op jit(solution)/shard_map/ppermute | solution.py:19
  296.4 7.4 %collective-permute-start.29 = (bf16[576,1728]{1,0:T(8,128)(2,1)}, bf16[576,1728]{1,0:T(8,128)(2,1)}, u32[]{:S(2)}, u32[]{:S(2)}) collective-permute-start(bf16[576,1728]{1,0:T(8,128)(2,1)} %get-tuple-element.187), channel_id=1, source_target_pairs={{0,16},{16,0},{1,17},{17,1},{2,18},{18,2},{3,19},{19,3},{4,20},{20... | collective-permute-start | bytes 5971976 | tf_op jit(solution)/shard_map/ppermute | solution.py:19
  313.1 11.2 %collective-permute-start.31 = (bf16[576,1024]{1,0:T(8,128)(2,1)}, bf16[576,1024]{1,0:T(8,128)(2,1)}, u32[]{:S(2)}, u32[]{:S(2)}) collective-permute-start(bf16[576,1024]{1,0:T(8,128)(2,1)} %get-tuple-element.193), channel_id=1, source_target_pairs={{0,16},{16,0},{1,17},{17,1},{2,18},{18,2},{3,19},{19,3},{4,20},{20... | collective-permute-start | bytes 3538952 | tf_op jit(solution)/shard_map/ppermute | solution.py:19
  320.7 9.4 %collective-permute-start.32 = (bf16[4,64,512]{2,1,0:T(8,128)(2,1)}, bf16[4,64,512]{2,1,0:T(8,128)(2,1)S(1)}, u32[]{:S(2)}, u32[]{:S(2)}) collective-permute-start(bf16[4,64,512]{2,1,0:T(8,128)(2,1)} %get-tuple-element.199), channel_id=1, source_target_pairs={{0,1},{1,0},{2,3},{3,2},{4,5},{5,4},{6,7},{7,6},{8,9},{9,8},{10,11... | collective-permute-start | bytes 786440 | tf_op jit(solution)/shard_map/ppermute | solution.py:19
  321.7 12.9 %collective-permute-start.33 = (bf16[4,64,512]{2,1,0:T(8,128)(2,1)}, bf16[4,64,512]{2,1,0:T(8,128)(2,1)S(1)}, u32[]{:S(2)}, u32[]{:S(2)}) collective-permute-start(bf16[4,64,512]{2,1,0:T(8,128)(2,1)} %get-tuple-element.200), channel_id=1, source_target_pairs={{0,2},{1,3},{2,0},{3,1},{4,6},{5,7},{6,4},{7,5},{8,10},{9,11},{10,... | collective-permute-start | bytes 786440 | tf_op jit(solution)/shard_map/ppermute | solution.py:19
  322.8 13.3 %collective-permute-start.34 = (bf16[4,64,512]{2,1,0:T(8,128)(2,1)}, bf16[4,64,512]{2,1,0:T(8,128)(2,1)}, u32[]{:S(2)}, u32[]{:S(2)}) collective-permute-start(bf16[4,64,512]{2,1,0:T(8,128)(2,1)} %get-tuple-element.201), channel_id=1, source_target_pairs={{0,3},{1,2},{2,1},{3,0},{4,7},{5,6},{6,5},{7,4},{8,11},{9,10},{10,... | collective-permute-start | bytes 786440 | tf_op jit(solution)/shard_map/ppermute | solution.py:19
  327.8 41.4 %collective-permute-start.48 = (f32[4,465]{1,0:T(4,128)S(1)}, f32[4,465]{1,0:T(4,128)S(1)}, u32[]{:S(2)}, u32[]{:S(2)}) collective-permute-start(f32[4,465]{1,0:T(4,128)S(1)} %dynamic-slice_bitcast_fusion.4), channel_id=1, source_target_pairs={{0,16},{16,0},{1,17},{17,1},{2,18},{18,2},{3,19},{19,3},{4,20},{20... | collective-permute-start | bytes 22328 | tf_op jit(solution)/shard_map/ppermute | solution.py:19
  337.5 24.5 %collective-permute-start.38 = (bf16[4,64,512]{2,1,0:T(8,128)(2,1)S(1)}, bf16[4,64,512]{2,1,0:T(8,128)(2,1)S(1)}, u32[]{:S(2)}, u32[]{:S(2)}) collective-permute-start(bf16[4,64,512]{2,1,0:T(8,128)(2,1)S(1)} %get-tuple-element.238), channel_id=1, source_target_pairs={{4,0},{8,4},{12,8},{5,1},{9,5},{13,9},{6,2},{10,6},{14,10},{7,3},{... | collective-permute-start | bytes 786440 | tf_op jit(solution)/shard_map/ppermute | solution.py:24
  338.8 9.5 %collective-permute-start.35 = (bf16[1,4,64,512]{3,2,1,0:T(8,128)(2,1)}, bf16[1,4,64,512]{3,2,1,0:T(8,128)(2,1)S(1)}, u32[]{:S(2)}, u32[]{:S(2)}) collective-permute-start(bf16[1,4,64,512]{3,2,1,0:T(8,128)(2,1)} %get-tuple-element.202), channel_id=1, source_target_pairs={{0,1},{1,0},{2,3},{3,2},{4,5},{5,4},{6,7},{7,6},{8,9},{9,8},{10,11... | collective-permute-start | bytes 786440 | tf_op jit(solution)/shard_map/ppermute | solution.py:19
  339.7 12.5 %collective-permute-start.36 = (bf16[1,4,64,512]{3,2,1,0:T(8,128)(2,1)}, bf16[1,4,64,512]{3,2,1,0:T(8,128)(2,1)S(1)}, u32[]{:S(2)}, u32[]{:S(2)}) collective-permute-start(bf16[1,4,64,512]{3,2,1,0:T(8,128)(2,1)} %get-tuple-element.204), channel_id=1, source_target_pairs={{0,2},{1,3},{2,0},{3,1},{4,6},{5,7},{6,4},{7,5},{8,10},{9,11},{10,... | collective-permute-start | bytes 786440 | tf_op jit(solution)/shard_map/ppermute | solution.py:19
  341.1 13.2 %collective-permute-start.37 = (bf16[1,4,64,512]{3,2,1,0:T(8,128)(2,1)}, bf16[1,4,64,512]{3,2,1,0:T(8,128)(2,1)S(1)}, u32[]{:S(2)}, u32[]{:S(2)}) collective-permute-start(bf16[1,4,64,512]{3,2,1,0:T(8,128)(2,1)} %get-tuple-element.206), channel_id=1, source_target_pairs={{0,3},{1,2},{2,1},{3,0},{4,7},{5,6},{6,5},{7,4},{8,11},{9,10},{10,... | collective-permute-start | bytes 786440 | tf_op jit(solution)/shard_map/ppermute | solution.py:19
  348.3 46.1 %collective-permute-start.40 = (bf16[832,256]{1,0:T(8,128)(2,1)}, bf16[832,256]{1,0:T(8,128)(2,1)}, u32[]{:S(2)}, u32[]{:S(2)}) collective-permute-start(bf16[832,256]{1,0:T(8,128)(2,1)} %pad_maximum_fusion.3), channel_id=1, source_target_pairs={{0,1},{1,0},{2,3},{3,2},{4,5},{5,4},{6,7},{7,6},{8,9},{9,8},{10,11... | collective-permute-start | bytes 1277960 | tf_op jit(solution)/shard_map/ppermute | solution.py:19
  352.2 42.2 %collective-permute-start.41 = (bf16[832,256]{1,0:T(8,128)(2,1)}, bf16[832,256]{1,0:T(8,128)(2,1)}, u32[]{:S(2)}, u32[]{:S(2)}) collective-permute-start(bf16[832,256]{1,0:T(8,128)(2,1)} %pad_maximum_fusion.4), channel_id=1, source_target_pairs={{0,2},{1,3},{2,0},{3,1},{4,6},{5,7},{6,4},{7,5},{8,10},{9,11},{10,... | collective-permute-start | bytes 1277960 | tf_op jit(solution)/shard_map/ppermute | solution.py:19
  354.3 40.1 %collective-permute-start.42 = (bf16[832,256]{1,0:T(8,128)(2,1)}, bf16[832,256]{1,0:T(8,128)(2,1)}, u32[]{:S(2)}, u32[]{:S(2)}) collective-permute-start(bf16[832,256]{1,0:T(8,128)(2,1)} %pad_maximum_fusion.5), channel_id=1, source_target_pairs={{0,3},{1,2},{2,1},{3,0},{4,7},{5,6},{6,5},{7,4},{8,11},{9,10},{10,... | collective-permute-start | bytes 1277960 | tf_op jit(solution)/shard_map/ppermute | solution.py:19
  363.9 24.9 %collective-permute-start.39 = (bf16[4,64,512]{2,1,0:T(8,128)(2,1)}, bf16[4,64,512]{2,1,0:T(8,128)(2,1)}, u32[]{:S(2)}, u32[]{:S(2)}) collective-permute-start(bf16[4,64,512]{2,1,0:T(8,128)(2,1)} %fusion.10), channel_id=1, source_target_pairs={{4,0},{8,4},{12,8},{5,1},{9,5},{13,9},{6,2},{10,6},{14,10},{7,3},{... | collective-permute-start | bytes 786440 | tf_op jit(solution)/shard_map/ppermute | solution.py:24
  392.5 7.8 %collective-permute-start.44 = (bf16[576,512]{1,0:T(8,128)(2,1)S(1)}, bf16[576,512]{1,0:T(8,128)(2,1)S(1)}, u32[]{:S(2)}, u32[]{:S(2)}) collective-permute-start(bf16[576,512]{1,0:T(8,128)(2,1)S(1)} %get-tuple-element.218), channel_id=1, source_target_pairs={{0,16},{16,0},{1,17},{17,1},{2,18},{18,2},{3,19},{19,3},{4,20},{20... | collective-permute-start | bytes 1769480 | tf_op jit(solution)/shard_map/ppermute | solution.py:19
  393.9 6.1 %collective-permute-start.49 = (f32[4,176]{1,0:T(4,128)S(1)}, f32[4,176]{1,0:T(4,128)S(1)}, u32[]{:S(2)}, u32[]{:S(2)}) collective-permute-start(f32[4,176]{1,0:T(4,128)S(1)} %fusion.23), channel_id=1, source_target_pairs={{0,16},{16,0},{1,17},{17,1},{2,18},{18,2},{3,19},{19,3},{4,20},{20... | collective-permute-start | bytes 8456 | tf_op jit(solution)/shard_map/ppermute | solution.py:19
  399.9 4.2 collective-permute-start.43
  400.6 6.7 %collective-permute-start.45 = (bf16[576,128]{1,0:T(8,128)(2,1)S(1)}, bf16[576,128]{1,0:T(8,128)(2,1)S(1)}, u32[]{:S(2)}, u32[]{:S(2)}) collective-permute-start(bf16[576,128]{1,0:T(8,128)(2,1)S(1)} %get-tuple-element.247), channel_id=1, source_target_pairs={{0,1},{1,0},{2,3},{3,2},{4,5},{5,4},{6,7},{7,6},{8,9},{9,8},{10,11... | collective-permute-start | bytes 442376 | tf_op jit(solution)/shard_map/ppermute | solution.py:19
  401.9 9.1 %collective-permute-start.46 = (bf16[576,128]{1,0:T(8,128)(2,1)S(1)}, bf16[576,128]{1,0:T(8,128)(2,1)S(1)}, u32[]{:S(2)}, u32[]{:S(2)}) collective-permute-start(bf16[576,128]{1,0:T(8,128)(2,1)S(1)} %get-tuple-element.249), channel_id=1, source_target_pairs={{0,2},{1,3},{2,0},{3,1},{4,6},{5,7},{6,4},{7,5},{8,10},{9,11},{10,... | collective-permute-start | bytes 442376 | tf_op jit(solution)/shard_map/ppermute | solution.py:19
  402.0 9.0 %collective-permute-start.47 = (bf16[576,128]{1,0:T(8,128)(2,1)S(1)}, bf16[576,128]{1,0:T(8,128)(2,1)S(1)}, u32[]{:S(2)}, u32[]{:S(2)}) collective-permute-start(bf16[576,128]{1,0:T(8,128)(2,1)S(1)} %get-tuple-element.248), channel_id=1, source_target_pairs={{0,3},{1,2},{2,1},{3,0},{4,7},{5,6},{6,5},{7,4},{8,11},{9,10},{10,... | collective-permute-start | bytes 442376 | tf_op jit(solution)/shard_map/ppermute | solution.py:19
  412.1 24.1 %all-to-all-start.1 = ((bf16[4,147,640]{2,1,0:T(8,128)(2,1)}), bf16[4,147,640]{2,1,0:T(8,128)(2,1)}, u32[]{:S(2)}, u32[]{:S(2)}) async-start(bf16[4,147,640]{2,1,0:T(8,128)(2,1)} %pad_maximum_fusion.1), calls=%async_computation.1 | async-start | bytes 1556480 | tf_op jit(solution)/shard_map/all_to_all | solution.py:28
  437.8 4.6 %collective-permute-start.50 = (f32[150,128]{1,0:T(8,128)S(1)}, f32[150,128]{1,0:T(8,128)S(1)}, u32[]{:S(2)}, u32[]{:S(2)}) collective-permute-start(f32[150,128]{1,0:T(8,128)S(1)} %get-tuple-element.262), channel_id=1, source_target_pairs={{0,1},{1,0},{2,3},{3,2},{4,5},{5,4},{6,7},{7,6},{8,9},{9,8},{10,11... | collective-permute-start | bytes 230408 | tf_op jit(solution)/shard_map/ppermute | solution.py:19
  438.0 4.9 %collective-permute-start.51 = (f32[150,128]{1,0:T(8,128)S(1)}, f32[150,128]{1,0:T(8,128)S(1)}, u32[]{:S(2)}, u32[]{:S(2)}) collective-permute-start(f32[150,128]{1,0:T(8,128)S(1)} %get-tuple-element.262), channel_id=1, source_target_pairs={{0,2},{1,3},{2,0},{3,1},{4,6},{5,7},{6,4},{7,5},{8,10},{9,11},{10,... | collective-permute-start | bytes 230408 | tf_op jit(solution)/shard_map/ppermute | solution.py:19
  439.9 5.3 %collective-permute-start.52 = (f32[150,128]{1,0:T(8,128)S(1)}, f32[150,128]{1,0:T(8,128)S(1)}, u32[]{:S(2)}, u32[]{:S(2)}) collective-permute-start(f32[150,128]{1,0:T(8,128)S(1)} %get-tuple-element.262), channel_id=1, source_target_pairs={{0,3},{1,2},{2,1},{3,0},{4,7},{5,6},{6,5},{7,4},{8,11},{9,10},{10,... | collective-permute-start | bytes 230408 | tf_op jit(solution)/shard_map/ppermute | solution.py:19
  (67 other events, 483.8 us)
Sparse Core Ops, SparseCore 0:
  10.2 33.8 all-gather.2
  45.7 119.5 all-gather.4
  276.9 46.3 reduce-scatter.4
  325.6 86.1 reduce-scatter.2
